TPU v7x, 128 devices: a whole 4x4x4 slice. The times are simulated.
128 devices in a mesh: img: 16 (over z, y), txt: 8 (over x, core).
Axes of the slice: x: 4, y: 4, z: 4, core: 2. Of those that a mesh axis runs over, the one named last changes fastest.
Arguments:
- image_emb: bfloat16 [24576, 512], P(('img', 'txt')), may hold values from -8 to 8, as said below
- text_emb: bfloat16 [24576, 512], P(('img', 'txt')), may hold values from -8 to 8
Outputs:
- loss: float32 [], replicated
- grad_image: float32 [24576, 512], P(('img', 'txt'))
- grad_text: float32 [24576, 512], P(('img', 'txt'))
Inputs may be any that keep to these rules, and one draw needn't show every extreme that they name: `image_emb`: image row k is, for most k, correlated with text row k.
All inputs are finite; a program needn't handle non-finite values.
Results may differ from a plain program's by a relative error of at most 0.004.
Values may be sent and summed in bfloat16 or wider, within the bound.
No kernel may reach another device: no remote copies, remote signals or barrier semaphores. Data moves between devices by JAX's collectives and lax.ppermute only.
A program may use at most 128 MiB of HBM per device.

v0:
```python
import math

import jax
import jax.numpy as jnp
from jax import lax
from jax.sharding import PartitionSpec as P

logit_scale = 10.0


def per_device(image_emb, text_emb):
    pair_rows = image_emb.shape[0]
    img_count = lax.axis_size("img")
    txt_count = lax.axis_size("txt")
    img_index = lax.axis_index("img")
    txt_index = lax.axis_index("txt")
    image_block = lax.all_gather(image_emb, "txt", axis=0, tiled=True)
    text_block = lax.all_gather(text_emb, "img", axis=0, tiled=True)
    image_local = jnp.arange(image_block.shape[0], dtype=jnp.int32)
    row_ids = img_index * txt_count * pair_rows + image_local
    text_local = jnp.arange(text_block.shape[0], dtype=jnp.int32)
    columns = (text_local // pair_rows * txt_count + txt_index) * pair_rows + text_local % pair_rows
    image_count = image_block.shape[0]
    text_count = text_block.shape[0]
    block_rows = math.gcd(image_count, 512)
    block_count = image_count // block_rows

    def block_parts(block_index):
        block_start = block_index * block_rows
        chosen = lax.dynamic_slice_in_dim(image_block, block_start, block_rows, 0)
        chosen_ids = lax.dynamic_slice_in_dim(row_ids, block_start, block_rows, 0)
        is_positive = chosen_ids[:, None] == columns[None, :]
        return (chosen, is_positive)

    def tile_logits(chosen):
        return logit_scale * lax.dot_general(
            chosen, text_block, (((1,), (1,)), ((), ())), preferred_element_type=jnp.float32
        )

    def forward(running, block_index):
        col_max, col_sum, diag_sum = running
        chosen, is_positive = block_parts(block_index)
        logits = tile_logits(chosen)
        row_max = jnp.max(logits, axis=1)
        row_sum = jnp.sum(jnp.exp(logits - row_max[:, None]), axis=1)
        new_max = jnp.maximum(col_max, jnp.max(logits, axis=0))
        col_sum = col_sum * jnp.exp(col_max - new_max) + jnp.sum(
            jnp.exp(logits - new_max[None, :]), axis=0
        )
        diag_sum = diag_sum + jnp.sum(jnp.where(is_positive, logits, 0.0))
        return ((new_max, col_sum, diag_sum), (row_max, row_sum))

    initial = (
        jnp.full((text_count,), -jnp.inf, jnp.float32),
        jnp.zeros((text_count,), jnp.float32),
        jnp.zeros((), jnp.float32),
    )
    block_ids = jnp.arange(block_count, dtype=jnp.int32)
    (col_max, col_sum, diag_sum), per_block = lax.scan(forward, initial, block_ids)
    row_max = per_block[0].reshape(image_count)
    row_sum = per_block[1].reshape(image_count)
    row_top = lax.pmax(row_max, "txt")
    row_total = lax.psum(row_sum * jnp.exp(row_max - row_top), "txt")
    col_top = lax.pmax(col_max, "img")
    col_total = lax.psum(col_sum * jnp.exp(col_max - col_top), "img")
    row_lse = row_top + jnp.log(row_total)
    col_lse = col_top + jnp.log(col_total)
    local_part = jnp.sum(row_lse) / txt_count + jnp.sum(col_lse) / img_count - 2.0 * diag_sum
    summed = lax.psum(local_part, ("img", "txt"))
    loss = 0.5 * summed / (pair_rows * img_count * txt_count)

    def backward(text_grad, inputs):
        chosen, is_positive = block_parts(inputs)
        logits = tile_logits(chosen)
        lse_rows = lax.dynamic_slice_in_dim(row_lse, inputs * block_rows, block_rows, 0)
        coeffs = 0.5 * (
            jnp.exp(logits - lse_rows[:, None]) + jnp.exp(logits - col_lse[None, :])
        ) - is_positive.astype(jnp.float32)
        coeffs = coeffs.astype(jnp.bfloat16)
        image_grad = logit_scale * jnp.dot(coeffs, text_block, preferred_element_type=jnp.float32)
        text_grad = text_grad + logit_scale * lax.dot_general(
            coeffs, chosen, (((0,), (0,)), ((), ())), preferred_element_type=jnp.float32
        )
        return (text_grad, image_grad)

    width = text_block.shape[1]
    text_partial, image_partial = lax.scan(
        backward, jnp.zeros((text_count, width), jnp.float32), block_ids
    )
    image_partial = image_partial.reshape(image_count, width)
    grad_image = lax.psum_scatter(image_partial, "txt", scatter_dimension=0, tiled=True)
    grad_text = lax.psum_scatter(text_partial, "img", scatter_dimension=0, tiled=True)
    return (loss, grad_image, grad_text)


def solution(mesh):
    return jax.shard_map(
        per_device,
        mesh=mesh,
        in_specs=(P(("img", "txt"), None), P(("img", "txt"), None)),
        out_specs=(P(), P(("img", "txt"), None), P(("img", "txt"), None)),
        check_vma=False,
    )
```

profile of v0, /device:TPU:1, one launch (start us, length us, event | category | flops | bytes accessed | tf_op | source)
XLA Modules:
  0.0 459.7 jit_solution(17307661290208264671)
XLA Ops:
  7.2 0.7 all-gather.3.cloned.1.call-update
  7.9 0.7 all-gather.5.cloned.1.call-update
  8.8 29.0 %all-gather.3.cloned.1.call-done = bf16[1536,512]{1,0:T(8,128)(2,1)} async-done(((bf16[192,512]{1,0:T(8,128)(2,1)}), bf16[1536,512]{1,0:T(8,128)(2,1)}) %all-gather.3.cloned.1.call-update) | async-done | bytes 1572880 | tf_op jit(solution)/shard_map/all_gather | solution.py:17
  37.8 49.8 %all-gather.5.cloned.1.call-done = bf16[3072,512]{1,0:T(8,128)(2,1)} async-done(((bf16[192,512]{1,0:T(8,128)(2,1)}), bf16[3072,512]{1,0:T(8,128)(2,1)}) %all-gather.5.cloned.1.call-update) | async-done | bytes 3145744 | tf_op jit(solution)/shard_map/all_gather | solution.py:18
  87.6 31.1 %while.32 = (s32[]{:T(128)}, f32[3072]{0:T(1024)S(1)}, f32[3072]{0:T(1024)S(1)}, f32[]{:T(128)}, f32[3,512]{1,0:T(4,128)S(1)}, /*index=5*/f32[3,512]{1,0:T(4,128...) while((s32[]{:T(128)}, f32[3072]{0:T(1024)S(1)}, ...), condition=%wide.region_6.7_spmd.clone, body=%wide.region_0.6_spmd.clone.sunk | while | flops 1626404864 | bytes 16457982 | solution.py:59
  87.6 0.6 dynamic_slice.46
  88.9 0.1 dynamic_slice.47
  89.0 4.0 fusion.56
  93.0 4.2 exponential_reduce_fusion.3
  98.0 0.6 dynamic_slice.46
  99.2 0.1 dynamic_slice.47
  99.3 4.0 fusion.56
  103.3 4.2 exponential_reduce_fusion.3
  108.4 0.6 dynamic_slice.46
  109.6 0.1 dynamic_slice.47
  109.7 4.0 fusion.56
  113.7 4.2 exponential_reduce_fusion.3
  118.7 13.0 %pmax.14 = f32[1536]{0:T(1024)S(1)} all-reduce(f32[1536]{0:T(1024)S(1)} %reshape.27), channel_id=1, replica_groups=mesh['img'=16,'txt'=8] {'txt'}, use_global_device_ids=true, to_apply=%region_7.8 | all-reduce | flops 1536 | bytes 12288 | tf_op jit(solution)/shard_map/pmax | solution.py:62
  131.7 14.5 %psum.21 = f32[1536]{0:T(1024)S(1)} all-reduce(f32[1536]{0:T(1024)S(1)} %exponential_multiply_fusion.1), channel_id=1, replica_groups=mesh['img'=16,'txt'=8] {'txt'}, use_global_device_ids=true, to_apply=%region_8.9 | all-reduce | flops 1536 | bytes 12288 | tf_op jit(solution)/shard_map/psum | solution.py:63
  146.2 0.6 fusion.37
  146.8 57.9 %pmax.15 = f32[3072]{0:T(1024)S(1)} all-reduce(f32[3072]{0:T(1024)S(1)} %get-tuple-element.119), channel_id=1, replica_groups=mesh['img'=16,'txt'=8] {'img'}, use_global_device_ids=true, to_apply=%region_10.11 | all-reduce | flops 3072 | bytes 24576 | tf_op jit(solution)/shard_map/pmax | solution.py:64
  204.7 55.9 %psum.22 = f32[3072]{0:T(1024)S(1)} all-reduce(f32[3072]{0:T(1024)S(1)} %exponential_multiply_fusion), channel_id=1, replica_groups=mesh['img'=16,'txt'=8] {'img'}, use_global_device_ids=true, to_apply=%region_11.12 | all-reduce | flops 3072 | bytes 24576 | tf_op jit(solution)/shard_map/psum | solution.py:65
  260.6 0.6 fusion.36
  261.2 49.8 %while.33 = (s32[]{:T(128)}, f32[3072,512]{1,0:T(8,128)}, f32[3,512,512]{2,1,0:T(8,128)}, s32[3]{0:T(128)S(1)}, bf16[1536,512]{1,0:T(8,128)(2,1)}, /*index=5*/bf...) while((s32[]{:T(128)}, f32[3072,512]{1,0:T(8,128)}, ...), condition=%wide.region_15.16_spmd.clone, body=%wide.region_14.15_spmd.clone.sunk | while | flops 4851023872 | bytes 93372728 | solution.py:87
  261.2 0.6 dynamic_slice.50
  262.5 0.1 dynamic_slice.52
  262.6 0.1 dynamic_slice.51
  262.7 5.5 %subtract_convert_fusion.2 = bf16[512,3072]{1,0:T(8,128)(2,1)S(1)} fusion(bf16[3072,512]{1,0:T(8,128)(2,1)} %get-tuple-element.469, s32[3072]{0:T(1024)S(1)} %fusion.65, f32[3072]{0:T(1024)S(1)} %get-tuple-element.471, f32[512]{0:T(512)S(1)} %dynamic_slice.51, s32[512]{0:T(512)S(1)} %dynamic_slice.52, bf16[1536,512]{1,0:T(8,128)(2,1)} %get-tuple-element.468, ...), kind=kOutput, calls=%fused_computation.27.clone.1 | convolution fusion | flops 1624768512 | bytes 6844420 | tf_op jit(solution)/shard_map/while/body/eval_jaxpr/dot_general | solution.py:36
  268.2 2.8 fusion.66
  271.0 4.2 select_add_fusion.2
  275.2 2.7 copy-done.1
  277.8 0.6 dynamic_slice.50
  279.1 0.1 dynamic_slice.52
  279.2 0.1 dynamic_slice.51
  279.3 5.5 %subtract_convert_fusion.2 = bf16[512,3072]{1,0:T(8,128)(2,1)S(1)} fusion(bf16[3072,512]{1,0:T(8,128)(2,1)} %get-tuple-element.469, s32[3072]{0:T(1024)S(1)} %fusion.65, f32[3072]{0:T(1024)S(1)} %get-tuple-element.471, f32[512]{0:T(512)S(1)} %dynamic_slice.51, s32[512]{0:T(512)S(1)} %dynamic_slice.52, bf16[1536,512]{1,0:T(8,128)(2,1)} %get-tuple-element.468, ...), kind=kOutput, calls=%fused_computation.27.clone.1 | convolution fusion | flops 1624768512 | bytes 6844420 | tf_op jit(solution)/shard_map/while/body/eval_jaxpr/dot_general | solution.py:36
  284.8 2.8 fusion.66
  287.6 4.2 select_add_fusion.2
  291.8 2.7 copy-done.1
  294.5 0.6 dynamic_slice.50
  295.7 0.1 dynamic_slice.52
  295.8 0.1 dynamic_slice.51
  295.9 5.5 %subtract_convert_fusion.2 = bf16[512,3072]{1,0:T(8,128)(2,1)S(1)} fusion(bf16[3072,512]{1,0:T(8,128)(2,1)} %get-tuple-element.469, s32[3072]{0:T(1024)S(1)} %fusion.65, f32[3072]{0:T(1024)S(1)} %get-tuple-element.471, f32[512]{0:T(512)S(1)} %dynamic_slice.51, s32[512]{0:T(512)S(1)} %dynamic_slice.52, bf16[1536,512]{1,0:T(8,128)(2,1)} %get-tuple-element.468, ...), kind=kOutput, calls=%fused_computation.27.clone.1 | convolution fusion | flops 1624768512 | bytes 6844420 | tf_op jit(solution)/shard_map/while/body/eval_jaxpr/dot_general | solution.py:36
  301.4 2.8 fusion.66
  304.2 4.2 select_add_fusion.2
  308.4 2.7 copy-done.1
  311.1 0.5 reduce-scatter.5.cloned.1.call-update
  313.0 90.9 %psum.23 = f32[]{:T(128)} all-reduce(f32[]{:T(128)S(6)} %sub.56), channel_id=1, replica_groups=mesh['img'=16,'txt'=8] {'img','txt'}, use_global_device_ids=true, to_apply=%region_13.14 | all-reduce | flops 1 | bytes 8 | tf_op jit(solution)/shard_map/psum | solution.py:69
  404.5 47.5 %reduce-scatter.5.cloned.1.call-done = f32[192,512]{1,0:T(8,128)} async-done(((f32[3072,512]{1,0:T(8,128)}), f32[192,512]{1,0:T(8,128)}) %reduce-scatter.5.cloned.1.call-update) | async-done | bytes 393232 | tf_op jit(solution)/shard_map/reduce_scatter | solution.py:92
  (55 shorter events, 0.7 us)
Async XLA Ops:
  7.2 30.6 %all-gather.3.cloned.1.call-start = ((), (), s32[]{:S(2)}) async-start(), calls=%async_computation.2 | async-start | bytes 1769472 | tf_op jit(solution)/shard_map/all_gather | solution.py:17
  7.9 79.7 %all-gather.5.cloned.1.call-start = ((), (), s32[]{:S(2)}) async-start(), calls=%async_computation.3 | async-start | bytes 3342336 | tf_op jit(solution)/shard_map/all_gather | solution.py:18
  8.6 395.9 %reduce-scatter.3.cloned.1.call-start = ((), (), s32[]{:S(2)}) async-start(), calls=%async_computation.4 | async-start | bytes 3538944 | tf_op jit(solution)/shard_map/reduce_scatter | solution.py:91
  262.7 5.5 %copy-start.2 = (bf16[3072,512]{1,0:T(8,128)(2,1)S(1)}, bf16[3072,512]{1,0:T(8,128)(2,1)}, u32[]{:S(2)}) copy-start(bf16[3072,512]{1,0:T(8,128)(2,1)} %get-tuple-element.469) | copy-start | bytes 9437188 | tf_op jit(solution)/shard_map/while
  268.2 2.8 copy-start
  275.2 2.7 copy-start.1
  279.3 5.5 %copy-start.2 = (bf16[3072,512]{1,0:T(8,128)(2,1)S(1)}, bf16[3072,512]{1,0:T(8,128)(2,1)}, u32[]{:S(2)}) copy-start(bf16[3072,512]{1,0:T(8,128)(2,1)} %get-tuple-element.469) | copy-start | bytes 9437188 | tf_op jit(solution)/shard_map/while
  284.8 2.8 copy-start
  291.8 2.7 copy-start.1
  295.9 5.5 %copy-start.2 = (bf16[3072,512]{1,0:T(8,128)(2,1)S(1)}, bf16[3072,512]{1,0:T(8,128)(2,1)}, u32[]{:S(2)}) copy-start(bf16[3072,512]{1,0:T(8,128)(2,1)} %get-tuple-element.469) | copy-start | bytes 9437188 | tf_op jit(solution)/shard_map/while
  301.4 2.8 copy-start
  308.4 2.7 copy-start.1
  311.1 140.9 %reduce-scatter.5.cloned.1.call-start = ((), (), s32[]{:S(2)}) async-start(), calls=%async_computation.5 | async-start | bytes 6684672 | tf_op jit(solution)/shard_map/reduce_scatter | solution.py:92
Sparse Core Ops, SparseCore 0:
  9.7 28.0 all-gather.2
  39.9 47.6 all-gather.4
  311.2 54.1 reduce-scatter.2
  369.3 82.7 reduce-scatter.4
where the time goes:
time: 461 us; the launch traced here: 460 us
  blocking collectives  232 us (50%)
  waiting for transfers between devices  128 us (28%)
  matrix products  49.3 us (11%)
  between operations  16.9 us (4%)
  other arithmetic  14.1 us (3%)
  local copies, waits for them, and re-layouts  12.8 us (3%)
  loops' own time  6.02 us (1%)
    psum x1, blocking collectives, per_device(): summed = lax.psum(local_part, ('img', 'txt'))  90.9 us
    pmax x1, blocking collectives, per_device(): col_top = lax.pmax(col_max, 'img')  57.9 us
    psum x1, blocking collectives, per_device(): col_total = lax.psum(col_sum * jnp.exp(col_max - col_top), 'img')  55.9 us
    all_gather x1, waiting for transfers between devices, per_device(): text_block = lax.all_gather(text_emb, 'img', axis=0, tiled=True)  49.8 us
    reduce_scatter x1, waiting for transfers between devices, per_device(): lax.psum_scatter(text_partial, 'img', scatter_dimension=0, tiled=True)  47.5 us
    all_gather x1, waiting for transfers between devices, per_device(): image_block = lax.all_gather(image_emb, 'txt', axis=0, tiled=True)  29 us
    dot_general x6, matrix products, tile_logits(): lax.dot_general(chosen, text_block, (((1,), (1,)), ((), ())), preferred_e...  28.4 us
    psum x1, blocking collectives, per_device(): row_total = lax.psum(row_sum * jnp.exp(row_max - row_top), 'txt')  14.5 us
  transfers between devices with their start and end apart: 4, of which 3 were waited for; matrix products, arithmetic and copies ran while one was open for 0% of the time, Pallas kernels for 0%

commit v1 on v0

v1 whole, which is shorter than its diff:
```python
import functools
import itertools
import math

import jax
import jax.numpy as jnp
from jax import lax
from jax.experimental import pallas as pl
from jax.experimental.pallas import tpu as pltpu
from jax.sharding import Mesh, PartitionSpec as P


logit_scale = 10.0
log2e = 1.4426950408889634
ln2 = 0.6931471805599453
lowest = -1e30
f32 = jnp.float32
bf16 = jnp.bfloat16
AXES = ("z", "y", "x", "c")
SWAP = ((0, 1), (1, 0))
FLIPS = ((0, 0, 1), (0, 1, 0), (1, 0, 0))
IMAGE_PAIR = (1, 0, 3, 2)
TEXT_PAIR = (3, 2, 1, 0)
VMEM = pl.BlockSpec(memory_space=pltpu.VMEM)
SMEM = pl.BlockSpec(memory_space=pltpu.SMEM)


def role_pairs(flip):
    pairs = []
    for z, y, x in itertools.product(range(4), repeat=3):
        for core, pair in ((0, IMAGE_PAIR), (1, TEXT_PAIR)):
            target = [pair[v] if f else v for v, f in zip((z, y, x), flip)]
            source_id = ((z * 4 + y) * 4 + x) * 2 + core
            target_id = ((target[0] * 4 + target[1]) * 4 + target[2]) * 2 + core
            pairs.append((source_id, target_id))
    return pairs


ROLE_PAIRS = [role_pairs(flip) for flip in FLIPS]


def flip_permute(x, dim):
    return lax.ppermute(x, AXES, ROLE_PAIRS[dim % 3])


def core_swap(x):
    return lax.ppermute(x, "c", SWAP)


def call(kernel, name, ins, outs, scratch=(), limit=26, flops=0, moved=0):
    in_specs = [SMEM if i == 0 else VMEM for i in range(len(ins))]
    return pl.pallas_call(
        kernel,
        in_specs=in_specs,
        out_specs=[VMEM] * len(outs),
        out_shape=list(outs),
        scratch_shapes=list(scratch),
        compiler_params=pltpu.CompilerParams(vmem_limit_bytes=limit << 20),
        cost_estimate=pl.CostEstimate(flops=flops, bytes_accessed=moved, transcendentals=0),
        name=name,
    )(*ins)


def held(x):
    return pltpu.with_memory_space_constraint(x, pltpu.VMEM)


def shape(*dims, dtype=f32):
    return jax.ShapeDtypeStruct(dims, dtype)


def forward_kernel(core_ref, image_ref, text_ref, *refs):
    near_x, far_x, near, far = refs[0:3], refs[3:6], refs[6:9], refs[9:12]
    rows_ref, cols_ref = refs[12:14]
    logit_refs = refs[14:17]
    send_ref, keep_ref = refs[17:19]
    core = core_ref[0]
    n = 512

    @pl.when(core == 0)
    def _():
        for q in range(3):
            rows_ref[q * n : q * n + n, :] = far[q][...]
            cols_ref[q * n : q * n + n, :] = near_x[q][...]
            cols_ref[(q + 3) * n : (q + 3) * n + n, :] = far_x[q][...]

    @pl.when(core != 0)
    def _():
        for q in range(3):
            rows_ref[q * n : q * n + n, :] = near_x[q][...]
            cols_ref[q * n : q * n + n, :] = near[q][...]
            cols_ref[(q + 3) * n : (q + 3) * n + n, :] = far[q][...]

    width = cols_ref.shape[0]
    top = jnp.full((1, width), -jnp.inf, f32)
    total = jnp.zeros((1, width), f32)
    row_blocks = []
    for q in range(3):
        logits = lax.dot_general(
            rows_ref[q * n : q * n + n, :], cols_ref[...], (((1,), (1,)), ((), ())), preferred_element_type=f32
        ) * (logit_scale * log2e)
        logit_refs[q][...] = logits
        row_top = jnp.max(logits, axis=1, keepdims=True)
        row_total = jnp.sum(jnp.exp2(logits - row_top), axis=1, keepdims=True)
        row = jnp.broadcast_to(row_top + jnp.log2(row_total), (n, 128)).T[0:1, :]
        row_blocks += [row[:, k * 128 : k * 128 + 128] for k in range(4)]
        new_top = jnp.maximum(top, jnp.max(logits, axis=0, keepdims=True))
        total = total * jnp.exp2(top - new_top) + jnp.sum(jnp.exp2(logits - new_top), axis=0, keepdims=True)
        top = new_top
    col = top + jnp.log2(total)
    positive = logit_scale * jnp.sum(image_ref[...].astype(f32) * text_ref[...].astype(f32))
    extra = jnp.full((8, 128), positive, f32)
    row_part = jnp.concatenate(row_blocks, 0)
    col_part = jnp.concatenate([col[:, k * 128 : k * 128 + 128] for k in range(24)], 0)
    blank = jnp.full((12, 128), lowest, f32)
    is_first = core == 0
    send_ref[0:24, :] = jnp.where(is_first, col_part, jnp.concatenate([row_part, blank], 0))
    keep_ref[0:24, :] = jnp.where(is_first, jnp.concatenate([blank, row_part], 0), col_part)
    send_ref[24:32, :] = extra
    keep_ref[24:32, :] = extra


def join_kernel(order, core_ref, mine_ref, got_ref, out_ref):
    a = mine_ref[0:24, :]
    got = got_ref[...]
    b = jnp.concatenate([got[k : k + 1, :] for k in order], 0)
    top = jnp.maximum(a, b)
    out_ref[0:24, :] = top + jnp.log2(jnp.exp2(a - top) + jnp.exp2(b - top))
    out_ref[24:32, :] = mine_ref[24:32, :] + got_ref[24:32, :]


def flip_order(dim):
    order = []
    for half, q, k in itertools.product(range(2), range(3), range(4)):
        j = (dim - q) % 3
        if j == 2:
            order.append((1 - half) * 12 + q * 4 + k)
        else:
            order.append(half * 12 + q * 4 + (k ^ (1 << j)))
    return order


def coeff_kernel(core_ref, mine_ref, got_ref, cols_ref, *refs):
    logit_refs = refs[0:3]
    coeff_ref = refs[3]
    grad_refs = refs[4:7]
    own_ref, loss_ref = refs[7:9]
    core = core_ref[0]
    is_first = core == 0
    n = 512
    mine = mine_ref[...]
    got = got_ref[...]
    row_lse = jnp.where(is_first, mine[12:24], got[0:12]) + 1.0
    col_lse = jnp.where(is_first, got[0:24], mine[0:24]) + 1.0
    row_lse = jnp.concatenate([row_lse[k : k + 1] for k in range(12)], 1)
    col_lse = jnp.concatenate([col_lse[k : k + 1] for k in range(24)], 1)
    lse_sum = jnp.sum(got[0:24]) * ln2
    loss_ref[...] = jnp.full((8, 128), lse_sum, f32) - jnp.where(is_first, 0.0, 2.0) * got[24:32]
    eye = lax.broadcasted_iota(jnp.int32, (128, 128), 0) == lax.broadcasted_iota(jnp.int32, (128, 128), 1)
    positive = jnp.where(jnp.logical_and(eye, core != 0), 1.0, 0.0)
    for q in range(3):
        row = jnp.broadcast_to(row_lse[:, q * n : q * n + n], (128, n)).T[:, 0:1]
        logits = logit_refs[q][...]
        coeffs = jnp.exp2(logits - row) + jnp.exp2(logits - col_lse)
        coeff_ref[q * n : q * n + n, :] = coeffs.astype(bf16)
        own = slice(q * n, q * n + 128)
        coeff_ref[own, own] = (coeffs[0:128, own] - positive).astype(bf16)
        grad = logit_scale * jnp.dot(coeff_ref[q * n : q * n + n, :], cols_ref[...], preferred_element_type=f32)
        own_ref[q * 128 : q * 128 + 128, :] = grad[0:128, :]
        grad_refs[q][0:128, :] = jnp.where(is_first, grad[0:128, :], 0.0).astype(bf16)
        grad_refs[q][128:n, :] = grad[128:n, :].astype(bf16)


def text_grad(coeff_ref, rows_ref, start):
    return logit_scale * lax.dot_general(
        coeff_ref[:, start : start + 512], rows_ref[...], (((0,), (0,)), ((), ())), preferred_element_type=f32
    )


def far_text_kernel(core_ref, coeff_ref, rows_ref, out_ref):
    for q in range(3):
        out_ref[q * 512 : q * 512 + 512, :] = text_grad(coeff_ref, rows_ref, 1536 + q * 512).astype(bf16)


def near_text_kernel(core_ref, coeff_ref, rows_ref, g0, g1, g2, loss_ref, loss_got, base_ref, send_ref, loss_out):
    core = core_ref[0]
    loss_out[...] = loss_ref[...] + loss_got[...]
    for q, g in enumerate((g0, g1, g2)):
        rows = slice(q * 512, q * 512 + 512)
        grad = text_grad(coeff_ref, rows_ref, q * 512)
        base_ref[rows, :] = jnp.where(core == 0, 0.0, grad)
        send_ref[rows, :] = jnp.where(core == 0, grad.astype(bf16), g[...])


def far_message_kernel(core_ref, g0, g1, g2, text_ref, got_ref, m0, m1, m2):
    core = core_ref[0]
    for q, (g, m) in enumerate(((g0, m0), (g1, m1), (g2, m2))):
        rows = slice(q * 512, q * 512 + 512)
        both = (text_ref[rows, :].astype(f32) + got_ref[rows, :].astype(f32)).astype(bf16)
        m[...] = jnp.where(core == 0, g[...], both)


def near_sum_kernel(core_ref, base_ref, got_ref, r0, r1, r2, loss_ref, loss_got, low_ref, s0, s1, s2, loss_out):
    loss_out[...] = loss_ref[...] + loss_got[...]
    for q, (r, s) in enumerate(((r0, s0), (r1, s1), (r2, s2))):
        rows = slice(q * 512, q * 512 + 512)
        total = base_ref[rows, :] + got_ref[rows, :].astype(f32) + r[...].astype(f32)
        low_ref[q * 256 : q * 256 + 256, :] = total[0:256]
        s[...] = total[256:512].astype(bf16)


def half_sum_kernel(core_ref, low_ref, r0, r1, r2, loss_ref, loss_got, out_ref, s0, s1, s2, loss_out):
    loss_out[...] = loss_ref[...] + loss_got[...]
    for q, (r, s) in enumerate(((r0, s0), (r1, s1), (r2, s2))):
        total = low_ref[q * 256 : q * 256 + 256, :] + r[...].astype(f32)
        out_ref[q * 128 : q * 128 + 128, :] = total[0:128]
        s[...] = total[128:256].astype(bf16)


def last_sum_kernel(core_ref, low_ref, r0, r1, r2, own_ref, loss_ref, keep_ref, send_ref):
    first = core_ref[0] == 0
    for q, r in enumerate((r0, r1, r2)):
        rows = slice(q * 64, q * 64 + 64)
        total = low_ref[q * 128 : q * 128 + 128, :] + r[...].astype(f32)
        keep_ref[rows, :] = jnp.where(first, total[0:64], total[64:128])
        send_ref[rows, :] = jnp.where(first, total[64:128], total[0:64])
        send_ref[192 + q * 64 : 192 + q * 64 + 64, :] = own_ref[q * 128 : q * 128 + 64, :]
    send_ref[384:392, :] = jnp.concatenate([loss_ref[...]] * 4, 1)


def finish_kernel(count, core_ref, keep_ref, got_ref, own_ref, loss_ref, image_out, text_out, loss_out):
    first = core_ref[0] == 0
    for q in range(3):
        rows = slice(q * 64, q * 64 + 64)
        keep = keep_ref[rows, :]
        got = got_ref[rows, :]
        own_mine = own_ref[q * 128 + 64 : q * 128 + 128, :]
        own_got = got_ref[192 + q * 64 : 192 + q * 64 + 64, :]
        image_out[rows, :] = jnp.where(first, keep + own_got, got + own_mine)
        text_out[rows, :] = jnp.where(first, got, keep)
    loss_out[...] = (loss_ref[...] + got_ref[384:392, 0:128]) * (0.5 / count)


def per_device(image_emb, text_emb):
    core = lax.axis_index("c")
    core_id = core.reshape(1).astype(jnp.int32)
    pair_rows, width = image_emb.shape
    count = pair_rows * 128

    swapped = core_swap(jnp.where(core == 0, text_emb, image_emb))
    near = []
    for q in range(3):
        rows = slice(q * 64, q * 64 + 64)
        first = jnp.where(core == 0, image_emb[rows], swapped[rows])
        second = jnp.where(core == 0, swapped[rows], text_emb[rows])
        near.append(jnp.concatenate([first, second], 0))
    for step in range(2):
        got = [flip_permute(near[q], q + step) for q in range(3)]
        near = [jnp.concatenate([a, b], 0) for a, b in zip(near, got)]
    far = [flip_permute(near[q], q + 2) for q in range(3)]
    near_x = [core_swap(a) for a in near]
    far_x = [core_swap(a) for a in far]

    rows, cols, l0, l1, l2, send, keep = call(
        forward_kernel,
        "forward",
        [core_id, image_emb, text_emb, *near_x, *far_x, *near, *far],
        [pltpu.VMEM((1536, width), bf16), pltpu.VMEM((3072, width), bf16)]
        + [pltpu.VMEM((512, 3072), f32)] * 3
        + [shape(32, 128), shape(32, 128)],
        flops=2 * 1536 * 3072 * 512,
    )

    mine = call(functools.partial(join_kernel, list(range(24))), "join", [core_id, keep, core_swap(send)], [shape(32, 128)])[0]
    for dim in range(3):
        got = flip_permute(mine, dim)
        mine = call(functools.partial(join_kernel, flip_order(dim)), "join", [core_id, mine, got], [shape(32, 128)])[0]
    other = core_swap(mine)

    coeffs, g0, g1, g2, own, loss = call(
        coeff_kernel,
        "coeffs",
        [core_id, mine, other, held(cols), held(l0), held(l1), held(l2)],
        [pltpu.VMEM((1536, 3072), bf16)] + [shape(512, width, dtype=bf16)] * 3 + [shape(384, width), shape(8, 128)],
        flops=2 * 1536 * 3072 * 512,
    )
    text_far = call(
        far_text_kernel, "text_far", [core_id, held(coeffs), held(rows)], [shape(1536, width, dtype=bf16)], flops=1536 * 3072 * 512
    )[0]
    text_far_got = core_swap(text_far)
    loss_got = flip_permute(loss, 0)
    base, near_send, loss = call(
        near_text_kernel,
        "text_near",
        [core_id, held(coeffs), held(rows), g0, g1, g2, loss, loss_got],
        [shape(1536, width), shape(1536, width, dtype=bf16), shape(8, 128)],
        flops=1536 * 3072 * 512,
    )
    near_got = core_swap(near_send)
    loss_got = flip_permute(loss, 1)
    messages = call(
        far_message_kernel, "far_message", [core_id, g0, g1, g2, text_far, text_far_got], [shape(512, width, dtype=bf16)] * 3
    )
    got = [flip_permute(messages[q], q + 2) for q in range(3)]
    low, *messages, loss = call(
        near_sum_kernel,
        "near_sum",
        [core_id, base, near_got, *got, loss, loss_got],
        [shape(768, width)] + [shape(256, width, dtype=bf16)] * 3 + [shape(8, 128)],
    )
    got = [flip_permute(messages[q], q + 1) for q in range(3)]
    loss_got = flip_permute(loss, 2)
    low, *messages, loss = call(
        half_sum_kernel,
        "half_sum",
        [core_id, low, *got, loss, loss_got],
        [shape(384, width)] + [shape(128, width, dtype=bf16)] * 3 + [shape(8, 128)],
    )
    got = [flip_permute(messages[q], q) for q in range(3)]
    keep, send = call(
        last_sum_kernel, "last_sum", [core_id, low, *got, own, loss], [shape(192, width), shape(392, width)]
    )
    swapped = core_swap(send)
    grad_image, grad_text, loss = call(
        functools.partial(finish_kernel, count),
        "finish",
        [core_id, keep, swapped, own, loss],
        [shape(192, width), shape(192, width), shape(8, 128)],
    )
    return loss[0, 0], grad_image, grad_text


def solution(mesh):
    fine = Mesh(mesh.devices.reshape(4, 4, 4, 2), AXES)
    return jax.shard_map(
        per_device,
        mesh=fine,
        in_specs=(P(AXES, None), P(AXES, None)),
        out_specs=(P(), P(AXES, None), P(AXES, None)),
        check_vma=False,
    )
```

time: 461 us -> 131 us (0.28)
  blocking collectives: 232 us -> 0 us
  waiting for transfers between devices: 128 us -> 36.1 us
  matrix products: 49.3 us -> 0 us
  starting transfers between devices: 0.16 us -> 48.7 us
  Pallas kernels: 0 us -> 27.1 us
  between operations: 16.9 us -> 0.87 us
  other arithmetic: 14.1 us -> 2.19 us
  loops' own time: 6.02 us -> 0 us
    psum x3 -> x0, blocking collectives: 161 us -> none  [the longest x1 90.9 us: per_device(): summed = lax.psum(local_part, ('img', 'txt'))]
    all_gather x2 -> x0, waiting for transfers between devices: 78.8 us -> none  [the longest x1 49.8 us: per_device(): text_block = lax.all_gather(text_emb, 'img', axis=0, tiled=True)]
    pmax x2 -> x0, blocking collectives: 70.8 us -> none  [the longest x1 57.9 us: per_device(): col_top = lax.pmax(col_max, 'img')]
    dot_general x12 -> x0, matrix products: 49.3 us -> none  [the longest x6 28.4 us: tile_logits(): lax.dot_general(chosen, text_block, (((1,), (1,)), ((), ())), preferred_e...]
    ppermute x0 -> x36, starting transfers between devices: none -> 48.7 us  [the longest x24 45.4 us: flip_permute(): return lax.ppermute(x, AXES, ROLE_PAIRS[dim % 3])]
    reduce_scatter x2 -> x0, waiting for transfers between devices: 47.5 us -> none  [the longest x1 47.5 us: per_device(): lax.psum_scatter(text_partial, 'img', scatter_dimension=0, tiled=True)]
    ppermute x0 -> x36, waiting for transfers between devices: none -> 36.1 us  [the longest x24 28.6 us: flip_permute(): return lax.ppermute(x, AXES, ROLE_PAIRS[dim % 3])]
    pallas_call x0 -> x13, Pallas kernels: none -> 27.1 us  [call(): pl.pallas_call(kernel, in_specs=in_specs, out_specs=[VMEM] * len(outs), o...]
  transfers between devices with their start and end apart: 4 -> 36, of which waited for: 3 -> 18; matrix products, arithmetic and copies ran while one was open for 0% -> 0% of each run, Pallas kernels for 0% -> 2%
where the time goes in v1:
time: 131 us
  starting transfers between devices  48.7 us (37%)
  waiting for transfers between devices  36.1 us (28%)
  Pallas kernels  27.1 us (21%)
  local copies, waits for them, and re-layouts  15.6 us (12%)
  other arithmetic  2.19 us (2%)
    ppermute x24, starting transfers between devices, flip_permute(): return lax.ppermute(x, AXES, ROLE_PAIRS[dim % 3])  45.4 us
    ppermute x24, waiting for transfers between devices, flip_permute(): return lax.ppermute(x, AXES, ROLE_PAIRS[dim % 3])  28.6 us
    pallas_call x13, Pallas kernels, call(): pl.pallas_call(kernel, in_specs=in_specs, out_specs=[VMEM] * len(outs), o...  27.1 us
    unnamed x34, local copies, waits for them, and re-layouts  15.1 us
    ppermute x12, waiting for transfers between devices, core_swap(): return lax.ppermute(x, 'c', SWAP)  7.47 us
    ppermute x12, starting transfers between devices, core_swap(): return lax.ppermute(x, 'c', SWAP)  3.25 us
  transfers between devices with their start and end apart: 36, of which 18 were waited for; matrix products, arithmetic and copies ran while one was open for 0% of the time, Pallas kernels for 2%

profile of v1, /device:TPU:1, one launch (start us, length us, event | category | flops | bytes accessed | tf_op | source)
XLA Modules:
  0.0 130.6 jit_solution(9337310731981594667)
XLA Ops:
  0.6 1.0 broadcast_select_fusion
  1.6 1.5 %collective-permute-start = (bf16[192,512]{1,0:T(8,128)(2,1)S(1)}, bf16[192,512]{1,0:T(8,128)(2,1)S(1)}, u32[]{:S(2)}, u32[]{:S(2)}) collective-permute-start(bf16[192,512]{1,0:T(8,128)(2,1)S(1)} %broadcast_select_fusion), channel_id=1, source_target_pairs={{0,1},{1,0},{2,3},{3,2},{4,5},{5,4},{6,7},{7,6},{8,9},{9,8},{10,11... | collective-permute-start | bytes 589832 | tf_op jit(solution)/shard_map/ppermute | solution.py:47
  3.1 1.1 collective-permute-done
  4.2 1.0 slice_select_fusion.1
  5.3 3.9 %collective-permute-start.7 = (bf16[128,512]{1,0:T(8,128)(2,1)S(1)}, bf16[128,512]{1,0:T(8,128)(2,1)S(1)}, u32[]{:S(2)}, u32[]{:S(2)}) collective-permute-start(bf16[128,512]{1,0:T(8,128)(2,1)S(1)} %pad_maximum_fusion.8), channel_id=1, source_target_pairs={{0,32},{1,97},{2,34},{3,99},{4,36},{5,101},{6,38},{7,103},{8,40},{... | collective-permute-start | bytes 393224 | tf_op jit(solution)/shard_map/ppermute | solution.py:43
  9.2 2.8 %collective-permute-start.4 = (bf16[128,512]{1,0:T(8,128)(2,1)S(1)}, bf16[128,512]{1,0:T(8,128)(2,1)S(1)}, u32[]{:S(2)}, u32[]{:S(2)}) collective-permute-start(bf16[128,512]{1,0:T(8,128)(2,1)S(1)} %pad_maximum_fusion.7), channel_id=1, source_target_pairs={{0,8},{1,25},{2,10},{3,27},{4,12},{5,29},{6,14},{7,31},{8,0},{9,17... | collective-permute-start | bytes 393224 | tf_op jit(solution)/shard_map/ppermute | solution.py:43
  12.0 2.6 %collective-permute-start.8 = (bf16[256,512]{1,0:T(8,128)(2,1)S(1)}, bf16[256,512]{1,0:T(8,128)(2,1)S(1)}, u32[]{:S(2)}, u32[]{:S(2)}) collective-permute-start(bf16[256,512]{1,0:T(8,128)(2,1)S(1)} %pad_maximum_fusion.5), channel_id=1, source_target_pairs={{0,2},{1,7},{2,0},{3,5},{4,6},{5,3},{6,4},{7,1},{8,10},{9,15},{10,... | collective-permute-start | bytes 786440 | tf_op jit(solution)/shard_map/ppermute | solution.py:43
  14.9 2.3 %collective-permute-start.5 = (bf16[256,512]{1,0:T(8,128)(2,1)S(1)}, bf16[256,512]{1,0:T(8,128)(2,1)S(1)}, u32[]{:S(2)}, u32[]{:S(2)}) collective-permute-start(bf16[256,512]{1,0:T(8,128)(2,1)S(1)} %pad_maximum_fusion.4), channel_id=1, source_target_pairs={{0,32},{1,97},{2,34},{3,99},{4,36},{5,101},{6,38},{7,103},{8,40},{... | collective-permute-start | bytes 786440 | tf_op jit(solution)/shard_map/ppermute | solution.py:43
  17.2 2.8 %collective-permute-done.1 = bf16[128,512]{1,0:T(8,128)(2,1)S(1)} collective-permute-done((bf16[128,512]{1,0:T(8,128)(2,1)S(1)}, bf16[128,512]{1,0:T(8,128)(2,1)S(1)}, u32[]{:S(2)}, u32[]{:S(2)}) %collective-permute-start.1) | collective-permute-done | bytes 131104 | tf_op jit(solution)/shard_map/ppermute | solution.py:43
  20.0 2.3 %collective-permute-start.2 = (bf16[256,512]{1,0:T(8,128)(2,1)S(1)}, bf16[256,512]{1,0:T(8,128)(2,1)S(1)}, u32[]{:S(2)}, u32[]{:S(2)}) collective-permute-start(bf16[256,512]{1,0:T(8,128)(2,1)S(1)} %pad_maximum_fusion.3), channel_id=1, source_target_pairs={{0,8},{1,25},{2,10},{3,27},{4,12},{5,29},{6,14},{7,31},{8,0},{9,17... | collective-permute-start | bytes 786440 | tf_op jit(solution)/shard_map/ppermute | solution.py:43
  22.9 2.6 %collective-permute-start.12 = (bf16[512,512]{1,0:T(8,128)(2,1)S(1)}, bf16[512,512]{1,0:T(8,128)(2,1)S(1)}, u32[]{:S(2)}, u32[]{:S(2)}) collective-permute-start(bf16[512,512]{1,0:T(8,128)(2,1)S(1)} %pad_maximum_fusion.1.refs_7_), channel_id=1, source_target_pairs={{0,2},{1,7},{2,0},{3,5},{4,6},{5,3},{6,4},{7,1},{8,10},{9,15},{10,... | collective-permute-start | bytes 1572872 | tf_op jit(solution)/shard_map/ppermute | solution.py:43
  25.5 1.0 collective-permute-done.2
  26.5 2.3 %collective-permute-start.10 = (bf16[512,512]{1,0:T(8,128)(2,1)S(1)}, bf16[512,512]{1,0:T(8,128)(2,1)S(1)}, u32[]{:S(2)}, u32[]{:S(2)}) collective-permute-start(bf16[512,512]{1,0:T(8,128)(2,1)S(1)} %pad_maximum_fusion.refs_6_), channel_id=1, source_target_pairs={{0,32},{1,97},{2,34},{3,99},{4,36},{5,101},{6,38},{7,103},{8,40},{... | collective-permute-start | bytes 1572872 | tf_op jit(solution)/shard_map/ppermute | solution.py:43
  28.9 3.2 %collective-permute-done.14.refs_11_ = bf16[512,512]{1,0:T(8,128)(2,1)S(1)} collective-permute-done((bf16[512,512]{1,0:T(8,128)(2,1)S(1)}, bf16[512,512]{1,0:T(8,128)(2,1)S(1)}, u32[]{:S(2)}, u32[]{:S(2)}) %collective-permute-start.14) | collective-permute-done | bytes 524320 | tf_op jit(solution)/shard_map/ppermute | solution.py:43
  32.7 3.1 %collective-permute-done.10.refs_9_ = bf16[512,512]{1,0:T(8,128)(2,1)S(1)} collective-permute-done((bf16[512,512]{1,0:T(8,128)(2,1)S(1)}, bf16[512,512]{1,0:T(8,128)(2,1)S(1)}, u32[]{:S(2)}, u32[]{:S(2)}) %collective-permute-start.10) | collective-permute-done | bytes 524320 | tf_op jit(solution)/shard_map/ppermute | solution.py:43
  35.9 1.9 %collective-permute-done.11.refs_3_ = bf16[512,512]{1,0:T(8,128)(2,1)S(1)} collective-permute-done((bf16[512,512]{1,0:T(8,128)(2,1)S(1)}, bf16[512,512]{1,0:T(8,128)(2,1)S(1)}, u32[]{:S(2)}, u32[]{:S(2)}) %collective-permute-start.11) | collective-permute-done | bytes 524320 | tf_op jit(solution)/shard_map/ppermute | solution.py:47
  37.8 12.4 %forward.1 = (bf16[1536,512]{1,0:T(8,128)(2,1)S(1)}, bf16[3072,512]{1,0:T(8,128)(2,1)S(1)}, f32[512,3072]{1,0:T(8,128)S(1)}, f32[512,3072]{1,0:T(8,128)S(1)}, f3...) custom-call(s32[1]{0:T(128)} %bitcast.core_ref, bf16[192,512]{1,0:T(8,128)(2,1)S(1)} %copy-done.10, ...), custom_call_target="tpu_custom_call" | custom-call | flops 4831838208 | tf_op jit(solution)/shard_map/forward/pallas_call | solution.py:52
  50.2 2.7 %copy-done = f32[512,3072]{1,0:T(8,128)} copy-done((f32[512,3072]{1,0:T(8,128)}, f32[512,3072]{1,0:T(8,128)S(1)}, u32[]{:S(2)}) %copy-start) | copy-done | bytes 6291480
  52.9 2.7 %copy-done.2 = f32[512,3072]{1,0:T(8,128)} copy-done((f32[512,3072]{1,0:T(8,128)}, f32[512,3072]{1,0:T(8,128)S(1)}, u32[]{:S(2)}) %copy-start.2) | copy-done | bytes 6291480
  55.6 1.7 %copy-done.4 = bf16[3072,512]{1,0:T(8,128)(2,1)} copy-done((bf16[3072,512]{1,0:T(8,128)(2,1)}, bf16[3072,512]{1,0:T(8,128)(2,1)S(1)}, u32[]{:S(2)}) %copy-start.4) | copy-done | bytes 3145752
  57.4 1.0 collective-permute-done.16.got_ref
  58.4 2.6 %collective-permute-start.17 = (f32[32,128]{1,0:T(8,128)S(1)}, f32[32,128]{1,0:T(8,128)S(1)}, u32[]{:S(2)}, u32[]{:S(2)}) collective-permute-start(f32[32,128]{1,0:T(8,128)S(1)} %join.4.mine_ref), channel_id=1, source_target_pairs={{0,2},{1,7},{2,0},{3,5},{4,6},{5,3},{6,4},{7,1},{8,10},{9,15},{10,... | collective-permute-start | bytes 49160 | tf_op jit(solution)/shard_map/ppermute | solution.py:43
  61.0 1.3 %collective-permute-done.17.got_ref = f32[32,128]{1,0:T(8,128)S(1)} collective-permute-done((f32[32,128]{1,0:T(8,128)S(1)}, f32[32,128]{1,0:T(8,128)S(1)}, u32[]{:S(2)}, u32[]{:S(2)}) %collective-permute-start.17) | collective-permute-done | bytes 16416 | tf_op jit(solution)/shard_map/ppermute | solution.py:43
  62.3 2.3 %collective-permute-start.18 = (f32[32,128]{1,0:T(8,128)S(1)}, f32[32,128]{1,0:T(8,128)S(1)}, u32[]{:S(2)}, u32[]{:S(2)}) collective-permute-start(f32[32,128]{1,0:T(8,128)S(1)} %join.5.mine_ref), channel_id=1, source_target_pairs={{0,8},{1,25},{2,10},{3,27},{4,12},{5,29},{6,14},{7,31},{8,0},{9,17... | collective-permute-start | bytes 49160 | tf_op jit(solution)/shard_map/ppermute | solution.py:43
  64.7 1.5 %collective-permute-done.18.got_ref = f32[32,128]{1,0:T(8,128)S(1)} collective-permute-done((f32[32,128]{1,0:T(8,128)S(1)}, f32[32,128]{1,0:T(8,128)S(1)}, u32[]{:S(2)}, u32[]{:S(2)}) %collective-permute-start.18) | collective-permute-done | bytes 16416 | tf_op jit(solution)/shard_map/ppermute | solution.py:43
  66.3 2.4 %collective-permute-start.19 = (f32[32,128]{1,0:T(8,128)S(1)}, f32[32,128]{1,0:T(8,128)S(1)}, u32[]{:S(2)}, u32[]{:S(2)}) collective-permute-start(f32[32,128]{1,0:T(8,128)S(1)} %join.6.mine_ref), channel_id=1, source_target_pairs={{0,32},{1,97},{2,34},{3,99},{4,36},{5,101},{6,38},{7,103},{8,40},{... | collective-permute-start | bytes 49160 | tf_op jit(solution)/shard_map/ppermute | solution.py:43
  68.6 1.5 %collective-permute-done.19.got_ref = f32[32,128]{1,0:T(8,128)S(1)} collective-permute-done((f32[32,128]{1,0:T(8,128)S(1)}, f32[32,128]{1,0:T(8,128)S(1)}, u32[]{:S(2)}, u32[]{:S(2)}) %collective-permute-start.19) | collective-permute-done | bytes 16416 | tf_op jit(solution)/shard_map/ppermute | solution.py:43
  70.5 1.2 collective-permute-done.20.got_ref
  71.7 0.6 copy-done.14
  72.3 2.8 %copy-done.1 = f32[512,3072]{1,0:T(8,128)S(1)} copy-done((f32[512,3072]{1,0:T(8,128)S(1)}, f32[512,3072]{1,0:T(8,128)}, u32[]{:S(2)}) %copy-start.1) | copy-done | bytes 6291480
  75.0 2.8 %copy-done.3 = f32[512,3072]{1,0:T(8,128)S(1)} copy-done((f32[512,3072]{1,0:T(8,128)S(1)}, f32[512,3072]{1,0:T(8,128)}, u32[]{:S(2)}) %copy-start.3) | copy-done | bytes 6291480
  77.8 1.9 %copy-done.5 = bf16[3072,512]{1,0:T(8,128)(2,1)S(1)} copy-done((bf16[3072,512]{1,0:T(8,128)(2,1)S(1)}, bf16[3072,512]{1,0:T(8,128)(2,1)}, u32[]{:S(2)}) %copy-start.5) | copy-done | bytes 3145752
  79.7 7.1 %coeffs.1 = (bf16[1536,3072]{1,0:T(8,128)(2,1)S(1)}, bf16[512,512]{1,0:T(8,128)(2,1)}, bf16[512,512]{1,0:T(8,128)(2,1)}, bf16[512,512]{1,0:T(8,128)(2,1)}, f32[384,512]{1,0:T(8,128)}, /*index=5*/f32[8,128]{1,0:T(8,128)}) custom-call(s32[1]{0:T(128)} %bitcast.core_ref, f32[32,128]{1,0:T(8,128)} %copy-done.12, f32[32,128]{1,0:T(8,128)} %copy-done.14, ...), custom_call_target="tpu_custom_call" | custom-call | flops 4831838208 | tf_op jit(solution)/shard_map/coeffs/pallas_call | solution.py:52
  86.8 2.6 %text_far.1.text_ref = bf16[1536,512]{1,0:T(8,128)(2,1)S(1)} custom-call(s32[1]{0:T(128)} %bitcast.core_ref, bf16[1536,3072]{1,0:T(8,128)(2,1)S(1)} %get-tuple-element.43.coeff_ref, bf16[1536,512]{1,0:T(8,128)(2,1)S(1)} %get-tuple-element.44.rows_ref), custom_call_target="tpu_custom_call" | custom-call | flops 2415919104 | tf_op jit(solution)/shard_map/text_far/pallas_call | solution.py:52
  89.7 2.5 %collective-permute-start.21 = (f32[8,128]{1,0:T(8,128)S(1)}, f32[8,128]{1,0:T(8,128)S(1)}, u32[]{:S(2)}, u32[]{:S(2)}) collective-permute-start(f32[8,128]{1,0:T(8,128)S(1)} %copy-done.13), channel_id=1, source_target_pairs={{0,2},{1,7},{2,0},{3,5},{4,6},{5,3},{6,4},{7,1},{8,10},{9,15},{10,... | collective-permute-start | bytes 12296 | tf_op jit(solution)/shard_map/ppermute | solution.py:43
  92.2 1.2 collective-permute-done.21.loss_got
  93.4 2.7 %text_near.1 = (f32[1536,512]{1,0:T(8,128)S(1)}, bf16[1536,512]{1,0:T(8,128)(2,1)S(1)}, f32[8,128]{1,0:T(8,128)S(1)}) custom-call(s32[1]{0:T(128)} %bitcast.core_ref, bf16[1536,3072]{1,0:T(8,128)(2,1)S(1)} %get-tuple-element.43.coeff_ref, bf16[1536,512]{1,0:T(8,128)(2,1)S(1)} %get-tuple-element.44.rows_ref, bf16[512,512]{1,0:T(8,128)(2,1)S(1)} %copy-done.7, ...), custom_call_target="tpu_custom_call" | custom-call | flops 2415919104 | tf_op jit(solution)/shard_map/text_near/pallas_call | solution.py:52
  96.8 2.4 %collective-permute-start.24 = (bf16[512,512]{1,0:T(8,128)(2,1)S(1)}, bf16[512,512]{1,0:T(8,128)(2,1)S(1)}, u32[]{:S(2)}, u32[]{:S(2)}) collective-permute-start(bf16[512,512]{1,0:T(8,128)(2,1)S(1)} %get-tuple-element.51), channel_id=1, source_target_pairs={{0,32},{1,97},{2,34},{3,99},{4,36},{5,101},{6,38},{7,103},{8,40},{... | collective-permute-start | bytes 1572872 | tf_op jit(solution)/shard_map/ppermute | solution.py:43
  99.2 2.5 %collective-permute-start.25 = (bf16[512,512]{1,0:T(8,128)(2,1)S(1)}, bf16[512,512]{1,0:T(8,128)(2,1)S(1)}, u32[]{:S(2)}, u32[]{:S(2)}) collective-permute-start(bf16[512,512]{1,0:T(8,128)(2,1)S(1)} %get-tuple-element.52), channel_id=1, source_target_pairs={{0,2},{1,7},{2,0},{3,5},{4,6},{5,3},{6,4},{7,1},{8,10},{9,15},{10,... | collective-permute-start | bytes 1572872 | tf_op jit(solution)/shard_map/ppermute | solution.py:43
  101.7 2.7 %collective-permute-start.26 = (bf16[512,512]{1,0:T(8,128)(2,1)S(1)}, bf16[512,512]{1,0:T(8,128)(2,1)S(1)}, u32[]{:S(2)}, u32[]{:S(2)}) collective-permute-start(bf16[512,512]{1,0:T(8,128)(2,1)S(1)} %get-tuple-element.53), channel_id=1, source_target_pairs={{0,8},{1,25},{2,10},{3,27},{4,12},{5,29},{6,14},{7,31},{8,0},{9,17... | collective-permute-start | bytes 1572872 | tf_op jit(solution)/shard_map/ppermute | solution.py:43
  104.4 6.6 %collective-permute-done.27.loss_got = f32[8,128]{1,0:T(8,128)S(1)} collective-permute-done((f32[8,128]{1,0:T(8,128)S(1)}, f32[8,128]{1,0:T(8,128)S(1)}, u32[]{:S(2)}, u32[]{:S(2)}) %collective-permute-start.27) | collective-permute-done | bytes 4128 | tf_op jit(solution)/shard_map/ppermute | solution.py:43
  111.5 2.7 %collective-permute-start.28 = (bf16[256,512]{1,0:T(8,128)(2,1)S(1)}, bf16[256,512]{1,0:T(8,128)(2,1)S(1)}, u32[]{:S(2)}, u32[]{:S(2)}) collective-permute-start(bf16[256,512]{1,0:T(8,128)(2,1)S(1)} %get-tuple-element.56), channel_id=1, source_target_pairs={{0,8},{1,25},{2,10},{3,27},{4,12},{5,29},{6,14},{7,31},{8,0},{9,17... | collective-permute-start | bytes 786440 | tf_op jit(solution)/shard_map/ppermute | solution.py:43
  114.6 2.6 %collective-permute-start.31 = (f32[8,128]{1,0:T(8,128)S(1)}, f32[8,128]{1,0:T(8,128)S(1)}, u32[]{:S(2)}, u32[]{:S(2)}) collective-permute-start(f32[8,128]{1,0:T(8,128)S(1)} %get-tuple-element.59.loss_ref), channel_id=1, source_target_pairs={{0,32},{1,97},{2,34},{3,99},{4,36},{5,101},{6,38},{7,103},{8,40},{... | collective-permute-start | bytes 12296 | tf_op jit(solution)/shard_map/ppermute | solution.py:43
  117.1 3.6 %collective-permute-done.31.loss_got = f32[8,128]{1,0:T(8,128)S(1)} collective-permute-done((f32[8,128]{1,0:T(8,128)S(1)}, f32[8,128]{1,0:T(8,128)S(1)}, u32[]{:S(2)}, u32[]{:S(2)}) %collective-permute-start.31) | collective-permute-done | bytes 4128 | tf_op jit(solution)/shard_map/ppermute | solution.py:43
  121.6 2.4 %collective-permute-start.34 = (bf16[128,512]{1,0:T(8,128)(2,1)S(1)}, bf16[128,512]{1,0:T(8,128)(2,1)S(1)}, u32[]{:S(2)}, u32[]{:S(2)}) collective-permute-start(bf16[128,512]{1,0:T(8,128)(2,1)S(1)} %get-tuple-element.63), channel_id=1, source_target_pairs={{0,32},{1,97},{2,34},{3,99},{4,36},{5,101},{6,38},{7,103},{8,40},{... | collective-permute-start | bytes 393224 | tf_op jit(solution)/shard_map/ppermute | solution.py:43
  123.9 2.1 %collective-permute-done.32.r0 = bf16[128,512]{1,0:T(8,128)(2,1)S(1)} collective-permute-done((bf16[128,512]{1,0:T(8,128)(2,1)S(1)}, bf16[128,512]{1,0:T(8,128)(2,1)S(1)}, u32[]{:S(2)}, u32[]{:S(2)}) %collective-permute-start.32) | collective-permute-done | bytes 131104 | tf_op jit(solution)/shard_map/ppermute | solution.py:43
  126.8 2.3 %collective-permute-done.35.got_ref = f32[392,512]{1,0:T(8,128)S(1)} collective-permute-done((f32[392,512]{1,0:T(8,128)S(1)}, f32[392,512]{1,0:T(8,128)S(1)}, u32[]{:S(2)}, u32[]{:S(2)}) %collective-permute-start.35) | collective-permute-done | bytes 802848 | tf_op jit(solution)/shard_map/ppermute | solution.py:47
  129.1 1.0 finish.1
  (83 shorter events, 6.1 us)
Async XLA Ops:
  1.6 36.2 %copy-start.10 = (bf16[192,512]{1,0:T(8,128)(2,1)S(1)}, bf16[192,512]{1,0:T(8,128)(2,1)}, u32[]{:S(2)}) copy-start(bf16[192,512]{1,0:T(8,128)(2,1)} %image_ref.1) | copy-start | bytes 589828
  1.6 36.2 %copy-start.11 = (bf16[192,512]{1,0:T(8,128)(2,1)S(1)}, bf16[192,512]{1,0:T(8,128)(2,1)}, u32[]{:S(2)}) copy-start(bf16[192,512]{1,0:T(8,128)(2,1)} %text_ref.1) | copy-start | bytes 589828
  1.6 2.6 %collective-permute-start = (bf16[192,512]{1,0:T(8,128)(2,1)S(1)}, bf16[192,512]{1,0:T(8,128)(2,1)S(1)}, u32[]{:S(2)}, u32[]{:S(2)}) collective-permute-start(bf16[192,512]{1,0:T(8,128)(2,1)S(1)} %broadcast_select_fusion), channel_id=1, source_target_pairs={{0,1},{1,0},{2,3},{3,2},{4,5},{5,4},{6,7},{7,6},{8,9},{9,8},{10,11... | collective-permute-start | bytes 589832 | tf_op jit(solution)/shard_map/ppermute | solution.py:47
  5.3 6.8 %collective-permute-start.7 = (bf16[128,512]{1,0:T(8,128)(2,1)S(1)}, bf16[128,512]{1,0:T(8,128)(2,1)S(1)}, u32[]{:S(2)}, u32[]{:S(2)}) collective-permute-start(bf16[128,512]{1,0:T(8,128)(2,1)S(1)} %pad_maximum_fusion.8), channel_id=1, source_target_pairs={{0,32},{1,97},{2,34},{3,99},{4,36},{5,101},{6,38},{7,103},{8,40},{... | collective-permute-start | bytes 393224 | tf_op jit(solution)/shard_map/ppermute | solution.py:43
  9.2 5.7 %collective-permute-start.4 = (bf16[128,512]{1,0:T(8,128)(2,1)S(1)}, bf16[128,512]{1,0:T(8,128)(2,1)S(1)}, u32[]{:S(2)}, u32[]{:S(2)}) collective-permute-start(bf16[128,512]{1,0:T(8,128)(2,1)S(1)} %pad_maximum_fusion.7), channel_id=1, source_target_pairs={{0,8},{1,25},{2,10},{3,27},{4,12},{5,29},{6,14},{7,31},{8,0},{9,17... | collective-permute-start | bytes 393224 | tf_op jit(solution)/shard_map/ppermute | solution.py:43
  12.0 10.3 %collective-permute-start.8 = (bf16[256,512]{1,0:T(8,128)(2,1)S(1)}, bf16[256,512]{1,0:T(8,128)(2,1)S(1)}, u32[]{:S(2)}, u32[]{:S(2)}) collective-permute-start(bf16[256,512]{1,0:T(8,128)(2,1)S(1)} %pad_maximum_fusion.5), channel_id=1, source_target_pairs={{0,2},{1,7},{2,0},{3,5},{4,6},{5,3},{6,4},{7,1},{8,10},{9,15},{10,... | collective-permute-start | bytes 786440 | tf_op jit(solution)/shard_map/ppermute | solution.py:43
  14.6 5.3 %collective-permute-start.1 = (bf16[128,512]{1,0:T(8,128)(2,1)S(1)}, bf16[128,512]{1,0:T(8,128)(2,1)S(1)}, u32[]{:S(2)}, u32[]{:S(2)}) collective-permute-start(bf16[128,512]{1,0:T(8,128)(2,1)S(1)} %pad_maximum_fusion.6), channel_id=1, source_target_pairs={{0,2},{1,7},{2,0},{3,5},{4,6},{5,3},{6,4},{7,1},{8,10},{9,15},{10,... | collective-permute-start | bytes 393224 | tf_op jit(solution)/shard_map/ppermute | solution.py:43
  14.9 7.9 %collective-permute-start.5 = (bf16[256,512]{1,0:T(8,128)(2,1)S(1)}, bf16[256,512]{1,0:T(8,128)(2,1)S(1)}, u32[]{:S(2)}, u32[]{:S(2)}) collective-permute-start(bf16[256,512]{1,0:T(8,128)(2,1)S(1)} %pad_maximum_fusion.4), channel_id=1, source_target_pairs={{0,32},{1,97},{2,34},{3,99},{4,36},{5,101},{6,38},{7,103},{8,40},{... | collective-permute-start | bytes 786440 | tf_op jit(solution)/shard_map/ppermute | solution.py:43
  20.0 6.5 %collective-permute-start.2 = (bf16[256,512]{1,0:T(8,128)(2,1)S(1)}, bf16[256,512]{1,0:T(8,128)(2,1)S(1)}, u32[]{:S(2)}, u32[]{:S(2)}) collective-permute-start(bf16[256,512]{1,0:T(8,128)(2,1)S(1)} %pad_maximum_fusion.3), channel_id=1, source_target_pairs={{0,8},{1,25},{2,10},{3,27},{4,12},{5,29},{6,14},{7,31},{8,0},{9,17... | collective-permute-start | bytes 786440 | tf_op jit(solution)/shard_map/ppermute | solution.py:43
  22.4 9.7 %collective-permute-start.14 = (bf16[512,512]{1,0:T(8,128)(2,1)S(1)}, bf16[512,512]{1,0:T(8,128)(2,1)S(1)}, u32[]{:S(2)}, u32[]{:S(2)}) collective-permute-start(bf16[512,512]{1,0:T(8,128)(2,1)S(1)} %pad_maximum_fusion.2.refs_8_), channel_id=1, source_target_pairs={{0,8},{1,25},{2,10},{3,27},{4,12},{5,29},{6,14},{7,31},{8,0},{9,17... | collective-permute-start | bytes 1572872 | tf_op jit(solution)/shard_map/ppermute | solution.py:43
  22.8 9.3 %collective-permute-start.9 = (bf16[512,512]{1,0:T(8,128)(2,1)S(1)}, bf16[512,512]{1,0:T(8,128)(2,1)S(1)}, u32[]{:S(2)}, u32[]{:S(2)}) collective-permute-start(bf16[512,512]{1,0:T(8,128)(2,1)S(1)} %pad_maximum_fusion.2.refs_8_), channel_id=1, source_target_pairs={{0,1},{1,0},{2,3},{3,2},{4,5},{5,4},{6,7},{7,6},{8,9},{9,8},{10,11... | collective-permute-start | bytes 1572872 | tf_op jit(solution)/shard_map/ppermute | solution.py:47
  22.9 9.7 %collective-permute-start.12 = (bf16[512,512]{1,0:T(8,128)(2,1)S(1)}, bf16[512,512]{1,0:T(8,128)(2,1)S(1)}, u32[]{:S(2)}, u32[]{:S(2)}) collective-permute-start(bf16[512,512]{1,0:T(8,128)(2,1)S(1)} %pad_maximum_fusion.1.refs_7_), channel_id=1, source_target_pairs={{0,2},{1,7},{2,0},{3,5},{4,6},{5,3},{6,4},{7,1},{8,10},{9,15},{10,... | collective-permute-start | bytes 1572872 | tf_op jit(solution)/shard_map/ppermute | solution.py:43
  26.5 9.3 %collective-permute-start.10 = (bf16[512,512]{1,0:T(8,128)(2,1)S(1)}, bf16[512,512]{1,0:T(8,128)(2,1)S(1)}, u32[]{:S(2)}, u32[]{:S(2)}) collective-permute-start(bf16[512,512]{1,0:T(8,128)(2,1)S(1)} %pad_maximum_fusion.refs_6_), channel_id=1, source_target_pairs={{0,32},{1,97},{2,34},{3,99},{4,36},{5,101},{6,38},{7,103},{8,40},{... | collective-permute-start | bytes 1572872 | tf_op jit(solution)/shard_map/ppermute | solution.py:43
  28.9 7.0 %collective-permute-start.6 = (bf16[512,512]{1,0:T(8,128)(2,1)S(1)}, bf16[512,512]{1,0:T(8,128)(2,1)S(1)}, u32[]{:S(2)}, u32[]{:S(2)}) collective-permute-start(bf16[512,512]{1,0:T(8,128)(2,1)S(1)} %pad_maximum_fusion.1.refs_7_), channel_id=1, source_target_pairs={{0,1},{1,0},{2,3},{3,2},{4,5},{5,4},{6,7},{7,6},{8,9},{9,8},{10,11... | collective-permute-start | bytes 1572872 | tf_op jit(solution)/shard_map/ppermute | solution.py:47
  32.1 5.7 %copy-start.15 = (bf16[512,512]{1,0:T(8,128)(2,1)}, bf16[512,512]{1,0:T(8,128)(2,1)S(1)}, u32[]{:S(2)}) copy-start(bf16[512,512]{1,0:T(8,128)(2,1)S(1)} %collective-permute-done.14.refs_11_) | copy-start | bytes 1572868
  32.1 3.8 %collective-permute-start.3 = (bf16[512,512]{1,0:T(8,128)(2,1)S(1)}, bf16[512,512]{1,0:T(8,128)(2,1)S(1)}, u32[]{:S(2)}, u32[]{:S(2)}) collective-permute-start(bf16[512,512]{1,0:T(8,128)(2,1)S(1)} %pad_maximum_fusion.refs_6_), channel_id=1, source_target_pairs={{0,1},{1,0},{2,3},{3,2},{4,5},{5,4},{6,7},{7,6},{8,9},{9,8},{10,11... | collective-permute-start | bytes 1572872 | tf_op jit(solution)/shard_map/ppermute | solution.py:47
  32.1 3.7 %collective-permute-start.15 = (bf16[512,512]{1,0:T(8,128)(2,1)S(1)}, bf16[512,512]{1,0:T(8,128)(2,1)S(1)}, u32[]{:S(2)}, u32[]{:S(2)}) collective-permute-start(bf16[512,512]{1,0:T(8,128)(2,1)S(1)} %collective-permute-done.14.refs_11_), channel_id=1, source_target_pairs={{0,1},{1,0},{2,3},{3,2},{4,5},{5,4},{6,7},{7,6},{8,9},{9,8},{10,11... | collective-permute-start | bytes 1572872 | tf_op jit(solution)/shard_map/ppermute | solution.py:47
  32.6 5.1 %copy-start.16 = (bf16[512,512]{1,0:T(8,128)(2,1)}, bf16[512,512]{1,0:T(8,128)(2,1)S(1)}, u32[]{:S(2)}) copy-start(bf16[512,512]{1,0:T(8,128)(2,1)S(1)} %collective-permute-done.12.refs_10_) | copy-start | bytes 1572868
  32.6 3.2 %collective-permute-start.13 = (bf16[512,512]{1,0:T(8,128)(2,1)S(1)}, bf16[512,512]{1,0:T(8,128)(2,1)S(1)}, u32[]{:S(2)}, u32[]{:S(2)}) collective-permute-start(bf16[512,512]{1,0:T(8,128)(2,1)S(1)} %collective-permute-done.12.refs_10_), channel_id=1, source_target_pairs={{0,1},{1,0},{2,3},{3,2},{4,5},{5,4},{6,7},{7,6},{8,9},{9,8},{10,11... | collective-permute-start | bytes 1572872 | tf_op jit(solution)/shard_map/ppermute | solution.py:47
  35.8 1.9 %collective-permute-start.11 = (bf16[512,512]{1,0:T(8,128)(2,1)S(1)}, bf16[512,512]{1,0:T(8,128)(2,1)S(1)}, u32[]{:S(2)}, u32[]{:S(2)}) collective-permute-start(bf16[512,512]{1,0:T(8,128)(2,1)S(1)} %collective-permute-done.10.refs_9_), channel_id=1, source_target_pairs={{0,1},{1,0},{2,3},{3,2},{4,5},{5,4},{6,7},{7,6},{8,9},{9,8},{10,11... | collective-permute-start | bytes 1572872 | tf_op jit(solution)/shard_map/ppermute | solution.py:47
  52.9 2.7 %copy-start.2 = (f32[512,3072]{1,0:T(8,128)}, f32[512,3072]{1,0:T(8,128)S(1)}, u32[]{:S(2)}) copy-start(f32[512,3072]{1,0:T(8,128)S(1)} %get-tuple-element.42.refs_2_) | copy-start | bytes 18874372
  57.2 1.2 collective-permute-start.16
  58.4 3.9 %collective-permute-start.17 = (f32[32,128]{1,0:T(8,128)S(1)}, f32[32,128]{1,0:T(8,128)S(1)}, u32[]{:S(2)}, u32[]{:S(2)}) collective-permute-start(f32[32,128]{1,0:T(8,128)S(1)} %join.4.mine_ref), channel_id=1, source_target_pairs={{0,2},{1,7},{2,0},{3,5},{4,6},{5,3},{6,4},{7,1},{8,10},{9,15},{10,... | collective-permute-start | bytes 49160 | tf_op jit(solution)/shard_map/ppermute | solution.py:43
  62.3 3.9 %collective-permute-start.18 = (f32[32,128]{1,0:T(8,128)S(1)}, f32[32,128]{1,0:T(8,128)S(1)}, u32[]{:S(2)}, u32[]{:S(2)}) collective-permute-start(f32[32,128]{1,0:T(8,128)S(1)} %join.5.mine_ref), channel_id=1, source_target_pairs={{0,8},{1,25},{2,10},{3,27},{4,12},{5,29},{6,14},{7,31},{8,0},{9,17... | collective-permute-start | bytes 49160 | tf_op jit(solution)/shard_map/ppermute | solution.py:43
  66.3 3.9 %collective-permute-start.19 = (f32[32,128]{1,0:T(8,128)S(1)}, f32[32,128]{1,0:T(8,128)S(1)}, u32[]{:S(2)}, u32[]{:S(2)}) collective-permute-start(f32[32,128]{1,0:T(8,128)S(1)} %join.6.mine_ref), channel_id=1, source_target_pairs={{0,32},{1,97},{2,34},{3,99},{4,36},{5,101},{6,38},{7,103},{8,40},{... | collective-permute-start | bytes 49160 | tf_op jit(solution)/shard_map/ppermute | solution.py:43
  70.2 1.5 %collective-permute-start.20 = (f32[32,128]{1,0:T(8,128)S(1)}, f32[32,128]{1,0:T(8,128)S(1)}, u32[]{:S(2)}, u32[]{:S(2)}) collective-permute-start(f32[32,128]{1,0:T(8,128)S(1)} %join.7.mine_ref), channel_id=1, source_target_pairs={{0,1},{1,0},{2,3},{3,2},{4,5},{5,4},{6,7},{7,6},{8,9},{9,8},{10,11... | collective-permute-start | bytes 49160 | tf_op jit(solution)/shard_map/ppermute | solution.py:47
  72.3 2.8 %copy-start.1 = (f32[512,3072]{1,0:T(8,128)S(1)}, f32[512,3072]{1,0:T(8,128)}, u32[]{:S(2)}) copy-start(f32[512,3072]{1,0:T(8,128)} %copy-done) | copy-start | bytes 18874372
  75.0 2.8 %copy-start.3 = (f32[512,3072]{1,0:T(8,128)S(1)}, f32[512,3072]{1,0:T(8,128)}, u32[]{:S(2)}) copy-start(f32[512,3072]{1,0:T(8,128)} %copy-done.2) | copy-start | bytes 18874372
  86.8 2.9 %copy-start.13 = (f32[8,128]{1,0:T(8,128)S(1)}, f32[8,128]{1,0:T(8,128)}, u32[]{:S(2)}) copy-start(f32[8,128]{1,0:T(8,128)} %get-tuple-element.48.loss_ref) | copy-start | bytes 12292
  86.8 6.6 %copy-start.7 = (bf16[512,512]{1,0:T(8,128)(2,1)S(1)}, bf16[512,512]{1,0:T(8,128)(2,1)}, u32[]{:S(2)}) copy-start(bf16[512,512]{1,0:T(8,128)(2,1)} %get-tuple-element.45.g0) | copy-start | bytes 1572868
  86.8 6.6 %copy-start.8 = (bf16[512,512]{1,0:T(8,128)(2,1)S(1)}, bf16[512,512]{1,0:T(8,128)(2,1)}, u32[]{:S(2)}) copy-start(bf16[512,512]{1,0:T(8,128)(2,1)} %get-tuple-element.46.g1) | copy-start | bytes 1572868
  86.8 6.6 %copy-start.9 = (bf16[512,512]{1,0:T(8,128)(2,1)S(1)}, bf16[512,512]{1,0:T(8,128)(2,1)}, u32[]{:S(2)}) copy-start(bf16[512,512]{1,0:T(8,128)(2,1)} %get-tuple-element.47.g2) | copy-start | bytes 1572868
  89.5 7.0 %collective-permute-start.23 = (bf16[1536,512]{1,0:T(8,128)(2,1)S(1)}, bf16[1536,512]{1,0:T(8,128)(2,1)S(1)}, u32[]{:S(2)}, u32[]{:S(2)}) collective-permute-start(bf16[1536,512]{1,0:T(8,128)(2,1)S(1)} %text_far.1.text_ref), channel_id=1, source_target_pairs={{0,1},{1,0},{2,3},{3,2},{4,5},{5,4},{6,7},{7,6},{8,9},{9,8},{10,11... | collective-permute-start | bytes 4718600 | tf_op jit(solution)/shard_map/ppermute | solution.py:47
  89.7 3.7 %collective-permute-start.21 = (f32[8,128]{1,0:T(8,128)S(1)}, f32[8,128]{1,0:T(8,128)S(1)}, u32[]{:S(2)}, u32[]{:S(2)}) collective-permute-start(f32[8,128]{1,0:T(8,128)S(1)} %copy-done.13), channel_id=1, source_target_pairs={{0,2},{1,7},{2,0},{3,5},{4,6},{5,3},{6,4},{7,1},{8,10},{9,15},{10,... | collective-permute-start | bytes 12296 | tf_op jit(solution)/shard_map/ppermute | solution.py:43
  96.1 14.9 %collective-permute-start.22 = (bf16[1536,512]{1,0:T(8,128)(2,1)S(1)}, bf16[1536,512]{1,0:T(8,128)(2,1)S(1)}, u32[]{:S(2)}, u32[]{:S(2)}) collective-permute-start(bf16[1536,512]{1,0:T(8,128)(2,1)S(1)} %get-tuple-element.50), channel_id=1, source_target_pairs={{0,1},{1,0},{2,3},{3,2},{4,5},{5,4},{6,7},{7,6},{8,9},{9,8},{10,11... | collective-permute-start | bytes 4718600 | tf_op jit(solution)/shard_map/ppermute | solution.py:47
  96.8 14.1 %collective-permute-start.24 = (bf16[512,512]{1,0:T(8,128)(2,1)S(1)}, bf16[512,512]{1,0:T(8,128)(2,1)S(1)}, u32[]{:S(2)}, u32[]{:S(2)}) collective-permute-start(bf16[512,512]{1,0:T(8,128)(2,1)S(1)} %get-tuple-element.51), channel_id=1, source_target_pairs={{0,32},{1,97},{2,34},{3,99},{4,36},{5,101},{6,38},{7,103},{8,40},{... | collective-permute-start | bytes 1572872 | tf_op jit(solution)/shard_map/ppermute | solution.py:43
  99.2 11.8 %collective-permute-start.25 = (bf16[512,512]{1,0:T(8,128)(2,1)S(1)}, bf16[512,512]{1,0:T(8,128)(2,1)S(1)}, u32[]{:S(2)}, u32[]{:S(2)}) collective-permute-start(bf16[512,512]{1,0:T(8,128)(2,1)S(1)} %get-tuple-element.52), channel_id=1, source_target_pairs={{0,2},{1,7},{2,0},{3,5},{4,6},{5,3},{6,4},{7,1},{8,10},{9,15},{10,... | collective-permute-start | bytes 1572872 | tf_op jit(solution)/shard_map/ppermute | solution.py:43
  101.7 9.3 %collective-permute-start.26 = (bf16[512,512]{1,0:T(8,128)(2,1)S(1)}, bf16[512,512]{1,0:T(8,128)(2,1)S(1)}, u32[]{:S(2)}, u32[]{:S(2)}) collective-permute-start(bf16[512,512]{1,0:T(8,128)(2,1)S(1)} %get-tuple-element.53), channel_id=1, source_target_pairs={{0,8},{1,25},{2,10},{3,27},{4,12},{5,29},{6,14},{7,31},{8,0},{9,17... | collective-permute-start | bytes 1572872 | tf_op jit(solution)/shard_map/ppermute | solution.py:43
  104.3 6.6 %collective-permute-start.27 = (f32[8,128]{1,0:T(8,128)S(1)}, f32[8,128]{1,0:T(8,128)S(1)}, u32[]{:S(2)}, u32[]{:S(2)}) collective-permute-start(f32[8,128]{1,0:T(8,128)S(1)} %get-tuple-element.54.loss_ref), channel_id=1, source_target_pairs={{0,8},{1,25},{2,10},{3,27},{4,12},{5,29},{6,14},{7,31},{8,0},{9,17... | collective-permute-start | bytes 12296 | tf_op jit(solution)/shard_map/ppermute | solution.py:43
  111.0 15.6 %copy-start.6 = (f32[384,512]{1,0:T(8,128)S(1)}, f32[384,512]{1,0:T(8,128)}, u32[]{:S(2)}) copy-start(f32[384,512]{1,0:T(8,128)} %get-tuple-element.64.own_ref) | copy-start | bytes 2359300
  111.5 9.2 %collective-permute-start.28 = (bf16[256,512]{1,0:T(8,128)(2,1)S(1)}, bf16[256,512]{1,0:T(8,128)(2,1)S(1)}, u32[]{:S(2)}, u32[]{:S(2)}) collective-permute-start(bf16[256,512]{1,0:T(8,128)(2,1)S(1)} %get-tuple-element.56), channel_id=1, source_target_pairs={{0,8},{1,25},{2,10},{3,27},{4,12},{5,29},{6,14},{7,31},{8,0},{9,17... | collective-permute-start | bytes 786440 | tf_op jit(solution)/shard_map/ppermute | solution.py:43
  114.3 6.5 %collective-permute-start.29 = (bf16[256,512]{1,0:T(8,128)(2,1)S(1)}, bf16[256,512]{1,0:T(8,128)(2,1)S(1)}, u32[]{:S(2)}, u32[]{:S(2)}) collective-permute-start(bf16[256,512]{1,0:T(8,128)(2,1)S(1)} %get-tuple-element.57), channel_id=1, source_target_pairs={{0,32},{1,97},{2,34},{3,99},{4,36},{5,101},{6,38},{7,103},{8,40},{... | collective-permute-start | bytes 786440 | tf_op jit(solution)/shard_map/ppermute | solution.py:43
  114.3 6.4 %collective-permute-start.30 = (bf16[256,512]{1,0:T(8,128)(2,1)S(1)}, bf16[256,512]{1,0:T(8,128)(2,1)S(1)}, u32[]{:S(2)}, u32[]{:S(2)}) collective-permute-start(bf16[256,512]{1,0:T(8,128)(2,1)S(1)} %get-tuple-element.58), channel_id=1, source_target_pairs={{0,2},{1,7},{2,0},{3,5},{4,6},{5,3},{6,4},{7,1},{8,10},{9,15},{10,... | collective-permute-start | bytes 786440 | tf_op jit(solution)/shard_map/ppermute | solution.py:43
  114.6 6.2 %collective-permute-start.31 = (f32[8,128]{1,0:T(8,128)S(1)}, f32[8,128]{1,0:T(8,128)S(1)}, u32[]{:S(2)}, u32[]{:S(2)}) collective-permute-start(f32[8,128]{1,0:T(8,128)S(1)} %get-tuple-element.59.loss_ref), channel_id=1, source_target_pairs={{0,32},{1,97},{2,34},{3,99},{4,36},{5,101},{6,38},{7,103},{8,40},{... | collective-permute-start | bytes 12296 | tf_op jit(solution)/shard_map/ppermute | solution.py:43
  121.0 5.1 %collective-permute-start.32 = (bf16[128,512]{1,0:T(8,128)(2,1)S(1)}, bf16[128,512]{1,0:T(8,128)(2,1)S(1)}, u32[]{:S(2)}, u32[]{:S(2)}) collective-permute-start(bf16[128,512]{1,0:T(8,128)(2,1)S(1)} %get-tuple-element.61), channel_id=1, source_target_pairs={{0,2},{1,7},{2,0},{3,5},{4,6},{5,3},{6,4},{7,1},{8,10},{9,15},{10,... | collective-permute-start | bytes 393224 | tf_op jit(solution)/shard_map/ppermute | solution.py:43
  121.3 5.0 %collective-permute-start.33 = (bf16[128,512]{1,0:T(8,128)(2,1)S(1)}, bf16[128,512]{1,0:T(8,128)(2,1)S(1)}, u32[]{:S(2)}, u32[]{:S(2)}) collective-permute-start(bf16[128,512]{1,0:T(8,128)(2,1)S(1)} %get-tuple-element.62), channel_id=1, source_target_pairs={{0,8},{1,25},{2,10},{3,27},{4,12},{5,29},{6,14},{7,31},{8,0},{9,17... | collective-permute-start | bytes 393224 | tf_op jit(solution)/shard_map/ppermute | solution.py:43
  121.6 5.0 %collective-permute-start.34 = (bf16[128,512]{1,0:T(8,128)(2,1)S(1)}, bf16[128,512]{1,0:T(8,128)(2,1)S(1)}, u32[]{:S(2)}, u32[]{:S(2)}) collective-permute-start(bf16[128,512]{1,0:T(8,128)(2,1)S(1)} %get-tuple-element.63), channel_id=1, source_target_pairs={{0,32},{1,97},{2,34},{3,99},{4,36},{5,101},{6,38},{7,103},{8,40},{... | collective-permute-start | bytes 393224 | tf_op jit(solution)/shard_map/ppermute | solution.py:43
  126.7 2.4 %collective-permute-start.35 = (f32[392,512]{1,0:T(8,128)S(1)}, f32[392,512]{1,0:T(8,128)S(1)}, u32[]{:S(2)}, u32[]{:S(2)}) collective-permute-start(f32[392,512]{1,0:T(8,128)S(1)} %get-tuple-element.67), channel_id=1, source_target_pairs={{0,1},{1,0},{2,3},{3,2},{4,5},{5,4},{6,7},{7,6},{8,9},{9,8},{10,11... | collective-permute-start | bytes 2408456 | tf_op jit(solution)/shard_map/ppermute | solution.py:47
  (5 other events, 8.3 us)

commit v2 on v1

--- a/solution.py
+++ b/solution.py
@@ -47,7 +47,7 @@
     return lax.ppermute(x, "c", SWAP)
 
 
-def call(kernel, name, ins, outs, scratch=(), limit=26, flops=0, moved=0):
+def call(kernel, name, ins, outs, scratch=(), limit=6, flops=0, moved=0):
     in_specs = [SMEM if i == 0 else VMEM for i in range(len(ins))]
     return pl.pallas_call(
         kernel,
@@ -182,9 +182,8 @@
         out_ref[q * 512 : q * 512 + 512, :] = text_grad(coeff_ref, rows_ref, 1536 + q * 512).astype(bf16)
 
 
-def near_text_kernel(core_ref, coeff_ref, rows_ref, g0, g1, g2, loss_ref, loss_got, base_ref, send_ref, loss_out):
+def near_text_kernel(core_ref, coeff_ref, rows_ref, g0, g1, g2, base_ref, send_ref):
     core = core_ref[0]
-    loss_out[...] = loss_ref[...] + loss_got[...]
     for q, g in enumerate((g0, g1, g2)):
         rows = slice(q * 512, q * 512 + 512)
         grad = text_grad(coeff_ref, rows_ref, q * 512)
@@ -217,15 +216,17 @@
         s[...] = total[128:256].astype(bf16)
 
 
-def last_sum_kernel(core_ref, low_ref, r0, r1, r2, own_ref, loss_ref, keep_ref, send_ref):
+def last_sum_kernel(core_ref, low_ref, r0, r1, r2, own_ref, loss_ref, loss_got, keep_ref, send_ref, loss_out):
     first = core_ref[0] == 0
+    loss = loss_ref[...] + loss_got[...]
+    loss_out[...] = loss
     for q, r in enumerate((r0, r1, r2)):
         rows = slice(q * 64, q * 64 + 64)
         total = low_ref[q * 128 : q * 128 + 128, :] + r[...].astype(f32)
         keep_ref[rows, :] = jnp.where(first, total[0:64], total[64:128])
         send_ref[rows, :] = jnp.where(first, total[64:128], total[0:64])
         send_ref[192 + q * 64 : 192 + q * 64 + 64, :] = own_ref[q * 128 : q * 128 + 64, :]
-    send_ref[384:392, :] = jnp.concatenate([loss_ref[...]] * 4, 1)
+    send_ref[384:392, :] = jnp.concatenate([loss] * 4, 1)
 
 
 def finish_kernel(count, core_ref, keep_ref, got_ref, own_ref, loss_ref, image_out, text_out, loss_out):
@@ -238,7 +239,7 @@
         own_got = got_ref[192 + q * 64 : 192 + q * 64 + 64, :]
         image_out[rows, :] = jnp.where(first, keep + own_got, got + own_mine)
         text_out[rows, :] = jnp.where(first, got, keep)
-    loss_out[...] = (loss_ref[...] + got_ref[384:392, 0:128]) * (0.5 / count)
+    loss_out[...] = (loss_ref[0:1, 0:1] + got_ref[384:385, 0:1]) * (0.5 / count)
 
 
 def per_device(image_emb, text_emb):
@@ -269,12 +270,13 @@
         + [pltpu.VMEM((512, 3072), f32)] * 3
         + [shape(32, 128), shape(32, 128)],
         flops=2 * 1536 * 3072 * 512,
-    )
-
-    mine = call(functools.partial(join_kernel, list(range(24))), "join", [core_id, keep, core_swap(send)], [shape(32, 128)])[0]
+        limit=12,
+    )
+
+    mine = call(functools.partial(join_kernel, list(range(24))), "join", [core_id, keep, core_swap(send)], [shape(32, 128)], limit=2)[0]
     for dim in range(3):
         got = flip_permute(mine, dim)
-        mine = call(functools.partial(join_kernel, flip_order(dim)), "join", [core_id, mine, got], [shape(32, 128)])[0]
+        mine = call(functools.partial(join_kernel, flip_order(dim)), "join", [core_id, mine, got], [shape(32, 128)], limit=2)[0]
     other = core_swap(mine)
 
     coeffs, g0, g1, g2, own, loss = call(
@@ -283,25 +285,25 @@
         [core_id, mine, other, held(cols), held(l0), held(l1), held(l2)],
         [pltpu.VMEM((1536, 3072), bf16)] + [shape(512, width, dtype=bf16)] * 3 + [shape(384, width), shape(8, 128)],
         flops=2 * 1536 * 3072 * 512,
+        limit=8,
     )
     text_far = call(
         far_text_kernel, "text_far", [core_id, held(coeffs), held(rows)], [shape(1536, width, dtype=bf16)], flops=1536 * 3072 * 512
     )[0]
     text_far_got = core_swap(text_far)
-    loss_got = flip_permute(loss, 0)
-    base, near_send, loss = call(
+    base, near_send = call(
         near_text_kernel,
         "text_near",
-        [core_id, held(coeffs), held(rows), g0, g1, g2, loss, loss_got],
-        [shape(1536, width), shape(1536, width, dtype=bf16), shape(8, 128)],
+        [core_id, held(coeffs), held(rows), g0, g1, g2],
+        [shape(1536, width), shape(1536, width, dtype=bf16)],
         flops=1536 * 3072 * 512,
     )
     near_got = core_swap(near_send)
-    loss_got = flip_permute(loss, 1)
     messages = call(
         far_message_kernel, "far_message", [core_id, g0, g1, g2, text_far, text_far_got], [shape(512, width, dtype=bf16)] * 3
     )
     got = [flip_permute(messages[q], q + 2) for q in range(3)]
+    loss_got = flip_permute(loss, 0)
     low, *messages, loss = call(
         near_sum_kernel,
         "near_sum",
@@ -309,7 +311,7 @@
         [shape(768, width)] + [shape(256, width, dtype=bf16)] * 3 + [shape(8, 128)],
     )
     got = [flip_permute(messages[q], q + 1) for q in range(3)]
-    loss_got = flip_permute(loss, 2)
+    loss_got = flip_permute(loss, 1)
     low, *messages, loss = call(
         half_sum_kernel,
         "half_sum",
@@ -317,17 +319,21 @@
         [shape(384, width)] + [shape(128, width, dtype=bf16)] * 3 + [shape(8, 128)],
     )
     got = [flip_permute(messages[q], q) for q in range(3)]
-    keep, send = call(
-        last_sum_kernel, "last_sum", [core_id, low, *got, own, loss], [shape(192, width), shape(392, width)]
+    loss_got = flip_permute(loss, 2)
+    keep, send, loss = call(
+        last_sum_kernel,
+        "last_sum",
+        [core_id, low, *got, own, loss, loss_got],
+        [shape(192, width), shape(392, width), shape(8, 128)],
     )
     swapped = core_swap(send)
     grad_image, grad_text, loss = call(
         functools.partial(finish_kernel, count),
         "finish",
         [core_id, keep, swapped, own, loss],
-        [shape(192, width), shape(192, width), shape(8, 128)],
-    )
-    return loss[0, 0], grad_image, grad_text
+        [shape(192, width), shape(192, width), shape(1, 1)],
+    )
+    return loss.reshape(()), grad_image, grad_text
 
 
 def solution(mesh):

time: 131 us -> 110 us (0.84)
  local copies, waits for them, and re-layouts: 15.6 us -> 0.01 us
  starting transfers between devices: 48.7 us -> 44.5 us
  Pallas kernels: 27.1 us -> 24.1 us
  waiting for transfers between devices: 36.1 us -> 37.8 us
    unnamed x34 -> x4, local copies, waits for them, and re-layouts: 15.1 us -> 0.01 us
    ppermute x24, starting transfers between devices: 45.4 us -> 41.2 us  [flip_permute(): return lax.ppermute(x, AXES, ROLE_PAIRS[dim % 3])]
    pallas_call x13, Pallas kernels: 27.1 us -> 24.1 us  [call(): pl.pallas_call(kernel, in_specs=in_specs, out_specs=[VMEM] * len(outs), o...]
    ppermute x24, waiting for transfers between devices: 28.6 us -> 30.2 us  [flip_permute(): return lax.ppermute(x, AXES, ROLE_PAIRS[dim % 3])]
  transfers between devices with their start and end apart: 36 -> 36, of which waited for: 18 -> 19; matrix products, arithmetic and copies ran while one was open for 0% -> 0% of each run, Pallas kernels for 2% -> 3%
where the time goes in v2:
time: 110 us; the launch traced here: 109 us
  starting transfers between devices  44.5 us (40%)
  waiting for transfers between devices  37.8 us (34%)
  Pallas kernels  24.1 us (22%)
  other arithmetic  2.19 us (2%)
    ppermute x24, starting transfers between devices, flip_permute(): return lax.ppermute(x, AXES, ROLE_PAIRS[dim % 3])  41.2 us
    ppermute x24, waiting for transfers between devices, flip_permute(): return lax.ppermute(x, AXES, ROLE_PAIRS[dim % 3])  30.2 us
    pallas_call x13, Pallas kernels, call(): pl.pallas_call(kernel, in_specs=in_specs, out_specs=[VMEM] * len(outs), o...  24.1 us
    ppermute x12, waiting for transfers between devices, core_swap(): return lax.ppermute(x, 'c', SWAP)  7.62 us
    ppermute x12, starting transfers between devices, core_swap(): return lax.ppermute(x, 'c', SWAP)  3.37 us
  transfers between devices with their start and end apart: 36, of which 19 were waited for; matrix products, arithmetic and copies ran while one was open for 0% of the time, Pallas kernels for 3%

profile of v2, /device:TPU:1, one launch (start us, length us, event | category | flops | bytes accessed | tf_op | source)
XLA Modules:
  0.0 109.5 jit_solution(13979555513021476448)
XLA Ops:
  0.6 1.0 broadcast_select_fusion
  1.6 1.5 %collective-permute-start = (bf16[192,512]{1,0:T(8,128)(2,1)S(1)}, bf16[192,512]{1,0:T(8,128)(2,1)S(1)}, u32[]{:S(2)}, u32[]{:S(2)}) collective-permute-start(bf16[192,512]{1,0:T(8,128)(2,1)S(1)} %broadcast_select_fusion), channel_id=1, source_target_pairs={{0,1},{1,0},{2,3},{3,2},{4,5},{5,4},{6,7},{7,6},{8,9},{9,8},{10,11... | collective-permute-start | bytes 589832 | tf_op jit(solution)/shard_map/ppermute | solution.py:47
  3.1 1.1 collective-permute-done
  4.2 1.0 slice_select_fusion.1
  5.3 3.9 %collective-permute-start.7 = (bf16[128,512]{1,0:T(8,128)(2,1)S(1)}, bf16[128,512]{1,0:T(8,128)(2,1)S(1)}, u32[]{:S(2)}, u32[]{:S(2)}) collective-permute-start(bf16[128,512]{1,0:T(8,128)(2,1)S(1)} %pad_maximum_fusion.8), channel_id=1, source_target_pairs={{0,32},{1,97},{2,34},{3,99},{4,36},{5,101},{6,38},{7,103},{8,40},{... | collective-permute-start | bytes 393224 | tf_op jit(solution)/shard_map/ppermute | solution.py:43
  9.2 2.8 %collective-permute-start.4 = (bf16[128,512]{1,0:T(8,128)(2,1)S(1)}, bf16[128,512]{1,0:T(8,128)(2,1)S(1)}, u32[]{:S(2)}, u32[]{:S(2)}) collective-permute-start(bf16[128,512]{1,0:T(8,128)(2,1)S(1)} %pad_maximum_fusion.7), channel_id=1, source_target_pairs={{0,8},{1,25},{2,10},{3,27},{4,12},{5,29},{6,14},{7,31},{8,0},{9,17... | collective-permute-start | bytes 393224 | tf_op jit(solution)/shard_map/ppermute | solution.py:43
  12.0 2.6 %collective-permute-start.8 = (bf16[256,512]{1,0:T(8,128)(2,1)S(1)}, bf16[256,512]{1,0:T(8,128)(2,1)S(1)}, u32[]{:S(2)}, u32[]{:S(2)}) collective-permute-start(bf16[256,512]{1,0:T(8,128)(2,1)S(1)} %pad_maximum_fusion.5), channel_id=1, source_target_pairs={{0,2},{1,7},{2,0},{3,5},{4,6},{5,3},{6,4},{7,1},{8,10},{9,15},{10,... | collective-permute-start | bytes 786440 | tf_op jit(solution)/shard_map/ppermute | solution.py:43
  14.9 2.3 %collective-permute-start.5 = (bf16[256,512]{1,0:T(8,128)(2,1)S(1)}, bf16[256,512]{1,0:T(8,128)(2,1)S(1)}, u32[]{:S(2)}, u32[]{:S(2)}) collective-permute-start(bf16[256,512]{1,0:T(8,128)(2,1)S(1)} %pad_maximum_fusion.4), channel_id=1, source_target_pairs={{0,32},{1,97},{2,34},{3,99},{4,36},{5,101},{6,38},{7,103},{8,40},{... | collective-permute-start | bytes 786440 | tf_op jit(solution)/shard_map/ppermute | solution.py:43
  17.2 2.8 %collective-permute-done.1 = bf16[128,512]{1,0:T(8,128)(2,1)S(1)} collective-permute-done((bf16[128,512]{1,0:T(8,128)(2,1)S(1)}, bf16[128,512]{1,0:T(8,128)(2,1)S(1)}, u32[]{:S(2)}, u32[]{:S(2)}) %collective-permute-start.1) | collective-permute-done | bytes 131104 | tf_op jit(solution)/shard_map/ppermute | solution.py:43
  20.0 2.3 %collective-permute-start.2 = (bf16[256,512]{1,0:T(8,128)(2,1)S(1)}, bf16[256,512]{1,0:T(8,128)(2,1)S(1)}, u32[]{:S(2)}, u32[]{:S(2)}) collective-permute-start(bf16[256,512]{1,0:T(8,128)(2,1)S(1)} %pad_maximum_fusion.3), channel_id=1, source_target_pairs={{0,8},{1,25},{2,10},{3,27},{4,12},{5,29},{6,14},{7,31},{8,0},{9,17... | collective-permute-start | bytes 786440 | tf_op jit(solution)/shard_map/ppermute | solution.py:43
  22.4 0.5 collective-permute-start.14
  22.9 2.6 %collective-permute-start.12 = (bf16[512,512]{1,0:T(8,128)(2,1)S(1)}, bf16[512,512]{1,0:T(8,128)(2,1)S(1)}, u32[]{:S(2)}, u32[]{:S(2)}) collective-permute-start(bf16[512,512]{1,0:T(8,128)(2,1)S(1)} %pad_maximum_fusion.1.refs_7_), channel_id=1, source_target_pairs={{0,2},{1,7},{2,0},{3,5},{4,6},{5,3},{6,4},{7,1},{8,10},{9,15},{10,... | collective-permute-start | bytes 1572872 | tf_op jit(solution)/shard_map/ppermute | solution.py:43
  25.5 1.0 collective-permute-done.2
  26.5 2.3 %collective-permute-start.10 = (bf16[512,512]{1,0:T(8,128)(2,1)S(1)}, bf16[512,512]{1,0:T(8,128)(2,1)S(1)}, u32[]{:S(2)}, u32[]{:S(2)}) collective-permute-start(bf16[512,512]{1,0:T(8,128)(2,1)S(1)} %pad_maximum_fusion.refs_6_), channel_id=1, source_target_pairs={{0,32},{1,97},{2,34},{3,99},{4,36},{5,101},{6,38},{7,103},{8,40},{... | collective-permute-start | bytes 1572872 | tf_op jit(solution)/shard_map/ppermute | solution.py:43
  28.9 3.2 %collective-permute-done.14.refs_11_ = bf16[512,512]{1,0:T(8,128)(2,1)S(1)} collective-permute-done((bf16[512,512]{1,0:T(8,128)(2,1)S(1)}, bf16[512,512]{1,0:T(8,128)(2,1)S(1)}, u32[]{:S(2)}, u32[]{:S(2)}) %collective-permute-start.14) | collective-permute-done | bytes 524320 | tf_op jit(solution)/shard_map/ppermute | solution.py:43
  32.1 0.5 collective-permute-start.15
  32.7 3.1 %collective-permute-done.10.refs_9_ = bf16[512,512]{1,0:T(8,128)(2,1)S(1)} collective-permute-done((bf16[512,512]{1,0:T(8,128)(2,1)S(1)}, bf16[512,512]{1,0:T(8,128)(2,1)S(1)}, u32[]{:S(2)}, u32[]{:S(2)}) %collective-permute-start.10) | collective-permute-done | bytes 524320 | tf_op jit(solution)/shard_map/ppermute | solution.py:43
  35.9 1.9 %collective-permute-done.11.refs_3_ = bf16[512,512]{1,0:T(8,128)(2,1)S(1)} collective-permute-done((bf16[512,512]{1,0:T(8,128)(2,1)S(1)}, bf16[512,512]{1,0:T(8,128)(2,1)S(1)}, u32[]{:S(2)}, u32[]{:S(2)}) %collective-permute-start.11) | collective-permute-done | bytes 524320 | tf_op jit(solution)/shard_map/ppermute | solution.py:47
  37.8 10.9 %forward.1 = (bf16[1536,512]{1,0:T(8,128)(2,1)S(1)}, bf16[3072,512]{1,0:T(8,128)(2,1)S(1)}, f32[512,3072]{1,0:T(8,128)S(1)}, f32[512,3072]{1,0:T(8,128)S(1)}, f3...) custom-call(s32[1]{0:T(128)} %bitcast.core_ref, bf16[192,512]{1,0:T(8,128)(2,1)S(1)} %copy-done, ...), custom_call_target="tpu_custom_call" | custom-call | flops 4831838208 | tf_op jit(solution)/shard_map/forward/pallas_call | solution.py:52
  48.8 1.0 collective-permute-done.16.got_ref
  49.9 2.6 %collective-permute-start.17 = (f32[32,128]{1,0:T(8,128)S(1)}, f32[32,128]{1,0:T(8,128)S(1)}, u32[]{:S(2)}, u32[]{:S(2)}) collective-permute-start(f32[32,128]{1,0:T(8,128)S(1)} %join.4.mine_ref), channel_id=1, source_target_pairs={{0,2},{1,7},{2,0},{3,5},{4,6},{5,3},{6,4},{7,1},{8,10},{9,15},{10,... | collective-permute-start | bytes 49160 | tf_op jit(solution)/shard_map/ppermute | solution.py:43
  52.4 1.3 %collective-permute-done.17.got_ref = f32[32,128]{1,0:T(8,128)S(1)} collective-permute-done((f32[32,128]{1,0:T(8,128)S(1)}, f32[32,128]{1,0:T(8,128)S(1)}, u32[]{:S(2)}, u32[]{:S(2)}) %collective-permute-start.17) | collective-permute-done | bytes 16416 | tf_op jit(solution)/shard_map/ppermute | solution.py:43
  53.8 2.3 %collective-permute-start.18 = (f32[32,128]{1,0:T(8,128)S(1)}, f32[32,128]{1,0:T(8,128)S(1)}, u32[]{:S(2)}, u32[]{:S(2)}) collective-permute-start(f32[32,128]{1,0:T(8,128)S(1)} %join.5.mine_ref), channel_id=1, source_target_pairs={{0,8},{1,25},{2,10},{3,27},{4,12},{5,29},{6,14},{7,31},{8,0},{9,17... | collective-permute-start | bytes 49160 | tf_op jit(solution)/shard_map/ppermute | solution.py:43
  56.1 1.5 %collective-permute-done.18.got_ref = f32[32,128]{1,0:T(8,128)S(1)} collective-permute-done((f32[32,128]{1,0:T(8,128)S(1)}, f32[32,128]{1,0:T(8,128)S(1)}, u32[]{:S(2)}, u32[]{:S(2)}) %collective-permute-start.18) | collective-permute-done | bytes 16416 | tf_op jit(solution)/shard_map/ppermute | solution.py:43
  57.7 2.3 %collective-permute-start.19 = (f32[32,128]{1,0:T(8,128)S(1)}, f32[32,128]{1,0:T(8,128)S(1)}, u32[]{:S(2)}, u32[]{:S(2)}) collective-permute-start(f32[32,128]{1,0:T(8,128)S(1)} %join.6.mine_ref), channel_id=1, source_target_pairs={{0,32},{1,97},{2,34},{3,99},{4,36},{5,101},{6,38},{7,103},{8,40},{... | collective-permute-start | bytes 49160 | tf_op jit(solution)/shard_map/ppermute | solution.py:43
  60.0 1.5 %collective-permute-done.19.got_ref = f32[32,128]{1,0:T(8,128)S(1)} collective-permute-done((f32[32,128]{1,0:T(8,128)S(1)}, f32[32,128]{1,0:T(8,128)S(1)}, u32[]{:S(2)}, u32[]{:S(2)}) %collective-permute-start.19) | collective-permute-done | bytes 16416 | tf_op jit(solution)/shard_map/ppermute | solution.py:43
  61.9 1.2 %collective-permute-done.20.got_ref = f32[32,128]{1,0:T(8,128)S(1)} collective-permute-done((f32[32,128]{1,0:T(8,128)S(1)}, f32[32,128]{1,0:T(8,128)S(1)}, u32[]{:S(2)}, u32[]{:S(2)}) %collective-permute-start.20) | collective-permute-done | bytes 16416 | tf_op jit(solution)/shard_map/ppermute | solution.py:47
  63.1 5.6 %coeffs.1 = (bf16[1536,3072]{1,0:T(8,128)(2,1)S(1)}, bf16[512,512]{1,0:T(8,128)(2,1)S(1)}, bf16[512,512]{1,0:T(8,128)(2,1)S(1)}, bf16[512,512]{1,0:T(8,128)(2,1)...) custom-call(s32[1]{0:T(128)} %bitcast.core_ref, f32[32,128]{1,0:T(8,128)S(1)} %join.7.mine_ref, ...), custom_call_target="tpu_custom_call" | custom-call | flops 4831838208 | tf_op jit(solution)/shard_map/coeffs/pallas_call | solution.py:52
  68.7 2.6 %text_far.1.text_ref = bf16[1536,512]{1,0:T(8,128)(2,1)S(1)} custom-call(s32[1]{0:T(128)} %bitcast.core_ref, bf16[1536,3072]{1,0:T(8,128)(2,1)S(1)} %get-tuple-element.43.coeff_ref, bf16[1536,512]{1,0:T(8,128)(2,1)S(1)} %get-tuple-element.44.rows_ref), custom_call_target="tpu_custom_call" | custom-call | flops 2415919104 | tf_op jit(solution)/shard_map/text_far/pallas_call | solution.py:52
  71.6 2.7 %text_near.1 = (f32[1536,512]{1,0:T(8,128)S(1)}, bf16[1536,512]{1,0:T(8,128)(2,1)S(1)}) custom-call(s32[1]{0:T(128)} %bitcast.core_ref, bf16[1536,3072]{1,0:T(8,128)(2,1)S(1)} %get-tuple-element.43.coeff_ref, bf16[1536,512]{1,0:T(8,128)(2,1)S(1)} %get-tuple-element.44.rows_ref, bf16[512,512]{1,0:T(8,128)(2,1)S(1)} %get-tuple-element.45.g0, ...), custom_call_target="tpu_custom_call" | custom-call | flops 2415919104 | tf_op jit(solution)/shard_map/text_near/pallas_call | solution.py:52
  74.3 0.4 collective-permute-start.21
  74.8 0.4 far_message.1
  75.2 2.3 %collective-permute-start.23 = (bf16[512,512]{1,0:T(8,128)(2,1)S(1)}, bf16[512,512]{1,0:T(8,128)(2,1)S(1)}, u32[]{:S(2)}, u32[]{:S(2)}) collective-permute-start(bf16[512,512]{1,0:T(8,128)(2,1)S(1)} %get-tuple-element.50), channel_id=1, source_target_pairs={{0,32},{1,97},{2,34},{3,99},{4,36},{5,101},{6,38},{7,103},{8,40},{... | collective-permute-start | bytes 1572872 | tf_op jit(solution)/shard_map/ppermute | solution.py:43
  77.6 2.5 %collective-permute-start.24 = (bf16[512,512]{1,0:T(8,128)(2,1)S(1)}, bf16[512,512]{1,0:T(8,128)(2,1)S(1)}, u32[]{:S(2)}, u32[]{:S(2)}) collective-permute-start(bf16[512,512]{1,0:T(8,128)(2,1)S(1)} %get-tuple-element.51), channel_id=1, source_target_pairs={{0,2},{1,7},{2,0},{3,5},{4,6},{5,3},{6,4},{7,1},{8,10},{9,15},{10,... | collective-permute-start | bytes 1572872 | tf_op jit(solution)/shard_map/ppermute | solution.py:43
  80.1 2.7 %collective-permute-start.25 = (bf16[512,512]{1,0:T(8,128)(2,1)S(1)}, bf16[512,512]{1,0:T(8,128)(2,1)S(1)}, u32[]{:S(2)}, u32[]{:S(2)}) collective-permute-start(bf16[512,512]{1,0:T(8,128)(2,1)S(1)} %get-tuple-element.52), channel_id=1, source_target_pairs={{0,8},{1,25},{2,10},{3,27},{4,12},{5,29},{6,14},{7,31},{8,0},{9,17... | collective-permute-start | bytes 1572872 | tf_op jit(solution)/shard_map/ppermute | solution.py:43
  82.9 3.9 %collective-permute-done.26.loss_got = f32[8,128]{1,0:T(8,128)S(1)} collective-permute-done((f32[8,128]{1,0:T(8,128)S(1)}, f32[8,128]{1,0:T(8,128)S(1)}, u32[]{:S(2)}, u32[]{:S(2)}) %collective-permute-start.26) | collective-permute-done | bytes 4128 | tf_op jit(solution)/shard_map/ppermute | solution.py:43
  86.9 2.4 %collective-permute-done.25.r2 = bf16[512,512]{1,0:T(8,128)(2,1)S(1)} collective-permute-done((bf16[512,512]{1,0:T(8,128)(2,1)S(1)}, bf16[512,512]{1,0:T(8,128)(2,1)S(1)}, u32[]{:S(2)}, u32[]{:S(2)}) %collective-permute-start.25) | collective-permute-done | bytes 524320 | tf_op jit(solution)/shard_map/ppermute | solution.py:43
  89.3 0.6 near_sum.1
  89.9 2.7 %collective-permute-start.27 = (bf16[256,512]{1,0:T(8,128)(2,1)S(1)}, bf16[256,512]{1,0:T(8,128)(2,1)S(1)}, u32[]{:S(2)}, u32[]{:S(2)}) collective-permute-start(bf16[256,512]{1,0:T(8,128)(2,1)S(1)} %get-tuple-element.55), channel_id=1, source_target_pairs={{0,8},{1,25},{2,10},{3,27},{4,12},{5,29},{6,14},{7,31},{8,0},{9,17... | collective-permute-start | bytes 786440 | tf_op jit(solution)/shard_map/ppermute | solution.py:43
  92.9 0.3 collective-permute-start.30
  93.2 3.3 %collective-permute-done.30.loss_got = f32[8,128]{1,0:T(8,128)S(1)} collective-permute-done((f32[8,128]{1,0:T(8,128)S(1)}, f32[8,128]{1,0:T(8,128)S(1)}, u32[]{:S(2)}, u32[]{:S(2)}) %collective-permute-start.30) | collective-permute-done | bytes 4128 | tf_op jit(solution)/shard_map/ppermute | solution.py:43
  96.6 2.5 %collective-permute-done.28.r1 = bf16[256,512]{1,0:T(8,128)(2,1)S(1)} collective-permute-done((bf16[256,512]{1,0:T(8,128)(2,1)S(1)}, bf16[256,512]{1,0:T(8,128)(2,1)S(1)}, u32[]{:S(2)}, u32[]{:S(2)}) %collective-permute-start.28) | collective-permute-done | bytes 262176 | tf_op jit(solution)/shard_map/ppermute | solution.py:43
  99.6 0.3 collective-permute-start.32
  99.9 2.4 %collective-permute-start.33 = (bf16[128,512]{1,0:T(8,128)(2,1)S(1)}, bf16[128,512]{1,0:T(8,128)(2,1)S(1)}, u32[]{:S(2)}, u32[]{:S(2)}) collective-permute-start(bf16[128,512]{1,0:T(8,128)(2,1)S(1)} %get-tuple-element.62), channel_id=1, source_target_pairs={{0,32},{1,97},{2,34},{3,99},{4,36},{5,101},{6,38},{7,103},{8,40},{... | collective-permute-start | bytes 393224 | tf_op jit(solution)/shard_map/ppermute | solution.py:43
  102.3 0.3 collective-permute-start.34
  102.6 3.3 %collective-permute-done.34.loss_got = f32[8,128]{1,0:T(8,128)S(1)} collective-permute-done((f32[8,128]{1,0:T(8,128)S(1)}, f32[8,128]{1,0:T(8,128)S(1)}, u32[]{:S(2)}, u32[]{:S(2)}) %collective-permute-start.34) | collective-permute-done | bytes 4128 | tf_op jit(solution)/shard_map/ppermute | solution.py:43
  106.2 2.3 %collective-permute-done.35.got_ref = f32[392,512]{1,0:T(8,128)S(1)} collective-permute-done((f32[392,512]{1,0:T(8,128)S(1)}, f32[392,512]{1,0:T(8,128)S(1)}, u32[]{:S(2)}, u32[]{:S(2)}) %collective-permute-start.35) | collective-permute-done | bytes 802848 | tf_op jit(solution)/shard_map/ppermute | solution.py:47
  108.5 1.0 finish.1
  (52 shorter events, 2.9 us)
Async XLA Ops:
  1.6 36.2 %copy-start = (bf16[192,512]{1,0:T(8,128)(2,1)S(1)}, bf16[192,512]{1,0:T(8,128)(2,1)}, u32[]{:S(2)}) copy-start(bf16[192,512]{1,0:T(8,128)(2,1)} %image_ref.1) | copy-start | bytes 589828
  1.6 36.1 %copy-start.1 = (bf16[192,512]{1,0:T(8,128)(2,1)S(1)}, bf16[192,512]{1,0:T(8,128)(2,1)}, u32[]{:S(2)}) copy-start(bf16[192,512]{1,0:T(8,128)(2,1)} %text_ref.1) | copy-start | bytes 589828
  1.6 2.6 %collective-permute-start = (bf16[192,512]{1,0:T(8,128)(2,1)S(1)}, bf16[192,512]{1,0:T(8,128)(2,1)S(1)}, u32[]{:S(2)}, u32[]{:S(2)}) collective-permute-start(bf16[192,512]{1,0:T(8,128)(2,1)S(1)} %broadcast_select_fusion), channel_id=1, source_target_pairs={{0,1},{1,0},{2,3},{3,2},{4,5},{5,4},{6,7},{7,6},{8,9},{9,8},{10,11... | collective-permute-start | bytes 589832 | tf_op jit(solution)/shard_map/ppermute | solution.py:47
  5.3 6.8 %collective-permute-start.7 = (bf16[128,512]{1,0:T(8,128)(2,1)S(1)}, bf16[128,512]{1,0:T(8,128)(2,1)S(1)}, u32[]{:S(2)}, u32[]{:S(2)}) collective-permute-start(bf16[128,512]{1,0:T(8,128)(2,1)S(1)} %pad_maximum_fusion.8), channel_id=1, source_target_pairs={{0,32},{1,97},{2,34},{3,99},{4,36},{5,101},{6,38},{7,103},{8,40},{... | collective-permute-start | bytes 393224 | tf_op jit(solution)/shard_map/ppermute | solution.py:43
  9.2 5.7 %collective-permute-start.4 = (bf16[128,512]{1,0:T(8,128)(2,1)S(1)}, bf16[128,512]{1,0:T(8,128)(2,1)S(1)}, u32[]{:S(2)}, u32[]{:S(2)}) collective-permute-start(bf16[128,512]{1,0:T(8,128)(2,1)S(1)} %pad_maximum_fusion.7), channel_id=1, source_target_pairs={{0,8},{1,25},{2,10},{3,27},{4,12},{5,29},{6,14},{7,31},{8,0},{9,17... | collective-permute-start | bytes 393224 | tf_op jit(solution)/shard_map/ppermute | solution.py:43
  12.0 10.3 %collective-permute-start.8 = (bf16[256,512]{1,0:T(8,128)(2,1)S(1)}, bf16[256,512]{1,0:T(8,128)(2,1)S(1)}, u32[]{:S(2)}, u32[]{:S(2)}) collective-permute-start(bf16[256,512]{1,0:T(8,128)(2,1)S(1)} %pad_maximum_fusion.5), channel_id=1, source_target_pairs={{0,2},{1,7},{2,0},{3,5},{4,6},{5,3},{6,4},{7,1},{8,10},{9,15},{10,... | collective-permute-start | bytes 786440 | tf_op jit(solution)/shard_map/ppermute | solution.py:43
  14.6 5.3 %collective-permute-start.1 = (bf16[128,512]{1,0:T(8,128)(2,1)S(1)}, bf16[128,512]{1,0:T(8,128)(2,1)S(1)}, u32[]{:S(2)}, u32[]{:S(2)}) collective-permute-start(bf16[128,512]{1,0:T(8,128)(2,1)S(1)} %pad_maximum_fusion.6), channel_id=1, source_target_pairs={{0,2},{1,7},{2,0},{3,5},{4,6},{5,3},{6,4},{7,1},{8,10},{9,15},{10,... | collective-permute-start | bytes 393224 | tf_op jit(solution)/shard_map/ppermute | solution.py:43
  14.9 7.9 %collective-permute-start.5 = (bf16[256,512]{1,0:T(8,128)(2,1)S(1)}, bf16[256,512]{1,0:T(8,128)(2,1)S(1)}, u32[]{:S(2)}, u32[]{:S(2)}) collective-permute-start(bf16[256,512]{1,0:T(8,128)(2,1)S(1)} %pad_maximum_fusion.4), channel_id=1, source_target_pairs={{0,32},{1,97},{2,34},{3,99},{4,36},{5,101},{6,38},{7,103},{8,40},{... | collective-permute-start | bytes 786440 | tf_op jit(solution)/shard_map/ppermute | solution.py:43
  20.0 6.5 %collective-permute-start.2 = (bf16[256,512]{1,0:T(8,128)(2,1)S(1)}, bf16[256,512]{1,0:T(8,128)(2,1)S(1)}, u32[]{:S(2)}, u32[]{:S(2)}) collective-permute-start(bf16[256,512]{1,0:T(8,128)(2,1)S(1)} %pad_maximum_fusion.3), channel_id=1, source_target_pairs={{0,8},{1,25},{2,10},{3,27},{4,12},{5,29},{6,14},{7,31},{8,0},{9,17... | collective-permute-start | bytes 786440 | tf_op jit(solution)/shard_map/ppermute | solution.py:43
  22.4 9.7 %collective-permute-start.14 = (bf16[512,512]{1,0:T(8,128)(2,1)S(1)}, bf16[512,512]{1,0:T(8,128)(2,1)S(1)}, u32[]{:S(2)}, u32[]{:S(2)}) collective-permute-start(bf16[512,512]{1,0:T(8,128)(2,1)S(1)} %pad_maximum_fusion.2.refs_8_), channel_id=1, source_target_pairs={{0,8},{1,25},{2,10},{3,27},{4,12},{5,29},{6,14},{7,31},{8,0},{9,17... | collective-permute-start | bytes 1572872 | tf_op jit(solution)/shard_map/ppermute | solution.py:43
  22.8 9.3 %collective-permute-start.9 = (bf16[512,512]{1,0:T(8,128)(2,1)S(1)}, bf16[512,512]{1,0:T(8,128)(2,1)S(1)}, u32[]{:S(2)}, u32[]{:S(2)}) collective-permute-start(bf16[512,512]{1,0:T(8,128)(2,1)S(1)} %pad_maximum_fusion.2.refs_8_), channel_id=1, source_target_pairs={{0,1},{1,0},{2,3},{3,2},{4,5},{5,4},{6,7},{7,6},{8,9},{9,8},{10,11... | collective-permute-start | bytes 1572872 | tf_op jit(solution)/shard_map/ppermute | solution.py:47
  22.9 9.7 %collective-permute-start.12 = (bf16[512,512]{1,0:T(8,128)(2,1)S(1)}, bf16[512,512]{1,0:T(8,128)(2,1)S(1)}, u32[]{:S(2)}, u32[]{:S(2)}) collective-permute-start(bf16[512,512]{1,0:T(8,128)(2,1)S(1)} %pad_maximum_fusion.1.refs_7_), channel_id=1, source_target_pairs={{0,2},{1,7},{2,0},{3,5},{4,6},{5,3},{6,4},{7,1},{8,10},{9,15},{10,... | collective-permute-start | bytes 1572872 | tf_op jit(solution)/shard_map/ppermute | solution.py:43
  26.5 9.3 %collective-permute-start.10 = (bf16[512,512]{1,0:T(8,128)(2,1)S(1)}, bf16[512,512]{1,0:T(8,128)(2,1)S(1)}, u32[]{:S(2)}, u32[]{:S(2)}) collective-permute-start(bf16[512,512]{1,0:T(8,128)(2,1)S(1)} %pad_maximum_fusion.refs_6_), channel_id=1, source_target_pairs={{0,32},{1,97},{2,34},{3,99},{4,36},{5,101},{6,38},{7,103},{8,40},{... | collective-permute-start | bytes 1572872 | tf_op jit(solution)/shard_map/ppermute | solution.py:43
  28.9 7.0 %collective-permute-start.6 = (bf16[512,512]{1,0:T(8,128)(2,1)S(1)}, bf16[512,512]{1,0:T(8,128)(2,1)S(1)}, u32[]{:S(2)}, u32[]{:S(2)}) collective-permute-start(bf16[512,512]{1,0:T(8,128)(2,1)S(1)} %pad_maximum_fusion.1.refs_7_), channel_id=1, source_target_pairs={{0,1},{1,0},{2,3},{3,2},{4,5},{5,4},{6,7},{7,6},{8,9},{9,8},{10,11... | collective-permute-start | bytes 1572872 | tf_op jit(solution)/shard_map/ppermute | solution.py:47
  32.1 3.8 %collective-permute-start.3 = (bf16[512,512]{1,0:T(8,128)(2,1)S(1)}, bf16[512,512]{1,0:T(8,128)(2,1)S(1)}, u32[]{:S(2)}, u32[]{:S(2)}) collective-permute-start(bf16[512,512]{1,0:T(8,128)(2,1)S(1)} %pad_maximum_fusion.refs_6_), channel_id=1, source_target_pairs={{0,1},{1,0},{2,3},{3,2},{4,5},{5,4},{6,7},{7,6},{8,9},{9,8},{10,11... | collective-permute-start | bytes 1572872 | tf_op jit(solution)/shard_map/ppermute | solution.py:47
  32.1 3.8 %collective-permute-start.15 = (bf16[512,512]{1,0:T(8,128)(2,1)S(1)}, bf16[512,512]{1,0:T(8,128)(2,1)S(1)}, u32[]{:S(2)}, u32[]{:S(2)}) collective-permute-start(bf16[512,512]{1,0:T(8,128)(2,1)S(1)} %collective-permute-done.14.refs_11_), channel_id=1, source_target_pairs={{0,1},{1,0},{2,3},{3,2},{4,5},{5,4},{6,7},{7,6},{8,9},{9,8},{10,11... | collective-permute-start | bytes 1572872 | tf_op jit(solution)/shard_map/ppermute | solution.py:47
  32.6 3.3 %collective-permute-start.13 = (bf16[512,512]{1,0:T(8,128)(2,1)S(1)}, bf16[512,512]{1,0:T(8,128)(2,1)S(1)}, u32[]{:S(2)}, u32[]{:S(2)}) collective-permute-start(bf16[512,512]{1,0:T(8,128)(2,1)S(1)} %collective-permute-done.12.refs_10_), channel_id=1, source_target_pairs={{0,1},{1,0},{2,3},{3,2},{4,5},{5,4},{6,7},{7,6},{8,9},{9,8},{10,11... | collective-permute-start | bytes 1572872 | tf_op jit(solution)/shard_map/ppermute | solution.py:47
  35.8 1.9 %collective-permute-start.11 = (bf16[512,512]{1,0:T(8,128)(2,1)S(1)}, bf16[512,512]{1,0:T(8,128)(2,1)S(1)}, u32[]{:S(2)}, u32[]{:S(2)}) collective-permute-start(bf16[512,512]{1,0:T(8,128)(2,1)S(1)} %collective-permute-done.10.refs_9_), channel_id=1, source_target_pairs={{0,1},{1,0},{2,3},{3,2},{4,5},{5,4},{6,7},{7,6},{8,9},{9,8},{10,11... | collective-permute-start | bytes 1572872 | tf_op jit(solution)/shard_map/ppermute | solution.py:47
  48.6 1.2 %collective-permute-start.16 = (f32[32,128]{1,0:T(8,128)S(1)}, f32[32,128]{1,0:T(8,128)S(1)}, u32[]{:S(2)}, u32[]{:S(2)}) collective-permute-start(f32[32,128]{1,0:T(8,128)S(1)} %get-tuple-element.38), channel_id=1, source_target_pairs={{0,1},{1,0},{2,3},{3,2},{4,5},{5,4},{6,7},{7,6},{8,9},{9,8},{10,11... | collective-permute-start | bytes 49160 | tf_op jit(solution)/shard_map/ppermute | solution.py:47
  49.9 3.9 %collective-permute-start.17 = (f32[32,128]{1,0:T(8,128)S(1)}, f32[32,128]{1,0:T(8,128)S(1)}, u32[]{:S(2)}, u32[]{:S(2)}) collective-permute-start(f32[32,128]{1,0:T(8,128)S(1)} %join.4.mine_ref), channel_id=1, source_target_pairs={{0,2},{1,7},{2,0},{3,5},{4,6},{5,3},{6,4},{7,1},{8,10},{9,15},{10,... | collective-permute-start | bytes 49160 | tf_op jit(solution)/shard_map/ppermute | solution.py:43
  53.8 3.9 %collective-permute-start.18 = (f32[32,128]{1,0:T(8,128)S(1)}, f32[32,128]{1,0:T(8,128)S(1)}, u32[]{:S(2)}, u32[]{:S(2)}) collective-permute-start(f32[32,128]{1,0:T(8,128)S(1)} %join.5.mine_ref), channel_id=1, source_target_pairs={{0,8},{1,25},{2,10},{3,27},{4,12},{5,29},{6,14},{7,31},{8,0},{9,17... | collective-permute-start | bytes 49160 | tf_op jit(solution)/shard_map/ppermute | solution.py:43
  57.7 3.9 %collective-permute-start.19 = (f32[32,128]{1,0:T(8,128)S(1)}, f32[32,128]{1,0:T(8,128)S(1)}, u32[]{:S(2)}, u32[]{:S(2)}) collective-permute-start(f32[32,128]{1,0:T(8,128)S(1)} %join.6.mine_ref), channel_id=1, source_target_pairs={{0,32},{1,97},{2,34},{3,99},{4,36},{5,101},{6,38},{7,103},{8,40},{... | collective-permute-start | bytes 49160 | tf_op jit(solution)/shard_map/ppermute | solution.py:43
  61.6 1.5 %collective-permute-start.20 = (f32[32,128]{1,0:T(8,128)S(1)}, f32[32,128]{1,0:T(8,128)S(1)}, u32[]{:S(2)}, u32[]{:S(2)}) collective-permute-start(f32[32,128]{1,0:T(8,128)S(1)} %join.7.mine_ref), channel_id=1, source_target_pairs={{0,1},{1,0},{2,3},{3,2},{4,5},{5,4},{6,7},{7,6},{8,9},{9,8},{10,11... | collective-permute-start | bytes 49160 | tf_op jit(solution)/shard_map/ppermute | solution.py:47
  71.3 3.5 %collective-permute-start.22 = (bf16[1536,512]{1,0:T(8,128)(2,1)S(1)}, bf16[1536,512]{1,0:T(8,128)(2,1)S(1)}, u32[]{:S(2)}, u32[]{:S(2)}) collective-permute-start(bf16[1536,512]{1,0:T(8,128)(2,1)S(1)} %text_far.1.text_ref), channel_id=1, source_target_pairs={{0,1},{1,0},{2,3},{3,2},{4,5},{5,4},{6,7},{7,6},{8,9},{9,8},{10,11... | collective-permute-start | bytes 4718600 | tf_op jit(solution)/shard_map/ppermute | solution.py:47
  74.3 12.6 %collective-permute-start.21 = (bf16[1536,512]{1,0:T(8,128)(2,1)S(1)}, bf16[1536,512]{1,0:T(8,128)(2,1)S(1)}, u32[]{:S(2)}, u32[]{:S(2)}) collective-permute-start(bf16[1536,512]{1,0:T(8,128)(2,1)S(1)} %get-tuple-element.49), channel_id=1, source_target_pairs={{0,1},{1,0},{2,3},{3,2},{4,5},{5,4},{6,7},{7,6},{8,9},{9,8},{10,11... | collective-permute-start | bytes 4718600 | tf_op jit(solution)/shard_map/ppermute | solution.py:47
  75.2 11.6 %collective-permute-start.23 = (bf16[512,512]{1,0:T(8,128)(2,1)S(1)}, bf16[512,512]{1,0:T(8,128)(2,1)S(1)}, u32[]{:S(2)}, u32[]{:S(2)}) collective-permute-start(bf16[512,512]{1,0:T(8,128)(2,1)S(1)} %get-tuple-element.50), channel_id=1, source_target_pairs={{0,32},{1,97},{2,34},{3,99},{4,36},{5,101},{6,38},{7,103},{8,40},{... | collective-permute-start | bytes 1572872 | tf_op jit(solution)/shard_map/ppermute | solution.py:43
  77.6 9.3 %collective-permute-start.24 = (bf16[512,512]{1,0:T(8,128)(2,1)S(1)}, bf16[512,512]{1,0:T(8,128)(2,1)S(1)}, u32[]{:S(2)}, u32[]{:S(2)}) collective-permute-start(bf16[512,512]{1,0:T(8,128)(2,1)S(1)} %get-tuple-element.51), channel_id=1, source_target_pairs={{0,2},{1,7},{2,0},{3,5},{4,6},{5,3},{6,4},{7,1},{8,10},{9,15},{10,... | collective-permute-start | bytes 1572872 | tf_op jit(solution)/shard_map/ppermute | solution.py:43
  80.1 9.2 %collective-permute-start.25 = (bf16[512,512]{1,0:T(8,128)(2,1)S(1)}, bf16[512,512]{1,0:T(8,128)(2,1)S(1)}, u32[]{:S(2)}, u32[]{:S(2)}) collective-permute-start(bf16[512,512]{1,0:T(8,128)(2,1)S(1)} %get-tuple-element.52), channel_id=1, source_target_pairs={{0,8},{1,25},{2,10},{3,27},{4,12},{5,29},{6,14},{7,31},{8,0},{9,17... | collective-permute-start | bytes 1572872 | tf_op jit(solution)/shard_map/ppermute | solution.py:43
  82.7 4.1 %collective-permute-start.26 = (f32[8,128]{1,0:T(8,128)S(1)}, f32[8,128]{1,0:T(8,128)S(1)}, u32[]{:S(2)}, u32[]{:S(2)}) collective-permute-start(f32[8,128]{1,0:T(8,128)S(1)} %get-tuple-element.53.loss_ref), channel_id=1, source_target_pairs={{0,2},{1,7},{2,0},{3,5},{4,6},{5,3},{6,4},{7,1},{8,10},{9,15},{10,... | collective-permute-start | bytes 12296 | tf_op jit(solution)/shard_map/ppermute | solution.py:43
  89.9 6.7 %collective-permute-start.27 = (bf16[256,512]{1,0:T(8,128)(2,1)S(1)}, bf16[256,512]{1,0:T(8,128)(2,1)S(1)}, u32[]{:S(2)}, u32[]{:S(2)}) collective-permute-start(bf16[256,512]{1,0:T(8,128)(2,1)S(1)} %get-tuple-element.55), channel_id=1, source_target_pairs={{0,8},{1,25},{2,10},{3,27},{4,12},{5,29},{6,14},{7,31},{8,0},{9,17... | collective-permute-start | bytes 786440 | tf_op jit(solution)/shard_map/ppermute | solution.py:43
  92.6 6.4 %collective-permute-start.28 = (bf16[256,512]{1,0:T(8,128)(2,1)S(1)}, bf16[256,512]{1,0:T(8,128)(2,1)S(1)}, u32[]{:S(2)}, u32[]{:S(2)}) collective-permute-start(bf16[256,512]{1,0:T(8,128)(2,1)S(1)} %get-tuple-element.56), channel_id=1, source_target_pairs={{0,32},{1,97},{2,34},{3,99},{4,36},{5,101},{6,38},{7,103},{8,40},{... | collective-permute-start | bytes 786440 | tf_op jit(solution)/shard_map/ppermute | solution.py:43
  92.7 6.4 %collective-permute-start.29 = (bf16[256,512]{1,0:T(8,128)(2,1)S(1)}, bf16[256,512]{1,0:T(8,128)(2,1)S(1)}, u32[]{:S(2)}, u32[]{:S(2)}) collective-permute-start(bf16[256,512]{1,0:T(8,128)(2,1)S(1)} %get-tuple-element.57), channel_id=1, source_target_pairs={{0,2},{1,7},{2,0},{3,5},{4,6},{5,3},{6,4},{7,1},{8,10},{9,15},{10,... | collective-permute-start | bytes 786440 | tf_op jit(solution)/shard_map/ppermute | solution.py:43
  92.9 3.7 %collective-permute-start.30 = (f32[8,128]{1,0:T(8,128)S(1)}, f32[8,128]{1,0:T(8,128)S(1)}, u32[]{:S(2)}, u32[]{:S(2)}) collective-permute-start(f32[8,128]{1,0:T(8,128)S(1)} %get-tuple-element.58.loss_ref), channel_id=1, source_target_pairs={{0,8},{1,25},{2,10},{3,27},{4,12},{5,29},{6,14},{7,31},{8,0},{9,17... | collective-permute-start | bytes 12296 | tf_op jit(solution)/shard_map/ppermute | solution.py:43
  99.3 6.6 %collective-permute-start.31 = (bf16[128,512]{1,0:T(8,128)(2,1)S(1)}, bf16[128,512]{1,0:T(8,128)(2,1)S(1)}, u32[]{:S(2)}, u32[]{:S(2)}) collective-permute-start(bf16[128,512]{1,0:T(8,128)(2,1)S(1)} %get-tuple-element.60), channel_id=1, source_target_pairs={{0,2},{1,7},{2,0},{3,5},{4,6},{5,3},{6,4},{7,1},{8,10},{9,15},{10,... | collective-permute-start | bytes 393224 | tf_op jit(solution)/shard_map/ppermute | solution.py:43
  99.6 6.4 %collective-permute-start.32 = (bf16[128,512]{1,0:T(8,128)(2,1)S(1)}, bf16[128,512]{1,0:T(8,128)(2,1)S(1)}, u32[]{:S(2)}, u32[]{:S(2)}) collective-permute-start(bf16[128,512]{1,0:T(8,128)(2,1)S(1)} %get-tuple-element.61), channel_id=1, source_target_pairs={{0,8},{1,25},{2,10},{3,27},{4,12},{5,29},{6,14},{7,31},{8,0},{9,17... | collective-permute-start | bytes 393224 | tf_op jit(solution)/shard_map/ppermute | solution.py:43
  99.9 6.0 %collective-permute-start.33 = (bf16[128,512]{1,0:T(8,128)(2,1)S(1)}, bf16[128,512]{1,0:T(8,128)(2,1)S(1)}, u32[]{:S(2)}, u32[]{:S(2)}) collective-permute-start(bf16[128,512]{1,0:T(8,128)(2,1)S(1)} %get-tuple-element.62), channel_id=1, source_target_pairs={{0,32},{1,97},{2,34},{3,99},{4,36},{5,101},{6,38},{7,103},{8,40},{... | collective-permute-start | bytes 393224 | tf_op jit(solution)/shard_map/ppermute | solution.py:43
  102.3 3.7 %collective-permute-start.34 = (f32[8,128]{1,0:T(8,128)S(1)}, f32[8,128]{1,0:T(8,128)S(1)}, u32[]{:S(2)}, u32[]{:S(2)}) collective-permute-start(f32[8,128]{1,0:T(8,128)S(1)} %get-tuple-element.64.loss_ref), channel_id=1, source_target_pairs={{0,32},{1,97},{2,34},{3,99},{4,36},{5,101},{6,38},{7,103},{8,40},{... | collective-permute-start | bytes 12296 | tf_op jit(solution)/shard_map/ppermute | solution.py:43
  106.1 2.4 %collective-permute-start.35 = (f32[392,512]{1,0:T(8,128)S(1)}, f32[392,512]{1,0:T(8,128)S(1)}, u32[]{:S(2)}, u32[]{:S(2)}) collective-permute-start(f32[392,512]{1,0:T(8,128)S(1)} %get-tuple-element.66), channel_id=1, source_target_pairs={{0,1},{1,0},{2,3},{3,2},{4,5},{5,4},{6,7},{7,6},{8,9},{9,8},{10,11... | collective-permute-start | bytes 2408456 | tf_op jit(solution)/shard_map/ppermute | solution.py:47

commit v3 on v2

--- a/solution.py
+++ b/solution.py
@@ -177,84 +177,116 @@
     )
 
 
-def far_text_kernel(core_ref, coeff_ref, rows_ref, out_ref):
-    for q in range(3):
-        out_ref[q * 512 : q * 512 + 512, :] = text_grad(coeff_ref, rows_ref, 1536 + q * 512).astype(bf16)
-
-
-def near_text_kernel(core_ref, coeff_ref, rows_ref, g0, g1, g2, base_ref, send_ref):
-    core = core_ref[0]
-    for q, g in enumerate((g0, g1, g2)):
+def far_text_kernel(q, core_ref, coeff_ref, rows_ref, out_ref):
+    out_ref[...] = text_grad(coeff_ref, rows_ref, 1536 + q * 512).astype(bf16)
+
+
+def near_text_kernel(core_ref, coeff_ref, rows_ref, g0, g1, g2, own_ref, after0, after1, after2, base_ref, s0, s1, s2, early_ref, kept_ref):
+    first = core_ref[0] == 0
+    for q, (g, s) in enumerate(((g0, s0), (g1, s1), (g2, s2))):
+        grad = text_grad(coeff_ref, rows_ref, q * 512)
+        own = slice(q * 64, q * 64 + 64)
+        early_ref[own, :] = own_ref[q * 128 : q * 128 + 64, :]
+        early_ref[192 + q * 64 : 192 + q * 64 + 64, :] = grad[0:64, :]
+        kept_ref[own, :] = grad[64:128, :]
+        base_ref[q * 512 : q * 512 + 128, :] = jnp.zeros((128, grad.shape[1]), f32)
+        base_ref[q * 512 + 128 : q * 512 + 512, :] = jnp.where(first, 0.0, grad[128:512, :])
+        s[...] = jnp.where(first, grad.astype(bf16), g[...])
+
+
+def split_terms(x):
+    high = x.astype(bf16)
+    rest = x - high.astype(f32)
+    middle = rest.astype(bf16)
+    low = (rest - middle.astype(f32)).astype(bf16)
+    pair = [jnp.concatenate([t, t], 0) for t in (high, middle, low)]
+    return jnp.concatenate(pair + [jnp.zeros((16, 128), bf16)], 1)
+
+
+def join_terms(ref, start):
+    x = ref[start : start + 16, :].astype(f32)
+    return (x[0:8, 0:128] + x[0:8, 128:256]) + x[0:8, 256:384]
+
+
+def far_message_kernel(core_ref, g, text_ref, got_ref, *refs):
+    both = (text_ref[...].astype(f32) + got_ref[...].astype(f32)).astype(bf16)
+    refs[-1][0:512, :] = jnp.where(core_ref[0] == 0, g[...], both)
+    if len(refs) == 2:
+        refs[-1][512:528, :] = split_terms(refs[0][...])
+
+
+def far_sum_kernel(core_ref, base_ref, r0, r1, r2, loss_ref, total_ref, loss_out):
+    loss_out[...] = loss_ref[...] + join_terms(r0, 512)
+    for q, r in enumerate((r0, r1, r2)):
         rows = slice(q * 512, q * 512 + 512)
-        grad = text_grad(coeff_ref, rows_ref, q * 512)
-        base_ref[rows, :] = jnp.where(core == 0, 0.0, grad)
-        send_ref[rows, :] = jnp.where(core == 0, grad.astype(bf16), g[...])
-
-
-def far_message_kernel(core_ref, g0, g1, g2, text_ref, got_ref, m0, m1, m2):
-    core = core_ref[0]
-    for q, (g, m) in enumerate(((g0, m0), (g1, m1), (g2, m2))):
+        total_ref[rows, :] = base_ref[rows, :] + r[0:512, :].astype(f32)
+
+
+def near_sum_kernel(core_ref, total_ref, g0, g1, g2, loss_ref, low_ref, s0, s1, s2):
+    s0[256:272, :] = split_terms(loss_ref[...])
+    for q, (g, s) in enumerate(((g0, s0), (g1, s1), (g2, s2))):
         rows = slice(q * 512, q * 512 + 512)
-        both = (text_ref[rows, :].astype(f32) + got_ref[rows, :].astype(f32)).astype(bf16)
-        m[...] = jnp.where(core == 0, g[...], both)
-
-
-def near_sum_kernel(core_ref, base_ref, got_ref, r0, r1, r2, loss_ref, loss_got, low_ref, s0, s1, s2, loss_out):
-    loss_out[...] = loss_ref[...] + loss_got[...]
+        total = total_ref[rows, :] + g[...].astype(f32)
+        low_ref[q * 256 : q * 256 + 256, :] = total[0:256]
+        s[0:256, :] = total[256:512].astype(bf16)
+
+
+def half_sum_kernel(core_ref, low_ref, r0, r1, r2, loss_ref, out_ref, s0, s1, s2, loss_out):
+    loss = loss_ref[...] + join_terms(r0, 256)
+    loss_out[...] = loss
+    s0[128:144, :] = split_terms(loss)
     for q, (r, s) in enumerate(((r0, s0), (r1, s1), (r2, s2))):
-        rows = slice(q * 512, q * 512 + 512)
-        total = base_ref[rows, :] + got_ref[rows, :].astype(f32) + r[...].astype(f32)
-        low_ref[q * 256 : q * 256 + 256, :] = total[0:256]
-        s[...] = total[256:512].astype(bf16)
-
-
-def half_sum_kernel(core_ref, low_ref, r0, r1, r2, loss_ref, loss_got, out_ref, s0, s1, s2, loss_out):
-    loss_out[...] = loss_ref[...] + loss_got[...]
-    for q, (r, s) in enumerate(((r0, s0), (r1, s1), (r2, s2))):
-        total = low_ref[q * 256 : q * 256 + 256, :] + r[...].astype(f32)
+        total = low_ref[q * 256 : q * 256 + 256, :] + r[0:256, :].astype(f32)
         out_ref[q * 128 : q * 128 + 128, :] = total[0:128]
-        s[...] = total[128:256].astype(bf16)
-
-
-def last_sum_kernel(core_ref, low_ref, r0, r1, r2, own_ref, loss_ref, loss_got, keep_ref, send_ref, loss_out):
+        s[0:128, :] = total[128:256].astype(bf16)
+
+
+def last_sum_kernel(core_ref, low_ref, r0, r1, r2, loss_ref, keep_ref, send_ref):
     first = core_ref[0] == 0
-    loss = loss_ref[...] + loss_got[...]
-    loss_out[...] = loss
+    loss = loss_ref[...] + join_terms(r0, 128)
+    send_ref[192:200, :] = jnp.concatenate([loss] * 4, 1)
+    keep_ref[192:200, :] = jnp.concatenate([loss] * 4, 1)
     for q, r in enumerate((r0, r1, r2)):
         rows = slice(q * 64, q * 64 + 64)
-        total = low_ref[q * 128 : q * 128 + 128, :] + r[...].astype(f32)
+        total = low_ref[q * 128 : q * 128 + 128, :] + r[0:128, :].astype(f32)
         keep_ref[rows, :] = jnp.where(first, total[0:64], total[64:128])
         send_ref[rows, :] = jnp.where(first, total[64:128], total[0:64])
-        send_ref[192 + q * 64 : 192 + q * 64 + 64, :] = own_ref[q * 128 : q * 128 + 64, :]
-    send_ref[384:392, :] = jnp.concatenate([loss] * 4, 1)
-
-
-def finish_kernel(count, core_ref, keep_ref, got_ref, own_ref, loss_ref, image_out, text_out, loss_out):
+
+
+def finish_kernel(count, core_ref, keep_ref, got_ref, own_ref, early_ref, kept_ref, image_out, text_out, loss_out):
     first = core_ref[0] == 0
     for q in range(3):
         rows = slice(q * 64, q * 64 + 64)
         keep = keep_ref[rows, :]
         got = got_ref[rows, :]
-        own_mine = own_ref[q * 128 + 64 : q * 128 + 128, :]
-        own_got = got_ref[192 + q * 64 : 192 + q * 64 + 64, :]
-        image_out[rows, :] = jnp.where(first, keep + own_got, got + own_mine)
-        text_out[rows, :] = jnp.where(first, got, keep)
-    loss_out[...] = (loss_ref[0:1, 0:1] + got_ref[384:385, 0:1]) * (0.5 / count)
+        own_image = jnp.where(first, early_ref[rows, :], own_ref[q * 128 + 64 : q * 128 + 128, :])
+        own_text = jnp.where(first, early_ref[192 + q * 64 : 192 + q * 64 + 64, :], kept_ref[rows, :])
+        image_out[rows, :] = jnp.where(first, keep, got) + own_image
+        text_out[rows, :] = jnp.where(first, got, keep) + own_text
+    loss_out[...] = (keep_ref[192:193, 0:1] + got_ref[192:193, 0:1]) * (0.5 / count)
+
+
+def select_kernel(core_ref, image_ref, text_ref, out_ref):
+    out_ref[...] = jnp.where(core_ref[0] == 0, text_ref[...], image_ref[...])
+
+
+def pair_kernel(core_ref, image_ref, text_ref, got_ref, *out_refs):
+    first = core_ref[0] == 0
+    for q, out in enumerate(out_refs):
+        rows = slice(q * 64, q * 64 + 64)
+        out[0:64, :] = jnp.where(first, image_ref[rows, :], got_ref[rows, :])
+        out[64:128, :] = jnp.where(first, got_ref[rows, :], text_ref[rows, :])
 
 
 def per_device(image_emb, text_emb):
-    core = lax.axis_index("c")
-    core_id = core.reshape(1).astype(jnp.int32)
+    core_id = lax.axis_index("c").reshape(1).astype(jnp.int32)
     pair_rows, width = image_emb.shape
     count = pair_rows * 128
 
-    swapped = core_swap(jnp.where(core == 0, text_emb, image_emb))
-    near = []
-    for q in range(3):
-        rows = slice(q * 64, q * 64 + 64)
-        first = jnp.where(core == 0, image_emb[rows], swapped[rows])
-        second = jnp.where(core == 0, swapped[rows], text_emb[rows])
-        near.append(jnp.concatenate([first, second], 0))
+    swapped = core_swap(call(select_kernel, "select", [core_id, image_emb, text_emb], [shape(pair_rows, width, dtype=bf16)], limit=4)[0])
+    near = call(
+        pair_kernel, "pair", [core_id, image_emb, text_emb, swapped], [shape(128, width, dtype=bf16)] * 3, limit=4
+    )
     for step in range(2):
         got = [flip_permute(near[q], q + step) for q in range(3)]
         near = [jnp.concatenate([a, b], 0) for a, b in zip(near, got)]
@@ -287,50 +319,52 @@
         flops=2 * 1536 * 3072 * 512,
         limit=8,
     )
-    text_far = call(
-        far_text_kernel, "text_far", [core_id, held(coeffs), held(rows)], [shape(1536, width, dtype=bf16)], flops=1536 * 3072 * 512
-    )[0]
-    text_far_got = core_swap(text_far)
-    base, near_send = call(
+    messages = []
+    for q, g in enumerate((g0, g1, g2)):
+        far_grad = call(
+            functools.partial(far_text_kernel, q),
+            "text_far",
+            [core_id, held(coeffs), held(rows)],
+            [shape(512, width, dtype=bf16)],
+            flops=512 * 3072 * 512,
+        )[0]
+        ins = [core_id, g, far_grad, core_swap(far_grad)]
+        if q == 0:
+            ins.append(loss)
+        messages.append(call(far_message_kernel, "far_message", ins, [shape(528 if q == 0 else 512, width, dtype=bf16)])[0])
+    got = [flip_permute(messages[q], q + 2) for q in range(3)]
+    base, *near_send, early, kept = call(
         near_text_kernel,
         "text_near",
-        [core_id, held(coeffs), held(rows), g0, g1, g2],
-        [shape(1536, width), shape(1536, width, dtype=bf16)],
+        [core_id, held(coeffs), held(rows), g0, g1, g2, own, *messages],
+        [shape(1536, width)] + [shape(512, width, dtype=bf16)] * 3 + [shape(384, width), shape(192, width)],
         flops=1536 * 3072 * 512,
     )
-    near_got = core_swap(near_send)
-    messages = call(
-        far_message_kernel, "far_message", [core_id, g0, g1, g2, text_far, text_far_got], [shape(512, width, dtype=bf16)] * 3
-    )
-    got = [flip_permute(messages[q], q + 2) for q in range(3)]
-    loss_got = flip_permute(loss, 0)
-    low, *messages, loss = call(
+    near_got = [core_swap(a) for a in near_send]
+    early = core_swap(early)
+    total, loss = call(far_sum_kernel, "far_sum", [core_id, base, *got, loss], [shape(1536, width), shape(8, 128)])
+    low, *messages = call(
         near_sum_kernel,
         "near_sum",
-        [core_id, base, near_got, *got, loss, loss_got],
-        [shape(768, width)] + [shape(256, width, dtype=bf16)] * 3 + [shape(8, 128)],
+        [core_id, total, *near_got, loss],
+        [shape(768, width)] + [shape(272 if q == 0 else 256, width, dtype=bf16) for q in range(3)],
     )
     got = [flip_permute(messages[q], q + 1) for q in range(3)]
-    loss_got = flip_permute(loss, 1)
     low, *messages, loss = call(
         half_sum_kernel,
         "half_sum",
-        [core_id, low, *got, loss, loss_got],
-        [shape(384, width)] + [shape(128, width, dtype=bf16)] * 3 + [shape(8, 128)],
+        [core_id, low, *got, loss],
+        [shape(384, width)] + [shape(144 if q == 0 else 128, width, dtype=bf16) for q in range(3)] + [shape(8, 128)],
     )
     got = [flip_permute(messages[q], q) for q in range(3)]
-    loss_got = flip_permute(loss, 2)
-    keep, send, loss = call(
-        last_sum_kernel,
-        "last_sum",
-        [core_id, low, *got, own, loss, loss_got],
-        [shape(192, width), shape(392, width), shape(8, 128)],
+    keep, send = call(
+        last_sum_kernel, "last_sum", [core_id, low, *got, loss], [shape(200, width), shape(200, width)]
     )
     swapped = core_swap(send)
     grad_image, grad_text, loss = call(
         functools.partial(finish_kernel, count),
         "finish",
-        [core_id, keep, swapped, own, loss],
+        [core_id, keep, swapped, own, early, kept],
         [shape(192, width), shape(192, width), shape(1, 1)],
     )
     return loss.reshape(()), grad_image, grad_text

time: 110 us -> 107 us (0.973)
  starting transfers between devices: 44.5 us -> 42.3 us
  other arithmetic: 2.19 us -> 0.06 us
  local copies, waits for them, and re-layouts: 0.01 us -> 1.97 us
    ppermute x24 -> x21, starting transfers between devices: 41.2 us -> 36.9 us  [flip_permute(): return lax.ppermute(x, AXES, ROLE_PAIRS[dim % 3])]
    select_n x2 -> x0, other arithmetic: 2 us -> none  [the longest x1 1.04 us: per_device(): first = jnp.where(core == 0, image_emb[rows], swapped[rows])]
    ppermute x12 -> x17, starting transfers between devices: 3.37 us -> 5.36 us  [core_swap(): return lax.ppermute(x, 'c', SWAP)]
    unnamed x4 -> x13, local copies, waits for them, and re-layouts: 0.01 us -> 1.91 us
    ppermute x12 -> x17, waiting for transfers between devices: 7.62 us -> 6.83 us  [core_swap(): return lax.ppermute(x, 'c', SWAP)]
    pallas_call x13 -> x20, Pallas kernels: 24.1 us -> 24.6 us  [call(): pl.pallas_call(kernel, in_specs=in_specs, out_specs=[VMEM] * len(outs), o...]
    ppermute x24 -> x21, waiting for transfers between devices: 30.2 us -> 30 us  [flip_permute(): return lax.ppermute(x, AXES, ROLE_PAIRS[dim % 3])]
  transfers between devices with their start and end apart: 36 -> 38, of which waited for: 19 -> 19; matrix products, arithmetic and copies ran while one was open for 0% -> 0% of each run, Pallas kernels for 3% -> 5%
where the time goes in v3:
time: 107 us
  starting transfers between devices  42.3 us (40%)
  waiting for transfers between devices  36.8 us (34%)
  Pallas kernels  24.6 us (23%)
  local copies, waits for them, and re-layouts  1.97 us (2%)
    ppermute x21, starting transfers between devices, flip_permute(): return lax.ppermute(x, AXES, ROLE_PAIRS[dim % 3])  36.9 us
    ppermute x21, waiting for transfers between devices, flip_permute(): return lax.ppermute(x, AXES, ROLE_PAIRS[dim % 3])  30 us
    pallas_call x20, Pallas kernels, call(): pl.pallas_call(kernel, in_specs=in_specs, out_specs=[VMEM] * len(outs), o...  24.6 us
    ppermute x17, waiting for transfers between devices, core_swap(): return lax.ppermute(x, 'c', SWAP)  6.83 us
    ppermute x17, starting transfers between devices, core_swap(): return lax.ppermute(x, 'c', SWAP)  5.36 us
  transfers between devices with their start and end apart: 38, of which 19 were waited for; matrix products, arithmetic and copies ran while one was open for 0% of the time, Pallas kernels for 5%

profile of v3, /device:TPU:1, one launch (start us, length us, event | category | flops | bytes accessed | tf_op | source)
XLA Modules:
  0.0 106.6 jit_solution(9129235012388527881)
XLA Ops:
  0.6 0.9 copy-done
  1.6 0.9 copy-done.2
  2.5 1.5 %collective-permute-start = (bf16[192,512]{1,0:T(8,128)(2,1)S(1)}, bf16[192,512]{1,0:T(8,128)(2,1)S(1)}, u32[]{:S(2)}, u32[]{:S(2)}) collective-permute-start(bf16[192,512]{1,0:T(8,128)(2,1)S(1)} %select.1), channel_id=1, source_target_pairs={{0,1},{1,0},{2,3},{3,2},{4,5},{5,4},{6,7},{7,6},{8,9},{9,8},{10,11... | collective-permute-start | bytes 589832 | tf_op jit(solution)/shard_map/ppermute | solution.py:47
  4.0 1.1 %collective-permute-done.got_ref = bf16[192,512]{1,0:T(8,128)(2,1)S(1)} collective-permute-done((bf16[192,512]{1,0:T(8,128)(2,1)S(1)}, bf16[192,512]{1,0:T(8,128)(2,1)S(1)}, u32[]{:S(2)}, u32[]{:S(2)}) %collective-permute-start) | collective-permute-done | bytes 196640 | tf_op jit(solution)/shard_map/ppermute | solution.py:47
  5.1 2.6 %collective-permute-start.1 = (bf16[128,512]{1,0:T(8,128)(2,1)S(1)}, bf16[128,512]{1,0:T(8,128)(2,1)S(1)}, u32[]{:S(2)}, u32[]{:S(2)}) collective-permute-start(bf16[128,512]{1,0:T(8,128)(2,1)S(1)} %get-tuple-element.41), channel_id=1, source_target_pairs={{0,2},{1,7},{2,0},{3,5},{4,6},{5,3},{6,4},{7,1},{8,10},{9,15},{10,... | collective-permute-start | bytes 393224 | tf_op jit(solution)/shard_map/ppermute | solution.py:43
  7.8 2.7 %collective-permute-start.4 = (bf16[128,512]{1,0:T(8,128)(2,1)S(1)}, bf16[128,512]{1,0:T(8,128)(2,1)S(1)}, u32[]{:S(2)}, u32[]{:S(2)}) collective-permute-start(bf16[128,512]{1,0:T(8,128)(2,1)S(1)} %get-tuple-element.42), channel_id=1, source_target_pairs={{0,8},{1,25},{2,10},{3,27},{4,12},{5,29},{6,14},{7,31},{8,0},{9,17... | collective-permute-start | bytes 393224 | tf_op jit(solution)/shard_map/ppermute | solution.py:43
  10.5 3.8 %collective-permute-start.7 = (bf16[128,512]{1,0:T(8,128)(2,1)S(1)}, bf16[128,512]{1,0:T(8,128)(2,1)S(1)}, u32[]{:S(2)}, u32[]{:S(2)}) collective-permute-start(bf16[128,512]{1,0:T(8,128)(2,1)S(1)} %get-tuple-element.43), channel_id=1, source_target_pairs={{0,32},{1,97},{2,34},{3,99},{4,36},{5,101},{6,38},{7,103},{8,40},{... | collective-permute-start | bytes 393224 | tf_op jit(solution)/shard_map/ppermute | solution.py:43
  14.5 2.5 %collective-permute-start.5 = (bf16[256,512]{1,0:T(8,128)(2,1)S(1)}, bf16[256,512]{1,0:T(8,128)(2,1)S(1)}, u32[]{:S(2)}, u32[]{:S(2)}) collective-permute-start(bf16[256,512]{1,0:T(8,128)(2,1)S(1)} %pad_maximum_fusion.1), channel_id=1, source_target_pairs={{0,32},{1,97},{2,34},{3,99},{4,36},{5,101},{6,38},{7,103},{8,40},{... | collective-permute-start | bytes 786440 | tf_op jit(solution)/shard_map/ppermute | solution.py:43
  17.0 2.6 %collective-permute-start.8 = (bf16[256,512]{1,0:T(8,128)(2,1)S(1)}, bf16[256,512]{1,0:T(8,128)(2,1)S(1)}, u32[]{:S(2)}, u32[]{:S(2)}) collective-permute-start(bf16[256,512]{1,0:T(8,128)(2,1)S(1)} %pad_maximum_fusion.2), channel_id=1, source_target_pairs={{0,2},{1,7},{2,0},{3,5},{4,6},{5,3},{6,4},{7,1},{8,10},{9,15},{10,... | collective-permute-start | bytes 786440 | tf_op jit(solution)/shard_map/ppermute | solution.py:43
  19.7 3.9 %collective-permute-done.8 = bf16[256,512]{1,0:T(8,128)(2,1)S(1)} collective-permute-done((bf16[256,512]{1,0:T(8,128)(2,1)S(1)}, bf16[256,512]{1,0:T(8,128)(2,1)S(1)}, u32[]{:S(2)}, u32[]{:S(2)}) %collective-permute-start.8) | collective-permute-done | bytes 262176 | tf_op jit(solution)/shard_map/ppermute | solution.py:43
  23.6 2.5 %collective-permute-start.14 = (bf16[512,512]{1,0:T(8,128)(2,1)S(1)}, bf16[512,512]{1,0:T(8,128)(2,1)S(1)}, u32[]{:S(2)}, u32[]{:S(2)}) collective-permute-start(bf16[512,512]{1,0:T(8,128)(2,1)S(1)} %constant_dynamic-update-slice_fusion.6.refs_8_), channel_id=1, source_target_pairs={{0,8},{1,25},{2,10},{3,27},{4,12},{5,29},{6,14},{7,31},{8,0},{9,17... | collective-permute-start | bytes 1572872 | tf_op jit(solution)/shard_map/ppermute | solution.py:43
  26.4 0.6 collective-permute-start.10
  27.0 5.9 %collective-permute-done.14.refs_11_ = bf16[512,512]{1,0:T(8,128)(2,1)S(1)} collective-permute-done((bf16[512,512]{1,0:T(8,128)(2,1)S(1)}, bf16[512,512]{1,0:T(8,128)(2,1)S(1)}, u32[]{:S(2)}, u32[]{:S(2)}) %collective-permute-start.14) | collective-permute-done | bytes 524320 | tf_op jit(solution)/shard_map/ppermute | solution.py:43
  33.4 2.0 %collective-permute-done.12.refs_10_ = bf16[512,512]{1,0:T(8,128)(2,1)S(1)} collective-permute-done((bf16[512,512]{1,0:T(8,128)(2,1)S(1)}, bf16[512,512]{1,0:T(8,128)(2,1)S(1)}, u32[]{:S(2)}, u32[]{:S(2)}) %collective-permute-start.12) | collective-permute-done | bytes 524320 | tf_op jit(solution)/shard_map/ppermute | solution.py:43
  36.0 1.4 %collective-permute-done.13.refs_4_ = bf16[512,512]{1,0:T(8,128)(2,1)S(1)} collective-permute-done((bf16[512,512]{1,0:T(8,128)(2,1)S(1)}, bf16[512,512]{1,0:T(8,128)(2,1)S(1)}, u32[]{:S(2)}, u32[]{:S(2)}) %collective-permute-start.13) | collective-permute-done | bytes 524320 | tf_op jit(solution)/shard_map/ppermute | solution.py:47
  37.4 0.7 collective-permute-done.11.refs_3_
  38.1 10.9 %forward.1 = (bf16[1536,512]{1,0:T(8,128)(2,1)S(1)}, bf16[3072,512]{1,0:T(8,128)(2,1)S(1)}, f32[512,3072]{1,0:T(8,128)S(1)}, f32[512,3072]{1,0:T(8,128)S(1)}, f3...) custom-call(s32[1]{0:T(128)} %bitcast.core_ref, bf16[192,512]{1,0:T(8,128)(2,1)S(1)} %copy-done.1, ...), custom_call_target="tpu_custom_call" | custom-call | flops 4831838208 | tf_op jit(solution)/shard_map/forward/pallas_call | solution.py:52
  49.4 0.8 collective-permute-done.16.got_ref
  50.3 2.0 %collective-permute-start.17 = (f32[32,128]{1,0:T(8,128)S(1)}, f32[32,128]{1,0:T(8,128)S(1)}, u32[]{:S(2)}, u32[]{:S(2)}) collective-permute-start(f32[32,128]{1,0:T(8,128)S(1)} %join.4.mine_ref), channel_id=1, source_target_pairs={{0,2},{1,7},{2,0},{3,5},{4,6},{5,3},{6,4},{7,1},{8,10},{9,15},{10,... | collective-permute-start | bytes 49160 | tf_op jit(solution)/shard_map/ppermute | solution.py:43
  52.3 1.9 %collective-permute-done.17.got_ref = f32[32,128]{1,0:T(8,128)S(1)} collective-permute-done((f32[32,128]{1,0:T(8,128)S(1)}, f32[32,128]{1,0:T(8,128)S(1)}, u32[]{:S(2)}, u32[]{:S(2)}) %collective-permute-start.17) | collective-permute-done | bytes 16416 | tf_op jit(solution)/shard_map/ppermute | solution.py:43
  54.2 2.1 %collective-permute-start.18 = (f32[32,128]{1,0:T(8,128)S(1)}, f32[32,128]{1,0:T(8,128)S(1)}, u32[]{:S(2)}, u32[]{:S(2)}) collective-permute-start(f32[32,128]{1,0:T(8,128)S(1)} %join.5.mine_ref), channel_id=1, source_target_pairs={{0,8},{1,25},{2,10},{3,27},{4,12},{5,29},{6,14},{7,31},{8,0},{9,17... | collective-permute-start | bytes 49160 | tf_op jit(solution)/shard_map/ppermute | solution.py:43
  56.3 1.8 %collective-permute-done.18.got_ref = f32[32,128]{1,0:T(8,128)S(1)} collective-permute-done((f32[32,128]{1,0:T(8,128)S(1)}, f32[32,128]{1,0:T(8,128)S(1)}, u32[]{:S(2)}, u32[]{:S(2)}) %collective-permute-start.18) | collective-permute-done | bytes 16416 | tf_op jit(solution)/shard_map/ppermute | solution.py:43
  58.1 1.4 %collective-permute-start.19 = (f32[32,128]{1,0:T(8,128)S(1)}, f32[32,128]{1,0:T(8,128)S(1)}, u32[]{:S(2)}, u32[]{:S(2)}) collective-permute-start(f32[32,128]{1,0:T(8,128)S(1)} %join.6.mine_ref), channel_id=1, source_target_pairs={{0,32},{1,97},{2,34},{3,99},{4,36},{5,101},{6,38},{7,103},{8,40},{... | collective-permute-start | bytes 49160 | tf_op jit(solution)/shard_map/ppermute | solution.py:43
  59.5 2.5 %collective-permute-done.19.got_ref = f32[32,128]{1,0:T(8,128)S(1)} collective-permute-done((f32[32,128]{1,0:T(8,128)S(1)}, f32[32,128]{1,0:T(8,128)S(1)}, u32[]{:S(2)}, u32[]{:S(2)}) %collective-permute-start.19) | collective-permute-done | bytes 16416 | tf_op jit(solution)/shard_map/ppermute | solution.py:43
  62.5 1.0 collective-permute-done.20.got_ref
  63.5 5.6 %coeffs.1 = (bf16[1536,3072]{1,0:T(8,128)(2,1)S(1)}, bf16[512,512]{1,0:T(8,128)(2,1)S(1)}, bf16[512,512]{1,0:T(8,128)(2,1)S(1)}, bf16[512,512]{1,0:T(8,128)(2,1)...) custom-call(s32[1]{0:T(128)} %bitcast.core_ref, f32[32,128]{1,0:T(8,128)S(1)} %join.7.mine_ref, ...), custom_call_target="tpu_custom_call" | custom-call | flops 4831838208 | tf_op jit(solution)/shard_map/coeffs/pallas_call | solution.py:52
  69.1 1.0 text_far.4.text_ref
  70.4 1.0 text_far.5.text_ref
  71.8 1.0 text_far.3.text_ref
  73.2 2.0 %collective-permute-start.25 = (bf16[512,512]{1,0:T(8,128)(2,1)S(1)}, bf16[512,512]{1,0:T(8,128)(2,1)S(1)}, u32[]{:S(2)}, u32[]{:S(2)}) collective-permute-start(bf16[512,512]{1,0:T(8,128)(2,1)S(1)} %far_message.4.after1), channel_id=1, source_target_pairs={{0,2},{1,7},{2,0},{3,5},{4,6},{5,3},{6,4},{7,1},{8,10},{9,15},{10,... | collective-permute-start | bytes 1572872 | tf_op jit(solution)/shard_map/ppermute | solution.py:43
  75.4 0.9 collective-permute-start.26
  76.4 1.9 %collective-permute-start.24 = (bf16[528,512]{1,0:T(8,128)(2,1)S(1)}, bf16[528,512]{1,0:T(8,128)(2,1)S(1)}, u32[]{:S(2)}, u32[]{:S(2)}) collective-permute-start(bf16[528,512]{1,0:T(8,128)(2,1)S(1)} %far_message.3.after0), channel_id=1, source_target_pairs={{0,32},{1,97},{2,34},{3,99},{4,36},{5,101},{6,38},{7,103},{8,40},{... | collective-permute-start | bytes 1622024 | tf_op jit(solution)/shard_map/ppermute | solution.py:43
  78.3 2.7 %text_near.1 = (f32[1536,512]{1,0:T(8,128)S(1)}, bf16[512,512]{1,0:T(8,128)(2,1)S(1)}, bf16[512,512]{1,0:T(8,128)(2,1)S(1)}, bf16[512,512]{1,0:T(8,128)(2,1)S(1)...) custom-call(s32[1]{0:T(128)} %bitcast.core_ref, bf16[1536,3072]{1,0:T(8,128)(2,1)S(1)} %get-tuple-element.50.coeff_ref, ...), custom_call_target="tpu_custom_call" | custom-call | flops 2415919104 | tf_op jit(solution)/shard_map/text_near/pallas_call | solution.py:52
  81.6 0.9 collective-permute-done.25.r1
  82.8 1.9 %collective-permute-done.26.r2 = bf16[512,512]{1,0:T(8,128)(2,1)S(1)} collective-permute-done((bf16[512,512]{1,0:T(8,128)(2,1)S(1)}, bf16[512,512]{1,0:T(8,128)(2,1)S(1)}, u32[]{:S(2)}, u32[]{:S(2)}) %collective-permute-start.26) | collective-permute-done | bytes 524320 | tf_op jit(solution)/shard_map/ppermute | solution.py:43
  84.7 1.3 %collective-permute-done.24.r0 = bf16[528,512]{1,0:T(8,128)(2,1)S(1)} collective-permute-done((bf16[528,512]{1,0:T(8,128)(2,1)S(1)}, bf16[528,512]{1,0:T(8,128)(2,1)S(1)}, u32[]{:S(2)}, u32[]{:S(2)}) %collective-permute-start.24) | collective-permute-done | bytes 540704 | tf_op jit(solution)/shard_map/ppermute | solution.py:43
  86.5 1.9 %collective-permute-start.30 = (bf16[272,512]{1,0:T(8,128)(2,1)S(1)}, bf16[272,512]{1,0:T(8,128)(2,1)S(1)}, u32[]{:S(2)}, u32[]{:S(2)}) collective-permute-start(bf16[272,512]{1,0:T(8,128)(2,1)S(1)} %get-tuple-element.64), channel_id=1, source_target_pairs={{0,8},{1,25},{2,10},{3,27},{4,12},{5,29},{6,14},{7,31},{8,0},{9,17... | collective-permute-start | bytes 835592 | tf_op jit(solution)/shard_map/ppermute | solution.py:43
  88.5 0.6 collective-permute-start.31
  89.0 1.5 %collective-permute-start.32 = (bf16[256,512]{1,0:T(8,128)(2,1)S(1)}, bf16[256,512]{1,0:T(8,128)(2,1)S(1)}, u32[]{:S(2)}, u32[]{:S(2)}) collective-permute-start(bf16[256,512]{1,0:T(8,128)(2,1)S(1)} %get-tuple-element.66), channel_id=1, source_target_pairs={{0,2},{1,7},{2,0},{3,5},{4,6},{5,3},{6,4},{7,1},{8,10},{9,15},{10,... | collective-permute-start | bytes 786440 | tf_op jit(solution)/shard_map/ppermute | solution.py:43
  90.5 4.4 %collective-permute-done.31.r1 = bf16[256,512]{1,0:T(8,128)(2,1)S(1)} collective-permute-done((bf16[256,512]{1,0:T(8,128)(2,1)S(1)}, bf16[256,512]{1,0:T(8,128)(2,1)S(1)}, u32[]{:S(2)}, u32[]{:S(2)}) %collective-permute-start.31) | collective-permute-done | bytes 262176 | tf_op jit(solution)/shard_map/ppermute | solution.py:43
  94.9 0.6 collective-permute-done.32.r2
  95.6 1.5 %collective-permute-start.33 = (bf16[144,512]{1,0:T(8,128)(2,1)S(1)}, bf16[144,512]{1,0:T(8,128)(2,1)S(1)}, u32[]{:S(2)}, u32[]{:S(2)}) collective-permute-start(bf16[144,512]{1,0:T(8,128)(2,1)S(1)} %get-tuple-element.68), channel_id=1, source_target_pairs={{0,2},{1,7},{2,0},{3,5},{4,6},{5,3},{6,4},{7,1},{8,10},{9,15},{10,... | collective-permute-start | bytes 442376 | tf_op jit(solution)/shard_map/ppermute | solution.py:43
  97.2 1.4 %collective-permute-start.34 = (bf16[128,512]{1,0:T(8,128)(2,1)S(1)}, bf16[128,512]{1,0:T(8,128)(2,1)S(1)}, u32[]{:S(2)}, u32[]{:S(2)}) collective-permute-start(bf16[128,512]{1,0:T(8,128)(2,1)S(1)} %get-tuple-element.69), channel_id=1, source_target_pairs={{0,8},{1,25},{2,10},{3,27},{4,12},{5,29},{6,14},{7,31},{8,0},{9,17... | collective-permute-start | bytes 393224 | tf_op jit(solution)/shard_map/ppermute | solution.py:43
  98.5 2.0 %collective-permute-start.35 = (bf16[128,512]{1,0:T(8,128)(2,1)S(1)}, bf16[128,512]{1,0:T(8,128)(2,1)S(1)}, u32[]{:S(2)}, u32[]{:S(2)}) collective-permute-start(bf16[128,512]{1,0:T(8,128)(2,1)S(1)} %get-tuple-element.70), channel_id=1, source_target_pairs={{0,32},{1,97},{2,34},{3,99},{4,36},{5,101},{6,38},{7,103},{8,40},{... | collective-permute-start | bytes 393224 | tf_op jit(solution)/shard_map/ppermute | solution.py:43
  100.6 1.6 %collective-permute-done.34.r1 = bf16[128,512]{1,0:T(8,128)(2,1)S(1)} collective-permute-done((bf16[128,512]{1,0:T(8,128)(2,1)S(1)}, bf16[128,512]{1,0:T(8,128)(2,1)S(1)}, u32[]{:S(2)}, u32[]{:S(2)}) %collective-permute-start.34) | collective-permute-done | bytes 131104 | tf_op jit(solution)/shard_map/ppermute | solution.py:43
  102.2 1.4 %collective-permute-done.35.r2 = bf16[128,512]{1,0:T(8,128)(2,1)S(1)} collective-permute-done((bf16[128,512]{1,0:T(8,128)(2,1)S(1)}, bf16[128,512]{1,0:T(8,128)(2,1)S(1)}, u32[]{:S(2)}, u32[]{:S(2)}) %collective-permute-start.35) | collective-permute-done | bytes 131104 | tf_op jit(solution)/shard_map/ppermute | solution.py:43
  103.8 1.7 %collective-permute-done.36.got_ref = f32[200,512]{1,0:T(8,128)S(1)} collective-permute-done((f32[200,512]{1,0:T(8,128)S(1)}, f32[200,512]{1,0:T(8,128)S(1)}, u32[]{:S(2)}, u32[]{:S(2)}) %collective-permute-start.36) | collective-permute-done | bytes 409632 | tf_op jit(solution)/shard_map/ppermute | solution.py:47
  105.5 1.1 %finish.1 = (f32[192,512]{1,0:T(8,128)}, f32[192,512]{1,0:T(8,128)}, f32[1,1]{1,0:T(1,128)}) custom-call(s32[1]{0:T(128)} %bitcast.core_ref, f32[200,512]{1,0:T(8,128)S(1)} %get-tuple-element.72.keep_ref, f32[200,512]{1,0:T(8,128)S(1)} %collective-permute-done.36.got_ref, f32[384,512]{1,0:T(8,128)S(1)} %get-tuple-element.55.own_ref, ...), custom_call_target="tpu_custom_call" | custom-call | tf_op jit(solution)/shard_map/finish/pallas_call | solution.py:52
  (67 shorter events, 5.8 us)
Async XLA Ops:
  0.6 0.9 copy-start
  1.6 0.9 copy-start.2
  2.5 35.6 %copy-start.1 = (bf16[192,512]{1,0:T(8,128)(2,1)S(1)}, bf16[192,512]{1,0:T(8,128)(2,1)}, u32[]{:S(2)}) copy-start(bf16[192,512]{1,0:T(8,128)(2,1)} %image_ref.5) | copy-start | bytes 589828
  2.5 35.6 %copy-start.3 = (bf16[192,512]{1,0:T(8,128)(2,1)S(1)}, bf16[192,512]{1,0:T(8,128)(2,1)}, u32[]{:S(2)}) copy-start(bf16[192,512]{1,0:T(8,128)(2,1)} %text_ref.5) | copy-start | bytes 589828
  2.5 2.6 %collective-permute-start = (bf16[192,512]{1,0:T(8,128)(2,1)S(1)}, bf16[192,512]{1,0:T(8,128)(2,1)S(1)}, u32[]{:S(2)}, u32[]{:S(2)}) collective-permute-start(bf16[192,512]{1,0:T(8,128)(2,1)S(1)} %select.1), channel_id=1, source_target_pairs={{0,1},{1,0},{2,3},{3,2},{4,5},{5,4},{6,7},{7,6},{8,9},{9,8},{10,11... | collective-permute-start | bytes 589832 | tf_op jit(solution)/shard_map/ppermute | solution.py:47
  5.1 9.2 %collective-permute-start.1 = (bf16[128,512]{1,0:T(8,128)(2,1)S(1)}, bf16[128,512]{1,0:T(8,128)(2,1)S(1)}, u32[]{:S(2)}, u32[]{:S(2)}) collective-permute-start(bf16[128,512]{1,0:T(8,128)(2,1)S(1)} %get-tuple-element.41), channel_id=1, source_target_pairs={{0,2},{1,7},{2,0},{3,5},{4,6},{5,3},{6,4},{7,1},{8,10},{9,15},{10,... | collective-permute-start | bytes 393224 | tf_op jit(solution)/shard_map/ppermute | solution.py:43
  7.8 6.7 %collective-permute-start.4 = (bf16[128,512]{1,0:T(8,128)(2,1)S(1)}, bf16[128,512]{1,0:T(8,128)(2,1)S(1)}, u32[]{:S(2)}, u32[]{:S(2)}) collective-permute-start(bf16[128,512]{1,0:T(8,128)(2,1)S(1)} %get-tuple-element.42), channel_id=1, source_target_pairs={{0,8},{1,25},{2,10},{3,27},{4,12},{5,29},{6,14},{7,31},{8,0},{9,17... | collective-permute-start | bytes 393224 | tf_op jit(solution)/shard_map/ppermute | solution.py:43
  10.5 6.5 %collective-permute-start.7 = (bf16[128,512]{1,0:T(8,128)(2,1)S(1)}, bf16[128,512]{1,0:T(8,128)(2,1)S(1)}, u32[]{:S(2)}, u32[]{:S(2)}) collective-permute-start(bf16[128,512]{1,0:T(8,128)(2,1)S(1)} %get-tuple-element.43), channel_id=1, source_target_pairs={{0,32},{1,97},{2,34},{3,99},{4,36},{5,101},{6,38},{7,103},{8,40},{... | collective-permute-start | bytes 393224 | tf_op jit(solution)/shard_map/ppermute | solution.py:43
  14.4 12.0 %collective-permute-start.2 = (bf16[256,512]{1,0:T(8,128)(2,1)S(1)}, bf16[256,512]{1,0:T(8,128)(2,1)S(1)}, u32[]{:S(2)}, u32[]{:S(2)}) collective-permute-start(bf16[256,512]{1,0:T(8,128)(2,1)S(1)} %pad_maximum_fusion), channel_id=1, source_target_pairs={{0,8},{1,25},{2,10},{3,27},{4,12},{5,29},{6,14},{7,31},{8,0},{9,17... | collective-permute-start | bytes 786440 | tf_op jit(solution)/shard_map/ppermute | solution.py:43
  14.5 11.5 %collective-permute-start.5 = (bf16[256,512]{1,0:T(8,128)(2,1)S(1)}, bf16[256,512]{1,0:T(8,128)(2,1)S(1)}, u32[]{:S(2)}, u32[]{:S(2)}) collective-permute-start(bf16[256,512]{1,0:T(8,128)(2,1)S(1)} %pad_maximum_fusion.1), channel_id=1, source_target_pairs={{0,32},{1,97},{2,34},{3,99},{4,36},{5,101},{6,38},{7,103},{8,40},{... | collective-permute-start | bytes 786440 | tf_op jit(solution)/shard_map/ppermute | solution.py:43
  17.0 6.5 %collective-permute-start.8 = (bf16[256,512]{1,0:T(8,128)(2,1)S(1)}, bf16[256,512]{1,0:T(8,128)(2,1)S(1)}, u32[]{:S(2)}, u32[]{:S(2)}) collective-permute-start(bf16[256,512]{1,0:T(8,128)(2,1)S(1)} %pad_maximum_fusion.2), channel_id=1, source_target_pairs={{0,2},{1,7},{2,0},{3,5},{4,6},{5,3},{6,4},{7,1},{8,10},{9,15},{10,... | collective-permute-start | bytes 786440 | tf_op jit(solution)/shard_map/ppermute | solution.py:43
  23.6 9.3 %collective-permute-start.14 = (bf16[512,512]{1,0:T(8,128)(2,1)S(1)}, bf16[512,512]{1,0:T(8,128)(2,1)S(1)}, u32[]{:S(2)}, u32[]{:S(2)}) collective-permute-start(bf16[512,512]{1,0:T(8,128)(2,1)S(1)} %constant_dynamic-update-slice_fusion.6.refs_8_), channel_id=1, source_target_pairs={{0,8},{1,25},{2,10},{3,27},{4,12},{5,29},{6,14},{7,31},{8,0},{9,17... | collective-permute-start | bytes 1572872 | tf_op jit(solution)/shard_map/ppermute | solution.py:43
  26.0 6.9 %collective-permute-start.9 = (bf16[512,512]{1,0:T(8,128)(2,1)S(1)}, bf16[512,512]{1,0:T(8,128)(2,1)S(1)}, u32[]{:S(2)}, u32[]{:S(2)}) collective-permute-start(bf16[512,512]{1,0:T(8,128)(2,1)S(1)} %constant_dynamic-update-slice_fusion.6.refs_8_), channel_id=1, source_target_pairs={{0,1},{1,0},{2,3},{3,2},{4,5},{5,4},{6,7},{7,6},{8,9},{9,8},{10,11... | collective-permute-start | bytes 1572872 | tf_op jit(solution)/shard_map/ppermute | solution.py:47
  26.1 9.3 %collective-permute-start.12 = (bf16[512,512]{1,0:T(8,128)(2,1)S(1)}, bf16[512,512]{1,0:T(8,128)(2,1)S(1)}, u32[]{:S(2)}, u32[]{:S(2)}) collective-permute-start(bf16[512,512]{1,0:T(8,128)(2,1)S(1)} %constant_dynamic-update-slice_fusion.3.refs_7_), channel_id=1, source_target_pairs={{0,2},{1,7},{2,0},{3,5},{4,6},{5,3},{6,4},{7,1},{8,10},{9,15},{10,... | collective-permute-start | bytes 1572872 | tf_op jit(solution)/shard_map/ppermute | solution.py:43
  26.4 9.4 %collective-permute-start.10 = (bf16[512,512]{1,0:T(8,128)(2,1)S(1)}, bf16[512,512]{1,0:T(8,128)(2,1)S(1)}, u32[]{:S(2)}, u32[]{:S(2)}) collective-permute-start(bf16[512,512]{1,0:T(8,128)(2,1)S(1)} %constant_dynamic-update-slice_fusion.refs_6_), channel_id=1, source_target_pairs={{0,32},{1,97},{2,34},{3,99},{4,36},{5,101},{6,38},{7,103},{8,40},{... | collective-permute-start | bytes 1572872 | tf_op jit(solution)/shard_map/ppermute | solution.py:43
  27.0 9.0 %collective-permute-start.6 = (bf16[512,512]{1,0:T(8,128)(2,1)S(1)}, bf16[512,512]{1,0:T(8,128)(2,1)S(1)}, u32[]{:S(2)}, u32[]{:S(2)}) collective-permute-start(bf16[512,512]{1,0:T(8,128)(2,1)S(1)} %constant_dynamic-update-slice_fusion.3.refs_7_), channel_id=1, source_target_pairs={{0,1},{1,0},{2,3},{3,2},{4,5},{5,4},{6,7},{7,6},{8,9},{9,8},{10,11... | collective-permute-start | bytes 1572872 | tf_op jit(solution)/shard_map/ppermute | solution.py:47
  32.9 3.1 %collective-permute-start.3 = (bf16[512,512]{1,0:T(8,128)(2,1)S(1)}, bf16[512,512]{1,0:T(8,128)(2,1)S(1)}, u32[]{:S(2)}, u32[]{:S(2)}) collective-permute-start(bf16[512,512]{1,0:T(8,128)(2,1)S(1)} %constant_dynamic-update-slice_fusion.refs_6_), channel_id=1, source_target_pairs={{0,1},{1,0},{2,3},{3,2},{4,5},{5,4},{6,7},{7,6},{8,9},{9,8},{10,11... | collective-permute-start | bytes 1572872 | tf_op jit(solution)/shard_map/ppermute | solution.py:47
  32.9 3.1 %collective-permute-start.15 = (bf16[512,512]{1,0:T(8,128)(2,1)S(1)}, bf16[512,512]{1,0:T(8,128)(2,1)S(1)}, u32[]{:S(2)}, u32[]{:S(2)}) collective-permute-start(bf16[512,512]{1,0:T(8,128)(2,1)S(1)} %collective-permute-done.14.refs_11_), channel_id=1, source_target_pairs={{0,1},{1,0},{2,3},{3,2},{4,5},{5,4},{6,7},{7,6},{8,9},{9,8},{10,11... | collective-permute-start | bytes 1572872 | tf_op jit(solution)/shard_map/ppermute | solution.py:47
  35.4 2.0 %collective-permute-start.13 = (bf16[512,512]{1,0:T(8,128)(2,1)S(1)}, bf16[512,512]{1,0:T(8,128)(2,1)S(1)}, u32[]{:S(2)}, u32[]{:S(2)}) collective-permute-start(bf16[512,512]{1,0:T(8,128)(2,1)S(1)} %collective-permute-done.12.refs_10_), channel_id=1, source_target_pairs={{0,1},{1,0},{2,3},{3,2},{4,5},{5,4},{6,7},{7,6},{8,9},{9,8},{10,11... | collective-permute-start | bytes 1572872 | tf_op jit(solution)/shard_map/ppermute | solution.py:47
  35.8 2.3 %collective-permute-start.11 = (bf16[512,512]{1,0:T(8,128)(2,1)S(1)}, bf16[512,512]{1,0:T(8,128)(2,1)S(1)}, u32[]{:S(2)}, u32[]{:S(2)}) collective-permute-start(bf16[512,512]{1,0:T(8,128)(2,1)S(1)} %collective-permute-done.10.refs_9_), channel_id=1, source_target_pairs={{0,1},{1,0},{2,3},{3,2},{4,5},{5,4},{6,7},{7,6},{8,9},{9,8},{10,11... | collective-permute-start | bytes 1572872 | tf_op jit(solution)/shard_map/ppermute | solution.py:47
  49.0 1.3 %collective-permute-start.16 = (f32[32,128]{1,0:T(8,128)S(1)}, f32[32,128]{1,0:T(8,128)S(1)}, u32[]{:S(2)}, u32[]{:S(2)}) collective-permute-start(f32[32,128]{1,0:T(8,128)S(1)} %get-tuple-element.45), channel_id=1, source_target_pairs={{0,1},{1,0},{2,3},{3,2},{4,5},{5,4},{6,7},{7,6},{8,9},{9,8},{10,11... | collective-permute-start | bytes 49160 | tf_op jit(solution)/shard_map/ppermute | solution.py:47
  50.3 3.9 %collective-permute-start.17 = (f32[32,128]{1,0:T(8,128)S(1)}, f32[32,128]{1,0:T(8,128)S(1)}, u32[]{:S(2)}, u32[]{:S(2)}) collective-permute-start(f32[32,128]{1,0:T(8,128)S(1)} %join.4.mine_ref), channel_id=1, source_target_pairs={{0,2},{1,7},{2,0},{3,5},{4,6},{5,3},{6,4},{7,1},{8,10},{9,15},{10,... | collective-permute-start | bytes 49160 | tf_op jit(solution)/shard_map/ppermute | solution.py:43
  54.2 3.9 %collective-permute-start.18 = (f32[32,128]{1,0:T(8,128)S(1)}, f32[32,128]{1,0:T(8,128)S(1)}, u32[]{:S(2)}, u32[]{:S(2)}) collective-permute-start(f32[32,128]{1,0:T(8,128)S(1)} %join.5.mine_ref), channel_id=1, source_target_pairs={{0,8},{1,25},{2,10},{3,27},{4,12},{5,29},{6,14},{7,31},{8,0},{9,17... | collective-permute-start | bytes 49160 | tf_op jit(solution)/shard_map/ppermute | solution.py:43
  58.1 3.9 %collective-permute-start.19 = (f32[32,128]{1,0:T(8,128)S(1)}, f32[32,128]{1,0:T(8,128)S(1)}, u32[]{:S(2)}, u32[]{:S(2)}) collective-permute-start(f32[32,128]{1,0:T(8,128)S(1)} %join.6.mine_ref), channel_id=1, source_target_pairs={{0,32},{1,97},{2,34},{3,99},{4,36},{5,101},{6,38},{7,103},{8,40},{... | collective-permute-start | bytes 49160 | tf_op jit(solution)/shard_map/ppermute | solution.py:43
  62.0 1.5 %collective-permute-start.20 = (f32[32,128]{1,0:T(8,128)S(1)}, f32[32,128]{1,0:T(8,128)S(1)}, u32[]{:S(2)}, u32[]{:S(2)}) collective-permute-start(f32[32,128]{1,0:T(8,128)S(1)} %join.7.mine_ref), channel_id=1, source_target_pairs={{0,1},{1,0},{2,3},{3,2},{4,5},{5,4},{6,7},{7,6},{8,9},{9,8},{10,11... | collective-permute-start | bytes 49160 | tf_op jit(solution)/shard_map/ppermute | solution.py:47
  70.1 3.0 %collective-permute-start.22 = (bf16[512,512]{1,0:T(8,128)(2,1)S(1)}, bf16[512,512]{1,0:T(8,128)(2,1)S(1)}, u32[]{:S(2)}, u32[]{:S(2)}) collective-permute-start(bf16[512,512]{1,0:T(8,128)(2,1)S(1)} %text_far.4.text_ref), channel_id=1, source_target_pairs={{0,1},{1,0},{2,3},{3,2},{4,5},{5,4},{6,7},{7,6},{8,9},{9,8},{10,11... | collective-permute-start | bytes 1572872 | tf_op jit(solution)/shard_map/ppermute | solution.py:47
  71.4 3.8 %collective-permute-start.23 = (bf16[512,512]{1,0:T(8,128)(2,1)S(1)}, bf16[512,512]{1,0:T(8,128)(2,1)S(1)}, u32[]{:S(2)}, u32[]{:S(2)}) collective-permute-start(bf16[512,512]{1,0:T(8,128)(2,1)S(1)} %text_far.5.text_ref), channel_id=1, source_target_pairs={{0,1},{1,0},{2,3},{3,2},{4,5},{5,4},{6,7},{7,6},{8,9},{9,8},{10,11... | collective-permute-start | bytes 1572872 | tf_op jit(solution)/shard_map/ppermute | solution.py:47
  72.8 3.5 %collective-permute-start.21 = (bf16[512,512]{1,0:T(8,128)(2,1)S(1)}, bf16[512,512]{1,0:T(8,128)(2,1)S(1)}, u32[]{:S(2)}, u32[]{:S(2)}) collective-permute-start(bf16[512,512]{1,0:T(8,128)(2,1)S(1)} %text_far.3.text_ref), channel_id=1, source_target_pairs={{0,1},{1,0},{2,3},{3,2},{4,5},{5,4},{6,7},{7,6},{8,9},{9,8},{10,11... | collective-permute-start | bytes 1572872 | tf_op jit(solution)/shard_map/ppermute | solution.py:47
  73.2 9.3 %collective-permute-start.25 = (bf16[512,512]{1,0:T(8,128)(2,1)S(1)}, bf16[512,512]{1,0:T(8,128)(2,1)S(1)}, u32[]{:S(2)}, u32[]{:S(2)}) collective-permute-start(bf16[512,512]{1,0:T(8,128)(2,1)S(1)} %far_message.4.after1), channel_id=1, source_target_pairs={{0,2},{1,7},{2,0},{3,5},{4,6},{5,3},{6,4},{7,1},{8,10},{9,15},{10,... | collective-permute-start | bytes 1572872 | tf_op jit(solution)/shard_map/ppermute | solution.py:43
  75.4 9.3 %collective-permute-start.26 = (bf16[512,512]{1,0:T(8,128)(2,1)S(1)}, bf16[512,512]{1,0:T(8,128)(2,1)S(1)}, u32[]{:S(2)}, u32[]{:S(2)}) collective-permute-start(bf16[512,512]{1,0:T(8,128)(2,1)S(1)} %far_message.5.after2), channel_id=1, source_target_pairs={{0,8},{1,25},{2,10},{3,27},{4,12},{5,29},{6,14},{7,31},{8,0},{9,17... | collective-permute-start | bytes 1572872 | tf_op jit(solution)/shard_map/ppermute | solution.py:43
  76.4 9.5 %collective-permute-start.24 = (bf16[528,512]{1,0:T(8,128)(2,1)S(1)}, bf16[528,512]{1,0:T(8,128)(2,1)S(1)}, u32[]{:S(2)}, u32[]{:S(2)}) collective-permute-start(bf16[528,512]{1,0:T(8,128)(2,1)S(1)} %far_message.3.after0), channel_id=1, source_target_pairs={{0,32},{1,97},{2,34},{3,99},{4,36},{5,101},{6,38},{7,103},{8,40},{... | collective-permute-start | bytes 1622024 | tf_op jit(solution)/shard_map/ppermute | solution.py:43
  81.0 5.2 %collective-permute-start.27 = (bf16[512,512]{1,0:T(8,128)(2,1)S(1)}, bf16[512,512]{1,0:T(8,128)(2,1)S(1)}, u32[]{:S(2)}, u32[]{:S(2)}) collective-permute-start(bf16[512,512]{1,0:T(8,128)(2,1)S(1)} %get-tuple-element.59), channel_id=1, source_target_pairs={{0,1},{1,0},{2,3},{3,2},{4,5},{5,4},{6,7},{7,6},{8,9},{9,8},{10,11... | collective-permute-start | bytes 1572872 | tf_op jit(solution)/shard_map/ppermute | solution.py:47
  81.1 5.1 %collective-permute-start.28 = (bf16[512,512]{1,0:T(8,128)(2,1)S(1)}, bf16[512,512]{1,0:T(8,128)(2,1)S(1)}, u32[]{:S(2)}, u32[]{:S(2)}) collective-permute-start(bf16[512,512]{1,0:T(8,128)(2,1)S(1)} %get-tuple-element.60), channel_id=1, source_target_pairs={{0,1},{1,0},{2,3},{3,2},{4,5},{5,4},{6,7},{7,6},{8,9},{9,8},{10,11... | collective-permute-start | bytes 1572872 | tf_op jit(solution)/shard_map/ppermute | solution.py:47
  82.5 3.7 %collective-permute-start.29 = (bf16[512,512]{1,0:T(8,128)(2,1)S(1)}, bf16[512,512]{1,0:T(8,128)(2,1)S(1)}, u32[]{:S(2)}, u32[]{:S(2)}) collective-permute-start(bf16[512,512]{1,0:T(8,128)(2,1)S(1)} %get-tuple-element.61), channel_id=1, source_target_pairs={{0,1},{1,0},{2,3},{3,2},{4,5},{5,4},{6,7},{7,6},{8,9},{9,8},{10,11... | collective-permute-start | bytes 1572872 | tf_op jit(solution)/shard_map/ppermute | solution.py:47
  86.5 8.9 %collective-permute-start.30 = (bf16[272,512]{1,0:T(8,128)(2,1)S(1)}, bf16[272,512]{1,0:T(8,128)(2,1)S(1)}, u32[]{:S(2)}, u32[]{:S(2)}) collective-permute-start(bf16[272,512]{1,0:T(8,128)(2,1)S(1)} %get-tuple-element.64), channel_id=1, source_target_pairs={{0,8},{1,25},{2,10},{3,27},{4,12},{5,29},{6,14},{7,31},{8,0},{9,17... | collective-permute-start | bytes 835592 | tf_op jit(solution)/shard_map/ppermute | solution.py:43
  88.5 6.4 %collective-permute-start.31 = (bf16[256,512]{1,0:T(8,128)(2,1)S(1)}, bf16[256,512]{1,0:T(8,128)(2,1)S(1)}, u32[]{:S(2)}, u32[]{:S(2)}) collective-permute-start(bf16[256,512]{1,0:T(8,128)(2,1)S(1)} %get-tuple-element.65), channel_id=1, source_target_pairs={{0,32},{1,97},{2,34},{3,99},{4,36},{5,101},{6,38},{7,103},{8,40},{... | collective-permute-start | bytes 786440 | tf_op jit(solution)/shard_map/ppermute | solution.py:43
  89.0 6.4 %collective-permute-start.32 = (bf16[256,512]{1,0:T(8,128)(2,1)S(1)}, bf16[256,512]{1,0:T(8,128)(2,1)S(1)}, u32[]{:S(2)}, u32[]{:S(2)}) collective-permute-start(bf16[256,512]{1,0:T(8,128)(2,1)S(1)} %get-tuple-element.66), channel_id=1, source_target_pairs={{0,2},{1,7},{2,0},{3,5},{4,6},{5,3},{6,4},{7,1},{8,10},{9,15},{10,... | collective-permute-start | bytes 786440 | tf_op jit(solution)/shard_map/ppermute | solution.py:43
  90.5 13.3 %collective-permute-start.37 = (f32[384,512]{1,0:T(8,128)S(1)}, f32[384,512]{1,0:T(8,128)S(1)}, u32[]{:S(2)}, u32[]{:S(2)}) collective-permute-start(f32[384,512]{1,0:T(8,128)S(1)} %get-tuple-element.74), channel_id=1, source_target_pairs={{0,1},{1,0},{2,3},{3,2},{4,5},{5,4},{6,7},{7,6},{8,9},{9,8},{10,11... | collective-permute-start | bytes 2359304 | tf_op jit(solution)/shard_map/ppermute | solution.py:47
  95.6 8.0 %collective-permute-start.33 = (bf16[144,512]{1,0:T(8,128)(2,1)S(1)}, bf16[144,512]{1,0:T(8,128)(2,1)S(1)}, u32[]{:S(2)}, u32[]{:S(2)}) collective-permute-start(bf16[144,512]{1,0:T(8,128)(2,1)S(1)} %get-tuple-element.68), channel_id=1, source_target_pairs={{0,2},{1,7},{2,0},{3,5},{4,6},{5,3},{6,4},{7,1},{8,10},{9,15},{10,... | collective-permute-start | bytes 442376 | tf_op jit(solution)/shard_map/ppermute | solution.py:43
  97.2 5.0 %collective-permute-start.34 = (bf16[128,512]{1,0:T(8,128)(2,1)S(1)}, bf16[128,512]{1,0:T(8,128)(2,1)S(1)}, u32[]{:S(2)}, u32[]{:S(2)}) collective-permute-start(bf16[128,512]{1,0:T(8,128)(2,1)S(1)} %get-tuple-element.69), channel_id=1, source_target_pairs={{0,8},{1,25},{2,10},{3,27},{4,12},{5,29},{6,14},{7,31},{8,0},{9,17... | collective-permute-start | bytes 393224 | tf_op jit(solution)/shard_map/ppermute | solution.py:43
  98.5 5.0 %collective-permute-start.35 = (bf16[128,512]{1,0:T(8,128)(2,1)S(1)}, bf16[128,512]{1,0:T(8,128)(2,1)S(1)}, u32[]{:S(2)}, u32[]{:S(2)}) collective-permute-start(bf16[128,512]{1,0:T(8,128)(2,1)S(1)} %get-tuple-element.70), channel_id=1, source_target_pairs={{0,32},{1,97},{2,34},{3,99},{4,36},{5,101},{6,38},{7,103},{8,40},{... | collective-permute-start | bytes 393224 | tf_op jit(solution)/shard_map/ppermute | solution.py:43
  103.7 1.8 %collective-permute-start.36 = (f32[200,512]{1,0:T(8,128)S(1)}, f32[200,512]{1,0:T(8,128)S(1)}, u32[]{:S(2)}, u32[]{:S(2)}) collective-permute-start(f32[200,512]{1,0:T(8,128)S(1)} %get-tuple-element.73), channel_id=1, source_target_pairs={{0,1},{1,0},{2,3},{3,2},{4,5},{5,4},{6,7},{7,6},{8,9},{9,8},{10,11... | collective-permute-start | bytes 1228808 | tf_op jit(solution)/shard_map/ppermute | solution.py:47

commit v4 on v3

v4 whole, which is shorter than its diff:
```python
import functools
import itertools
import math

import jax
import jax.numpy as jnp
from jax import lax
from jax.experimental import pallas as pl
from jax.experimental.pallas import tpu as pltpu
from jax.sharding import Mesh, PartitionSpec as P


logit_scale = 10.0
log2e = 1.4426950408889634
ln2 = 0.6931471805599453
lowest = -1e30
f32 = jnp.float32
bf16 = jnp.bfloat16
AXES = ("z", "y", "x", "c")
SWAP = ((0, 1), (1, 0))
FLIPS = ((0, 0, 1), (0, 1, 0), (1, 0, 0))
IMAGE_PAIR = (1, 0, 3, 2)
TEXT_PAIR = (3, 2, 1, 0)
VMEM = pl.BlockSpec(memory_space=pltpu.VMEM)
SMEM = pl.BlockSpec(memory_space=pltpu.SMEM)


def role_pairs(flip):
    pairs = []
    for z, y, x in itertools.product(range(4), repeat=3):
        for core, pair in ((0, IMAGE_PAIR), (1, TEXT_PAIR)):
            target = [pair[v] if f else v for v, f in zip((z, y, x), flip)]
            source_id = ((z * 4 + y) * 4 + x) * 2 + core
            target_id = ((target[0] * 4 + target[1]) * 4 + target[2]) * 2 + core
            pairs.append((source_id, target_id))
    return pairs


ROLE_PAIRS = [role_pairs(flip) for flip in FLIPS]


def flip_permute(x, dim):
    return lax.ppermute(x, AXES, ROLE_PAIRS[dim % 3])


def core_swap(x):
    return lax.ppermute(x, "c", SWAP)


def call(kernel, name, ins, outs, scratch=(), limit=6, flops=0, moved=0):
    in_specs = [SMEM if i == 0 else VMEM for i in range(len(ins))]
    return pl.pallas_call(
        kernel,
        in_specs=in_specs,
        out_specs=[VMEM] * len(outs),
        out_shape=list(outs),
        scratch_shapes=list(scratch),
        compiler_params=pltpu.CompilerParams(vmem_limit_bytes=limit << 20),
        cost_estimate=pl.CostEstimate(flops=flops, bytes_accessed=moved, transcendentals=0),
        name=name,
    )(*ins)


def held(x):
    return pltpu.with_memory_space_constraint(x, pltpu.VMEM)


def shape(*dims, dtype=f32):
    return jax.ShapeDtypeStruct(dims, dtype)


ROW_AT = (0, 768, 1024, 1280, 1536)
COL_AT = (0, 1536, 2048, 2560, 3072)
CONTRACT_LAST = (((1,), (1,)), ((), ()))
CONTRACT_FIRST = (((0,), (0,)), ((), ()))


def log_add(a, b):
    top = jnp.maximum(a, b)
    return top + jnp.log2(jnp.exp2(a - top) + jnp.exp2(b - top))


def lane_blocks(x):
    return [x[:, k : k + 128] for k in range(0, x.shape[1], 128)]


def row_stat(logits):
    top = jnp.max(logits, axis=1, keepdims=True)
    total = jnp.sum(jnp.exp2(logits - top), axis=1, keepdims=True)
    lse = top + jnp.log2(total)
    return jnp.concatenate(lane_blocks(jnp.broadcast_to(lse, (lse.shape[0], 128)).T[0:1, :]), 0)


def column_step(logits, state):
    top = jnp.max(logits, axis=0, keepdims=True)
    if state is None:
        return top, jnp.sum(jnp.exp2(logits - top), axis=0, keepdims=True)
    new_top = jnp.maximum(state[0], top)
    total = state[1] * jnp.exp2(state[0] - new_top) + jnp.sum(jnp.exp2(logits - new_top), axis=0, keepdims=True)
    return new_top, total


def column_stat(state):
    return jnp.concatenate(lane_blocks(state[0] + jnp.log2(state[1])), 0)


def forward_kernel(stage, core_ref, *refs):
    refs = list(refs)
    take = lambda n: [refs.pop(0) for _ in range(n)]
    n = 3 if stage == 0 else 1
    mine, swapped = take(n), take(n)
    rows, cols = take(stage), take(stage)
    row_old, col_old = take(2) if stage else (None, None)
    image_ref, text_ref = take(2) if stage == 3 else (None, None)
    rows_ref, cols_ref, wide_ref = take(3)
    tall_ref = take(1)[0] if stage else None
    first = core_ref[0] == 0

    @pl.when(first)
    def _():
        for i in range(n):
            rows_ref[i * 256 : i * 256 + 256, :] = mine[i][0:256, :]
            cols_ref[i * 512 : i * 512 + 512, :] = swapped[i][...]

    @pl.when(jnp.logical_not(first))
    def _():
        for i in range(n):
            rows_ref[i * 256 : i * 256 + 256, :] = swapped[i][256:512, :]
            cols_ref[i * 512 : i * 512 + 512, :] = mine[i][...]

    def product(a, b):
        return lax.dot_general(a, b, CONTRACT_LAST, preferred_element_type=f32) * (logit_scale * log2e)

    cols = cols + [cols_ref]
    new_rows = []
    state = None
    for block in range(n):
        part = slice(block * 256, block * 256 + 256)
        for p in range(stage + 1):
            wide_ref[part, COL_AT[p] : COL_AT[p + 1]] = product(rows_ref[part, :], cols[p][...])
        logits = wide_ref[part, :]
        new_rows.append(row_stat(logits))
        state = column_step(logits, state)
    col = column_stat(state)
    row = jnp.concatenate(new_rows, 0)
    if stage:
        state = None
        old = []
        for p in range(stage):
            for start in range(0, rows[p].shape[0], 256):
                part = slice(ROW_AT[p] + start, ROW_AT[p] + start + 256)
                tall_ref[part, :] = product(rows[p][start : start + 256, :], cols_ref[...])
                logits = tall_ref[part, :]
                old.append(row_stat(logits))
                state = column_step(logits, state)
        row = jnp.concatenate([log_add(row_old[...], jnp.concatenate(old, 0)), row], 0)
        col = log_add(col, jnp.concatenate([col_old[...], column_stat(state)], 0))
    if stage < 3:
        row_out, col_out = take(2)
        row_out[...] = row
        col_out[...] = col
        return
    send_ref, keep_ref = take(2)
    positive = logit_scale * jnp.sum(image_ref[...].astype(f32) * text_ref[...].astype(f32))
    extra = jnp.full((8, 128), positive, f32)
    blank = jnp.full((2, 128), lowest, f32)
    low_half = jnp.concatenate([x for g in range(6) for x in (row[2 * g : 2 * g + 2], blank)], 0)
    high_half = jnp.concatenate([x for g in range(6) for x in (blank, row[2 * g : 2 * g + 2])], 0)
    send_ref[0:24, :] = jnp.where(first, col, high_half)
    keep_ref[0:24, :] = jnp.where(first, low_half, col)
    send_ref[24:32, :] = extra
    keep_ref[24:32, :] = extra


def join_kernel(order, core_ref, mine_ref, got_ref, out_ref):
    got = got_ref[...]
    out_ref[0:24, :] = log_add(mine_ref[0:24, :], jnp.concatenate([got[k : k + 1, :] for k in order], 0))
    out_ref[24:32, :] = mine_ref[24:32, :] + got_ref[24:32, :]


def flip_order(dim):
    order = []
    for half, q, k in itertools.product(range(2), range(3), range(4)):
        j = (dim - q) % 3
        if j == 2:
            order.append((1 - half) * 12 + q * 4 + k)
        else:
            order.append(half * 12 + q * 4 + (k ^ (1 << j)))
    return order


def tile_lse(first, mine_ref, other_ref):
    mine, other = mine_ref[0:24, :], other_ref[0:24, :]
    row = jnp.where(first, mine, other)
    col = jnp.where(first, other, mine)
    row = [jnp.where(first, row[4 * g + b : 4 * g + b + 1], row[4 * g + b + 2 : 4 * g + b + 3]) for g in range(6) for b in range(2)]
    row = jnp.concatenate(row, 1) + 1.0
    col = jnp.concatenate([col[k : k + 1] for k in range(24)], 1) + 1.0
    return row, col


def coefficients(logits, row, col):
    n = logits.shape[0]
    row = jnp.broadcast_to(row, (128, n)).T[:, 0:1]
    return jnp.exp2(logits - row) + jnp.exp2(logits - col)


def total_of(terms):
    total = terms[0]
    for term in terms[1:]:
        total = total + term
    return logit_scale * total


def times(a, b):
    return jnp.dot(a, b, preferred_element_type=f32)


def transposed_times(a, b):
    return lax.dot_general(a, b, CONTRACT_FIRST, preferred_element_type=f32)


def far_grad_kernel(stage, core_ref, mine_ref, other_ref, *refs):
    refs = list(refs)
    take = lambda n: [refs.pop(0) for _ in range(n)]
    wide_in, tall_in = take(2)
    rows, cols = take(4), take(4)
    wide = [None] * (stage + 1) + take(3 - stage)
    tall = [None] * (stage + 1) + take(3 - stage)
    wide[stage], tall[stage] = take(2)
    kept_ref, send_ref = take(2)
    first = core_ref[0] == 0
    row, col = tile_lse(first, mine_ref, other_ref)
    if stage == 3:
        loss_ref = take(1)[0]
        loss_ref[...] = jnp.sum(other_ref[0:24, :]) * ln2 - jnp.where(first, 0.0, 2.0) * other_ref[24:32, :]
    wide[stage][...] = coefficients(
        wide_in[...], row[:, ROW_AT[stage] : ROW_AT[stage + 1]], col[:, 0 : COL_AT[stage + 1]]
    ).astype(bf16)
    for start in range(0, ROW_AT[stage], 256):
        part = slice(start, start + 256)
        tall[stage][part, :] = coefficients(
            tall_in[part, :], row[:, part], col[:, COL_AT[stage] : COL_AT[stage + 1]]
        ).astype(bf16)
    here = slice(ROW_AT[stage], ROW_AT[stage + 1])
    image = [times(wide[stage][:, COL_AT[p] : COL_AT[p + 1]], cols[p][...]) for p in range(stage + 1)]
    image += [times(tall[p][here, :], cols[p][...]) for p in range(stage + 1, 4)]
    image = total_of(image).astype(bf16)
    here = slice(COL_AT[stage], COL_AT[stage + 1])
    text = [transposed_times(tall[stage][ROW_AT[p] : ROW_AT[p + 1], :], rows[p][...]) for p in range(stage)]
    text += [transposed_times(wide[p][:, here], rows[p][...]) for p in range(stage, 4)]
    text = total_of(text).astype(bf16)
    kept_ref[0:256, :] = jnp.where(first, image, text[0:256])
    send_ref[0:256, :] = jnp.where(first, text[0:256], image)
    kept_ref[256:512, :] = text[256:512]
    send_ref[256:512, :] = text[256:512]


def near_grad_kernel(core_ref, mine_ref, other_ref, *refs):
    refs = list(refs)
    take = lambda n: [refs.pop(0) for _ in range(n)]
    wide_in = take(1)[0]
    rows, cols = take(4), take(4)
    wide, tall = [None] + take(3), [None] + take(3)
    take(3)
    base_ref, *send_refs = take(4)
    early_ref, kept_ref, block_ref = take(3)
    first = core_ref[0] == 0
    row, col = tile_lse(first, mine_ref, other_ref)
    eye = lax.broadcasted_iota(jnp.int32, (128, 128), 0) == lax.broadcasted_iota(jnp.int32, (128, 128), 1)
    positive = jnp.where(jnp.logical_and(eye, first), 1.0, 0.0)
    for q in range(3):
        part = slice(q * 256, q * 256 + 256)
        coeffs = coefficients(wide_in[part, :], row[:, part], col[:, 0:1536])
        block_ref[part, :] = coeffs.astype(bf16)
        own = slice(q * 512, q * 512 + 128)
        block_ref[q * 256 : q * 256 + 128, own] = (coeffs[0:128, own] - positive).astype(bf16)
    for q in range(3):
        part = slice(q * 256, q * 256 + 256)
        image = total_of(
            [times(block_ref[part, :], cols[0][...])] + [times(tall[p][part, :], cols[p][...]) for p in range(1, 4)]
        )
        here = slice(q * 512, q * 512 + 512)
        text = total_of(
            [transposed_times(block_ref[:, here], rows[0][...])]
            + [transposed_times(wide[p][:, here], rows[p][...]) for p in range(1, 4)]
        )
        own, own_text = slice(q * 64, q * 64 + 64), slice(192 + q * 64, 192 + q * 64 + 64)
        kept_ref[own, :] = image[0:64]
        kept_ref[own_text, :] = text[0:64]
        early_ref[own, :] = image[64:128]
        early_ref[own_text, :] = text[64:128]
        at = q * 512
        base_ref[at : at + 128, :] = jnp.where(first, 0.0, text[0:128])
        base_ref[at + 128 : at + 256, :] = jnp.where(first, image[128:256], text[128:256])
        base_ref[at + 256 : at + 512, :] = jnp.where(first, 0.0, text[256:512])
        send = send_refs[q]
        send[0:128, :] = jnp.where(first, 0.0, image[0:128]).astype(bf16)
        send[128:256, :] = jnp.where(first, text[128:256], image[128:256]).astype(bf16)
        send[256:512, :] = text[256:512].astype(bf16)


def split_terms(x):
    high = x.astype(bf16)
    rest = x - high.astype(f32)
    middle = rest.astype(bf16)
    low = (rest - middle.astype(f32)).astype(bf16)
    pair = [jnp.concatenate([t, t], 0) for t in (high, middle, low)]
    return jnp.concatenate(pair + [jnp.zeros((16, 128), bf16)], 1)


def join_terms(ref, start):
    x = ref[start : start + 16, :].astype(f32)
    return (x[0:8, 0:128] + x[0:8, 128:256]) + x[0:8, 256:384]


def far_message_kernel(core_ref, mine_ref, got_ref, *refs):
    first = core_ref[0] == 0
    got = got_ref[...]
    both = (mine_ref[...].astype(f32) + got.astype(f32)).astype(bf16)
    refs[-1][0:256, :] = jnp.where(first, mine_ref[0:256, :], both[0:256])
    refs[-1][256:512, :] = jnp.where(first, got[0:256], both[256:512])
    if len(refs) == 2:
        refs[-1][512:528, :] = split_terms(refs[0][...])


def far_sum_kernel(core_ref, base_ref, r0, r1, r2, loss_ref, total_ref, loss_out):
    loss_out[...] = loss_ref[...] + join_terms(r0, 512)
    for q, r in enumerate((r0, r1, r2)):
        rows = slice(q * 512, q * 512 + 512)
        total_ref[rows, :] = base_ref[rows, :] + r[0:512, :].astype(f32)


def near_sum_kernel(core_ref, total_ref, g0, g1, g2, loss_ref, low_ref, s0, s1, s2):
    first = core_ref[0] == 0
    s0[256:272, :] = split_terms(loss_ref[...])
    for q, (g, s) in enumerate(((g0, s0), (g1, s1), (g2, s2))):
        at = q * 512
        got = g[...].astype(f32)
        low_ref[q * 256 : q * 256 + 256, :] = total_ref[at : at + 256, :] + jnp.where(first, 0.0, got[0:256])
        s[0:256, :] = (total_ref[at + 256 : at + 512, :] + jnp.where(first, got[0:256], got[256:512])).astype(bf16)


def half_sum_kernel(core_ref, low_ref, r0, r1, r2, loss_ref, out_ref, s0, s1, s2, loss_out):
    loss = loss_ref[...] + join_terms(r0, 256)
    loss_out[...] = loss
    s0[128:144, :] = split_terms(loss)
    for q, (r, s) in enumerate(((r0, s0), (r1, s1), (r2, s2))):
        total = low_ref[q * 256 : q * 256 + 256, :] + r[0:256, :].astype(f32)
        out_ref[q * 128 : q * 128 + 128, :] = total[0:128]
        s[0:128, :] = total[128:256].astype(bf16)


def last_sum_kernel(core_ref, low_ref, r0, r1, r2, loss_ref, keep_ref, send_ref):
    first = core_ref[0] == 0
    loss = loss_ref[...] + join_terms(r0, 128)
    send_ref[192:200, :] = jnp.concatenate([loss] * 4, 1)
    keep_ref[192:200, :] = jnp.concatenate([loss] * 4, 1)
    for q, r in enumerate((r0, r1, r2)):
        rows = slice(q * 64, q * 64 + 64)
        total = low_ref[q * 128 : q * 128 + 128, :] + r[0:128, :].astype(f32)
        keep_ref[rows, :] = jnp.where(first, total[0:64], total[64:128])
        send_ref[rows, :] = jnp.where(first, total[64:128], total[0:64])


def finish_kernel(count, core_ref, keep_ref, got_ref, kept_ref, early_ref, image_out, text_out, loss_out):
    first = core_ref[0] == 0
    for q in range(3):
        rows = slice(q * 64, q * 64 + 64)
        keep = keep_ref[rows, :]
        got = got_ref[rows, :]
        text_rows = slice(192 + q * 64, 192 + q * 64 + 64)
        own_image = jnp.where(first, kept_ref[rows, :], early_ref[rows, :])
        own_text = jnp.where(first, kept_ref[text_rows, :], early_ref[text_rows, :])
        image_out[rows, :] = jnp.where(first, keep, got) + own_image
        text_out[rows, :] = jnp.where(first, got, keep) + own_text
    loss_out[...] = (keep_ref[192:193, 0:1] + got_ref[192:193, 0:1]) * (0.5 / count)


def select_kernel(core_ref, image_ref, text_ref, out_ref):
    out_ref[...] = jnp.where(core_ref[0] == 0, text_ref[...], image_ref[...])


def pair_kernel(core_ref, image_ref, text_ref, got_ref, *out_refs):
    first = core_ref[0] == 0
    for q, out in enumerate(out_refs):
        rows = slice(q * 64, q * 64 + 64)
        out[0:64, :] = jnp.where(first, image_ref[rows, :], got_ref[rows, :])
        out[64:128, :] = jnp.where(first, got_ref[rows, :], text_ref[rows, :])


def per_device(image_emb, text_emb):
    core_id = lax.axis_index("c").reshape(1).astype(jnp.int32)
    pair_rows, width = image_emb.shape
    count = pair_rows * 128

    swapped = core_swap(call(select_kernel, "select", [core_id, image_emb, text_emb], [shape(pair_rows, width, dtype=bf16)], limit=4)[0])
    near = call(
        pair_kernel, "pair", [core_id, image_emb, text_emb, swapped], [shape(128, width, dtype=bf16)] * 3, limit=4
    )
    for step in range(2):
        got = [flip_permute(near[q], q + step) for q in range(3)]
        near = [jnp.concatenate([a, b], 0) for a, b in zip(near, got)]
    far = [flip_permute(near[q], q + 2) for q in range(3)]
    near_x = [core_swap(a) for a in near]
    far_x = [core_swap(a) for a in far]

    rows, cols, wide, tall = [], [], [], [None]
    stat = []
    for stage in range(4):
        ins = [core_id] + (near + near_x if stage == 0 else [far[stage - 1], far_x[stage - 1]])
        ins += [held(a) for a in rows + cols] + stat
        if stage == 3:
            ins += [image_emb, text_emb]
        new_rows = 768 if stage == 0 else 256
        new_cols = 1536 if stage == 0 else 512
        outs = [pltpu.VMEM((new_rows, width), bf16), pltpu.VMEM((new_cols, width), bf16)]
        outs.append(pltpu.VMEM((new_rows, COL_AT[stage + 1]), f32))
        if stage:
            outs.append(pltpu.VMEM((ROW_AT[stage], new_cols), f32))
        if stage < 3:
            outs += [shape(ROW_AT[stage + 1] // 128, 128), shape(COL_AT[stage + 1] // 128, 128)]
        else:
            outs += [shape(32, 128), shape(32, 128)]
        area = new_rows * COL_AT[stage + 1] + ROW_AT[stage] * new_cols
        got = call(functools.partial(forward_kernel, stage), "forward", ins, outs, limit=10, flops=2 * area * width)
        rows.append(got[0])
        cols.append(got[1])
        wide.append(got[2])
        if stage:
            tall.append(got[3])
        stat = list(got[-2:])
    send, keep = stat

    mine = call(functools.partial(join_kernel, list(range(24))), "join", [core_id, keep, core_swap(send)], [shape(32, 128)], limit=2)[0]
    for dim in range(3):
        got = flip_permute(mine, dim)
        mine = call(functools.partial(join_kernel, flip_order(dim)), "join", [core_id, mine, got], [shape(32, 128)], limit=2)[0]
    other = core_swap(mine)

    held_rows, held_cols = [held(a) for a in rows], [held(a) for a in cols]
    wide_coeffs, tall_coeffs = [], []
    messages = [None] * 3
    for stage in (3, 2, 1):
        ins = [core_id, mine, other, held(wide[stage]), held(tall[stage]), *held_rows, *held_cols]
        ins += [held(a) for a in wide_coeffs + tall_coeffs]
        outs = [pltpu.VMEM((256, COL_AT[stage + 1]), bf16), pltpu.VMEM((ROW_AT[stage], 512), bf16)]
        outs += [shape(512, width, dtype=bf16)] * 2
        if stage == 3:
            outs.append(shape(8, 128))
        got = call(
            functools.partial(far_grad_kernel, stage),
            "far_grad",
            ins,
            outs,
            limit=10,
            flops=2 * (256 * 3072 + 1536 * 512) * width,
        )
        wide_coeffs.insert(0, got[0])
        tall_coeffs.insert(0, got[1])
        if stage == 3:
            loss = got[4]
        ins = [core_id, got[2], core_swap(got[3])]
        if stage == 1:
            ins.append(loss)
        messages[stage - 1] = call(
            far_message_kernel, "far_message", ins, [shape(528 if stage == 1 else 512, width, dtype=bf16)]
        )[0]
    got = [flip_permute(messages[q], q + 2) for q in range(3)]
    base, *near_send, early, kept = call(
        near_grad_kernel,
        "near_grad",
        [core_id, mine, other, held(wide[0]), *held_rows, *held_cols]
        + [held(a) for a in wide_coeffs + tall_coeffs]
        + messages,
        [shape(1536, width)] + [shape(512, width, dtype=bf16)] * 3 + [shape(384, width), shape(384, width)],
        scratch=[pltpu.VMEM((768, 1536), bf16)],
        limit=10,
        flops=2 * (768 * 3072 + 1536 * 1536) * width,
    )
    near_got = [core_swap(a) for a in near_send]
    early = core_swap(early)
    total, loss = call(far_sum_kernel, "far_sum", [core_id, base, *got, loss], [shape(1536, width), shape(8, 128)])
    low, *messages = call(
        near_sum_kernel,
        "near_sum",
        [core_id, total, *near_got, loss],
        [shape(768, width)] + [shape(272 if q == 0 else 256, width, dtype=bf16) for q in range(3)],
    )
    got = [flip_permute(messages[q], q + 1) for q in range(3)]
    low, *messages, loss = call(
        half_sum_kernel,
        "half_sum",
        [core_id, low, *got, loss],
        [shape(384, width)] + [shape(144 if q == 0 else 128, width, dtype=bf16) for q in range(3)] + [shape(8, 128)],
    )
    got = [flip_permute(messages[q], q) for q in range(3)]
    keep, send = call(
        last_sum_kernel, "last_sum", [core_id, low, *got, loss], [shape(200, width), shape(200, width)]
    )
    swapped = core_swap(send)
    grad_image, grad_text, loss = call(
        functools.partial(finish_kernel, count),
        "finish",
        [core_id, keep, swapped, kept, early],
        [shape(192, width), shape(192, width), shape(1, 1)],
    )
    return loss.reshape(()), grad_image, grad_text


def solution(mesh):
    fine = Mesh(mesh.devices.reshape(4, 4, 4, 2), AXES)
    return jax.shard_map(
        per_device,
        mesh=fine,
        in_specs=(P(AXES, None), P(AXES, None)),
        out_specs=(P(), P(AXES, None), P(AXES, None)),
        check_vma=False,
    )
```

time: 107 us -> 108 us (level)
  Pallas kernels: 24.6 us -> 28.9 us
  starting transfers between devices: 42.3 us -> 39.3 us
    pallas_call x20 -> x22, Pallas kernels: 24.6 us -> 28.9 us  [call(): pl.pallas_call(kernel, in_specs=in_specs, out_specs=[VMEM] * len(outs), o...]
    ppermute x21, starting transfers between devices: 36.9 us -> 34.6 us  [flip_permute(): return lax.ppermute(x, AXES, ROLE_PAIRS[dim % 3])]
  transfers between devices with their start and end apart: 38 -> 38, of which waited for: 19 -> 19; matrix products, arithmetic and copies ran while one was open for 0% -> 0% of each run, Pallas kernels for 5% -> 19%
where the time goes in v4:
time: 108 us
  starting transfers between devices  39.3 us (36%)
  waiting for transfers between devices  36.9 us (34%)
  Pallas kernels  28.9 us (27%)
  local copies, waits for them, and re-layouts  1.97 us (2%)
    ppermute x21, starting transfers between devices, flip_permute(): return lax.ppermute(x, AXES, ROLE_PAIRS[dim % 3])  34.6 us
    ppermute x21, waiting for transfers between devices, flip_permute(): return lax.ppermute(x, AXES, ROLE_PAIRS[dim % 3])  29.2 us
    pallas_call x22, Pallas kernels, call(): pl.pallas_call(kernel, in_specs=in_specs, out_specs=[VMEM] * len(outs), o...  28.9 us
    ppermute x17, waiting for transfers between devices, core_swap(): return lax.ppermute(x, 'c', SWAP)  7.63 us
    ppermute x17, starting transfers between devices, core_swap(): return lax.ppermute(x, 'c', SWAP)  4.67 us
  transfers between devices with their start and end apart: 38, of which 19 were waited for; matrix products, arithmetic and copies ran while one was open for 0% of the time, Pallas kernels for 19%

profile of v4, /device:TPU:1, one launch (start us, length us, event | category | flops | bytes accessed | tf_op | source)
XLA Modules:
  0.0 108.0 jit_solution(14966297274218471409)
XLA Ops:
  0.6 0.9 copy-done
  1.6 0.9 copy-done.2
  2.5 1.5 %collective-permute-start = (bf16[192,512]{1,0:T(8,128)(2,1)S(1)}, bf16[192,512]{1,0:T(8,128)(2,1)S(1)}, u32[]{:S(2)}, u32[]{:S(2)}) collective-permute-start(bf16[192,512]{1,0:T(8,128)(2,1)S(1)} %select.1), channel_id=1, source_target_pairs={{0,1},{1,0},{2,3},{3,2},{4,5},{5,4},{6,7},{7,6},{8,9},{9,8},{10,11... | collective-permute-start | bytes 589832 | tf_op jit(solution)/shard_map/ppermute | solution.py:47
  4.0 1.1 collective-permute-done.got_ref
  5.1 3.9 %collective-permute-start.1 = (bf16[128,512]{1,0:T(8,128)(2,1)S(1)}, bf16[128,512]{1,0:T(8,128)(2,1)S(1)}, u32[]{:S(2)}, u32[]{:S(2)}) collective-permute-start(bf16[128,512]{1,0:T(8,128)(2,1)S(1)} %get-tuple-element.64), channel_id=1, source_target_pairs={{0,32},{1,97},{2,34},{3,99},{4,36},{5,101},{6,38},{7,103},{8,40},{... | collective-permute-start | bytes 393224 | tf_op jit(solution)/shard_map/ppermute | solution.py:43
  9.0 2.5 %collective-permute-start.5 = (bf16[128,512]{1,0:T(8,128)(2,1)S(1)}, bf16[128,512]{1,0:T(8,128)(2,1)S(1)}, u32[]{:S(2)}, u32[]{:S(2)}) collective-permute-start(bf16[128,512]{1,0:T(8,128)(2,1)S(1)} %get-tuple-element.65), channel_id=1, source_target_pairs={{0,2},{1,7},{2,0},{3,5},{4,6},{5,3},{6,4},{7,1},{8,10},{9,15},{10,... | collective-permute-start | bytes 393224 | tf_op jit(solution)/shard_map/ppermute | solution.py:43
  11.5 2.8 %collective-permute-start.7 = (bf16[128,512]{1,0:T(8,128)(2,1)S(1)}, bf16[128,512]{1,0:T(8,128)(2,1)S(1)}, u32[]{:S(2)}, u32[]{:S(2)}) collective-permute-start(bf16[128,512]{1,0:T(8,128)(2,1)S(1)} %get-tuple-element.66), channel_id=1, source_target_pairs={{0,8},{1,25},{2,10},{3,27},{4,12},{5,29},{6,14},{7,31},{8,0},{9,17... | collective-permute-start | bytes 393224 | tf_op jit(solution)/shard_map/ppermute | solution.py:43
  14.7 2.0 %collective-permute-done.7 = bf16[128,512]{1,0:T(8,128)(2,1)S(1)} collective-permute-done((bf16[128,512]{1,0:T(8,128)(2,1)S(1)}, bf16[128,512]{1,0:T(8,128)(2,1)S(1)}, u32[]{:S(2)}, u32[]{:S(2)}) %collective-permute-start.7) | collective-permute-done | bytes 131104 | tf_op jit(solution)/shard_map/ppermute | solution.py:43
  16.9 2.8 %collective-permute-start.6 = (bf16[256,512]{1,0:T(8,128)(2,1)S(1)}, bf16[256,512]{1,0:T(8,128)(2,1)S(1)}, u32[]{:S(2)}, u32[]{:S(2)}) collective-permute-start(bf16[256,512]{1,0:T(8,128)(2,1)S(1)} %pad_maximum_fusion.1), channel_id=1, source_target_pairs={{0,8},{1,25},{2,10},{3,27},{4,12},{5,29},{6,14},{7,31},{8,0},{9,17... | collective-permute-start | bytes 786440 | tf_op jit(solution)/shard_map/ppermute | solution.py:43
  19.7 3.5 %collective-permute-done.8 = bf16[256,512]{1,0:T(8,128)(2,1)S(1)} collective-permute-done((bf16[256,512]{1,0:T(8,128)(2,1)S(1)}, bf16[256,512]{1,0:T(8,128)(2,1)S(1)}, u32[]{:S(2)}, u32[]{:S(2)}) %collective-permute-start.8) | collective-permute-done | bytes 262176 | tf_op jit(solution)/shard_map/ppermute | solution.py:43
  23.3 0.5 collective-permute-start.14
  23.8 2.3 %collective-permute-start.12 = (bf16[512,512]{1,0:T(8,128)(2,1)S(1)}, bf16[512,512]{1,0:T(8,128)(2,1)S(1)}, u32[]{:S(2)}, u32[]{:S(2)}) collective-permute-start(bf16[512,512]{1,0:T(8,128)(2,1)S(1)} %constant_dynamic-update-slice_fusion.3.refs_0_), channel_id=1, source_target_pairs={{0,32},{1,97},{2,34},{3,99},{4,36},{5,101},{6,38},{7,103},{8,40},{... | collective-permute-start | bytes 1572872 | tf_op jit(solution)/shard_map/ppermute | solution.py:43
  26.3 2.8 %collective-permute-start.3 = (bf16[512,512]{1,0:T(8,128)(2,1)S(1)}, bf16[512,512]{1,0:T(8,128)(2,1)S(1)}, u32[]{:S(2)}, u32[]{:S(2)}) collective-permute-start(bf16[512,512]{1,0:T(8,128)(2,1)S(1)} %constant_dynamic-update-slice_fusion.refs_2_), channel_id=1, source_target_pairs={{0,8},{1,25},{2,10},{3,27},{4,12},{5,29},{6,14},{7,31},{8,0},{9,17... | collective-permute-start | bytes 1572872 | tf_op jit(solution)/shard_map/ppermute | solution.py:43
  29.0 3.6 %collective-permute-done.14.refs_0_ = bf16[512,512]{1,0:T(8,128)(2,1)S(1)} collective-permute-done((bf16[512,512]{1,0:T(8,128)(2,1)S(1)}, bf16[512,512]{1,0:T(8,128)(2,1)S(1)}, u32[]{:S(2)}, u32[]{:S(2)}) %collective-permute-start.14) | collective-permute-done | bytes 524320 | tf_op jit(solution)/shard_map/ppermute | solution.py:43
  32.6 0.6 collective-permute-done.12.refs_0_
  33.7 1.9 %collective-permute-done.3.refs_0_ = bf16[512,512]{1,0:T(8,128)(2,1)S(1)} collective-permute-done((bf16[512,512]{1,0:T(8,128)(2,1)S(1)}, bf16[512,512]{1,0:T(8,128)(2,1)S(1)}, u32[]{:S(2)}, u32[]{:S(2)}) %collective-permute-start.3) | collective-permute-done | bytes 524320 | tf_op jit(solution)/shard_map/ppermute | solution.py:43
  36.0 2.8 %forward.4 = (bf16[768,512]{1,0:T(8,128)(2,1)S(1)}, bf16[1536,512]{1,0:T(8,128)(2,1)S(1)}, f32[768,1536]{1,0:T(8,128)S(1)}, f32[6,128]{1,0:T(8,128)S(1)}, f32[12,128]{1,0:T(8,128)S(1)}) custom-call(s32[1]{0:T(128)} %bitcast.core_ref, bf16[512,512]{1,0:T(8,128)(2,1)S(1)} %constant_dynamic-update-slice_fusion.3.refs_0_, ...), custom_call_target="tpu_custom_call" | custom-call | flops 1207959552 | tf_op jit(solution)/shard_map/forward/pallas_call | solution.py:52
  38.9 2.4 %forward.5 = (bf16[256,512]{1,0:T(8,128)(2,1)S(1)}, bf16[512,512]{1,0:T(8,128)(2,1)S(1)}, f32[256,2048]{1,0:T(8,128)S(1)}, f32[768,512]{1,0:T(8,128)S(1)}, f32[8,128]{1,0:T(8,128)S(1)}, /*index=5*/f32[16,128]{1,0:T(8,128)S(1)}) custom-call(s32[1]{0:T(128)} %bitcast.core_ref, bf16[512,512]{1,0:T(8,128)(2,1)S(1)} %collective-permute-done.12.refs_0_, ...), custom_call_target="tpu_custom_call" | custom-call | flops 939524096 | tf_op jit(solution)/shard_map/forward/pallas_call | solution.py:52
  41.3 3.3 %forward.6 = (bf16[256,512]{1,0:T(8,128)(2,1)S(1)}, bf16[512,512]{1,0:T(8,128)(2,1)S(1)}, f32[256,2560]{1,0:T(8,128)S(1)}, f32[1024,512]{1,0:T(8,128)S(1)}, f32[...) custom-call(s32[1]{0:T(128)} %bitcast.core_ref, bf16[512,512]{1,0:T(8,128)(2,1)S(1)} %collective-permute-done.14.refs_0_, ...), custom_call_target="tpu_custom_call" | custom-call | flops 1207959552 | tf_op jit(solution)/shard_map/forward/pallas_call | solution.py:52
  44.6 3.9 %forward.7 = (bf16[256,512]{1,0:T(8,128)(2,1)S(1)}, bf16[512,512]{1,0:T(8,128)(2,1)S(1)}, f32[256,3072]{1,0:T(8,128)S(1)}, f32[1280,512]{1,0:T(8,128)S(1)}, f32[...) custom-call(s32[1]{0:T(128)} %bitcast.core_ref, bf16[512,512]{1,0:T(8,128)(2,1)S(1)} %collective-permute-done.3.refs_0_, ...), custom_call_target="tpu_custom_call" | custom-call | flops 1476395008 | tf_op jit(solution)/shard_map/forward/pallas_call | solution.py:52
  48.8 1.1 %collective-permute-done.16.got_ref = f32[32,128]{1,0:T(8,128)S(1)} collective-permute-done((f32[32,128]{1,0:T(8,128)S(1)}, f32[32,128]{1,0:T(8,128)S(1)}, u32[]{:S(2)}, u32[]{:S(2)}) %collective-permute-start.16) | collective-permute-done | bytes 16416 | tf_op jit(solution)/shard_map/ppermute | solution.py:47
  49.9 0.5 collective-permute-start.17
  50.4 3.3 %collective-permute-done.17.got_ref = f32[32,128]{1,0:T(8,128)S(1)} collective-permute-done((f32[32,128]{1,0:T(8,128)S(1)}, f32[32,128]{1,0:T(8,128)S(1)}, u32[]{:S(2)}, u32[]{:S(2)}) %collective-permute-start.17) | collective-permute-done | bytes 16416 | tf_op jit(solution)/shard_map/ppermute | solution.py:43
  53.8 2.8 %collective-permute-start.18 = (f32[32,128]{1,0:T(8,128)S(1)}, f32[32,128]{1,0:T(8,128)S(1)}, u32[]{:S(2)}, u32[]{:S(2)}) collective-permute-start(f32[32,128]{1,0:T(8,128)S(1)} %join.5.mine_ref), channel_id=1, source_target_pairs={{0,8},{1,25},{2,10},{3,27},{4,12},{5,29},{6,14},{7,31},{8,0},{9,17... | collective-permute-start | bytes 49160 | tf_op jit(solution)/shard_map/ppermute | solution.py:43
  56.5 1.1 %collective-permute-done.18.got_ref = f32[32,128]{1,0:T(8,128)S(1)} collective-permute-done((f32[32,128]{1,0:T(8,128)S(1)}, f32[32,128]{1,0:T(8,128)S(1)}, u32[]{:S(2)}, u32[]{:S(2)}) %collective-permute-start.18) | collective-permute-done | bytes 16416 | tf_op jit(solution)/shard_map/ppermute | solution.py:43
  57.7 0.5 collective-permute-start.19
  58.2 3.4 %collective-permute-done.19.got_ref = f32[32,128]{1,0:T(8,128)S(1)} collective-permute-done((f32[32,128]{1,0:T(8,128)S(1)}, f32[32,128]{1,0:T(8,128)S(1)}, u32[]{:S(2)}, u32[]{:S(2)}) %collective-permute-start.19) | collective-permute-done | bytes 16416 | tf_op jit(solution)/shard_map/ppermute | solution.py:43
  61.7 1.2 %collective-permute-done.20.other_ref = f32[32,128]{1,0:T(8,128)S(1)} collective-permute-done((f32[32,128]{1,0:T(8,128)S(1)}, f32[32,128]{1,0:T(8,128)S(1)}, u32[]{:S(2)}, u32[]{:S(2)}) %collective-permute-start.20) | collective-permute-done | bytes 16416 | tf_op jit(solution)/shard_map/ppermute | solution.py:47
  62.8 2.7 %far_grad.3 = (bf16[256,3072]{1,0:T(8,128)(2,1)S(1)}, bf16[1280,512]{1,0:T(8,128)(2,1)S(1)}, bf16[512,512]{1,0:T(8,128)(2,1)S(1)}, bf16[512,512]{1,0:T(8,128)(2,1)S(1)}, f32[8,128]{1,0:T(8,128)S(1)}) custom-call(s32[1]{0:T(128)} %bitcast.core_ref, f32[32,128]{1,0:T(8,128)S(1)} %join.7.mine_ref, f32[32,128]{1,0:T(8,128)S(1)} %collective-permute-done.20.other_ref, ...), custom_call_target="tpu_custom_call" | custom-call | flops 1610612736 | tf_op jit(solution)/shard_map/far_grad/pallas_call | solution.py:52
  65.8 2.5 %far_grad.4 = (bf16[256,2560]{1,0:T(8,128)(2,1)S(1)}, bf16[1024,512]{1,0:T(8,128)(2,1)S(1)}, bf16[512,512]{1,0:T(8,128)(2,1)S(1)}, bf16[512,512]{1,0:T(8,128)(2,1)S(1)}) custom-call(s32[1]{0:T(128)} %bitcast.core_ref, f32[32,128]{1,0:T(8,128)S(1)} %join.7.mine_ref, f32[32,128]{1,0:T(8,128)S(1)} %collective-permute-done.20.other_ref, ...), custom_call_target="tpu_custom_call" | custom-call | flops 1610612736 | tf_op jit(solution)/shard_map/far_grad/pallas_call | solution.py:52
  68.3 0.6 collective-permute-start.22
  69.0 2.3 %far_grad.5 = (bf16[256,2048]{1,0:T(8,128)(2,1)S(1)}, bf16[768,512]{1,0:T(8,128)(2,1)S(1)}, bf16[512,512]{1,0:T(8,128)(2,1)S(1)}, bf16[512,512]{1,0:T(8,128)(2,1)S(1)}) custom-call(s32[1]{0:T(128)} %bitcast.core_ref, f32[32,128]{1,0:T(8,128)S(1)} %join.7.mine_ref, f32[32,128]{1,0:T(8,128)S(1)} %collective-permute-done.20.other_ref, ...), custom_call_target="tpu_custom_call" | custom-call | flops 1610612736 | tf_op jit(solution)/shard_map/far_grad/pallas_call | solution.py:52
  71.7 2.7 %collective-permute-start.26 = (bf16[512,512]{1,0:T(8,128)(2,1)S(1)}, bf16[512,512]{1,0:T(8,128)(2,1)S(1)}, u32[]{:S(2)}, u32[]{:S(2)}) collective-permute-start(bf16[512,512]{1,0:T(8,128)(2,1)S(1)} %far_message.5.refs_17_), channel_id=1, source_target_pairs={{0,8},{1,25},{2,10},{3,27},{4,12},{5,29},{6,14},{7,31},{8,0},{9,17... | collective-permute-start | bytes 1572872 | tf_op jit(solution)/shard_map/ppermute | solution.py:43
  75.0 2.6 %collective-permute-start.24 = (bf16[528,512]{1,0:T(8,128)(2,1)S(1)}, bf16[528,512]{1,0:T(8,128)(2,1)S(1)}, u32[]{:S(2)}, u32[]{:S(2)}) collective-permute-start(bf16[528,512]{1,0:T(8,128)(2,1)S(1)} %far_message.3.refs_15_), channel_id=1, source_target_pairs={{0,32},{1,97},{2,34},{3,99},{4,36},{5,101},{6,38},{7,103},{8,40},{... | collective-permute-start | bytes 1622024 | tf_op jit(solution)/shard_map/ppermute | solution.py:43
  77.6 6.2 %near_grad.1 = (f32[1536,512]{1,0:T(8,128)S(1)}, bf16[512,512]{1,0:T(8,128)(2,1)S(1)}, bf16[512,512]{1,0:T(8,128)(2,1)S(1)}, bf16[512,512]{1,0:T(8,128)(2,1)S(1)...) custom-call(s32[1]{0:T(128)} %bitcast.core_ref, f32[32,128]{1,0:T(8,128)S(1)} %join.7.mine_ref, ...), custom_call_target="tpu_custom_call" | custom-call | flops 4831838208 | tf_op jit(solution)/shard_map/near_grad/pallas_call | solution.py:52
  84.8 1.0 collective-permute-done.27.g0
  85.8 0.7 collective-permute-done.28.g1
  86.6 0.7 collective-permute-done.29.g2
  87.9 1.3 %collective-permute-start.31 = (bf16[256,512]{1,0:T(8,128)(2,1)S(1)}, bf16[256,512]{1,0:T(8,128)(2,1)S(1)}, u32[]{:S(2)}, u32[]{:S(2)}) collective-permute-start(bf16[256,512]{1,0:T(8,128)(2,1)S(1)} %get-tuple-element.111), channel_id=1, source_target_pairs={{0,32},{1,97},{2,34},{3,99},{4,36},{5,101},{6,38},{7,103},{8,40},{... | collective-permute-start | bytes 786440 | tf_op jit(solution)/shard_map/ppermute | solution.py:43
  89.2 1.5 %collective-permute-start.32 = (bf16[256,512]{1,0:T(8,128)(2,1)S(1)}, bf16[256,512]{1,0:T(8,128)(2,1)S(1)}, u32[]{:S(2)}, u32[]{:S(2)}) collective-permute-start(bf16[256,512]{1,0:T(8,128)(2,1)S(1)} %get-tuple-element.112), channel_id=1, source_target_pairs={{0,2},{1,7},{2,0},{3,5},{4,6},{5,3},{6,4},{7,1},{8,10},{9,15},{10,... | collective-permute-start | bytes 786440 | tf_op jit(solution)/shard_map/ppermute | solution.py:43
  90.7 3.7 %collective-permute-done.31.r1 = bf16[256,512]{1,0:T(8,128)(2,1)S(1)} collective-permute-done((bf16[256,512]{1,0:T(8,128)(2,1)S(1)}, bf16[256,512]{1,0:T(8,128)(2,1)S(1)}, u32[]{:S(2)}, u32[]{:S(2)}) %collective-permute-start.31) | collective-permute-done | bytes 262176 | tf_op jit(solution)/shard_map/ppermute | solution.py:43
  94.4 1.2 %collective-permute-done.32.r2 = bf16[256,512]{1,0:T(8,128)(2,1)S(1)} collective-permute-done((bf16[256,512]{1,0:T(8,128)(2,1)S(1)}, bf16[256,512]{1,0:T(8,128)(2,1)S(1)}, u32[]{:S(2)}, u32[]{:S(2)}) %collective-permute-start.32) | collective-permute-done | bytes 262176 | tf_op jit(solution)/shard_map/ppermute | solution.py:43
  95.8 1.6 %collective-permute-start.33 = (bf16[144,512]{1,0:T(8,128)(2,1)S(1)}, bf16[144,512]{1,0:T(8,128)(2,1)S(1)}, u32[]{:S(2)}, u32[]{:S(2)}) collective-permute-start(bf16[144,512]{1,0:T(8,128)(2,1)S(1)} %get-tuple-element.114), channel_id=1, source_target_pairs={{0,2},{1,7},{2,0},{3,5},{4,6},{5,3},{6,4},{7,1},{8,10},{9,15},{10,... | collective-permute-start | bytes 442376 | tf_op jit(solution)/shard_map/ppermute | solution.py:43
  97.3 2.6 %collective-permute-start.34 = (bf16[128,512]{1,0:T(8,128)(2,1)S(1)}, bf16[128,512]{1,0:T(8,128)(2,1)S(1)}, u32[]{:S(2)}, u32[]{:S(2)}) collective-permute-start(bf16[128,512]{1,0:T(8,128)(2,1)S(1)} %get-tuple-element.115), channel_id=1, source_target_pairs={{0,8},{1,25},{2,10},{3,27},{4,12},{5,29},{6,14},{7,31},{8,0},{9,17... | collective-permute-start | bytes 393224 | tf_op jit(solution)/shard_map/ppermute | solution.py:43
  100.1 2.3 %collective-permute-done.34.r1 = bf16[128,512]{1,0:T(8,128)(2,1)S(1)} collective-permute-done((bf16[128,512]{1,0:T(8,128)(2,1)S(1)}, bf16[128,512]{1,0:T(8,128)(2,1)S(1)}, u32[]{:S(2)}, u32[]{:S(2)}) %collective-permute-start.34) | collective-permute-done | bytes 131104 | tf_op jit(solution)/shard_map/ppermute | solution.py:43
  102.3 2.6 %collective-permute-done.35.r2 = bf16[128,512]{1,0:T(8,128)(2,1)S(1)} collective-permute-done((bf16[128,512]{1,0:T(8,128)(2,1)S(1)}, bf16[128,512]{1,0:T(8,128)(2,1)S(1)}, u32[]{:S(2)}, u32[]{:S(2)}) %collective-permute-start.35) | collective-permute-done | bytes 131104 | tf_op jit(solution)/shard_map/ppermute | solution.py:43
  105.1 1.7 %collective-permute-done.36.got_ref = f32[200,512]{1,0:T(8,128)S(1)} collective-permute-done((f32[200,512]{1,0:T(8,128)S(1)}, f32[200,512]{1,0:T(8,128)S(1)}, u32[]{:S(2)}, u32[]{:S(2)}) %collective-permute-start.36) | collective-permute-done | bytes 409632 | tf_op jit(solution)/shard_map/ppermute | solution.py:47
  106.9 1.1 %finish.1 = (f32[192,512]{1,0:T(8,128)}, f32[192,512]{1,0:T(8,128)}, f32[1,1]{1,0:T(1,128)}) custom-call(s32[1]{0:T(128)} %bitcast.core_ref, f32[200,512]{1,0:T(8,128)S(1)} %get-tuple-element.118.keep_ref, f32[200,512]{1,0:T(8,128)S(1)} %collective-permute-done.36.got_ref, f32[384,512]{1,0:T(8,128)S(1)} %get-tuple-element.120.kept_ref, ...), custom_call_target="tpu_custom_call" | custom-call | tf_op jit(solution)/shard_map/finish/pallas_call | solution.py:52
  (69 shorter events, 5.4 us)
Async XLA Ops:
  0.6 0.9 copy-start
  1.6 0.9 copy-start.2
  2.5 2.6 %collective-permute-start = (bf16[192,512]{1,0:T(8,128)(2,1)S(1)}, bf16[192,512]{1,0:T(8,128)(2,1)S(1)}, u32[]{:S(2)}, u32[]{:S(2)}) collective-permute-start(bf16[192,512]{1,0:T(8,128)(2,1)S(1)} %select.1), channel_id=1, source_target_pairs={{0,1},{1,0},{2,3},{3,2},{4,5},{5,4},{6,7},{7,6},{8,9},{9,8},{10,11... | collective-permute-start | bytes 589832 | tf_op jit(solution)/shard_map/ppermute | solution.py:47
  5.1 9.2 %collective-permute-start.1 = (bf16[128,512]{1,0:T(8,128)(2,1)S(1)}, bf16[128,512]{1,0:T(8,128)(2,1)S(1)}, u32[]{:S(2)}, u32[]{:S(2)}) collective-permute-start(bf16[128,512]{1,0:T(8,128)(2,1)S(1)} %get-tuple-element.64), channel_id=1, source_target_pairs={{0,32},{1,97},{2,34},{3,99},{4,36},{5,101},{6,38},{7,103},{8,40},{... | collective-permute-start | bytes 393224 | tf_op jit(solution)/shard_map/ppermute | solution.py:43
  9.0 7.9 %collective-permute-start.5 = (bf16[128,512]{1,0:T(8,128)(2,1)S(1)}, bf16[128,512]{1,0:T(8,128)(2,1)S(1)}, u32[]{:S(2)}, u32[]{:S(2)}) collective-permute-start(bf16[128,512]{1,0:T(8,128)(2,1)S(1)} %get-tuple-element.65), channel_id=1, source_target_pairs={{0,2},{1,7},{2,0},{3,5},{4,6},{5,3},{6,4},{7,1},{8,10},{9,15},{10,... | collective-permute-start | bytes 393224 | tf_op jit(solution)/shard_map/ppermute | solution.py:43
  11.5 5.2 %collective-permute-start.7 = (bf16[128,512]{1,0:T(8,128)(2,1)S(1)}, bf16[128,512]{1,0:T(8,128)(2,1)S(1)}, u32[]{:S(2)}, u32[]{:S(2)}) collective-permute-start(bf16[128,512]{1,0:T(8,128)(2,1)S(1)} %get-tuple-element.66), channel_id=1, source_target_pairs={{0,8},{1,25},{2,10},{3,27},{4,12},{5,29},{6,14},{7,31},{8,0},{9,17... | collective-permute-start | bytes 393224 | tf_op jit(solution)/shard_map/ppermute | solution.py:43
  14.4 11.8 %collective-permute-start.2 = (bf16[256,512]{1,0:T(8,128)(2,1)S(1)}, bf16[256,512]{1,0:T(8,128)(2,1)S(1)}, u32[]{:S(2)}, u32[]{:S(2)}) collective-permute-start(bf16[256,512]{1,0:T(8,128)(2,1)S(1)} %pad_maximum_fusion), channel_id=1, source_target_pairs={{0,2},{1,7},{2,0},{3,5},{4,6},{5,3},{6,4},{7,1},{8,10},{9,15},{10,... | collective-permute-start | bytes 786440 | tf_op jit(solution)/shard_map/ppermute | solution.py:43
  16.7 6.5 %collective-permute-start.8 = (bf16[256,512]{1,0:T(8,128)(2,1)S(1)}, bf16[256,512]{1,0:T(8,128)(2,1)S(1)}, u32[]{:S(2)}, u32[]{:S(2)}) collective-permute-start(bf16[256,512]{1,0:T(8,128)(2,1)S(1)} %pad_maximum_fusion.2), channel_id=1, source_target_pairs={{0,32},{1,97},{2,34},{3,99},{4,36},{5,101},{6,38},{7,103},{8,40},{... | collective-permute-start | bytes 786440 | tf_op jit(solution)/shard_map/ppermute | solution.py:43
  16.9 6.9 %collective-permute-start.6 = (bf16[256,512]{1,0:T(8,128)(2,1)S(1)}, bf16[256,512]{1,0:T(8,128)(2,1)S(1)}, u32[]{:S(2)}, u32[]{:S(2)}) collective-permute-start(bf16[256,512]{1,0:T(8,128)(2,1)S(1)} %pad_maximum_fusion.1), channel_id=1, source_target_pairs={{0,8},{1,25},{2,10},{3,27},{4,12},{5,29},{6,14},{7,31},{8,0},{9,17... | collective-permute-start | bytes 786440 | tf_op jit(solution)/shard_map/ppermute | solution.py:43
  23.3 9.3 %collective-permute-start.14 = (bf16[512,512]{1,0:T(8,128)(2,1)S(1)}, bf16[512,512]{1,0:T(8,128)(2,1)S(1)}, u32[]{:S(2)}, u32[]{:S(2)}) collective-permute-start(bf16[512,512]{1,0:T(8,128)(2,1)S(1)} %constant_dynamic-update-slice_fusion.6.refs_1_), channel_id=1, source_target_pairs={{0,2},{1,7},{2,0},{3,5},{4,6},{5,3},{6,4},{7,1},{8,10},{9,15},{10,... | collective-permute-start | bytes 1572872 | tf_op jit(solution)/shard_map/ppermute | solution.py:43
  23.8 9.3 %collective-permute-start.12 = (bf16[512,512]{1,0:T(8,128)(2,1)S(1)}, bf16[512,512]{1,0:T(8,128)(2,1)S(1)}, u32[]{:S(2)}, u32[]{:S(2)}) collective-permute-start(bf16[512,512]{1,0:T(8,128)(2,1)S(1)} %constant_dynamic-update-slice_fusion.3.refs_0_), channel_id=1, source_target_pairs={{0,32},{1,97},{2,34},{3,99},{4,36},{5,101},{6,38},{7,103},{8,40},{... | collective-permute-start | bytes 1572872 | tf_op jit(solution)/shard_map/ppermute | solution.py:43
  26.2 7.0 %collective-permute-start.10 = (bf16[512,512]{1,0:T(8,128)(2,1)S(1)}, bf16[512,512]{1,0:T(8,128)(2,1)S(1)}, u32[]{:S(2)}, u32[]{:S(2)}) collective-permute-start(bf16[512,512]{1,0:T(8,128)(2,1)S(1)} %constant_dynamic-update-slice_fusion.6.refs_1_), channel_id=1, source_target_pairs={{0,1},{1,0},{2,3},{3,2},{4,5},{5,4},{6,7},{7,6},{8,9},{9,8},{10,11... | collective-permute-start | bytes 1572872 | tf_op jit(solution)/shard_map/ppermute | solution.py:47
  26.3 9.3 %collective-permute-start.3 = (bf16[512,512]{1,0:T(8,128)(2,1)S(1)}, bf16[512,512]{1,0:T(8,128)(2,1)S(1)}, u32[]{:S(2)}, u32[]{:S(2)}) collective-permute-start(bf16[512,512]{1,0:T(8,128)(2,1)S(1)} %constant_dynamic-update-slice_fusion.refs_2_), channel_id=1, source_target_pairs={{0,8},{1,25},{2,10},{3,27},{4,12},{5,29},{6,14},{7,31},{8,0},{9,17... | collective-permute-start | bytes 1572872 | tf_op jit(solution)/shard_map/ppermute | solution.py:43
  29.0 7.0 %collective-permute-start.9 = (bf16[512,512]{1,0:T(8,128)(2,1)S(1)}, bf16[512,512]{1,0:T(8,128)(2,1)S(1)}, u32[]{:S(2)}, u32[]{:S(2)}) collective-permute-start(bf16[512,512]{1,0:T(8,128)(2,1)S(1)} %constant_dynamic-update-slice_fusion.3.refs_0_), channel_id=1, source_target_pairs={{0,1},{1,0},{2,3},{3,2},{4,5},{5,4},{6,7},{7,6},{8,9},{9,8},{10,11... | collective-permute-start | bytes 1572872 | tf_op jit(solution)/shard_map/ppermute | solution.py:47
  32.6 3.4 %collective-permute-start.11 = (bf16[512,512]{1,0:T(8,128)(2,1)S(1)}, bf16[512,512]{1,0:T(8,128)(2,1)S(1)}, u32[]{:S(2)}, u32[]{:S(2)}) collective-permute-start(bf16[512,512]{1,0:T(8,128)(2,1)S(1)} %constant_dynamic-update-slice_fusion.refs_2_), channel_id=1, source_target_pairs={{0,1},{1,0},{2,3},{3,2},{4,5},{5,4},{6,7},{7,6},{8,9},{9,8},{10,11... | collective-permute-start | bytes 1572872 | tf_op jit(solution)/shard_map/ppermute | solution.py:47
  33.2 5.7 %collective-permute-start.13 = (bf16[512,512]{1,0:T(8,128)(2,1)S(1)}, bf16[512,512]{1,0:T(8,128)(2,1)S(1)}, u32[]{:S(2)}, u32[]{:S(2)}) collective-permute-start(bf16[512,512]{1,0:T(8,128)(2,1)S(1)} %collective-permute-done.12.refs_0_), channel_id=1, source_target_pairs={{0,1},{1,0},{2,3},{3,2},{4,5},{5,4},{6,7},{7,6},{8,9},{9,8},{10,11... | collective-permute-start | bytes 1572872 | tf_op jit(solution)/shard_map/ppermute | solution.py:47
  33.2 8.1 %collective-permute-start.15 = (bf16[512,512]{1,0:T(8,128)(2,1)S(1)}, bf16[512,512]{1,0:T(8,128)(2,1)S(1)}, u32[]{:S(2)}, u32[]{:S(2)}) collective-permute-start(bf16[512,512]{1,0:T(8,128)(2,1)S(1)} %collective-permute-done.14.refs_0_), channel_id=1, source_target_pairs={{0,1},{1,0},{2,3},{3,2},{4,5},{5,4},{6,7},{7,6},{8,9},{9,8},{10,11... | collective-permute-start | bytes 1572872 | tf_op jit(solution)/shard_map/ppermute | solution.py:47
  35.6 9.0 %collective-permute-start.4 = (bf16[512,512]{1,0:T(8,128)(2,1)S(1)}, bf16[512,512]{1,0:T(8,128)(2,1)S(1)}, u32[]{:S(2)}, u32[]{:S(2)}) collective-permute-start(bf16[512,512]{1,0:T(8,128)(2,1)S(1)} %collective-permute-done.3.refs_0_), channel_id=1, source_target_pairs={{0,1},{1,0},{2,3},{3,2},{4,5},{5,4},{6,7},{7,6},{8,9},{9,8},{10,11... | collective-permute-start | bytes 1572872 | tf_op jit(solution)/shard_map/ppermute | solution.py:47
  41.3 3.3 %copy-start.1 = (bf16[192,512]{1,0:T(8,128)(2,1)S(1)}, bf16[192,512]{1,0:T(8,128)(2,1)}, u32[]{:S(2)}) copy-start(bf16[192,512]{1,0:T(8,128)(2,1)} %refs_10_.1) | copy-start | bytes 589828
  41.3 3.3 %copy-start.3 = (bf16[192,512]{1,0:T(8,128)(2,1)S(1)}, bf16[192,512]{1,0:T(8,128)(2,1)}, u32[]{:S(2)}) copy-start(bf16[192,512]{1,0:T(8,128)(2,1)} %refs_11_.1) | copy-start | bytes 589828
  48.6 1.3 %collective-permute-start.16 = (f32[32,128]{1,0:T(8,128)S(1)}, f32[32,128]{1,0:T(8,128)S(1)}, u32[]{:S(2)}, u32[]{:S(2)}) collective-permute-start(f32[32,128]{1,0:T(8,128)S(1)} %get-tuple-element.80), channel_id=1, source_target_pairs={{0,1},{1,0},{2,3},{3,2},{4,5},{5,4},{6,7},{7,6},{8,9},{9,8},{10,11... | collective-permute-start | bytes 49160 | tf_op jit(solution)/shard_map/ppermute | solution.py:47
  49.9 3.9 %collective-permute-start.17 = (f32[32,128]{1,0:T(8,128)S(1)}, f32[32,128]{1,0:T(8,128)S(1)}, u32[]{:S(2)}, u32[]{:S(2)}) collective-permute-start(f32[32,128]{1,0:T(8,128)S(1)} %join.4.mine_ref), channel_id=1, source_target_pairs={{0,2},{1,7},{2,0},{3,5},{4,6},{5,3},{6,4},{7,1},{8,10},{9,15},{10,... | collective-permute-start | bytes 49160 | tf_op jit(solution)/shard_map/ppermute | solution.py:43
  53.8 3.9 %collective-permute-start.18 = (f32[32,128]{1,0:T(8,128)S(1)}, f32[32,128]{1,0:T(8,128)S(1)}, u32[]{:S(2)}, u32[]{:S(2)}) collective-permute-start(f32[32,128]{1,0:T(8,128)S(1)} %join.5.mine_ref), channel_id=1, source_target_pairs={{0,8},{1,25},{2,10},{3,27},{4,12},{5,29},{6,14},{7,31},{8,0},{9,17... | collective-permute-start | bytes 49160 | tf_op jit(solution)/shard_map/ppermute | solution.py:43
  57.7 3.9 %collective-permute-start.19 = (f32[32,128]{1,0:T(8,128)S(1)}, f32[32,128]{1,0:T(8,128)S(1)}, u32[]{:S(2)}, u32[]{:S(2)}) collective-permute-start(f32[32,128]{1,0:T(8,128)S(1)} %join.6.mine_ref), channel_id=1, source_target_pairs={{0,32},{1,97},{2,34},{3,99},{4,36},{5,101},{6,38},{7,103},{8,40},{... | collective-permute-start | bytes 49160 | tf_op jit(solution)/shard_map/ppermute | solution.py:43
  61.6 1.3 %collective-permute-start.20 = (f32[32,128]{1,0:T(8,128)S(1)}, f32[32,128]{1,0:T(8,128)S(1)}, u32[]{:S(2)}, u32[]{:S(2)}) collective-permute-start(f32[32,128]{1,0:T(8,128)S(1)} %join.7.mine_ref), channel_id=1, source_target_pairs={{0,1},{1,0},{2,3},{3,2},{4,5},{5,4},{6,7},{7,6},{8,9},{9,8},{10,11... | collective-permute-start | bytes 49160 | tf_op jit(solution)/shard_map/ppermute | solution.py:47
  65.5 6.0 %collective-permute-start.23 = (bf16[512,512]{1,0:T(8,128)(2,1)S(1)}, bf16[512,512]{1,0:T(8,128)(2,1)S(1)}, u32[]{:S(2)}, u32[]{:S(2)}) collective-permute-start(bf16[512,512]{1,0:T(8,128)(2,1)S(1)} %get-tuple-element.102), channel_id=1, source_target_pairs={{0,1},{1,0},{2,3},{3,2},{4,5},{5,4},{6,7},{7,6},{8,9},{9,8},{10,11... | collective-permute-start | bytes 1572872 | tf_op jit(solution)/shard_map/ppermute | solution.py:47
  68.3 6.1 %collective-permute-start.22 = (bf16[512,512]{1,0:T(8,128)(2,1)S(1)}, bf16[512,512]{1,0:T(8,128)(2,1)S(1)}, u32[]{:S(2)}, u32[]{:S(2)}) collective-permute-start(bf16[512,512]{1,0:T(8,128)(2,1)S(1)} %get-tuple-element.100), channel_id=1, source_target_pairs={{0,1},{1,0},{2,3},{3,2},{4,5},{5,4},{6,7},{7,6},{8,9},{9,8},{10,11... | collective-permute-start | bytes 1572872 | tf_op jit(solution)/shard_map/ppermute | solution.py:47
  71.3 3.6 %collective-permute-start.21 = (bf16[512,512]{1,0:T(8,128)(2,1)S(1)}, bf16[512,512]{1,0:T(8,128)(2,1)S(1)}, u32[]{:S(2)}, u32[]{:S(2)}) collective-permute-start(bf16[512,512]{1,0:T(8,128)(2,1)S(1)} %get-tuple-element.97), channel_id=1, source_target_pairs={{0,1},{1,0},{2,3},{3,2},{4,5},{5,4},{6,7},{7,6},{8,9},{9,8},{10,11... | collective-permute-start | bytes 1572872 | tf_op jit(solution)/shard_map/ppermute | solution.py:47
  71.7 12.8 %collective-permute-start.26 = (bf16[512,512]{1,0:T(8,128)(2,1)S(1)}, bf16[512,512]{1,0:T(8,128)(2,1)S(1)}, u32[]{:S(2)}, u32[]{:S(2)}) collective-permute-start(bf16[512,512]{1,0:T(8,128)(2,1)S(1)} %far_message.5.refs_17_), channel_id=1, source_target_pairs={{0,8},{1,25},{2,10},{3,27},{4,12},{5,29},{6,14},{7,31},{8,0},{9,17... | collective-permute-start | bytes 1572872 | tf_op jit(solution)/shard_map/ppermute | solution.py:43
  74.6 10.0 %collective-permute-start.25 = (bf16[512,512]{1,0:T(8,128)(2,1)S(1)}, bf16[512,512]{1,0:T(8,128)(2,1)S(1)}, u32[]{:S(2)}, u32[]{:S(2)}) collective-permute-start(bf16[512,512]{1,0:T(8,128)(2,1)S(1)} %far_message.4.refs_16_), channel_id=1, source_target_pairs={{0,2},{1,7},{2,0},{3,5},{4,6},{5,3},{6,4},{7,1},{8,10},{9,15},{10,... | collective-permute-start | bytes 1572872 | tf_op jit(solution)/shard_map/ppermute | solution.py:43
  75.0 9.5 %collective-permute-start.24 = (bf16[528,512]{1,0:T(8,128)(2,1)S(1)}, bf16[528,512]{1,0:T(8,128)(2,1)S(1)}, u32[]{:S(2)}, u32[]{:S(2)}) collective-permute-start(bf16[528,512]{1,0:T(8,128)(2,1)S(1)} %far_message.3.refs_15_), channel_id=1, source_target_pairs={{0,32},{1,97},{2,34},{3,99},{4,36},{5,101},{6,38},{7,103},{8,40},{... | collective-permute-start | bytes 1622024 | tf_op jit(solution)/shard_map/ppermute | solution.py:43
  83.8 2.0 %collective-permute-start.27 = (bf16[512,512]{1,0:T(8,128)(2,1)S(1)}, bf16[512,512]{1,0:T(8,128)(2,1)S(1)}, u32[]{:S(2)}, u32[]{:S(2)}) collective-permute-start(bf16[512,512]{1,0:T(8,128)(2,1)S(1)} %get-tuple-element.105), channel_id=1, source_target_pairs={{0,1},{1,0},{2,3},{3,2},{4,5},{5,4},{6,7},{7,6},{8,9},{9,8},{10,11... | collective-permute-start | bytes 1572872 | tf_op jit(solution)/shard_map/ppermute | solution.py:47
  83.9 2.6 %collective-permute-start.28 = (bf16[512,512]{1,0:T(8,128)(2,1)S(1)}, bf16[512,512]{1,0:T(8,128)(2,1)S(1)}, u32[]{:S(2)}, u32[]{:S(2)}) collective-permute-start(bf16[512,512]{1,0:T(8,128)(2,1)S(1)} %get-tuple-element.106), channel_id=1, source_target_pairs={{0,1},{1,0},{2,3},{3,2},{4,5},{5,4},{6,7},{7,6},{8,9},{9,8},{10,11... | collective-permute-start | bytes 1572872 | tf_op jit(solution)/shard_map/ppermute | solution.py:47
  84.4 2.9 %collective-permute-start.29 = (bf16[512,512]{1,0:T(8,128)(2,1)S(1)}, bf16[512,512]{1,0:T(8,128)(2,1)S(1)}, u32[]{:S(2)}, u32[]{:S(2)}) collective-permute-start(bf16[512,512]{1,0:T(8,128)(2,1)S(1)} %get-tuple-element.107), channel_id=1, source_target_pairs={{0,1},{1,0},{2,3},{3,2},{4,5},{5,4},{6,7},{7,6},{8,9},{9,8},{10,11... | collective-permute-start | bytes 1572872 | tf_op jit(solution)/shard_map/ppermute | solution.py:47
  87.8 7.8 %collective-permute-start.30 = (bf16[272,512]{1,0:T(8,128)(2,1)S(1)}, bf16[272,512]{1,0:T(8,128)(2,1)S(1)}, u32[]{:S(2)}, u32[]{:S(2)}) collective-permute-start(bf16[272,512]{1,0:T(8,128)(2,1)S(1)} %get-tuple-element.110), channel_id=1, source_target_pairs={{0,8},{1,25},{2,10},{3,27},{4,12},{5,29},{6,14},{7,31},{8,0},{9,17... | collective-permute-start | bytes 835592 | tf_op jit(solution)/shard_map/ppermute | solution.py:43
  87.9 6.5 %collective-permute-start.31 = (bf16[256,512]{1,0:T(8,128)(2,1)S(1)}, bf16[256,512]{1,0:T(8,128)(2,1)S(1)}, u32[]{:S(2)}, u32[]{:S(2)}) collective-permute-start(bf16[256,512]{1,0:T(8,128)(2,1)S(1)} %get-tuple-element.111), channel_id=1, source_target_pairs={{0,32},{1,97},{2,34},{3,99},{4,36},{5,101},{6,38},{7,103},{8,40},{... | collective-permute-start | bytes 786440 | tf_op jit(solution)/shard_map/ppermute | solution.py:43
  89.2 6.4 %collective-permute-start.32 = (bf16[256,512]{1,0:T(8,128)(2,1)S(1)}, bf16[256,512]{1,0:T(8,128)(2,1)S(1)}, u32[]{:S(2)}, u32[]{:S(2)}) collective-permute-start(bf16[256,512]{1,0:T(8,128)(2,1)S(1)} %get-tuple-element.112), channel_id=1, source_target_pairs={{0,2},{1,7},{2,0},{3,5},{4,6},{5,3},{6,4},{7,1},{8,10},{9,15},{10,... | collective-permute-start | bytes 786440 | tf_op jit(solution)/shard_map/ppermute | solution.py:43
  90.7 14.5 %collective-permute-start.37 = (f32[384,512]{1,0:T(8,128)S(1)}, f32[384,512]{1,0:T(8,128)S(1)}, u32[]{:S(2)}, u32[]{:S(2)}) collective-permute-start(f32[384,512]{1,0:T(8,128)S(1)} %get-tuple-element.121), channel_id=1, source_target_pairs={{0,1},{1,0},{2,3},{3,2},{4,5},{5,4},{6,7},{7,6},{8,9},{9,8},{10,11... | collective-permute-start | bytes 2359304 | tf_op jit(solution)/shard_map/ppermute | solution.py:47
  95.8 9.2 %collective-permute-start.33 = (bf16[144,512]{1,0:T(8,128)(2,1)S(1)}, bf16[144,512]{1,0:T(8,128)(2,1)S(1)}, u32[]{:S(2)}, u32[]{:S(2)}) collective-permute-start(bf16[144,512]{1,0:T(8,128)(2,1)S(1)} %get-tuple-element.114), channel_id=1, source_target_pairs={{0,2},{1,7},{2,0},{3,5},{4,6},{5,3},{6,4},{7,1},{8,10},{9,15},{10,... | collective-permute-start | bytes 442376 | tf_op jit(solution)/shard_map/ppermute | solution.py:43
  97.3 5.0 %collective-permute-start.34 = (bf16[128,512]{1,0:T(8,128)(2,1)S(1)}, bf16[128,512]{1,0:T(8,128)(2,1)S(1)}, u32[]{:S(2)}, u32[]{:S(2)}) collective-permute-start(bf16[128,512]{1,0:T(8,128)(2,1)S(1)} %get-tuple-element.115), channel_id=1, source_target_pairs={{0,8},{1,25},{2,10},{3,27},{4,12},{5,29},{6,14},{7,31},{8,0},{9,17... | collective-permute-start | bytes 393224 | tf_op jit(solution)/shard_map/ppermute | solution.py:43
  99.9 5.0 %collective-permute-start.35 = (bf16[128,512]{1,0:T(8,128)(2,1)S(1)}, bf16[128,512]{1,0:T(8,128)(2,1)S(1)}, u32[]{:S(2)}, u32[]{:S(2)}) collective-permute-start(bf16[128,512]{1,0:T(8,128)(2,1)S(1)} %get-tuple-element.116), channel_id=1, source_target_pairs={{0,32},{1,97},{2,34},{3,99},{4,36},{5,101},{6,38},{7,103},{8,40},{... | collective-permute-start | bytes 393224 | tf_op jit(solution)/shard_map/ppermute | solution.py:43
  105.0 1.8 %collective-permute-start.36 = (f32[200,512]{1,0:T(8,128)S(1)}, f32[200,512]{1,0:T(8,128)S(1)}, u32[]{:S(2)}, u32[]{:S(2)}) collective-permute-start(f32[200,512]{1,0:T(8,128)S(1)} %get-tuple-element.119), channel_id=1, source_target_pairs={{0,1},{1,0},{2,3},{3,2},{4,5},{5,4},{6,7},{7,6},{8,9},{9,8},{10,11... | collective-permute-start | bytes 1228808 | tf_op jit(solution)/shard_map/ppermute | solution.py:47

commit v5 on v4

--- a/solution.py
+++ b/solution.py
@@ -69,6 +69,7 @@
     return jax.ShapeDtypeStruct(dims, dtype)
 
 
+PACKED = 2
 ROW_AT = (0, 768, 1024, 1280, 1536)
 COL_AT = (0, 1536, 2048, 2560, 3072)
 CONTRACT_LAST = (((1,), (1,)), ((), ()))
@@ -108,7 +109,12 @@
     refs = list(refs)
     take = lambda n: [refs.pop(0) for _ in range(n)]
     n = 3 if stage == 0 else 1
-    mine, swapped = take(n), take(n)
+    mine = take(n)
+    if stage == 0:
+        packed_ref = take(1)[0]
+        swapped = [packed_ref.at[k * 512 : k * 512 + 512] for k in range(PACKED)] + take(3 - PACKED)
+    else:
+        swapped = take(1)
     rows, cols = take(stage), take(stage)
     row_old, col_old = take(2) if stage else (None, None)
     image_ref, text_ref = take(2) if stage == 3 else (None, None)
@@ -172,6 +178,27 @@
     keep_ref[24:32, :] = extra
 
 
+def pack_kernel(core_ref, *refs):
+    for k, ref in enumerate(refs[:-1]):
+        refs[-1][k * 512 : k * 512 + 512, :] = ref[...]
+
+
+def gate_kernel(value_ref, token_ref, out_ref):
+    pass
+
+
+def after(value, token):
+    anywhere = pl.BlockSpec(memory_space=pl.ANY)
+    return pl.pallas_call(
+        gate_kernel,
+        in_specs=[anywhere, anywhere],
+        out_specs=anywhere,
+        out_shape=jax.ShapeDtypeStruct(value.shape, value.dtype),
+        input_output_aliases={0: 0},
+        name="after",
+    )(value, token)
+
+
 def join_kernel(order, core_ref, mine_ref, got_ref, out_ref):
     got = got_ref[...]
     out_ref[0:24, :] = log_add(mine_ref[0:24, :], jnp.concatenate([got[k : k + 1, :] for k in order], 0))
@@ -256,48 +283,44 @@
     send_ref[256:512, :] = text[256:512]
 
 
-def near_grad_kernel(core_ref, mine_ref, other_ref, *refs):
+def near_grad_kernel(q, core_ref, mine_ref, other_ref, *refs):
     refs = list(refs)
     take = lambda n: [refs.pop(0) for _ in range(n)]
-    wide_in = take(1)[0]
+    source_ref = take(1)[0]
     rows, cols = take(4), take(4)
     wide, tall = [None] + take(3), [None] + take(3)
     take(3)
-    base_ref, *send_refs = take(4)
-    early_ref, kept_ref, block_ref = take(3)
-    first = core_ref[0] == 0
-    row, col = tile_lse(first, mine_ref, other_ref)
-    eye = lax.broadcasted_iota(jnp.int32, (128, 128), 0) == lax.broadcasted_iota(jnp.int32, (128, 128), 1)
-    positive = jnp.where(jnp.logical_and(eye, first), 1.0, 0.0)
-    for q in range(3):
-        part = slice(q * 256, q * 256 + 256)
-        coeffs = coefficients(wide_in[part, :], row[:, part], col[:, 0:1536])
-        block_ref[part, :] = coeffs.astype(bf16)
-        own = slice(q * 512, q * 512 + 128)
-        block_ref[q * 256 : q * 256 + 128, own] = (coeffs[0:128, own] - positive).astype(bf16)
-    for q in range(3):
-        part = slice(q * 256, q * 256 + 256)
-        image = total_of(
-            [times(block_ref[part, :], cols[0][...])] + [times(tall[p][part, :], cols[p][...]) for p in range(1, 4)]
-        )
-        here = slice(q * 512, q * 512 + 512)
-        text = total_of(
-            [transposed_times(block_ref[:, here], rows[0][...])]
-            + [transposed_times(wide[p][:, here], rows[p][...]) for p in range(1, 4)]
-        )
-        own, own_text = slice(q * 64, q * 64 + 64), slice(192 + q * 64, 192 + q * 64 + 64)
-        kept_ref[own, :] = image[0:64]
-        kept_ref[own_text, :] = text[0:64]
-        early_ref[own, :] = image[64:128]
-        early_ref[own_text, :] = text[64:128]
-        at = q * 512
-        base_ref[at : at + 128, :] = jnp.where(first, 0.0, text[0:128])
-        base_ref[at + 128 : at + 256, :] = jnp.where(first, image[128:256], text[128:256])
-        base_ref[at + 256 : at + 512, :] = jnp.where(first, 0.0, text[256:512])
-        send = send_refs[q]
-        send[0:128, :] = jnp.where(first, 0.0, image[0:128]).astype(bf16)
-        send[128:256, :] = jnp.where(first, text[128:256], image[128:256]).astype(bf16)
-        send[256:512, :] = text[256:512].astype(bf16)
+    base_ref, send_ref, own_ref = take(3)
+    first = core_ref[0] == 0
+    block_ref = source_ref
+    if q == 0:
+        block_ref = take(1)[0]
+        row, col = tile_lse(first, mine_ref, other_ref)
+        eye = lax.broadcasted_iota(jnp.int32, (128, 128), 0) == lax.broadcasted_iota(jnp.int32, (128, 128), 1)
+        positive = jnp.where(jnp.logical_and(eye, first), 1.0, 0.0)
+        for k in range(3):
+            part = slice(k * 256, k * 256 + 256)
+            coeffs = coefficients(source_ref[part, :], row[:, part], col[:, 0:1536])
+            block_ref[part, :] = coeffs.astype(bf16)
+            own = slice(k * 512, k * 512 + 128)
+            block_ref[k * 256 : k * 256 + 128, own] = (coeffs[0:128, own] - positive).astype(bf16)
+    part = slice(q * 256, q * 256 + 256)
+    image = total_of(
+        [times(block_ref[part, :], cols[0][...])] + [times(tall[p][part, :], cols[p][...]) for p in range(1, 4)]
+    )
+    here = slice(q * 512, q * 512 + 512)
+    text = total_of(
+        [transposed_times(block_ref[:, here], rows[0][...])]
+        + [transposed_times(wide[p][:, here], rows[p][...]) for p in range(1, 4)]
+    )
+    own_ref[0:128, :] = image[0:128]
+    own_ref[128:256, :] = text[0:128]
+    base_ref[0:128, :] = jnp.where(first, 0.0, text[0:128])
+    base_ref[128:256, :] = jnp.where(first, image[128:256], text[128:256])
+    base_ref[256:512, :] = jnp.where(first, 0.0, text[256:512])
+    send_ref[0:128, :] = jnp.where(first, 0.0, image[0:128]).astype(bf16)
+    send_ref[128:256, :] = jnp.where(first, text[128:256], image[128:256]).astype(bf16)
+    send_ref[256:512, :] = text[256:512].astype(bf16)
 
 
 def split_terms(x):
@@ -324,11 +347,10 @@
         refs[-1][512:528, :] = split_terms(refs[0][...])
 
 
-def far_sum_kernel(core_ref, base_ref, r0, r1, r2, loss_ref, total_ref, loss_out):
+def far_sum_kernel(core_ref, b0, b1, b2, r0, r1, r2, loss_ref, total_ref, loss_out):
     loss_out[...] = loss_ref[...] + join_terms(r0, 512)
-    for q, r in enumerate((r0, r1, r2)):
-        rows = slice(q * 512, q * 512 + 512)
-        total_ref[rows, :] = base_ref[rows, :] + r[0:512, :].astype(f32)
+    for q, (b, r) in enumerate(((b0, r0), (b1, r1), (b2, r2))):
+        total_ref[q * 512 : q * 512 + 512, :] = b[...] + r[0:512, :].astype(f32)
 
 
 def near_sum_kernel(core_ref, total_ref, g0, g1, g2, loss_ref, low_ref, s0, s1, s2):
@@ -351,30 +373,27 @@
         s[0:128, :] = total[128:256].astype(bf16)
 
 
-def last_sum_kernel(core_ref, low_ref, r0, r1, r2, loss_ref, keep_ref, send_ref):
+def last_sum_kernel(core_ref, low_ref, r0, r1, r2, o0, o1, o2, loss_ref, keep_ref, send_ref):
     first = core_ref[0] == 0
     loss = loss_ref[...] + join_terms(r0, 128)
-    send_ref[192:200, :] = jnp.concatenate([loss] * 4, 1)
-    keep_ref[192:200, :] = jnp.concatenate([loss] * 4, 1)
-    for q, r in enumerate((r0, r1, r2)):
-        rows = slice(q * 64, q * 64 + 64)
+    keep_ref[384:392, :] = jnp.concatenate([loss] * 4, 1)
+    send_ref[384:392, :] = jnp.concatenate([loss] * 4, 1)
+    for q, (r, own) in enumerate(((r0, o0), (r1, o1), (r2, o2))):
+        rows, text_rows = slice(q * 64, q * 64 + 64), slice(192 + q * 64, 192 + q * 64 + 64)
         total = low_ref[q * 128 : q * 128 + 128, :] + r[0:128, :].astype(f32)
-        keep_ref[rows, :] = jnp.where(first, total[0:64], total[64:128])
-        send_ref[rows, :] = jnp.where(first, total[64:128], total[0:64])
-
-
-def finish_kernel(count, core_ref, keep_ref, got_ref, kept_ref, early_ref, image_out, text_out, loss_out):
-    first = core_ref[0] == 0
-    for q in range(3):
-        rows = slice(q * 64, q * 64 + 64)
-        keep = keep_ref[rows, :]
-        got = got_ref[rows, :]
-        text_rows = slice(192 + q * 64, 192 + q * 64 + 64)
-        own_image = jnp.where(first, kept_ref[rows, :], early_ref[rows, :])
-        own_text = jnp.where(first, kept_ref[text_rows, :], early_ref[text_rows, :])
-        image_out[rows, :] = jnp.where(first, keep, got) + own_image
-        text_out[rows, :] = jnp.where(first, got, keep) + own_text
-    loss_out[...] = (keep_ref[192:193, 0:1] + got_ref[192:193, 0:1]) * (0.5 / count)
+        keep_ref[rows, :] = jnp.where(first, total[0:64] + own[0:64, :], total[64:128])
+        keep_ref[text_rows, :] = own[128:192, :]
+        send_ref[rows, :] = jnp.where(first, total[64:128] + own[64:128, :], total[0:64])
+        send_ref[text_rows, :] = own[192:256, :]
+
+
+def finish_kernel(count, core_ref, keep_ref, got_ref, image_out, text_out, loss_out):
+    first = core_ref[0] == 0
+    image_out[...] = jnp.where(first, keep_ref[0:192, :], got_ref[0:192, :])
+    text_out[...] = jnp.where(
+        first, got_ref[0:192, :] + keep_ref[192:384, :], keep_ref[0:192, :] + got_ref[192:384, :]
+    )
+    loss_out[...] = (keep_ref[384:385, 0:1] + got_ref[384:385, 0:1]) * (0.5 / count)
 
 
 def select_kernel(core_ref, image_ref, text_ref, out_ref):
@@ -402,12 +421,16 @@
         got = [flip_permute(near[q], q + step) for q in range(3)]
         near = [jnp.concatenate([a, b], 0) for a, b in zip(near, got)]
     far = [flip_permute(near[q], q + 2) for q in range(3)]
-    near_x = [core_swap(a) for a in near]
-    far_x = [core_swap(a) for a in far]
+    packed = call(pack_kernel, "pack", [core_id, *near[:PACKED]], [shape(512 * PACKED, width, dtype=bf16)], limit=4)[0]
+    near_x = [core_swap(packed)] + [core_swap(a) for a in near[PACKED:]]
+    far_x = [None] * 3
 
     rows, cols, wide, tall = [], [], [], [None]
     stat = []
     for stage in range(4):
+        for q in {1: (0, 1, 2)}.get(stage, ()):
+            far[q] = after(far[q], stat[0])
+            far_x[q] = core_swap(far[q])
         ins = [core_id] + (near + near_x if stage == 0 else [far[stage - 1], far_x[stage - 1]])
         ins += [held(a) for a in rows + cols] + stat
         if stage == 3:
@@ -467,20 +490,26 @@
             far_message_kernel, "far_message", ins, [shape(528 if stage == 1 else 512, width, dtype=bf16)]
         )[0]
     got = [flip_permute(messages[q], q + 2) for q in range(3)]
-    base, *near_send, early, kept = call(
-        near_grad_kernel,
-        "near_grad",
-        [core_id, mine, other, held(wide[0]), *held_rows, *held_cols]
-        + [held(a) for a in wide_coeffs + tall_coeffs]
-        + messages,
-        [shape(1536, width)] + [shape(512, width, dtype=bf16)] * 3 + [shape(384, width), shape(384, width)],
-        scratch=[pltpu.VMEM((768, 1536), bf16)],
-        limit=10,
-        flops=2 * (768 * 3072 + 1536 * 1536) * width,
-    )
-    near_got = [core_swap(a) for a in near_send]
-    early = core_swap(early)
-    total, loss = call(far_sum_kernel, "far_sum", [core_id, base, *got, loss], [shape(1536, width), shape(8, 128)])
+    bases, near_got, owns = [], [], []
+    source = wide[0]
+    for q in range(3):
+        got_q = call(
+            functools.partial(near_grad_kernel, q),
+            "near_grad",
+            [core_id, mine, other, held(source), *held_rows, *held_cols]
+            + [held(a) for a in wide_coeffs + tall_coeffs]
+            + messages,
+            [shape(512, width), shape(512, width, dtype=bf16), shape(256, width)]
+            + ([pltpu.VMEM((768, 1536), bf16)] if q == 0 else []),
+            limit=10,
+            flops=2 * (256 * 3072 + 1536 * 512) * width,
+        )
+        bases.append(got_q[0])
+        near_got.append(core_swap(got_q[1]))
+        owns.append(got_q[2])
+        if q == 0:
+            source = got_q[3]
+    total, loss = call(far_sum_kernel, "far_sum", [core_id, *bases, *got, loss], [shape(1536, width), shape(8, 128)])
     low, *messages = call(
         near_sum_kernel,
         "near_sum",
@@ -496,13 +525,12 @@
     )
     got = [flip_permute(messages[q], q) for q in range(3)]
     keep, send = call(
-        last_sum_kernel, "last_sum", [core_id, low, *got, loss], [shape(200, width), shape(200, width)]
-    )
-    swapped = core_swap(send)
+        last_sum_kernel, "last_sum", [core_id, low, *got, *owns, loss], [shape(392, width), shape(392, width)]
+    )
     grad_image, grad_text, loss = call(
         functools.partial(finish_kernel, count),
         "finish",
-        [core_id, keep, swapped, kept, early],
+        [core_id, keep, core_swap(send)],
         [shape(192, width), shape(192, width), shape(1, 1)],
     )
     return loss.reshape(()), grad_image, grad_text

time: 108 us -> 115 us (1.065)
  local copies, waits for them, and re-layouts: 1.97 us -> 8.39 us
  starting transfers between devices: 39.3 us -> 36.1 us
  Pallas kernels: 28.9 us -> 30.6 us
  waiting for transfers between devices: 36.9 us -> 38.2 us
    unnamed x13 -> x31, local copies, waits for them, and re-layouts: 1.92 us -> 7.64 us
    ppermute x21, starting transfers between devices: 34.6 us -> 31.3 us  [flip_permute(): return lax.ppermute(x, AXES, ROLE_PAIRS[dim % 3])]
    ppermute x21, waiting for transfers between devices: 29.2 us -> 31.7 us  [flip_permute(): return lax.ppermute(x, AXES, ROLE_PAIRS[dim % 3])]
    pallas_call x22 -> x25, Pallas kernels: 28.9 us -> 30.6 us  [call(): pl.pallas_call(kernel, in_specs=in_specs, out_specs=[VMEM] * len(outs), o...]
    ppermute x17 -> x15, waiting for transfers between devices: 7.63 us -> 6.47 us  [core_swap(): return lax.ppermute(x, 'c', SWAP)]
    ppermute x17 -> x15, starting transfers between devices: 4.67 us -> 4.87 us  [core_swap(): return lax.ppermute(x, 'c', SWAP)]
  transfers between devices with their start and end apart: 38 -> 36, of which waited for: 19 -> 17; matrix products, arithmetic and copies ran while one was open for 0% -> 2% of each run, Pallas kernels for 19% -> 20%
where the time goes in v5:
time: 115 us; the launch traced here: 114 us
  waiting for transfers between devices  38.2 us (33%)
  starting transfers between devices  36.1 us (31%)
  Pallas kernels  30.6 us (27%)
  local copies, waits for them, and re-layouts  8.39 us (7%)
    ppermute x21, waiting for transfers between devices, flip_permute(): return lax.ppermute(x, AXES, ROLE_PAIRS[dim % 3])  31.7 us
    ppermute x21, starting transfers between devices, flip_permute(): return lax.ppermute(x, AXES, ROLE_PAIRS[dim % 3])  31.3 us
    pallas_call x25, Pallas kernels, call(): pl.pallas_call(kernel, in_specs=in_specs, out_specs=[VMEM] * len(outs), o...  30.6 us
    unnamed x31, local copies, waits for them, and re-layouts  7.64 us
    ppermute x15, waiting for transfers between devices, core_swap(): return lax.ppermute(x, 'c', SWAP)  6.47 us
    ppermute x15, starting transfers between devices, core_swap(): return lax.ppermute(x, 'c', SWAP)  4.87 us
  transfers between devices with their start and end apart: 36, of which 17 were waited for; matrix products, arithmetic and copies ran while one was open for 2% of the time, Pallas kernels for 20%

profile of v5, /device:TPU:1, one launch (start us, length us, event | category | flops | bytes accessed | tf_op | source)
XLA Modules:
  0.0 114.4 jit_solution(6563508106858592988)
XLA Ops:
  0.6 0.9 copy-done.1
  1.6 0.9 copy-done.3
  2.5 1.5 %collective-permute-start = (bf16[192,512]{1,0:T(8,128)(2,1)S(1)}, bf16[192,512]{1,0:T(8,128)(2,1)S(1)}, u32[]{:S(2)}, u32[]{:S(2)}) collective-permute-start(bf16[192,512]{1,0:T(8,128)(2,1)S(1)} %select.1), channel_id=1, source_target_pairs={{0,1},{1,0},{2,3},{3,2},{4,5},{5,4},{6,7},{7,6},{8,9},{9,8},{10,11... | collective-permute-start | bytes 589832 | tf_op jit(solution)/shard_map/ppermute | solution.py:47
  4.0 1.1 collective-permute-done.got_ref
  5.1 3.9 %collective-permute-start.1 = (bf16[128,512]{1,0:T(8,128)(2,1)S(1)}, bf16[128,512]{1,0:T(8,128)(2,1)S(1)}, u32[]{:S(2)}, u32[]{:S(2)}) collective-permute-start(bf16[128,512]{1,0:T(8,128)(2,1)S(1)} %get-tuple-element.68), channel_id=1, source_target_pairs={{0,32},{1,97},{2,34},{3,99},{4,36},{5,101},{6,38},{7,103},{8,40},{... | collective-permute-start | bytes 393224 | tf_op jit(solution)/shard_map/ppermute | solution.py:43
  9.0 2.5 %collective-permute-start.4 = (bf16[128,512]{1,0:T(8,128)(2,1)S(1)}, bf16[128,512]{1,0:T(8,128)(2,1)S(1)}, u32[]{:S(2)}, u32[]{:S(2)}) collective-permute-start(bf16[128,512]{1,0:T(8,128)(2,1)S(1)} %get-tuple-element.69), channel_id=1, source_target_pairs={{0,2},{1,7},{2,0},{3,5},{4,6},{5,3},{6,4},{7,1},{8,10},{9,15},{10,... | collective-permute-start | bytes 393224 | tf_op jit(solution)/shard_map/ppermute | solution.py:43
  11.5 2.7 %collective-permute-start.6 = (bf16[128,512]{1,0:T(8,128)(2,1)S(1)}, bf16[128,512]{1,0:T(8,128)(2,1)S(1)}, u32[]{:S(2)}, u32[]{:S(2)}) collective-permute-start(bf16[128,512]{1,0:T(8,128)(2,1)S(1)} %get-tuple-element.70), channel_id=1, source_target_pairs={{0,8},{1,25},{2,10},{3,27},{4,12},{5,29},{6,14},{7,31},{8,0},{9,17... | collective-permute-start | bytes 393224 | tf_op jit(solution)/shard_map/ppermute | solution.py:43
  14.3 0.7 constant_dynamic-update-slice_fusion.2
  14.9 1.7 %collective-permute-done.6 = bf16[128,512]{1,0:T(8,128)(2,1)S(1)} collective-permute-done((bf16[128,512]{1,0:T(8,128)(2,1)S(1)}, bf16[128,512]{1,0:T(8,128)(2,1)S(1)}, u32[]{:S(2)}, u32[]{:S(2)}) %collective-permute-start.6) | collective-permute-done | bytes 131104 | tf_op jit(solution)/shard_map/ppermute | solution.py:43
  16.8 2.8 %collective-permute-start.5 = (bf16[256,512]{1,0:T(8,128)(2,1)S(1)}, bf16[256,512]{1,0:T(8,128)(2,1)S(1)}, u32[]{:S(2)}, u32[]{:S(2)}) collective-permute-start(bf16[256,512]{1,0:T(8,128)(2,1)S(1)} %pad_maximum_fusion.1), channel_id=1, source_target_pairs={{0,8},{1,25},{2,10},{3,27},{4,12},{5,29},{6,14},{7,31},{8,0},{9,17... | collective-permute-start | bytes 786440 | tf_op jit(solution)/shard_map/ppermute | solution.py:43
  19.6 3.5 %collective-permute-done.7 = bf16[256,512]{1,0:T(8,128)(2,1)S(1)} collective-permute-done((bf16[256,512]{1,0:T(8,128)(2,1)S(1)}, bf16[256,512]{1,0:T(8,128)(2,1)S(1)}, u32[]{:S(2)}, u32[]{:S(2)}) %collective-permute-start.7) | collective-permute-done | bytes 262176 | tf_op jit(solution)/shard_map/ppermute | solution.py:43
  23.9 0.7 constant_dynamic-update-slice_fusion.1
  24.5 5.6 %collective-permute-done.2 = bf16[256,512]{1,0:T(8,128)(2,1)S(1)} collective-permute-done((bf16[256,512]{1,0:T(8,128)(2,1)S(1)}, bf16[256,512]{1,0:T(8,128)(2,1)S(1)}, u32[]{:S(2)}, u32[]{:S(2)}) %collective-permute-start.2) | collective-permute-done | bytes 262176 | tf_op jit(solution)/shard_map/ppermute | solution.py:43
  30.1 0.7 constant_dynamic-update-slice_fusion.refs_2_
  31.2 2.6 %collective-permute-start.11 = (bf16[512,512]{1,0:T(8,128)(2,1)S(1)}, bf16[512,512]{1,0:T(8,128)(2,1)S(1)}, u32[]{:S(2)}, u32[]{:S(2)}) collective-permute-start(bf16[512,512]{1,0:T(8,128)(2,1)S(1)} %constant_dynamic-update-slice_fusion.3.refs_0_), channel_id=1, source_target_pairs={{0,32},{1,97},{2,34},{3,99},{4,36},{5,101},{6,38},{7,103},{8,40},{... | collective-permute-start | bytes 1572872 | tf_op jit(solution)/shard_map/ppermute | solution.py:43
  34.0 2.7 %collective-permute-start.3 = (bf16[512,512]{1,0:T(8,128)(2,1)}, bf16[512,512]{1,0:T(8,128)(2,1)S(1)}, u32[]{:S(2)}, u32[]{:S(2)}) collective-permute-start(bf16[512,512]{1,0:T(8,128)(2,1)} %constant_dynamic-update-slice_fusion.refs_2_), channel_id=1, source_target_pairs={{0,8},{1,25},{2,10},{3,27},{4,12},{5,29},{6,14},{7,31},{8,0},{9,17... | collective-permute-start | bytes 1572872 | tf_op jit(solution)/shard_map/ppermute | solution.py:43
  36.7 4.0 %forward.4 = (bf16[768,512]{1,0:T(8,128)(2,1)S(1)}, bf16[1536,512]{1,0:T(8,128)(2,1)S(1)}, f32[768,1536]{1,0:T(8,128)S(1)}, f32[6,128]{1,0:T(8,128)S(1)}, f32[12,128]{1,0:T(8,128)S(1)}) custom-call(s32[1]{0:T(128)} %bitcast.core_ref, bf16[512,512]{1,0:T(8,128)(2,1)S(1)} %constant_dynamic-update-slice_fusion.3.refs_0_, ...), custom_call_target="tpu_custom_call" | custom-call | flops 1207959552 | tf_op jit(solution)/shard_map/forward/pallas_call | solution.py:52
  40.7 2.2 %copy-done = f32[768,1536]{1,0:T(8,128)} copy-done((f32[768,1536]{1,0:T(8,128)}, f32[768,1536]{1,0:T(8,128)S(1)}, u32[]{:S(2)}) %copy-start) | copy-done | bytes 4718616
  43.5 0.8 copy-done.7
  44.9 0.8 copy-done.5
  45.8 0.8 collective-permute-done.12.refs_1_
  46.6 3.3 %forward.5 = (bf16[256,512]{1,0:T(8,128)(2,1)S(1)}, bf16[512,512]{1,0:T(8,128)(2,1)S(1)}, f32[256,2048]{1,0:T(8,128)S(1)}, f32[768,512]{1,0:T(8,128)S(1)}, f32[8,128]{1,0:T(8,128)S(1)}, /*index=5*/f32[16,128]{1,0:T(8,128)S(1)}) custom-call(s32[1]{0:T(128)} %bitcast.core_ref, bf16[512,512]{1,0:T(8,128)(2,1)S(1)} %copy-done.8, ...), custom_call_target="tpu_custom_call" | custom-call | flops 939524096 | tf_op jit(solution)/shard_map/forward/pallas_call | solution.py:52
  50.0 4.1 %forward.6 = (bf16[256,512]{1,0:T(8,128)(2,1)S(1)}, bf16[512,512]{1,0:T(8,128)(2,1)S(1)}, f32[256,2560]{1,0:T(8,128)S(1)}, f32[1024,512]{1,0:T(8,128)S(1)}, f32[...) custom-call(s32[1]{0:T(128)} %bitcast.core_ref, bf16[512,512]{1,0:T(8,128)(2,1)} %after.5.refs_0_, ...), custom_call_target="tpu_custom_call" | custom-call | flops 1207959552 | tf_op jit(solution)/shard_map/forward/pallas_call | solution.py:52
  54.1 3.3 %forward.7 = (bf16[256,512]{1,0:T(8,128)(2,1)S(1)}, bf16[512,512]{1,0:T(8,128)(2,1)S(1)}, f32[256,3072]{1,0:T(8,128)S(1)}, f32[1280,512]{1,0:T(8,128)S(1)}, f32[...) custom-call(s32[1]{0:T(128)} %bitcast.core_ref, bf16[512,512]{1,0:T(8,128)(2,1)S(1)} %copy-done.6, ...), custom_call_target="tpu_custom_call" | custom-call | flops 1476395008 | tf_op jit(solution)/shard_map/forward/pallas_call | solution.py:52
  57.7 1.0 collective-permute-done.15.got_ref
  58.7 2.6 %collective-permute-start.16 = (f32[32,128]{1,0:T(8,128)S(1)}, f32[32,128]{1,0:T(8,128)S(1)}, u32[]{:S(2)}, u32[]{:S(2)}) collective-permute-start(f32[32,128]{1,0:T(8,128)S(1)} %join.4.mine_ref), channel_id=1, source_target_pairs={{0,2},{1,7},{2,0},{3,5},{4,6},{5,3},{6,4},{7,1},{8,10},{9,15},{10,... | collective-permute-start | bytes 49160 | tf_op jit(solution)/shard_map/ppermute | solution.py:43
  61.3 1.3 %collective-permute-done.16.got_ref = f32[32,128]{1,0:T(8,128)S(1)} collective-permute-done((f32[32,128]{1,0:T(8,128)S(1)}, f32[32,128]{1,0:T(8,128)S(1)}, u32[]{:S(2)}, u32[]{:S(2)}) %collective-permute-start.16) | collective-permute-done | bytes 16416 | tf_op jit(solution)/shard_map/ppermute | solution.py:43
  63.2 3.3 %collective-permute-done.17.got_ref = f32[32,128]{1,0:T(8,128)S(1)} collective-permute-done((f32[32,128]{1,0:T(8,128)S(1)}, f32[32,128]{1,0:T(8,128)S(1)}, u32[]{:S(2)}, u32[]{:S(2)}) %collective-permute-start.17) | collective-permute-done | bytes 16416 | tf_op jit(solution)/shard_map/ppermute | solution.py:43
  66.7 3.7 %collective-permute-done.18.got_ref = f32[32,128]{1,0:T(8,128)S(1)} collective-permute-done((f32[32,128]{1,0:T(8,128)S(1)}, f32[32,128]{1,0:T(8,128)S(1)}, u32[]{:S(2)}, u32[]{:S(2)}) %collective-permute-start.18) | collective-permute-done | bytes 16416 | tf_op jit(solution)/shard_map/ppermute | solution.py:43
  70.5 1.2 %collective-permute-done.19.other_ref = f32[32,128]{1,0:T(8,128)S(1)} collective-permute-done((f32[32,128]{1,0:T(8,128)S(1)}, f32[32,128]{1,0:T(8,128)S(1)}, u32[]{:S(2)}, u32[]{:S(2)}) %collective-permute-start.19) | collective-permute-done | bytes 16416 | tf_op jit(solution)/shard_map/ppermute | solution.py:47
  71.7 2.6 %far_grad.3 = (bf16[256,3072]{1,0:T(8,128)(2,1)S(1)}, bf16[1280,512]{1,0:T(8,128)(2,1)S(1)}, bf16[512,512]{1,0:T(8,128)(2,1)S(1)}, bf16[512,512]{1,0:T(8,128)(2,1)S(1)}, f32[8,128]{1,0:T(8,128)S(1)}) custom-call(s32[1]{0:T(128)} %bitcast.core_ref, f32[32,128]{1,0:T(8,128)S(1)} %join.7.mine_ref, f32[32,128]{1,0:T(8,128)S(1)} %collective-permute-done.19.other_ref, ...), custom_call_target="tpu_custom_call" | custom-call | flops 1610612736 | tf_op jit(solution)/shard_map/far_grad/pallas_call | solution.py:52
  74.5 2.4 %far_grad.4 = (bf16[256,2560]{1,0:T(8,128)(2,1)S(1)}, bf16[1024,512]{1,0:T(8,128)(2,1)S(1)}, bf16[512,512]{1,0:T(8,128)(2,1)S(1)}, bf16[512,512]{1,0:T(8,128)(2,1)S(1)}) custom-call(s32[1]{0:T(128)} %bitcast.core_ref, f32[32,128]{1,0:T(8,128)S(1)} %join.7.mine_ref, f32[32,128]{1,0:T(8,128)S(1)} %collective-permute-done.19.other_ref, ...), custom_call_target="tpu_custom_call" | custom-call | flops 1610612736 | tf_op jit(solution)/shard_map/far_grad/pallas_call | solution.py:52
  77.5 2.1 %far_grad.5 = (bf16[256,2048]{1,0:T(8,128)(2,1)S(1)}, bf16[768,512]{1,0:T(8,128)(2,1)S(1)}, bf16[512,512]{1,0:T(8,128)(2,1)S(1)}, bf16[512,512]{1,0:T(8,128)(2,1)S(1)}) custom-call(s32[1]{0:T(128)} %bitcast.core_ref, f32[32,128]{1,0:T(8,128)S(1)} %join.7.mine_ref, f32[32,128]{1,0:T(8,128)S(1)} %collective-permute-done.19.other_ref, ...), custom_call_target="tpu_custom_call" | custom-call | flops 1610612736 | tf_op jit(solution)/shard_map/far_grad/pallas_call | solution.py:52
  80.8 2.5 %collective-permute-start.24 = (bf16[512,512]{1,0:T(8,128)(2,1)S(1)}, bf16[512,512]{1,0:T(8,128)(2,1)S(1)}, u32[]{:S(2)}, u32[]{:S(2)}) collective-permute-start(bf16[512,512]{1,0:T(8,128)(2,1)S(1)} %far_message.4.refs_16_), channel_id=1, source_target_pairs={{0,2},{1,7},{2,0},{3,5},{4,6},{5,3},{6,4},{7,1},{8,10},{9,15},{10,... | collective-permute-start | bytes 1572872 | tf_op jit(solution)/shard_map/ppermute | solution.py:43
  83.7 2.6 %near_grad.3 = (f32[512,512]{1,0:T(8,128)S(1)}, bf16[512,512]{1,0:T(8,128)(2,1)S(1)}, f32[256,512]{1,0:T(8,128)S(1)}, bf16[768,1536]{1,0:T(8,128)(2,1)S(1)}) custom-call(s32[1]{0:T(128)} %bitcast.core_ref, f32[32,128]{1,0:T(8,128)S(1)} %join.7.mine_ref, f32[32,128]{1,0:T(8,128)S(1)} %collective-permute-done.19.other_ref, f32[768,1536]{1,0:T(8,128)S(1)} %bitcast.3, ...), custom_call_target="tpu_custom_call" | custom-call | flops 1610612736 | tf_op jit(solution)/shard_map/near_grad/pallas_call | solution.py:52
  86.4 1.8 %near_grad.5 = (f32[512,512]{1,0:T(8,128)S(1)}, bf16[512,512]{1,0:T(8,128)(2,1)S(1)}, f32[256,512]{1,0:T(8,128)S(1)}) custom-call(s32[1]{0:T(128)} %bitcast.core_ref, f32[32,128]{1,0:T(8,128)S(1)} %join.7.mine_ref, f32[32,128]{1,0:T(8,128)S(1)} %collective-permute-done.19.other_ref, bf16[768,1536]{1,0:T(8,128)(2,1)S(1)} %get-tuple-element.108.refs_0_, ...), custom_call_target="tpu_custom_call" | custom-call | flops 1610612736 | tf_op jit(solution)/shard_map/near_grad/pallas_call | solution.py:52
  88.8 1.8 %near_grad.4 = (f32[512,512]{1,0:T(8,128)S(1)}, bf16[512,512]{1,0:T(8,128)(2,1)S(1)}, f32[256,512]{1,0:T(8,128)S(1)}) custom-call(s32[1]{0:T(128)} %bitcast.core_ref, f32[32,128]{1,0:T(8,128)S(1)} %join.7.mine_ref, f32[32,128]{1,0:T(8,128)S(1)} %collective-permute-done.19.other_ref, bf16[768,1536]{1,0:T(8,128)(2,1)S(1)} %get-tuple-element.108.refs_0_, ...), custom_call_target="tpu_custom_call" | custom-call | flops 1610612736 | tf_op jit(solution)/shard_map/near_grad/pallas_call | solution.py:52
  90.7 2.3 %collective-permute-done.23.r0 = bf16[528,512]{1,0:T(8,128)(2,1)S(1)} collective-permute-done((bf16[528,512]{1,0:T(8,128)(2,1)S(1)}, bf16[528,512]{1,0:T(8,128)(2,1)S(1)}, u32[]{:S(2)}, u32[]{:S(2)}) %collective-permute-start.23) | collective-permute-done | bytes 540704 | tf_op jit(solution)/shard_map/ppermute | solution.py:43
  93.7 2.3 %collective-permute-start.29 = (bf16[272,512]{1,0:T(8,128)(2,1)S(1)}, bf16[272,512]{1,0:T(8,128)(2,1)S(1)}, u32[]{:S(2)}, u32[]{:S(2)}) collective-permute-start(bf16[272,512]{1,0:T(8,128)(2,1)S(1)} %get-tuple-element.117), channel_id=1, source_target_pairs={{0,8},{1,25},{2,10},{3,27},{4,12},{5,29},{6,14},{7,31},{8,0},{9,17... | collective-permute-start | bytes 835592 | tf_op jit(solution)/shard_map/ppermute | solution.py:43
  96.0 1.9 %collective-permute-start.30 = (bf16[256,512]{1,0:T(8,128)(2,1)S(1)}, bf16[256,512]{1,0:T(8,128)(2,1)S(1)}, u32[]{:S(2)}, u32[]{:S(2)}) collective-permute-start(bf16[256,512]{1,0:T(8,128)(2,1)S(1)} %get-tuple-element.118), channel_id=1, source_target_pairs={{0,32},{1,97},{2,34},{3,99},{4,36},{5,101},{6,38},{7,103},{8,40},{... | collective-permute-start | bytes 786440 | tf_op jit(solution)/shard_map/ppermute | solution.py:43
  98.0 4.4 %collective-permute-done.30.r1 = bf16[256,512]{1,0:T(8,128)(2,1)S(1)} collective-permute-done((bf16[256,512]{1,0:T(8,128)(2,1)S(1)}, bf16[256,512]{1,0:T(8,128)(2,1)S(1)}, u32[]{:S(2)}, u32[]{:S(2)}) %collective-permute-start.30) | collective-permute-done | bytes 262176 | tf_op jit(solution)/shard_map/ppermute | solution.py:43
  102.4 1.9 %collective-permute-done.31.r2 = bf16[256,512]{1,0:T(8,128)(2,1)S(1)} collective-permute-done((bf16[256,512]{1,0:T(8,128)(2,1)S(1)}, bf16[256,512]{1,0:T(8,128)(2,1)S(1)}, u32[]{:S(2)}, u32[]{:S(2)}) %collective-permute-start.31) | collective-permute-done | bytes 262176 | tf_op jit(solution)/shard_map/ppermute | solution.py:43
  104.7 1.1 collective-permute-start.33
  105.8 1.1 collective-permute-start.34
  106.9 2.8 %collective-permute-done.33.r1 = bf16[128,512]{1,0:T(8,128)(2,1)S(1)} collective-permute-done((bf16[128,512]{1,0:T(8,128)(2,1)S(1)}, bf16[128,512]{1,0:T(8,128)(2,1)S(1)}, u32[]{:S(2)}, u32[]{:S(2)}) %collective-permute-start.33) | collective-permute-done | bytes 131104 | tf_op jit(solution)/shard_map/ppermute | solution.py:43
  109.7 1.1 collective-permute-done.34.r2
  111.1 2.3 %collective-permute-done.35.got_ref = f32[392,512]{1,0:T(8,128)S(1)} collective-permute-done((f32[392,512]{1,0:T(8,128)S(1)}, f32[392,512]{1,0:T(8,128)S(1)}, u32[]{:S(2)}, u32[]{:S(2)}) %collective-permute-start.35) | collective-permute-done | bytes 802848 | tf_op jit(solution)/shard_map/ppermute | solution.py:47
  113.4 1.0 finish.1
  (90 shorter events, 8.6 us)
Async XLA Ops:
  0.6 0.9 copy-start.1
  1.6 0.9 copy-start.3
  2.5 2.6 %collective-permute-start = (bf16[192,512]{1,0:T(8,128)(2,1)S(1)}, bf16[192,512]{1,0:T(8,128)(2,1)S(1)}, u32[]{:S(2)}, u32[]{:S(2)}) collective-permute-start(bf16[192,512]{1,0:T(8,128)(2,1)S(1)} %select.1), channel_id=1, source_target_pairs={{0,1},{1,0},{2,3},{3,2},{4,5},{5,4},{6,7},{7,6},{8,9},{9,8},{10,11... | collective-permute-start | bytes 589832 | tf_op jit(solution)/shard_map/ppermute | solution.py:47
  5.1 18.4 %collective-permute-start.1 = (bf16[128,512]{1,0:T(8,128)(2,1)S(1)}, bf16[128,512]{1,0:T(8,128)(2,1)S(1)}, u32[]{:S(2)}, u32[]{:S(2)}) collective-permute-start(bf16[128,512]{1,0:T(8,128)(2,1)S(1)} %get-tuple-element.68), channel_id=1, source_target_pairs={{0,32},{1,97},{2,34},{3,99},{4,36},{5,101},{6,38},{7,103},{8,40},{... | collective-permute-start | bytes 393224 | tf_op jit(solution)/shard_map/ppermute | solution.py:43
  9.0 7.8 %collective-permute-start.4 = (bf16[128,512]{1,0:T(8,128)(2,1)S(1)}, bf16[128,512]{1,0:T(8,128)(2,1)S(1)}, u32[]{:S(2)}, u32[]{:S(2)}) collective-permute-start(bf16[128,512]{1,0:T(8,128)(2,1)S(1)} %get-tuple-element.69), channel_id=1, source_target_pairs={{0,2},{1,7},{2,0},{3,5},{4,6},{5,3},{6,4},{7,1},{8,10},{9,15},{10,... | collective-permute-start | bytes 393224 | tf_op jit(solution)/shard_map/ppermute | solution.py:43
  11.5 5.1 %collective-permute-start.6 = (bf16[128,512]{1,0:T(8,128)(2,1)S(1)}, bf16[128,512]{1,0:T(8,128)(2,1)S(1)}, u32[]{:S(2)}, u32[]{:S(2)}) collective-permute-start(bf16[128,512]{1,0:T(8,128)(2,1)S(1)} %get-tuple-element.70), channel_id=1, source_target_pairs={{0,8},{1,25},{2,10},{3,27},{4,12},{5,29},{6,14},{7,31},{8,0},{9,17... | collective-permute-start | bytes 393224 | tf_op jit(solution)/shard_map/ppermute | solution.py:43
  16.6 6.5 %collective-permute-start.7 = (bf16[256,512]{1,0:T(8,128)(2,1)S(1)}, bf16[256,512]{1,0:T(8,128)(2,1)S(1)}, u32[]{:S(2)}, u32[]{:S(2)}) collective-permute-start(bf16[256,512]{1,0:T(8,128)(2,1)S(1)} %pad_maximum_fusion.2), channel_id=1, source_target_pairs={{0,32},{1,97},{2,34},{3,99},{4,36},{5,101},{6,38},{7,103},{8,40},{... | collective-permute-start | bytes 786440 | tf_op jit(solution)/shard_map/ppermute | solution.py:43
  16.8 6.5 %collective-permute-start.5 = (bf16[256,512]{1,0:T(8,128)(2,1)S(1)}, bf16[256,512]{1,0:T(8,128)(2,1)S(1)}, u32[]{:S(2)}, u32[]{:S(2)}) collective-permute-start(bf16[256,512]{1,0:T(8,128)(2,1)S(1)} %pad_maximum_fusion.1), channel_id=1, source_target_pairs={{0,8},{1,25},{2,10},{3,27},{4,12},{5,29},{6,14},{7,31},{8,0},{9,17... | collective-permute-start | bytes 786440 | tf_op jit(solution)/shard_map/ppermute | solution.py:43
  23.5 13.2 %collective-permute-start.8 = (bf16[1024,512]{1,0:T(8,128)(2,1)S(1)}, bf16[1024,512]{1,0:T(8,128)(2,1)S(1)}, u32[]{:S(2)}, u32[]{:S(2)}) collective-permute-start(bf16[1024,512]{1,0:T(8,128)(2,1)S(1)} %pack.1), channel_id=1, source_target_pairs={{0,1},{1,0},{2,3},{3,2},{4,5},{5,4},{6,7},{7,6},{8,9},{9,8},{10,11... | collective-permute-start | bytes 3145736 | tf_op jit(solution)/shard_map/ppermute | solution.py:47
  23.6 6.5 %collective-permute-start.2 = (bf16[256,512]{1,0:T(8,128)(2,1)S(1)}, bf16[256,512]{1,0:T(8,128)(2,1)S(1)}, u32[]{:S(2)}, u32[]{:S(2)}) collective-permute-start(bf16[256,512]{1,0:T(8,128)(2,1)S(1)} %pad_maximum_fusion), channel_id=1, source_target_pairs={{0,2},{1,7},{2,0},{3,5},{4,6},{5,3},{6,4},{7,1},{8,10},{9,15},{10,... | collective-permute-start | bytes 786440 | tf_op jit(solution)/shard_map/ppermute | solution.py:43
  30.8 5.9 %collective-permute-start.9 = (bf16[512,512]{1,0:T(8,128)(2,1)}, bf16[512,512]{1,0:T(8,128)(2,1)S(1)}, u32[]{:S(2)}, u32[]{:S(2)}) collective-permute-start(bf16[512,512]{1,0:T(8,128)(2,1)} %constant_dynamic-update-slice_fusion.refs_2_), channel_id=1, source_target_pairs={{0,1},{1,0},{2,3},{3,2},{4,5},{5,4},{6,7},{7,6},{8,9},{9,8},{10,11... | collective-permute-start | bytes 1572872 | tf_op jit(solution)/shard_map/ppermute | solution.py:47
  31.2 12.3 %collective-permute-start.11 = (bf16[512,512]{1,0:T(8,128)(2,1)S(1)}, bf16[512,512]{1,0:T(8,128)(2,1)S(1)}, u32[]{:S(2)}, u32[]{:S(2)}) collective-permute-start(bf16[512,512]{1,0:T(8,128)(2,1)S(1)} %constant_dynamic-update-slice_fusion.3.refs_0_), channel_id=1, source_target_pairs={{0,32},{1,97},{2,34},{3,99},{4,36},{5,101},{6,38},{7,103},{8,40},{... | collective-permute-start | bytes 1572872 | tf_op jit(solution)/shard_map/ppermute | solution.py:43
  33.8 10.5 %collective-permute-start.13 = (bf16[512,512]{1,0:T(8,128)(2,1)S(1)}, bf16[512,512]{1,0:T(8,128)(2,1)}, u32[]{:S(2)}, u32[]{:S(2)}) collective-permute-start(bf16[512,512]{1,0:T(8,128)(2,1)S(1)} %constant_dynamic-update-slice_fusion.6.refs_1_), channel_id=1, source_target_pairs={{0,2},{1,7},{2,0},{3,5},{4,6},{5,3},{6,4},{7,1},{8,10},{9,15},{10,... | collective-permute-start | bytes 1572872 | tf_op jit(solution)/shard_map/ppermute | solution.py:43
  34.0 10.9 %collective-permute-start.3 = (bf16[512,512]{1,0:T(8,128)(2,1)}, bf16[512,512]{1,0:T(8,128)(2,1)S(1)}, u32[]{:S(2)}, u32[]{:S(2)}) collective-permute-start(bf16[512,512]{1,0:T(8,128)(2,1)} %constant_dynamic-update-slice_fusion.refs_2_), channel_id=1, source_target_pairs={{0,8},{1,25},{2,10},{3,27},{4,12},{5,29},{6,14},{7,31},{8,0},{9,17... | collective-permute-start | bytes 1572872 | tf_op jit(solution)/shard_map/ppermute | solution.py:43
  40.7 2.2 %copy-start = (f32[768,1536]{1,0:T(8,128)}, f32[768,1536]{1,0:T(8,128)S(1)}, u32[]{:S(2)}) copy-start(f32[768,1536]{1,0:T(8,128)S(1)} %get-tuple-element.85.refs_0_) | copy-start | bytes 14155780
  43.5 0.8 copy-start.7
  44.4 2.3 %copy-start.10 = (f32[6,128]{1,0:T(8,128)S(1)}, f32[6,128]{1,0:T(8,128)}, u32[]{:S(2)}) copy-start(f32[6,128]{1,0:T(8,128)} %copy-done.9) | copy-start | bytes 9220
  44.4 2.3 %collective-permute-start.12 = (bf16[512,512]{1,0:T(8,128)(2,1)}, bf16[512,512]{1,0:T(8,128)(2,1)}, u32[]{:S(2)}, u32[]{:S(2)}) collective-permute-start(bf16[512,512]{1,0:T(8,128)(2,1)} %after.4.refs_0_), channel_id=1, source_target_pairs={{0,1},{1,0},{2,3},{3,2},{4,5},{5,4},{6,7},{7,6},{8,9},{9,8},{10,11... | collective-permute-start | bytes 1572872 | tf_op jit(solution)/shard_map/ppermute | solution.py:47
  44.4 2.2 %copy-start.8 = (bf16[512,512]{1,0:T(8,128)(2,1)S(1)}, bf16[512,512]{1,0:T(8,128)(2,1)}, u32[]{:S(2)}) copy-start(bf16[512,512]{1,0:T(8,128)(2,1)} %after.4.refs_0_) | copy-start | bytes 1572868
  44.4 5.5 %collective-permute-start.14 = (bf16[512,512]{1,0:T(8,128)(2,1)}, bf16[512,512]{1,0:T(8,128)(2,1)}, u32[]{:S(2)}, u32[]{:S(2)}) collective-permute-start(bf16[512,512]{1,0:T(8,128)(2,1)} %after.5.refs_0_), channel_id=1, source_target_pairs={{0,1},{1,0},{2,3},{3,2},{4,5},{5,4},{6,7},{7,6},{8,9},{9,8},{10,11... | collective-permute-start | bytes 1572872 | tf_op jit(solution)/shard_map/ppermute | solution.py:47
  44.9 0.8 copy-start.5
  45.7 8.4 %collective-permute-start.10 = (bf16[512,512]{1,0:T(8,128)(2,1)}, bf16[512,512]{1,0:T(8,128)(2,1)S(1)}, u32[]{:S(2)}, u32[]{:S(2)}) collective-permute-start(bf16[512,512]{1,0:T(8,128)(2,1)} %after.3.refs_0_), channel_id=1, source_target_pairs={{0,1},{1,0},{2,3},{3,2},{4,5},{5,4},{6,7},{7,6},{8,9},{9,8},{10,11... | collective-permute-start | bytes 1572872 | tf_op jit(solution)/shard_map/ppermute | solution.py:47
  49.9 4.2 %copy-start.2 = (bf16[192,512]{1,0:T(8,128)(2,1)S(1)}, bf16[192,512]{1,0:T(8,128)(2,1)}, u32[]{:S(2)}) copy-start(bf16[192,512]{1,0:T(8,128)(2,1)} %refs_10_.1) | copy-start | bytes 589828
  50.0 4.2 %copy-start.4 = (bf16[192,512]{1,0:T(8,128)(2,1)S(1)}, bf16[192,512]{1,0:T(8,128)(2,1)}, u32[]{:S(2)}) copy-start(bf16[192,512]{1,0:T(8,128)(2,1)} %refs_11_.1) | copy-start | bytes 589828
  50.0 4.1 %copy-start.6 = (bf16[512,512]{1,0:T(8,128)(2,1)S(1)}, bf16[512,512]{1,0:T(8,128)(2,1)}, u32[]{:S(2)}) copy-start(bf16[512,512]{1,0:T(8,128)(2,1)} %after.3.refs_0_) | copy-start | bytes 1572868
  57.4 1.3 %collective-permute-start.15 = (f32[32,128]{1,0:T(8,128)S(1)}, f32[32,128]{1,0:T(8,128)S(1)}, u32[]{:S(2)}, u32[]{:S(2)}) collective-permute-start(f32[32,128]{1,0:T(8,128)S(1)} %get-tuple-element.84), channel_id=1, source_target_pairs={{0,1},{1,0},{2,3},{3,2},{4,5},{5,4},{6,7},{7,6},{8,9},{9,8},{10,11... | collective-permute-start | bytes 49160 | tf_op jit(solution)/shard_map/ppermute | solution.py:47
  58.7 3.9 %collective-permute-start.16 = (f32[32,128]{1,0:T(8,128)S(1)}, f32[32,128]{1,0:T(8,128)S(1)}, u32[]{:S(2)}, u32[]{:S(2)}) collective-permute-start(f32[32,128]{1,0:T(8,128)S(1)} %join.4.mine_ref), channel_id=1, source_target_pairs={{0,2},{1,7},{2,0},{3,5},{4,6},{5,3},{6,4},{7,1},{8,10},{9,15},{10,... | collective-permute-start | bytes 49160 | tf_op jit(solution)/shard_map/ppermute | solution.py:43
  62.6 3.9 %collective-permute-start.17 = (f32[32,128]{1,0:T(8,128)S(1)}, f32[32,128]{1,0:T(8,128)S(1)}, u32[]{:S(2)}, u32[]{:S(2)}) collective-permute-start(f32[32,128]{1,0:T(8,128)S(1)} %join.5.mine_ref), channel_id=1, source_target_pairs={{0,8},{1,25},{2,10},{3,27},{4,12},{5,29},{6,14},{7,31},{8,0},{9,17... | collective-permute-start | bytes 49160 | tf_op jit(solution)/shard_map/ppermute | solution.py:43
  66.5 3.9 %collective-permute-start.18 = (f32[32,128]{1,0:T(8,128)S(1)}, f32[32,128]{1,0:T(8,128)S(1)}, u32[]{:S(2)}, u32[]{:S(2)}) collective-permute-start(f32[32,128]{1,0:T(8,128)S(1)} %join.6.mine_ref), channel_id=1, source_target_pairs={{0,32},{1,97},{2,34},{3,99},{4,36},{5,101},{6,38},{7,103},{8,40},{... | collective-permute-start | bytes 49160 | tf_op jit(solution)/shard_map/ppermute | solution.py:43
  70.4 1.3 %collective-permute-start.19 = (f32[32,128]{1,0:T(8,128)S(1)}, f32[32,128]{1,0:T(8,128)S(1)}, u32[]{:S(2)}, u32[]{:S(2)}) collective-permute-start(f32[32,128]{1,0:T(8,128)S(1)} %join.7.mine_ref), channel_id=1, source_target_pairs={{0,1},{1,0},{2,3},{3,2},{4,5},{5,4},{6,7},{7,6},{8,9},{9,8},{10,11... | collective-permute-start | bytes 49160 | tf_op jit(solution)/shard_map/ppermute | solution.py:47
  74.3 5.6 %collective-permute-start.22 = (bf16[512,512]{1,0:T(8,128)(2,1)S(1)}, bf16[512,512]{1,0:T(8,128)(2,1)S(1)}, u32[]{:S(2)}, u32[]{:S(2)}) collective-permute-start(bf16[512,512]{1,0:T(8,128)(2,1)S(1)} %get-tuple-element.106), channel_id=1, source_target_pairs={{0,1},{1,0},{2,3},{3,2},{4,5},{5,4},{6,7},{7,6},{8,9},{9,8},{10,11... | collective-permute-start | bytes 1572872 | tf_op jit(solution)/shard_map/ppermute | solution.py:47
  76.9 3.8 %collective-permute-start.21 = (bf16[512,512]{1,0:T(8,128)(2,1)S(1)}, bf16[512,512]{1,0:T(8,128)(2,1)S(1)}, u32[]{:S(2)}, u32[]{:S(2)}) collective-permute-start(bf16[512,512]{1,0:T(8,128)(2,1)S(1)} %get-tuple-element.104), channel_id=1, source_target_pairs={{0,1},{1,0},{2,3},{3,2},{4,5},{5,4},{6,7},{7,6},{8,9},{9,8},{10,11... | collective-permute-start | bytes 1572872 | tf_op jit(solution)/shard_map/ppermute | solution.py:47
  77.5 6.1 %slice-start = ((s8[4718592]{0:T(1024)(128)(4,1)}), s8[4194304]{0:T(1024)(128)(4,1)S(1)}, s32[]{:S(2)}) async-start(s8[4718592]{0:T(1024)(128)(4,1)} %bitcast.2), calls=%async_computation | async-start | bytes 8388608
  77.5 6.1 %slice-start.1 = ((s8[4718592]{0:T(1024)(128)(4,1)}), s8[524288]{0:T(1024)(128)(4,1)S(1)}, s32[]{:S(2)}) async-start(s8[4718592]{0:T(1024)(128)(4,1)} %bitcast.2), calls=%async_computation.1 | async-start | bytes 1048576
  79.7 3.7 %collective-permute-start.20 = (bf16[512,512]{1,0:T(8,128)(2,1)S(1)}, bf16[512,512]{1,0:T(8,128)(2,1)S(1)}, u32[]{:S(2)}, u32[]{:S(2)}) collective-permute-start(bf16[512,512]{1,0:T(8,128)(2,1)S(1)} %get-tuple-element.101), channel_id=1, source_target_pairs={{0,1},{1,0},{2,3},{3,2},{4,5},{5,4},{6,7},{7,6},{8,9},{9,8},{10,11... | collective-permute-start | bytes 1572872 | tf_op jit(solution)/shard_map/ppermute | solution.py:47
  80.1 10.5 %collective-permute-start.25 = (bf16[512,512]{1,0:T(8,128)(2,1)S(1)}, bf16[512,512]{1,0:T(8,128)(2,1)S(1)}, u32[]{:S(2)}, u32[]{:S(2)}) collective-permute-start(bf16[512,512]{1,0:T(8,128)(2,1)S(1)} %far_message.5.refs_17_), channel_id=1, source_target_pairs={{0,8},{1,25},{2,10},{3,27},{4,12},{5,29},{6,14},{7,31},{8,0},{9,17... | collective-permute-start | bytes 1572872 | tf_op jit(solution)/shard_map/ppermute | solution.py:43
  80.8 9.9 %collective-permute-start.24 = (bf16[512,512]{1,0:T(8,128)(2,1)S(1)}, bf16[512,512]{1,0:T(8,128)(2,1)S(1)}, u32[]{:S(2)}, u32[]{:S(2)}) collective-permute-start(bf16[512,512]{1,0:T(8,128)(2,1)S(1)} %far_message.4.refs_16_), channel_id=1, source_target_pairs={{0,2},{1,7},{2,0},{3,5},{4,6},{5,3},{6,4},{7,1},{8,10},{9,15},{10,... | collective-permute-start | bytes 1572872 | tf_op jit(solution)/shard_map/ppermute | solution.py:43
  83.5 9.5 %collective-permute-start.23 = (bf16[528,512]{1,0:T(8,128)(2,1)S(1)}, bf16[528,512]{1,0:T(8,128)(2,1)S(1)}, u32[]{:S(2)}, u32[]{:S(2)}) collective-permute-start(bf16[528,512]{1,0:T(8,128)(2,1)S(1)} %far_message.3.refs_15_), channel_id=1, source_target_pairs={{0,32},{1,97},{2,34},{3,99},{4,36},{5,101},{6,38},{7,103},{8,40},{... | collective-permute-start | bytes 1622024 | tf_op jit(solution)/shard_map/ppermute | solution.py:43
  86.3 6.9 %collective-permute-start.26 = (bf16[512,512]{1,0:T(8,128)(2,1)S(1)}, bf16[512,512]{1,0:T(8,128)(2,1)S(1)}, u32[]{:S(2)}, u32[]{:S(2)}) collective-permute-start(bf16[512,512]{1,0:T(8,128)(2,1)S(1)} %get-tuple-element.112), channel_id=1, source_target_pairs={{0,1},{1,0},{2,3},{3,2},{4,5},{5,4},{6,7},{7,6},{8,9},{9,8},{10,11... | collective-permute-start | bytes 1572872 | tf_op jit(solution)/shard_map/ppermute | solution.py:47
  88.2 5.0 %collective-permute-start.28 = (bf16[512,512]{1,0:T(8,128)(2,1)S(1)}, bf16[512,512]{1,0:T(8,128)(2,1)S(1)}, u32[]{:S(2)}, u32[]{:S(2)}) collective-permute-start(bf16[512,512]{1,0:T(8,128)(2,1)S(1)} %get-tuple-element.114), channel_id=1, source_target_pairs={{0,1},{1,0},{2,3},{3,2},{4,5},{5,4},{6,7},{7,6},{8,9},{9,8},{10,11... | collective-permute-start | bytes 1572872 | tf_op jit(solution)/shard_map/ppermute | solution.py:47
  90.6 2.7 %collective-permute-start.27 = (bf16[512,512]{1,0:T(8,128)(2,1)S(1)}, bf16[512,512]{1,0:T(8,128)(2,1)S(1)}, u32[]{:S(2)}, u32[]{:S(2)}) collective-permute-start(bf16[512,512]{1,0:T(8,128)(2,1)S(1)} %get-tuple-element.113), channel_id=1, source_target_pairs={{0,1},{1,0},{2,3},{3,2},{4,5},{5,4},{6,7},{7,6},{8,9},{9,8},{10,11... | collective-permute-start | bytes 1572872 | tf_op jit(solution)/shard_map/ppermute | solution.py:47
  93.7 10.6 %collective-permute-start.29 = (bf16[272,512]{1,0:T(8,128)(2,1)S(1)}, bf16[272,512]{1,0:T(8,128)(2,1)S(1)}, u32[]{:S(2)}, u32[]{:S(2)}) collective-permute-start(bf16[272,512]{1,0:T(8,128)(2,1)S(1)} %get-tuple-element.117), channel_id=1, source_target_pairs={{0,8},{1,25},{2,10},{3,27},{4,12},{5,29},{6,14},{7,31},{8,0},{9,17... | collective-permute-start | bytes 835592 | tf_op jit(solution)/shard_map/ppermute | solution.py:43
  96.0 6.4 %collective-permute-start.30 = (bf16[256,512]{1,0:T(8,128)(2,1)S(1)}, bf16[256,512]{1,0:T(8,128)(2,1)S(1)}, u32[]{:S(2)}, u32[]{:S(2)}) collective-permute-start(bf16[256,512]{1,0:T(8,128)(2,1)S(1)} %get-tuple-element.118), channel_id=1, source_target_pairs={{0,32},{1,97},{2,34},{3,99},{4,36},{5,101},{6,38},{7,103},{8,40},{... | collective-permute-start | bytes 786440 | tf_op jit(solution)/shard_map/ppermute | solution.py:43
  97.8 6.4 %collective-permute-start.31 = (bf16[256,512]{1,0:T(8,128)(2,1)S(1)}, bf16[256,512]{1,0:T(8,128)(2,1)S(1)}, u32[]{:S(2)}, u32[]{:S(2)}) collective-permute-start(bf16[256,512]{1,0:T(8,128)(2,1)S(1)} %get-tuple-element.119), channel_id=1, source_target_pairs={{0,2},{1,7},{2,0},{3,5},{4,6},{5,3},{6,4},{7,1},{8,10},{9,15},{10,... | collective-permute-start | bytes 786440 | tf_op jit(solution)/shard_map/ppermute | solution.py:43
  104.4 6.4 %collective-permute-start.32 = (bf16[144,512]{1,0:T(8,128)(2,1)S(1)}, bf16[144,512]{1,0:T(8,128)(2,1)S(1)}, u32[]{:S(2)}, u32[]{:S(2)}) collective-permute-start(bf16[144,512]{1,0:T(8,128)(2,1)S(1)} %get-tuple-element.121), channel_id=1, source_target_pairs={{0,2},{1,7},{2,0},{3,5},{4,6},{5,3},{6,4},{7,1},{8,10},{9,15},{10,... | collective-permute-start | bytes 442376 | tf_op jit(solution)/shard_map/ppermute | solution.py:43
  104.7 5.0 %collective-permute-start.33 = (bf16[128,512]{1,0:T(8,128)(2,1)S(1)}, bf16[128,512]{1,0:T(8,128)(2,1)S(1)}, u32[]{:S(2)}, u32[]{:S(2)}) collective-permute-start(bf16[128,512]{1,0:T(8,128)(2,1)S(1)} %get-tuple-element.122), channel_id=1, source_target_pairs={{0,8},{1,25},{2,10},{3,27},{4,12},{5,29},{6,14},{7,31},{8,0},{9,17... | collective-permute-start | bytes 393224 | tf_op jit(solution)/shard_map/ppermute | solution.py:43
  105.8 5.0 %collective-permute-start.34 = (bf16[128,512]{1,0:T(8,128)(2,1)S(1)}, bf16[128,512]{1,0:T(8,128)(2,1)S(1)}, u32[]{:S(2)}, u32[]{:S(2)}) collective-permute-start(bf16[128,512]{1,0:T(8,128)(2,1)S(1)} %get-tuple-element.123), channel_id=1, source_target_pairs={{0,32},{1,97},{2,34},{3,99},{4,36},{5,101},{6,38},{7,103},{8,40},{... | collective-permute-start | bytes 393224 | tf_op jit(solution)/shard_map/ppermute | solution.py:43
  111.0 2.4 %collective-permute-start.35 = (f32[392,512]{1,0:T(8,128)S(1)}, f32[392,512]{1,0:T(8,128)S(1)}, u32[]{:S(2)}, u32[]{:S(2)}) collective-permute-start(f32[392,512]{1,0:T(8,128)S(1)} %get-tuple-element.129), channel_id=1, source_target_pairs={{0,1},{1,0},{2,3},{3,2},{4,5},{5,4},{6,7},{7,6},{8,9},{9,8},{10,11... | collective-permute-start | bytes 2408456 | tf_op jit(solution)/shard_map/ppermute | solution.py:47
  (1 other events, 0.6 us)

commit v6 on v5

--- a/solution.py
+++ b/solution.py
@@ -69,7 +69,6 @@
     return jax.ShapeDtypeStruct(dims, dtype)
 
 
-PACKED = 2
 ROW_AT = (0, 768, 1024, 1280, 1536)
 COL_AT = (0, 1536, 2048, 2560, 3072)
 CONTRACT_LAST = (((1,), (1,)), ((), ()))
@@ -112,7 +111,7 @@
     mine = take(n)
     if stage == 0:
         packed_ref = take(1)[0]
-        swapped = [packed_ref.at[k * 512 : k * 512 + 512] for k in range(PACKED)] + take(3 - PACKED)
+        swapped = [packed_ref.at[k * 512 : k * 512 + 512] for k in range(3)]
     else:
         swapped = take(1)
     rows, cols = take(stage), take(stage)
@@ -178,9 +177,16 @@
     keep_ref[24:32, :] = extra
 
 
-def pack_kernel(core_ref, *refs):
-    for k, ref in enumerate(refs[:-1]):
-        refs[-1][k * 512 : k * 512 + 512, :] = ref[...]
+def stack_kernel(core_ref, *refs):
+    packed = len(refs) == 10
+    for q in range(3):
+        a, b, out = refs[q], refs[q + 3], refs[q + 6]
+        rows = a.shape[0]
+        out[0:rows, :] = a[...]
+        out[rows : 2 * rows, :] = b[...]
+        if packed:
+            refs[9][q * 512 : q * 512 + rows, :] = a[...]
+            refs[9][q * 512 + rows : q * 512 + 512, :] = b[...]
 
 
 def gate_kernel(value_ref, token_ref, out_ref):
@@ -188,15 +194,15 @@
 
 
 def after(value, token):
-    anywhere = pl.BlockSpec(memory_space=pl.ANY)
     return pl.pallas_call(
         gate_kernel,
-        in_specs=[anywhere, anywhere],
-        out_specs=anywhere,
-        out_shape=jax.ShapeDtypeStruct(value.shape, value.dtype),
+        in_specs=[VMEM, VMEM],
+        out_specs=VMEM,
+        out_shape=pltpu.VMEM(value.shape, value.dtype),
         input_output_aliases={0: 0},
+        compiler_params=pltpu.CompilerParams(vmem_limit_bytes=1 << 20),
         name="after",
-    )(value, token)
+    )(held(value), token)
 
 
 def join_kernel(order, core_ref, mine_ref, got_ref, out_ref):
@@ -419,10 +425,11 @@
     )
     for step in range(2):
         got = [flip_permute(near[q], q + step) for q in range(3)]
-        near = [jnp.concatenate([a, b], 0) for a, b in zip(near, got)]
+        outs = [shape(256 << step, width, dtype=bf16)] * 3 + [shape(1536, width, dtype=bf16)] * step
+        near = call(stack_kernel, "stack", [core_id, *near, *got], outs, limit=2)
+    *near, packed = near
+    near_x = [core_swap(packed)]
     far = [flip_permute(near[q], q + 2) for q in range(3)]
-    packed = call(pack_kernel, "pack", [core_id, *near[:PACKED]], [shape(512 * PACKED, width, dtype=bf16)], limit=4)[0]
-    near_x = [core_swap(packed)] + [core_swap(a) for a in near[PACKED:]]
     far_x = [None] * 3
 
     rows, cols, wide, tall = [], [], [], [None]

time: 115 us -> 106 us (0.922)
  local copies, waits for them, and re-layouts: 8.39 us -> 1.86 us
  waiting for transfers between devices: 38.2 us -> 35.3 us
  starting transfers between devices: 36.1 us -> 39 us
  Pallas kernels: 30.6 us -> 29.1 us
    unnamed x31 -> x8, local copies, waits for them, and re-layouts: 7.64 us -> 1.86 us
    ppermute x21, waiting for transfers between devices: 31.7 us -> 27.4 us  [flip_permute(): return lax.ppermute(x, AXES, ROLE_PAIRS[dim % 3])]
    ppermute x21, starting transfers between devices: 31.3 us -> 34.3 us  [flip_permute(): return lax.ppermute(x, AXES, ROLE_PAIRS[dim % 3])]
    pallas_call x25 -> x26, Pallas kernels: 30.6 us -> 29.1 us  [call(): pl.pallas_call(kernel, in_specs=in_specs, out_specs=[VMEM] * len(outs), o...]
    ppermute x15 -> x14, waiting for transfers between devices: 6.47 us -> 7.88 us  [core_swap(): return lax.ppermute(x, 'c', SWAP)]
    ppermute x15 -> x14, starting transfers between devices: 4.87 us -> 4.75 us  [core_swap(): return lax.ppermute(x, 'c', SWAP)]
  transfers between devices with their start and end apart: 36 -> 35, of which waited for: 17 -> 19; matrix products, arithmetic and copies ran while one was open for 2% -> 0% of each run, Pallas kernels for 20% -> 19%
where the time goes in v6:
time: 106 us
  starting transfers between devices  39 us (37%)
  waiting for transfers between devices  35.3 us (33%)
  Pallas kernels  29.1 us (27%)
  local copies, waits for them, and re-layouts  1.86 us (2%)
    ppermute x21, starting transfers between devices, flip_permute(): return lax.ppermute(x, AXES, ROLE_PAIRS[dim % 3])  34.3 us
    pallas_call x26, Pallas kernels, call(): pl.pallas_call(kernel, in_specs=in_specs, out_specs=[VMEM] * len(outs), o...  29.1 us
    ppermute x21, waiting for transfers between devices, flip_permute(): return lax.ppermute(x, AXES, ROLE_PAIRS[dim % 3])  27.4 us
    ppermute x14, waiting for transfers between devices, core_swap(): return lax.ppermute(x, 'c', SWAP)  7.88 us
    ppermute x14, starting transfers between devices, core_swap(): return lax.ppermute(x, 'c', SWAP)  4.75 us
  transfers between devices with their start and end apart: 35, of which 19 were waited for; matrix products, arithmetic and copies ran while one was open for 0% of the time, Pallas kernels for 19%

profile of v6, /device:TPU:1, one launch (start us, length us, event | category | flops | bytes accessed | tf_op | source)
XLA Modules:
  0.0 106.2 jit_solution(2246749792406830032)
XLA Ops:
  0.6 0.9 copy-done
  1.6 0.9 copy-done.2
  2.5 1.5 %collective-permute-start = (bf16[192,512]{1,0:T(8,128)(2,1)S(1)}, bf16[192,512]{1,0:T(8,128)(2,1)S(1)}, u32[]{:S(2)}, u32[]{:S(2)}) collective-permute-start(bf16[192,512]{1,0:T(8,128)(2,1)S(1)} %select.1), channel_id=1, source_target_pairs={{0,1},{1,0},{2,3},{3,2},{4,5},{5,4},{6,7},{7,6},{8,9},{9,8},{10,11... | collective-permute-start | bytes 589832 | tf_op jit(solution)/shard_map/ppermute | solution.py:47
  4.0 1.1 %collective-permute-done.got_ref = bf16[192,512]{1,0:T(8,128)(2,1)S(1)} collective-permute-done((bf16[192,512]{1,0:T(8,128)(2,1)S(1)}, bf16[192,512]{1,0:T(8,128)(2,1)S(1)}, u32[]{:S(2)}, u32[]{:S(2)}) %collective-permute-start) | collective-permute-done | bytes 196640 | tf_op jit(solution)/shard_map/ppermute | solution.py:47
  5.1 2.6 %collective-permute-start.1 = (bf16[128,512]{1,0:T(8,128)(2,1)S(1)}, bf16[128,512]{1,0:T(8,128)(2,1)S(1)}, u32[]{:S(2)}, u32[]{:S(2)}) collective-permute-start(bf16[128,512]{1,0:T(8,128)(2,1)S(1)} %get-tuple-element.75.refs_0_), channel_id=1, source_target_pairs={{0,2},{1,7},{2,0},{3,5},{4,6},{5,3},{6,4},{7,1},{8,10},{9,15},{10,... | collective-permute-start | bytes 393224 | tf_op jit(solution)/shard_map/ppermute | solution.py:43
  7.8 2.7 %collective-permute-start.2 = (bf16[128,512]{1,0:T(8,128)(2,1)S(1)}, bf16[128,512]{1,0:T(8,128)(2,1)S(1)}, u32[]{:S(2)}, u32[]{:S(2)}) collective-permute-start(bf16[128,512]{1,0:T(8,128)(2,1)S(1)} %get-tuple-element.76.refs_1_), channel_id=1, source_target_pairs={{0,8},{1,25},{2,10},{3,27},{4,12},{5,29},{6,14},{7,31},{8,0},{9,17... | collective-permute-start | bytes 393224 | tf_op jit(solution)/shard_map/ppermute | solution.py:43
  10.5 3.8 %collective-permute-start.3 = (bf16[128,512]{1,0:T(8,128)(2,1)S(1)}, bf16[128,512]{1,0:T(8,128)(2,1)S(1)}, u32[]{:S(2)}, u32[]{:S(2)}) collective-permute-start(bf16[128,512]{1,0:T(8,128)(2,1)S(1)} %get-tuple-element.77.refs_2_), channel_id=1, source_target_pairs={{0,32},{1,97},{2,34},{3,99},{4,36},{5,101},{6,38},{7,103},{8,40},{... | collective-permute-start | bytes 393224 | tf_op jit(solution)/shard_map/ppermute | solution.py:43
  14.3 2.3 %collective-permute-done.3.refs_5_ = bf16[128,512]{1,0:T(8,128)(2,1)S(1)} collective-permute-done((bf16[128,512]{1,0:T(8,128)(2,1)S(1)}, bf16[128,512]{1,0:T(8,128)(2,1)S(1)}, u32[]{:S(2)}, u32[]{:S(2)}) %collective-permute-start.3) | collective-permute-done | bytes 131104 | tf_op jit(solution)/shard_map/ppermute | solution.py:43
  16.8 2.8 %collective-permute-start.5 = (bf16[256,512]{1,0:T(8,128)(2,1)S(1)}, bf16[256,512]{1,0:T(8,128)(2,1)S(1)}, u32[]{:S(2)}, u32[]{:S(2)}) collective-permute-start(bf16[256,512]{1,0:T(8,128)(2,1)S(1)} %get-tuple-element.79.refs_1_), channel_id=1, source_target_pairs={{0,32},{1,97},{2,34},{3,99},{4,36},{5,101},{6,38},{7,103},{8,40},{... | collective-permute-start | bytes 786440 | tf_op jit(solution)/shard_map/ppermute | solution.py:43
  19.7 3.5 %collective-permute-done.4.refs_3_ = bf16[256,512]{1,0:T(8,128)(2,1)S(1)} collective-permute-done((bf16[256,512]{1,0:T(8,128)(2,1)S(1)}, bf16[256,512]{1,0:T(8,128)(2,1)S(1)}, u32[]{:S(2)}, u32[]{:S(2)}) %collective-permute-start.4) | collective-permute-done | bytes 262176 | tf_op jit(solution)/shard_map/ppermute | solution.py:43
  23.3 2.7 %collective-permute-done.6.refs_5_ = bf16[256,512]{1,0:T(8,128)(2,1)S(1)} collective-permute-done((bf16[256,512]{1,0:T(8,128)(2,1)S(1)}, bf16[256,512]{1,0:T(8,128)(2,1)S(1)}, u32[]{:S(2)}, u32[]{:S(2)}) %collective-permute-start.6) | collective-permute-done | bytes 262176 | tf_op jit(solution)/shard_map/ppermute | solution.py:43
  26.9 2.7 %collective-permute-start.7 = (bf16[512,512]{1,0:T(8,128)(2,1)S(1)}, bf16[512,512]{1,0:T(8,128)(2,1)S(1)}, u32[]{:S(2)}, u32[]{:S(2)}) collective-permute-start(bf16[512,512]{1,0:T(8,128)(2,1)S(1)} %get-tuple-element.81.refs_2_), channel_id=1, source_target_pairs={{0,8},{1,25},{2,10},{3,27},{4,12},{5,29},{6,14},{7,31},{8,0},{9,17... | collective-permute-start | bytes 1572872 | tf_op jit(solution)/shard_map/ppermute | solution.py:43
  29.7 2.8 %forward.4 = (bf16[768,512]{1,0:T(8,128)(2,1)S(1)}, bf16[1536,512]{1,0:T(8,128)(2,1)S(1)}, f32[768,1536]{1,0:T(8,128)S(1)}, f32[6,128]{1,0:T(8,128)S(1)}, f32[12,128]{1,0:T(8,128)S(1)}) custom-call(s32[1]{0:T(128)} %bitcast.core_ref, bf16[512,512]{1,0:T(8,128)(2,1)S(1)} %get-tuple-element.82.refs_0_, bf16[512,512]{1,0:T(8,128)(2,1)S(1)} %get-tuple-element.83.refs_1_, ...), custom_call_target="tpu_custom_call" | custom-call | flops 1207959552 | tf_op jit(solution)/shard_map/forward/pallas_call | solution.py:52
  32.5 3.1 %collective-permute-done.10.value_ref = bf16[512,512]{1,0:T(8,128)(2,1)S(1)} collective-permute-done((bf16[512,512]{1,0:T(8,128)(2,1)S(1)}, bf16[512,512]{1,0:T(8,128)(2,1)S(1)}, u32[]{:S(2)}, u32[]{:S(2)}) %collective-permute-start.10) | collective-permute-done | bytes 524320 | tf_op jit(solution)/shard_map/ppermute | solution.py:43
  36.5 1.0 collective-permute-done.11.refs_1_
  37.5 2.5 %forward.5 = (bf16[256,512]{1,0:T(8,128)(2,1)S(1)}, bf16[512,512]{1,0:T(8,128)(2,1)S(1)}, f32[256,2048]{1,0:T(8,128)S(1)}, f32[768,512]{1,0:T(8,128)S(1)}, f32[8,128]{1,0:T(8,128)S(1)}, /*index=5*/f32[16,128]{1,0:T(8,128)S(1)}) custom-call(s32[1]{0:T(128)} %bitcast.core_ref, bf16[512,512]{1,0:T(8,128)(2,1)S(1)} %after.4.refs_0_, ...), custom_call_target="tpu_custom_call" | custom-call | flops 939524096 | tf_op jit(solution)/shard_map/forward/pallas_call | solution.py:52
  40.0 3.0 %forward.6 = (bf16[256,512]{1,0:T(8,128)(2,1)S(1)}, bf16[512,512]{1,0:T(8,128)(2,1)S(1)}, f32[256,2560]{1,0:T(8,128)S(1)}, f32[1024,512]{1,0:T(8,128)S(1)}, f32[...) custom-call(s32[1]{0:T(128)} %bitcast.core_ref, bf16[512,512]{1,0:T(8,128)(2,1)S(1)} %after.5.refs_0_, ...), custom_call_target="tpu_custom_call" | custom-call | flops 1207959552 | tf_op jit(solution)/shard_map/forward/pallas_call | solution.py:52
  43.1 4.1 %forward.7 = (bf16[256,512]{1,0:T(8,128)(2,1)S(1)}, bf16[512,512]{1,0:T(8,128)(2,1)S(1)}, f32[256,3072]{1,0:T(8,128)S(1)}, f32[1280,512]{1,0:T(8,128)S(1)}, f32[...) custom-call(s32[1]{0:T(128)} %bitcast.core_ref, bf16[512,512]{1,0:T(8,128)(2,1)S(1)} %after.3.refs_0_, ...), custom_call_target="tpu_custom_call" | custom-call | flops 1476395008 | tf_op jit(solution)/shard_map/forward/pallas_call | solution.py:52
  47.6 0.8 collective-permute-done.14.got_ref
  48.4 1.1 %collective-permute-start.15 = (f32[32,128]{1,0:T(8,128)S(1)}, f32[32,128]{1,0:T(8,128)S(1)}, u32[]{:S(2)}, u32[]{:S(2)}) collective-permute-start(f32[32,128]{1,0:T(8,128)S(1)} %join.4.mine_ref), channel_id=1, source_target_pairs={{0,2},{1,7},{2,0},{3,5},{4,6},{5,3},{6,4},{7,1},{8,10},{9,15},{10,... | collective-permute-start | bytes 49160 | tf_op jit(solution)/shard_map/ppermute | solution.py:43
  49.5 2.8 %collective-permute-done.15.got_ref = f32[32,128]{1,0:T(8,128)S(1)} collective-permute-done((f32[32,128]{1,0:T(8,128)S(1)}, f32[32,128]{1,0:T(8,128)S(1)}, u32[]{:S(2)}, u32[]{:S(2)}) %collective-permute-start.15) | collective-permute-done | bytes 16416 | tf_op jit(solution)/shard_map/ppermute | solution.py:43
  52.3 2.7 %collective-permute-start.16 = (f32[32,128]{1,0:T(8,128)S(1)}, f32[32,128]{1,0:T(8,128)S(1)}, u32[]{:S(2)}, u32[]{:S(2)}) collective-permute-start(f32[32,128]{1,0:T(8,128)S(1)} %join.5.mine_ref), channel_id=1, source_target_pairs={{0,8},{1,25},{2,10},{3,27},{4,12},{5,29},{6,14},{7,31},{8,0},{9,17... | collective-permute-start | bytes 49160 | tf_op jit(solution)/shard_map/ppermute | solution.py:43
  55.0 1.2 %collective-permute-done.16.got_ref = f32[32,128]{1,0:T(8,128)S(1)} collective-permute-done((f32[32,128]{1,0:T(8,128)S(1)}, f32[32,128]{1,0:T(8,128)S(1)}, u32[]{:S(2)}, u32[]{:S(2)}) %collective-permute-start.16) | collective-permute-done | bytes 16416 | tf_op jit(solution)/shard_map/ppermute | solution.py:43
  56.2 1.4 %collective-permute-start.17 = (f32[32,128]{1,0:T(8,128)S(1)}, f32[32,128]{1,0:T(8,128)S(1)}, u32[]{:S(2)}, u32[]{:S(2)}) collective-permute-start(f32[32,128]{1,0:T(8,128)S(1)} %join.6.mine_ref), channel_id=1, source_target_pairs={{0,32},{1,97},{2,34},{3,99},{4,36},{5,101},{6,38},{7,103},{8,40},{... | collective-permute-start | bytes 49160 | tf_op jit(solution)/shard_map/ppermute | solution.py:43
  57.6 2.5 %collective-permute-done.17.got_ref = f32[32,128]{1,0:T(8,128)S(1)} collective-permute-done((f32[32,128]{1,0:T(8,128)S(1)}, f32[32,128]{1,0:T(8,128)S(1)}, u32[]{:S(2)}, u32[]{:S(2)}) %collective-permute-start.17) | collective-permute-done | bytes 16416 | tf_op jit(solution)/shard_map/ppermute | solution.py:43
  60.4 1.0 collective-permute-done.18.other_ref
  61.4 2.7 %far_grad.3 = (bf16[256,3072]{1,0:T(8,128)(2,1)S(1)}, bf16[1280,512]{1,0:T(8,128)(2,1)S(1)}, bf16[512,512]{1,0:T(8,128)(2,1)S(1)}, bf16[512,512]{1,0:T(8,128)(2,1)S(1)}, f32[8,128]{1,0:T(8,128)S(1)}) custom-call(s32[1]{0:T(128)} %bitcast.core_ref, f32[32,128]{1,0:T(8,128)S(1)} %join.7.mine_ref, f32[32,128]{1,0:T(8,128)S(1)} %collective-permute-done.18.other_ref, ...), custom_call_target="tpu_custom_call" | custom-call | flops 1610612736 | tf_op jit(solution)/shard_map/far_grad/pallas_call | solution.py:52
  64.4 2.5 %far_grad.4 = (bf16[256,2560]{1,0:T(8,128)(2,1)S(1)}, bf16[1024,512]{1,0:T(8,128)(2,1)S(1)}, bf16[512,512]{1,0:T(8,128)(2,1)S(1)}, bf16[512,512]{1,0:T(8,128)(2,1)S(1)}) custom-call(s32[1]{0:T(128)} %bitcast.core_ref, f32[32,128]{1,0:T(8,128)S(1)} %join.7.mine_ref, f32[32,128]{1,0:T(8,128)S(1)} %collective-permute-done.18.other_ref, ...), custom_call_target="tpu_custom_call" | custom-call | flops 1610612736 | tf_op jit(solution)/shard_map/far_grad/pallas_call | solution.py:52
  67.3 2.3 %far_grad.5 = (bf16[256,2048]{1,0:T(8,128)(2,1)S(1)}, bf16[768,512]{1,0:T(8,128)(2,1)S(1)}, bf16[512,512]{1,0:T(8,128)(2,1)S(1)}, bf16[512,512]{1,0:T(8,128)(2,1)S(1)}) custom-call(s32[1]{0:T(128)} %bitcast.core_ref, f32[32,128]{1,0:T(8,128)S(1)} %join.7.mine_ref, f32[32,128]{1,0:T(8,128)S(1)} %collective-permute-done.18.other_ref, ...), custom_call_target="tpu_custom_call" | custom-call | flops 1610612736 | tf_op jit(solution)/shard_map/far_grad/pallas_call | solution.py:52
  70.0 2.7 %collective-permute-start.24 = (bf16[512,512]{1,0:T(8,128)(2,1)S(1)}, bf16[512,512]{1,0:T(8,128)(2,1)S(1)}, u32[]{:S(2)}, u32[]{:S(2)}) collective-permute-start(bf16[512,512]{1,0:T(8,128)(2,1)S(1)} %far_message.5.refs_17_), channel_id=1, source_target_pairs={{0,8},{1,25},{2,10},{3,27},{4,12},{5,29},{6,14},{7,31},{8,0},{9,17... | collective-permute-start | bytes 1572872 | tf_op jit(solution)/shard_map/ppermute | solution.py:43
  72.8 1.3 %collective-permute-start.23 = (bf16[512,512]{1,0:T(8,128)(2,1)S(1)}, bf16[512,512]{1,0:T(8,128)(2,1)S(1)}, u32[]{:S(2)}, u32[]{:S(2)}) collective-permute-start(bf16[512,512]{1,0:T(8,128)(2,1)S(1)} %far_message.4.refs_16_), channel_id=1, source_target_pairs={{0,2},{1,7},{2,0},{3,5},{4,6},{5,3},{6,4},{7,1},{8,10},{9,15},{10,... | collective-permute-start | bytes 1572872 | tf_op jit(solution)/shard_map/ppermute | solution.py:43
  74.3 2.7 %collective-permute-start.22 = (bf16[528,512]{1,0:T(8,128)(2,1)S(1)}, bf16[528,512]{1,0:T(8,128)(2,1)S(1)}, u32[]{:S(2)}, u32[]{:S(2)}) collective-permute-start(bf16[528,512]{1,0:T(8,128)(2,1)S(1)} %far_message.3.refs_15_), channel_id=1, source_target_pairs={{0,32},{1,97},{2,34},{3,99},{4,36},{5,101},{6,38},{7,103},{8,40},{... | collective-permute-start | bytes 1622024 | tf_op jit(solution)/shard_map/ppermute | solution.py:43
  77.0 2.8 %near_grad.3 = (f32[512,512]{1,0:T(8,128)S(1)}, bf16[512,512]{1,0:T(8,128)(2,1)S(1)}, f32[256,512]{1,0:T(8,128)S(1)}, bf16[768,1536]{1,0:T(8,128)(2,1)S(1)}) custom-call(s32[1]{0:T(128)} %bitcast.core_ref, f32[32,128]{1,0:T(8,128)S(1)} %join.7.mine_ref, f32[32,128]{1,0:T(8,128)S(1)} %collective-permute-done.18.other_ref, ...), custom_call_target="tpu_custom_call" | custom-call | flops 1610612736 | tf_op jit(solution)/shard_map/near_grad/pallas_call | solution.py:52
  79.8 1.8 %near_grad.5 = (f32[512,512]{1,0:T(8,128)S(1)}, bf16[512,512]{1,0:T(8,128)(2,1)S(1)}, f32[256,512]{1,0:T(8,128)S(1)}) custom-call(s32[1]{0:T(128)} %bitcast.core_ref, f32[32,128]{1,0:T(8,128)S(1)} %join.7.mine_ref, f32[32,128]{1,0:T(8,128)S(1)} %collective-permute-done.18.other_ref, bf16[768,1536]{1,0:T(8,128)(2,1)S(1)} %get-tuple-element.122.refs_0_, ...), custom_call_target="tpu_custom_call" | custom-call | flops 1610612736 | tf_op jit(solution)/shard_map/near_grad/pallas_call | solution.py:52
  81.6 0.6 collective-permute-start.27
  82.2 1.8 %near_grad.4 = (f32[512,512]{1,0:T(8,128)S(1)}, bf16[512,512]{1,0:T(8,128)(2,1)S(1)}, f32[256,512]{1,0:T(8,128)S(1)}) custom-call(s32[1]{0:T(128)} %bitcast.core_ref, f32[32,128]{1,0:T(8,128)S(1)} %join.7.mine_ref, f32[32,128]{1,0:T(8,128)S(1)} %collective-permute-done.18.other_ref, bf16[768,1536]{1,0:T(8,128)(2,1)S(1)} %get-tuple-element.122.refs_0_, ...), custom_call_target="tpu_custom_call" | custom-call | flops 1610612736 | tf_op jit(solution)/shard_map/near_grad/pallas_call | solution.py:52
  84.4 1.6 %collective-permute-done.26.g1 = bf16[512,512]{1,0:T(8,128)(2,1)S(1)} collective-permute-done((bf16[512,512]{1,0:T(8,128)(2,1)S(1)}, bf16[512,512]{1,0:T(8,128)(2,1)S(1)}, u32[]{:S(2)}, u32[]{:S(2)}) %collective-permute-start.26) | collective-permute-done | bytes 524320 | tf_op jit(solution)/shard_map/ppermute | solution.py:47
  86.6 0.7 collective-permute-start.29
  87.3 1.1 %collective-permute-start.30 = (bf16[256,512]{1,0:T(8,128)(2,1)S(1)}, bf16[256,512]{1,0:T(8,128)(2,1)S(1)}, u32[]{:S(2)}, u32[]{:S(2)}) collective-permute-start(bf16[256,512]{1,0:T(8,128)(2,1)S(1)} %get-tuple-element.133), channel_id=1, source_target_pairs={{0,2},{1,7},{2,0},{3,5},{4,6},{5,3},{6,4},{7,1},{8,10},{9,15},{10,... | collective-permute-start | bytes 786440 | tf_op jit(solution)/shard_map/ppermute | solution.py:43
  88.4 4.7 %collective-permute-done.29.r1 = bf16[256,512]{1,0:T(8,128)(2,1)S(1)} collective-permute-done((bf16[256,512]{1,0:T(8,128)(2,1)S(1)}, bf16[256,512]{1,0:T(8,128)(2,1)S(1)}, u32[]{:S(2)}, u32[]{:S(2)}) %collective-permute-start.29) | collective-permute-done | bytes 262176 | tf_op jit(solution)/shard_map/ppermute | solution.py:43
  93.0 0.7 collective-permute-done.30.r2
  93.9 1.2 %collective-permute-start.31 = (bf16[144,512]{1,0:T(8,128)(2,1)S(1)}, bf16[144,512]{1,0:T(8,128)(2,1)S(1)}, u32[]{:S(2)}, u32[]{:S(2)}) collective-permute-start(bf16[144,512]{1,0:T(8,128)(2,1)S(1)} %get-tuple-element.135), channel_id=1, source_target_pairs={{0,2},{1,7},{2,0},{3,5},{4,6},{5,3},{6,4},{7,1},{8,10},{9,15},{10,... | collective-permute-start | bytes 442376 | tf_op jit(solution)/shard_map/ppermute | solution.py:43
  95.0 2.6 %collective-permute-start.32 = (bf16[128,512]{1,0:T(8,128)(2,1)S(1)}, bf16[128,512]{1,0:T(8,128)(2,1)S(1)}, u32[]{:S(2)}, u32[]{:S(2)}) collective-permute-start(bf16[128,512]{1,0:T(8,128)(2,1)S(1)} %get-tuple-element.136), channel_id=1, source_target_pairs={{0,8},{1,25},{2,10},{3,27},{4,12},{5,29},{6,14},{7,31},{8,0},{9,17... | collective-permute-start | bytes 393224 | tf_op jit(solution)/shard_map/ppermute | solution.py:43
  97.6 1.3 %collective-permute-start.33 = (bf16[128,512]{1,0:T(8,128)(2,1)S(1)}, bf16[128,512]{1,0:T(8,128)(2,1)S(1)}, u32[]{:S(2)}, u32[]{:S(2)}) collective-permute-start(bf16[128,512]{1,0:T(8,128)(2,1)S(1)} %get-tuple-element.137), channel_id=1, source_target_pairs={{0,32},{1,97},{2,34},{3,99},{4,36},{5,101},{6,38},{7,103},{8,40},{... | collective-permute-start | bytes 393224 | tf_op jit(solution)/shard_map/ppermute | solution.py:43
  98.9 1.2 %collective-permute-done.32.r1 = bf16[128,512]{1,0:T(8,128)(2,1)S(1)} collective-permute-done((bf16[128,512]{1,0:T(8,128)(2,1)S(1)}, bf16[128,512]{1,0:T(8,128)(2,1)S(1)}, u32[]{:S(2)}, u32[]{:S(2)}) %collective-permute-start.32) | collective-permute-done | bytes 131104 | tf_op jit(solution)/shard_map/ppermute | solution.py:43
  100.1 2.6 %collective-permute-done.33.r2 = bf16[128,512]{1,0:T(8,128)(2,1)S(1)} collective-permute-done((bf16[128,512]{1,0:T(8,128)(2,1)S(1)}, bf16[128,512]{1,0:T(8,128)(2,1)S(1)}, u32[]{:S(2)}, u32[]{:S(2)}) %collective-permute-start.33) | collective-permute-done | bytes 131104 | tf_op jit(solution)/shard_map/ppermute | solution.py:43
  102.9 2.3 %collective-permute-done.34.got_ref = f32[392,512]{1,0:T(8,128)S(1)} collective-permute-done((f32[392,512]{1,0:T(8,128)S(1)}, f32[392,512]{1,0:T(8,128)S(1)}, u32[]{:S(2)}, u32[]{:S(2)}) %collective-permute-start.34) | collective-permute-done | bytes 802848 | tf_op jit(solution)/shard_map/ppermute | solution.py:47
  105.2 1.0 finish.1
  (59 shorter events, 6.0 us)
Async XLA Ops:
  0.6 0.9 copy-start
  1.6 0.9 copy-start.2
  2.5 2.6 %collective-permute-start = (bf16[192,512]{1,0:T(8,128)(2,1)S(1)}, bf16[192,512]{1,0:T(8,128)(2,1)S(1)}, u32[]{:S(2)}, u32[]{:S(2)}) collective-permute-start(bf16[192,512]{1,0:T(8,128)(2,1)S(1)} %select.1), channel_id=1, source_target_pairs={{0,1},{1,0},{2,3},{3,2},{4,5},{5,4},{6,7},{7,6},{8,9},{9,8},{10,11... | collective-permute-start | bytes 589832 | tf_op jit(solution)/shard_map/ppermute | solution.py:47
  5.1 9.1 %collective-permute-start.1 = (bf16[128,512]{1,0:T(8,128)(2,1)S(1)}, bf16[128,512]{1,0:T(8,128)(2,1)S(1)}, u32[]{:S(2)}, u32[]{:S(2)}) collective-permute-start(bf16[128,512]{1,0:T(8,128)(2,1)S(1)} %get-tuple-element.75.refs_0_), channel_id=1, source_target_pairs={{0,2},{1,7},{2,0},{3,5},{4,6},{5,3},{6,4},{7,1},{8,10},{9,15},{10,... | collective-permute-start | bytes 393224 | tf_op jit(solution)/shard_map/ppermute | solution.py:43
  7.8 6.5 %collective-permute-start.2 = (bf16[128,512]{1,0:T(8,128)(2,1)S(1)}, bf16[128,512]{1,0:T(8,128)(2,1)S(1)}, u32[]{:S(2)}, u32[]{:S(2)}) collective-permute-start(bf16[128,512]{1,0:T(8,128)(2,1)S(1)} %get-tuple-element.76.refs_1_), channel_id=1, source_target_pairs={{0,8},{1,25},{2,10},{3,27},{4,12},{5,29},{6,14},{7,31},{8,0},{9,17... | collective-permute-start | bytes 393224 | tf_op jit(solution)/shard_map/ppermute | solution.py:43
  10.5 6.1 %collective-permute-start.3 = (bf16[128,512]{1,0:T(8,128)(2,1)S(1)}, bf16[128,512]{1,0:T(8,128)(2,1)S(1)}, u32[]{:S(2)}, u32[]{:S(2)}) collective-permute-start(bf16[128,512]{1,0:T(8,128)(2,1)S(1)} %get-tuple-element.77.refs_2_), channel_id=1, source_target_pairs={{0,32},{1,97},{2,34},{3,99},{4,36},{5,101},{6,38},{7,103},{8,40},{... | collective-permute-start | bytes 393224 | tf_op jit(solution)/shard_map/ppermute | solution.py:43
  16.7 6.5 %collective-permute-start.4 = (bf16[256,512]{1,0:T(8,128)(2,1)S(1)}, bf16[256,512]{1,0:T(8,128)(2,1)S(1)}, u32[]{:S(2)}, u32[]{:S(2)}) collective-permute-start(bf16[256,512]{1,0:T(8,128)(2,1)S(1)} %get-tuple-element.78.refs_0_), channel_id=1, source_target_pairs={{0,8},{1,25},{2,10},{3,27},{4,12},{5,29},{6,14},{7,31},{8,0},{9,17... | collective-permute-start | bytes 786440 | tf_op jit(solution)/shard_map/ppermute | solution.py:43
  16.8 6.5 %collective-permute-start.5 = (bf16[256,512]{1,0:T(8,128)(2,1)S(1)}, bf16[256,512]{1,0:T(8,128)(2,1)S(1)}, u32[]{:S(2)}, u32[]{:S(2)}) collective-permute-start(bf16[256,512]{1,0:T(8,128)(2,1)S(1)} %get-tuple-element.79.refs_1_), channel_id=1, source_target_pairs={{0,32},{1,97},{2,34},{3,99},{4,36},{5,101},{6,38},{7,103},{8,40},{... | collective-permute-start | bytes 786440 | tf_op jit(solution)/shard_map/ppermute | solution.py:43
  19.5 6.4 %collective-permute-start.6 = (bf16[256,512]{1,0:T(8,128)(2,1)S(1)}, bf16[256,512]{1,0:T(8,128)(2,1)S(1)}, u32[]{:S(2)}, u32[]{:S(2)}) collective-permute-start(bf16[256,512]{1,0:T(8,128)(2,1)S(1)} %get-tuple-element.80.refs_2_), channel_id=1, source_target_pairs={{0,2},{1,7},{2,0},{3,5},{4,6},{5,3},{6,4},{7,1},{8,10},{9,15},{10,... | collective-permute-start | bytes 786440 | tf_op jit(solution)/shard_map/ppermute | solution.py:43
  26.2 3.5 %collective-permute-start.8 = (bf16[1536,512]{1,0:T(8,128)(2,1)S(1)}, bf16[1536,512]{1,0:T(8,128)(2,1)S(1)}, u32[]{:S(2)}, u32[]{:S(2)}) collective-permute-start(bf16[1536,512]{1,0:T(8,128)(2,1)S(1)} %get-tuple-element.84), channel_id=1, source_target_pairs={{0,1},{1,0},{2,3},{3,2},{4,5},{5,4},{6,7},{7,6},{8,9},{9,8},{10,11... | collective-permute-start | bytes 4718600 | tf_op jit(solution)/shard_map/ppermute | solution.py:47
  26.3 9.3 %collective-permute-start.10 = (bf16[512,512]{1,0:T(8,128)(2,1)S(1)}, bf16[512,512]{1,0:T(8,128)(2,1)S(1)}, u32[]{:S(2)}, u32[]{:S(2)}) collective-permute-start(bf16[512,512]{1,0:T(8,128)(2,1)S(1)} %get-tuple-element.82.refs_0_), channel_id=1, source_target_pairs={{0,32},{1,97},{2,34},{3,99},{4,36},{5,101},{6,38},{7,103},{8,40},{... | collective-permute-start | bytes 1572872 | tf_op jit(solution)/shard_map/ppermute | solution.py:43
  26.4 9.5 %collective-permute-start.12 = (bf16[512,512]{1,0:T(8,128)(2,1)S(1)}, bf16[512,512]{1,0:T(8,128)(2,1)S(1)}, u32[]{:S(2)}, u32[]{:S(2)}) collective-permute-start(bf16[512,512]{1,0:T(8,128)(2,1)S(1)} %get-tuple-element.83.refs_1_), channel_id=1, source_target_pairs={{0,2},{1,7},{2,0},{3,5},{4,6},{5,3},{6,4},{7,1},{8,10},{9,15},{10,... | collective-permute-start | bytes 1572872 | tf_op jit(solution)/shard_map/ppermute | solution.py:43
  26.9 9.3 %collective-permute-start.7 = (bf16[512,512]{1,0:T(8,128)(2,1)S(1)}, bf16[512,512]{1,0:T(8,128)(2,1)S(1)}, u32[]{:S(2)}, u32[]{:S(2)}) collective-permute-start(bf16[512,512]{1,0:T(8,128)(2,1)S(1)} %get-tuple-element.81.refs_2_), channel_id=1, source_target_pairs={{0,8},{1,25},{2,10},{3,27},{4,12},{5,29},{6,14},{7,31},{8,0},{9,17... | collective-permute-start | bytes 1572872 | tf_op jit(solution)/shard_map/ppermute | solution.py:43
  35.6 1.9 %collective-permute-start.11 = (bf16[512,512]{1,0:T(8,128)(2,1)S(1)}, bf16[512,512]{1,0:T(8,128)(2,1)S(1)}, u32[]{:S(2)}, u32[]{:S(2)}) collective-permute-start(bf16[512,512]{1,0:T(8,128)(2,1)S(1)} %after.4.refs_0_), channel_id=1, source_target_pairs={{0,1},{1,0},{2,3},{3,2},{4,5},{5,4},{6,7},{7,6},{8,9},{9,8},{10,11... | collective-permute-start | bytes 1572872 | tf_op jit(solution)/shard_map/ppermute | solution.py:47
  35.9 4.0 %collective-permute-start.13 = (bf16[512,512]{1,0:T(8,128)(2,1)S(1)}, bf16[512,512]{1,0:T(8,128)(2,1)S(1)}, u32[]{:S(2)}, u32[]{:S(2)}) collective-permute-start(bf16[512,512]{1,0:T(8,128)(2,1)S(1)} %after.5.refs_0_), channel_id=1, source_target_pairs={{0,1},{1,0},{2,3},{3,2},{4,5},{5,4},{6,7},{7,6},{8,9},{9,8},{10,11... | collective-permute-start | bytes 1572872 | tf_op jit(solution)/shard_map/ppermute | solution.py:47
  36.2 6.8 %collective-permute-start.9 = (bf16[512,512]{1,0:T(8,128)(2,1)S(1)}, bf16[512,512]{1,0:T(8,128)(2,1)S(1)}, u32[]{:S(2)}, u32[]{:S(2)}) collective-permute-start(bf16[512,512]{1,0:T(8,128)(2,1)S(1)} %after.3.refs_0_), channel_id=1, source_target_pairs={{0,1},{1,0},{2,3},{3,2},{4,5},{5,4},{6,7},{7,6},{8,9},{9,8},{10,11... | collective-permute-start | bytes 1572872 | tf_op jit(solution)/shard_map/ppermute | solution.py:47
  40.0 3.1 %copy-start.1 = (bf16[192,512]{1,0:T(8,128)(2,1)S(1)}, bf16[192,512]{1,0:T(8,128)(2,1)}, u32[]{:S(2)}) copy-start(bf16[192,512]{1,0:T(8,128)(2,1)} %refs_10_.1) | copy-start | bytes 589828
  40.0 3.1 %copy-start.3 = (bf16[192,512]{1,0:T(8,128)(2,1)S(1)}, bf16[192,512]{1,0:T(8,128)(2,1)}, u32[]{:S(2)}) copy-start(bf16[192,512]{1,0:T(8,128)(2,1)} %refs_11_.1) | copy-start | bytes 589828
  47.1 1.3 %collective-permute-start.14 = (f32[32,128]{1,0:T(8,128)S(1)}, f32[32,128]{1,0:T(8,128)S(1)}, u32[]{:S(2)}, u32[]{:S(2)}) collective-permute-start(f32[32,128]{1,0:T(8,128)S(1)} %get-tuple-element.98), channel_id=1, source_target_pairs={{0,1},{1,0},{2,3},{3,2},{4,5},{5,4},{6,7},{7,6},{8,9},{9,8},{10,11... | collective-permute-start | bytes 49160 | tf_op jit(solution)/shard_map/ppermute | solution.py:47
  48.4 3.9 %collective-permute-start.15 = (f32[32,128]{1,0:T(8,128)S(1)}, f32[32,128]{1,0:T(8,128)S(1)}, u32[]{:S(2)}, u32[]{:S(2)}) collective-permute-start(f32[32,128]{1,0:T(8,128)S(1)} %join.4.mine_ref), channel_id=1, source_target_pairs={{0,2},{1,7},{2,0},{3,5},{4,6},{5,3},{6,4},{7,1},{8,10},{9,15},{10,... | collective-permute-start | bytes 49160 | tf_op jit(solution)/shard_map/ppermute | solution.py:43
  52.3 3.9 %collective-permute-start.16 = (f32[32,128]{1,0:T(8,128)S(1)}, f32[32,128]{1,0:T(8,128)S(1)}, u32[]{:S(2)}, u32[]{:S(2)}) collective-permute-start(f32[32,128]{1,0:T(8,128)S(1)} %join.5.mine_ref), channel_id=1, source_target_pairs={{0,8},{1,25},{2,10},{3,27},{4,12},{5,29},{6,14},{7,31},{8,0},{9,17... | collective-permute-start | bytes 49160 | tf_op jit(solution)/shard_map/ppermute | solution.py:43
  56.2 3.9 %collective-permute-start.17 = (f32[32,128]{1,0:T(8,128)S(1)}, f32[32,128]{1,0:T(8,128)S(1)}, u32[]{:S(2)}, u32[]{:S(2)}) collective-permute-start(f32[32,128]{1,0:T(8,128)S(1)} %join.6.mine_ref), channel_id=1, source_target_pairs={{0,32},{1,97},{2,34},{3,99},{4,36},{5,101},{6,38},{7,103},{8,40},{... | collective-permute-start | bytes 49160 | tf_op jit(solution)/shard_map/ppermute | solution.py:43
  60.1 1.3 %collective-permute-start.18 = (f32[32,128]{1,0:T(8,128)S(1)}, f32[32,128]{1,0:T(8,128)S(1)}, u32[]{:S(2)}, u32[]{:S(2)}) collective-permute-start(f32[32,128]{1,0:T(8,128)S(1)} %join.7.mine_ref), channel_id=1, source_target_pairs={{0,1},{1,0},{2,3},{3,2},{4,5},{5,4},{6,7},{7,6},{8,9},{9,8},{10,11... | collective-permute-start | bytes 49160 | tf_op jit(solution)/shard_map/ppermute | solution.py:47
  64.1 5.7 %collective-permute-start.21 = (bf16[512,512]{1,0:T(8,128)(2,1)S(1)}, bf16[512,512]{1,0:T(8,128)(2,1)S(1)}, u32[]{:S(2)}, u32[]{:S(2)}) collective-permute-start(bf16[512,512]{1,0:T(8,128)(2,1)S(1)} %get-tuple-element.120), channel_id=1, source_target_pairs={{0,1},{1,0},{2,3},{3,2},{4,5},{5,4},{6,7},{7,6},{8,9},{9,8},{10,11... | collective-permute-start | bytes 1572872 | tf_op jit(solution)/shard_map/ppermute | solution.py:47
  66.9 5.8 %collective-permute-start.20 = (bf16[512,512]{1,0:T(8,128)(2,1)S(1)}, bf16[512,512]{1,0:T(8,128)(2,1)S(1)}, u32[]{:S(2)}, u32[]{:S(2)}) collective-permute-start(bf16[512,512]{1,0:T(8,128)(2,1)S(1)} %get-tuple-element.118), channel_id=1, source_target_pairs={{0,1},{1,0},{2,3},{3,2},{4,5},{5,4},{6,7},{7,6},{8,9},{9,8},{10,11... | collective-permute-start | bytes 1572872 | tf_op jit(solution)/shard_map/ppermute | solution.py:47
  69.6 4.5 %collective-permute-start.19 = (bf16[512,512]{1,0:T(8,128)(2,1)S(1)}, bf16[512,512]{1,0:T(8,128)(2,1)S(1)}, u32[]{:S(2)}, u32[]{:S(2)}) collective-permute-start(bf16[512,512]{1,0:T(8,128)(2,1)S(1)} %get-tuple-element.115), channel_id=1, source_target_pairs={{0,1},{1,0},{2,3},{3,2},{4,5},{5,4},{6,7},{7,6},{8,9},{9,8},{10,11... | collective-permute-start | bytes 1572872 | tf_op jit(solution)/shard_map/ppermute | solution.py:47
  70.0 14.0 %collective-permute-start.24 = (bf16[512,512]{1,0:T(8,128)(2,1)S(1)}, bf16[512,512]{1,0:T(8,128)(2,1)S(1)}, u32[]{:S(2)}, u32[]{:S(2)}) collective-permute-start(bf16[512,512]{1,0:T(8,128)(2,1)S(1)} %far_message.5.refs_17_), channel_id=1, source_target_pairs={{0,8},{1,25},{2,10},{3,27},{4,12},{5,29},{6,14},{7,31},{8,0},{9,17... | collective-permute-start | bytes 1572872 | tf_op jit(solution)/shard_map/ppermute | solution.py:43
  72.8 11.3 %collective-permute-start.23 = (bf16[512,512]{1,0:T(8,128)(2,1)S(1)}, bf16[512,512]{1,0:T(8,128)(2,1)S(1)}, u32[]{:S(2)}, u32[]{:S(2)}) collective-permute-start(bf16[512,512]{1,0:T(8,128)(2,1)S(1)} %far_message.4.refs_16_), channel_id=1, source_target_pairs={{0,2},{1,7},{2,0},{3,5},{4,6},{5,3},{6,4},{7,1},{8,10},{9,15},{10,... | collective-permute-start | bytes 1572872 | tf_op jit(solution)/shard_map/ppermute | solution.py:43
  74.3 9.8 %collective-permute-start.22 = (bf16[528,512]{1,0:T(8,128)(2,1)S(1)}, bf16[528,512]{1,0:T(8,128)(2,1)S(1)}, u32[]{:S(2)}, u32[]{:S(2)}) collective-permute-start(bf16[528,512]{1,0:T(8,128)(2,1)S(1)} %far_message.3.refs_15_), channel_id=1, source_target_pairs={{0,32},{1,97},{2,34},{3,99},{4,36},{5,101},{6,38},{7,103},{8,40},{... | collective-permute-start | bytes 1622024 | tf_op jit(solution)/shard_map/ppermute | solution.py:43
  79.7 4.7 %collective-permute-start.25 = (bf16[512,512]{1,0:T(8,128)(2,1)S(1)}, bf16[512,512]{1,0:T(8,128)(2,1)S(1)}, u32[]{:S(2)}, u32[]{:S(2)}) collective-permute-start(bf16[512,512]{1,0:T(8,128)(2,1)S(1)} %get-tuple-element.126), channel_id=1, source_target_pairs={{0,1},{1,0},{2,3},{3,2},{4,5},{5,4},{6,7},{7,6},{8,9},{9,8},{10,11... | collective-permute-start | bytes 1572872 | tf_op jit(solution)/shard_map/ppermute | solution.py:47
  81.6 2.8 %collective-permute-start.27 = (bf16[512,512]{1,0:T(8,128)(2,1)S(1)}, bf16[512,512]{1,0:T(8,128)(2,1)S(1)}, u32[]{:S(2)}, u32[]{:S(2)}) collective-permute-start(bf16[512,512]{1,0:T(8,128)(2,1)S(1)} %get-tuple-element.128), channel_id=1, source_target_pairs={{0,1},{1,0},{2,3},{3,2},{4,5},{5,4},{6,7},{7,6},{8,9},{9,8},{10,11... | collective-permute-start | bytes 1572872 | tf_op jit(solution)/shard_map/ppermute | solution.py:47
  84.0 2.0 %collective-permute-start.26 = (bf16[512,512]{1,0:T(8,128)(2,1)S(1)}, bf16[512,512]{1,0:T(8,128)(2,1)S(1)}, u32[]{:S(2)}, u32[]{:S(2)}) collective-permute-start(bf16[512,512]{1,0:T(8,128)(2,1)S(1)} %get-tuple-element.127), channel_id=1, source_target_pairs={{0,1},{1,0},{2,3},{3,2},{4,5},{5,4},{6,7},{7,6},{8,9},{9,8},{10,11... | collective-permute-start | bytes 1572872 | tf_op jit(solution)/shard_map/ppermute | solution.py:47
  86.4 7.3 %collective-permute-start.28 = (bf16[272,512]{1,0:T(8,128)(2,1)S(1)}, bf16[272,512]{1,0:T(8,128)(2,1)S(1)}, u32[]{:S(2)}, u32[]{:S(2)}) collective-permute-start(bf16[272,512]{1,0:T(8,128)(2,1)S(1)} %get-tuple-element.131), channel_id=1, source_target_pairs={{0,8},{1,25},{2,10},{3,27},{4,12},{5,29},{6,14},{7,31},{8,0},{9,17... | collective-permute-start | bytes 835592 | tf_op jit(solution)/shard_map/ppermute | solution.py:43
  86.6 6.4 %collective-permute-start.29 = (bf16[256,512]{1,0:T(8,128)(2,1)S(1)}, bf16[256,512]{1,0:T(8,128)(2,1)S(1)}, u32[]{:S(2)}, u32[]{:S(2)}) collective-permute-start(bf16[256,512]{1,0:T(8,128)(2,1)S(1)} %get-tuple-element.132), channel_id=1, source_target_pairs={{0,32},{1,97},{2,34},{3,99},{4,36},{5,101},{6,38},{7,103},{8,40},{... | collective-permute-start | bytes 786440 | tf_op jit(solution)/shard_map/ppermute | solution.py:43
  87.3 6.4 %collective-permute-start.30 = (bf16[256,512]{1,0:T(8,128)(2,1)S(1)}, bf16[256,512]{1,0:T(8,128)(2,1)S(1)}, u32[]{:S(2)}, u32[]{:S(2)}) collective-permute-start(bf16[256,512]{1,0:T(8,128)(2,1)S(1)} %get-tuple-element.133), channel_id=1, source_target_pairs={{0,2},{1,7},{2,0},{3,5},{4,6},{5,3},{6,4},{7,1},{8,10},{9,15},{10,... | collective-permute-start | bytes 786440 | tf_op jit(solution)/shard_map/ppermute | solution.py:43
  93.9 8.8 %collective-permute-start.31 = (bf16[144,512]{1,0:T(8,128)(2,1)S(1)}, bf16[144,512]{1,0:T(8,128)(2,1)S(1)}, u32[]{:S(2)}, u32[]{:S(2)}) collective-permute-start(bf16[144,512]{1,0:T(8,128)(2,1)S(1)} %get-tuple-element.135), channel_id=1, source_target_pairs={{0,2},{1,7},{2,0},{3,5},{4,6},{5,3},{6,4},{7,1},{8,10},{9,15},{10,... | collective-permute-start | bytes 442376 | tf_op jit(solution)/shard_map/ppermute | solution.py:43
  95.0 5.0 %collective-permute-start.32 = (bf16[128,512]{1,0:T(8,128)(2,1)S(1)}, bf16[128,512]{1,0:T(8,128)(2,1)S(1)}, u32[]{:S(2)}, u32[]{:S(2)}) collective-permute-start(bf16[128,512]{1,0:T(8,128)(2,1)S(1)} %get-tuple-element.136), channel_id=1, source_target_pairs={{0,8},{1,25},{2,10},{3,27},{4,12},{5,29},{6,14},{7,31},{8,0},{9,17... | collective-permute-start | bytes 393224 | tf_op jit(solution)/shard_map/ppermute | solution.py:43
  97.6 5.0 %collective-permute-start.33 = (bf16[128,512]{1,0:T(8,128)(2,1)S(1)}, bf16[128,512]{1,0:T(8,128)(2,1)S(1)}, u32[]{:S(2)}, u32[]{:S(2)}) collective-permute-start(bf16[128,512]{1,0:T(8,128)(2,1)S(1)} %get-tuple-element.137), channel_id=1, source_target_pairs={{0,32},{1,97},{2,34},{3,99},{4,36},{5,101},{6,38},{7,103},{8,40},{... | collective-permute-start | bytes 393224 | tf_op jit(solution)/shard_map/ppermute | solution.py:43
  102.8 2.4 %collective-permute-start.34 = (f32[392,512]{1,0:T(8,128)S(1)}, f32[392,512]{1,0:T(8,128)S(1)}, u32[]{:S(2)}, u32[]{:S(2)}) collective-permute-start(f32[392,512]{1,0:T(8,128)S(1)} %get-tuple-element.143), channel_id=1, source_target_pairs={{0,1},{1,0},{2,3},{3,2},{4,5},{5,4},{6,7},{7,6},{8,9},{9,8},{10,11... | collective-permute-start | bytes 2408456 | tf_op jit(solution)/shard_map/ppermute | solution.py:47

commit v7 on v6

--- a/solution.py
+++ b/solution.py
@@ -270,15 +270,15 @@
     wide[stage][...] = coefficients(
         wide_in[...], row[:, ROW_AT[stage] : ROW_AT[stage + 1]], col[:, 0 : COL_AT[stage + 1]]
     ).astype(bf16)
+    here = slice(ROW_AT[stage], ROW_AT[stage + 1])
+    image = [times(wide[stage][:, COL_AT[p] : COL_AT[p + 1]], cols[p][...]) for p in range(stage + 1)]
+    image += [times(tall[p][here, :], cols[p][...]) for p in range(stage + 1, 4)]
+    image = total_of(image).astype(bf16)
     for start in range(0, ROW_AT[stage], 256):
         part = slice(start, start + 256)
         tall[stage][part, :] = coefficients(
             tall_in[part, :], row[:, part], col[:, COL_AT[stage] : COL_AT[stage + 1]]
         ).astype(bf16)
-    here = slice(ROW_AT[stage], ROW_AT[stage + 1])
-    image = [times(wide[stage][:, COL_AT[p] : COL_AT[p + 1]], cols[p][...]) for p in range(stage + 1)]
-    image += [times(tall[p][here, :], cols[p][...]) for p in range(stage + 1, 4)]
-    image = total_of(image).astype(bf16)
     here = slice(COL_AT[stage], COL_AT[stage + 1])
     text = [transposed_times(tall[stage][ROW_AT[p] : ROW_AT[p + 1], :], rows[p][...]) for p in range(stage)]
     text += [transposed_times(wide[p][:, here], rows[p][...]) for p in range(stage, 4)]
@@ -304,16 +304,22 @@
         row, col = tile_lse(first, mine_ref, other_ref)
         eye = lax.broadcasted_iota(jnp.int32, (128, 128), 0) == lax.broadcasted_iota(jnp.int32, (128, 128), 1)
         positive = jnp.where(jnp.logical_and(eye, first), 1.0, 0.0)
+    def image_grad():
+        part = slice(q * 256, q * 256 + 256)
+        terms = [times(block_ref[part, :], cols[0][...])]
+        return total_of(terms + [times(tall[p][part, :], cols[p][...]) for p in range(1, 4)])
+
+    if q == 0:
         for k in range(3):
             part = slice(k * 256, k * 256 + 256)
             coeffs = coefficients(source_ref[part, :], row[:, part], col[:, 0:1536])
             block_ref[part, :] = coeffs.astype(bf16)
             own = slice(k * 512, k * 512 + 128)
             block_ref[k * 256 : k * 256 + 128, own] = (coeffs[0:128, own] - positive).astype(bf16)
-    part = slice(q * 256, q * 256 + 256)
-    image = total_of(
-        [times(block_ref[part, :], cols[0][...])] + [times(tall[p][part, :], cols[p][...]) for p in range(1, 4)]
-    )
+            if k == 0:
+                image = image_grad()
+    else:
+        image = image_grad()
     here = slice(q * 512, q * 512 + 512)
     text = total_of(
         [transposed_times(block_ref[:, here], rows[0][...])]
@@ -402,16 +408,12 @@
     loss_out[...] = (keep_ref[384:385, 0:1] + got_ref[384:385, 0:1]) * (0.5 / count)
 
 
-def select_kernel(core_ref, image_ref, text_ref, out_ref):
-    out_ref[...] = jnp.where(core_ref[0] == 0, text_ref[...], image_ref[...])
-
-
-def pair_kernel(core_ref, image_ref, text_ref, got_ref, *out_refs):
+def pair_kernel(core_ref, image_ref, text_ref, image_got, text_got, *out_refs):
     first = core_ref[0] == 0
     for q, out in enumerate(out_refs):
         rows = slice(q * 64, q * 64 + 64)
-        out[0:64, :] = jnp.where(first, image_ref[rows, :], got_ref[rows, :])
-        out[64:128, :] = jnp.where(first, got_ref[rows, :], text_ref[rows, :])
+        out[0:64, :] = jnp.where(first, image_ref[rows, :], text_got[rows, :])
+        out[64:128, :] = jnp.where(first, image_got[rows, :], text_ref[rows, :])
 
 
 def per_device(image_emb, text_emb):
@@ -419,9 +421,9 @@
     pair_rows, width = image_emb.shape
     count = pair_rows * 128
 
-    swapped = core_swap(call(select_kernel, "select", [core_id, image_emb, text_emb], [shape(pair_rows, width, dtype=bf16)], limit=4)[0])
+    got = [core_swap(image_emb), core_swap(text_emb)]
     near = call(
-        pair_kernel, "pair", [core_id, image_emb, text_emb, swapped], [shape(128, width, dtype=bf16)] * 3, limit=4
+        pair_kernel, "pair", [core_id, image_emb, text_emb, *got], [shape(128, width, dtype=bf16)] * 3, limit=4
     )
     for step in range(2):
         got = [flip_permute(near[q], q + step) for q in range(3)]

time: 106 us -> 107 us (level)
    ppermute x14 -> x15, waiting for transfers between devices: 7.88 us -> 8.45 us  [core_swap(): return lax.ppermute(x, 'c', SWAP)]
    ppermute x14 -> x15, starting transfers between devices: 4.75 us -> 5.16 us  [core_swap(): return lax.ppermute(x, 'c', SWAP)]
    pallas_call x26 -> x25, Pallas kernels: 29.1 us -> 29.1 us  [call(): pl.pallas_call(kernel, in_specs=in_specs, out_specs=[VMEM] * len(outs), o...]
  transfers between devices with their start and end apart: 35 -> 36, of which waited for: 19 -> 20; matrix products, arithmetic and copies ran while one was open for 0% -> 0% of each run, Pallas kernels for 19% -> 19%
where the time goes in v7:
time: 107 us
  starting transfers between devices  39.3 us (37%)
  waiting for transfers between devices  35.7 us (33%)
  Pallas kernels  29.1 us (27%)
  local copies, waits for them, and re-layouts  1.87 us (2%)
    ppermute x21, starting transfers between devices, flip_permute(): return lax.ppermute(x, AXES, ROLE_PAIRS[dim % 3])  34.1 us
    pallas_call x25, Pallas kernels, call(): pl.pallas_call(kernel, in_specs=in_specs, out_specs=[VMEM] * len(outs), o...  29.1 us
    ppermute x21, waiting for transfers between devices, flip_permute(): return lax.ppermute(x, AXES, ROLE_PAIRS[dim % 3])  27.2 us
    ppermute x15, waiting for transfers between devices, core_swap(): return lax.ppermute(x, 'c', SWAP)  8.45 us
    ppermute x15, starting transfers between devices, core_swap(): return lax.ppermute(x, 'c', SWAP)  5.16 us
  transfers between devices with their start and end apart: 36, of which 20 were waited for; matrix products, arithmetic and copies ran while one was open for 0% of the time, Pallas kernels for 19%

profile of v7, /device:TPU:1, one launch (start us, length us, event | category | flops | bytes accessed | tf_op | source)
XLA Modules:
  0.0 106.8 jit_solution(7466175179889334137)
XLA Ops:
  0.6 1.5 %collective-permute-start = (bf16[192,512]{1,0:T(8,128)(2,1)}, bf16[192,512]{1,0:T(8,128)(2,1)S(1)}, u32[]{:S(2)}, u32[]{:S(2)}) collective-permute-start(bf16[192,512]{1,0:T(8,128)(2,1)} %refs_10_.1), channel_id=1, source_target_pairs={{0,1},{1,0},{2,3},{3,2},{4,5},{5,4},{6,7},{7,6},{8,9},{9,8},{10,11... | collective-permute-start | bytes 589832 | tf_op jit(solution)/shard_map/ppermute | solution.py:47
  2.2 1.2 %collective-permute-done.image_got = bf16[192,512]{1,0:T(8,128)(2,1)S(1)} collective-permute-done((bf16[192,512]{1,0:T(8,128)(2,1)}, bf16[192,512]{1,0:T(8,128)(2,1)S(1)}, u32[]{:S(2)}, u32[]{:S(2)}) %collective-permute-start) | collective-permute-done | bytes 196640 | tf_op jit(solution)/shard_map/ppermute | solution.py:47
  3.8 0.9 copy-done
  4.7 0.9 copy-done.2
  5.7 2.6 %collective-permute-start.2 = (bf16[128,512]{1,0:T(8,128)(2,1)S(1)}, bf16[128,512]{1,0:T(8,128)(2,1)S(1)}, u32[]{:S(2)}, u32[]{:S(2)}) collective-permute-start(bf16[128,512]{1,0:T(8,128)(2,1)S(1)} %get-tuple-element.75.refs_0_), channel_id=1, source_target_pairs={{0,2},{1,7},{2,0},{3,5},{4,6},{5,3},{6,4},{7,1},{8,10},{9,15},{10,... | collective-permute-start | bytes 393224 | tf_op jit(solution)/shard_map/ppermute | solution.py:43
  8.3 2.7 %collective-permute-start.3 = (bf16[128,512]{1,0:T(8,128)(2,1)S(1)}, bf16[128,512]{1,0:T(8,128)(2,1)S(1)}, u32[]{:S(2)}, u32[]{:S(2)}) collective-permute-start(bf16[128,512]{1,0:T(8,128)(2,1)S(1)} %get-tuple-element.76.refs_1_), channel_id=1, source_target_pairs={{0,8},{1,25},{2,10},{3,27},{4,12},{5,29},{6,14},{7,31},{8,0},{9,17... | collective-permute-start | bytes 393224 | tf_op jit(solution)/shard_map/ppermute | solution.py:43
  11.1 3.8 %collective-permute-start.4 = (bf16[128,512]{1,0:T(8,128)(2,1)S(1)}, bf16[128,512]{1,0:T(8,128)(2,1)S(1)}, u32[]{:S(2)}, u32[]{:S(2)}) collective-permute-start(bf16[128,512]{1,0:T(8,128)(2,1)S(1)} %get-tuple-element.77.refs_2_), channel_id=1, source_target_pairs={{0,32},{1,97},{2,34},{3,99},{4,36},{5,101},{6,38},{7,103},{8,40},{... | collective-permute-start | bytes 393224 | tf_op jit(solution)/shard_map/ppermute | solution.py:43
  14.8 2.3 %collective-permute-done.4.refs_5_ = bf16[128,512]{1,0:T(8,128)(2,1)S(1)} collective-permute-done((bf16[128,512]{1,0:T(8,128)(2,1)S(1)}, bf16[128,512]{1,0:T(8,128)(2,1)S(1)}, u32[]{:S(2)}, u32[]{:S(2)}) %collective-permute-start.4) | collective-permute-done | bytes 131104 | tf_op jit(solution)/shard_map/ppermute | solution.py:43
  17.3 2.8 %collective-permute-start.6 = (bf16[256,512]{1,0:T(8,128)(2,1)S(1)}, bf16[256,512]{1,0:T(8,128)(2,1)S(1)}, u32[]{:S(2)}, u32[]{:S(2)}) collective-permute-start(bf16[256,512]{1,0:T(8,128)(2,1)S(1)} %get-tuple-element.79.refs_1_), channel_id=1, source_target_pairs={{0,32},{1,97},{2,34},{3,99},{4,36},{5,101},{6,38},{7,103},{8,40},{... | collective-permute-start | bytes 786440 | tf_op jit(solution)/shard_map/ppermute | solution.py:43
  20.3 3.5 %collective-permute-done.5.refs_3_ = bf16[256,512]{1,0:T(8,128)(2,1)S(1)} collective-permute-done((bf16[256,512]{1,0:T(8,128)(2,1)S(1)}, bf16[256,512]{1,0:T(8,128)(2,1)S(1)}, u32[]{:S(2)}, u32[]{:S(2)}) %collective-permute-start.5) | collective-permute-done | bytes 262176 | tf_op jit(solution)/shard_map/ppermute | solution.py:43
  23.8 2.7 %collective-permute-done.7.refs_5_ = bf16[256,512]{1,0:T(8,128)(2,1)S(1)} collective-permute-done((bf16[256,512]{1,0:T(8,128)(2,1)S(1)}, bf16[256,512]{1,0:T(8,128)(2,1)S(1)}, u32[]{:S(2)}, u32[]{:S(2)}) %collective-permute-start.7) | collective-permute-done | bytes 262176 | tf_op jit(solution)/shard_map/ppermute | solution.py:43
  27.4 2.7 %collective-permute-start.8 = (bf16[512,512]{1,0:T(8,128)(2,1)S(1)}, bf16[512,512]{1,0:T(8,128)(2,1)S(1)}, u32[]{:S(2)}, u32[]{:S(2)}) collective-permute-start(bf16[512,512]{1,0:T(8,128)(2,1)S(1)} %get-tuple-element.81.refs_2_), channel_id=1, source_target_pairs={{0,8},{1,25},{2,10},{3,27},{4,12},{5,29},{6,14},{7,31},{8,0},{9,17... | collective-permute-start | bytes 1572872 | tf_op jit(solution)/shard_map/ppermute | solution.py:43
  30.2 2.8 %forward.4 = (bf16[768,512]{1,0:T(8,128)(2,1)S(1)}, bf16[1536,512]{1,0:T(8,128)(2,1)S(1)}, f32[768,1536]{1,0:T(8,128)S(1)}, f32[6,128]{1,0:T(8,128)S(1)}, f32[12,128]{1,0:T(8,128)S(1)}) custom-call(s32[1]{0:T(128)} %bitcast.core_ref, bf16[512,512]{1,0:T(8,128)(2,1)S(1)} %get-tuple-element.82.refs_0_, bf16[512,512]{1,0:T(8,128)(2,1)S(1)} %get-tuple-element.83.refs_1_, ...), custom_call_target="tpu_custom_call" | custom-call | flops 1207959552 | tf_op jit(solution)/shard_map/forward/pallas_call | solution.py:52
  33.0 3.1 %collective-permute-done.11.value_ref = bf16[512,512]{1,0:T(8,128)(2,1)S(1)} collective-permute-done((bf16[512,512]{1,0:T(8,128)(2,1)S(1)}, bf16[512,512]{1,0:T(8,128)(2,1)S(1)}, u32[]{:S(2)}, u32[]{:S(2)}) %collective-permute-start.11) | collective-permute-done | bytes 524320 | tf_op jit(solution)/shard_map/ppermute | solution.py:43
  37.0 1.0 collective-permute-done.12.refs_1_
  38.0 2.5 %forward.5 = (bf16[256,512]{1,0:T(8,128)(2,1)S(1)}, bf16[512,512]{1,0:T(8,128)(2,1)S(1)}, f32[256,2048]{1,0:T(8,128)S(1)}, f32[768,512]{1,0:T(8,128)S(1)}, f32[8,128]{1,0:T(8,128)S(1)}, /*index=5*/f32[16,128]{1,0:T(8,128)S(1)}) custom-call(s32[1]{0:T(128)} %bitcast.core_ref, bf16[512,512]{1,0:T(8,128)(2,1)S(1)} %after.4.refs_0_, ...), custom_call_target="tpu_custom_call" | custom-call | flops 939524096 | tf_op jit(solution)/shard_map/forward/pallas_call | solution.py:52
  40.6 3.2 %forward.6 = (bf16[256,512]{1,0:T(8,128)(2,1)S(1)}, bf16[512,512]{1,0:T(8,128)(2,1)S(1)}, f32[256,2560]{1,0:T(8,128)S(1)}, f32[1024,512]{1,0:T(8,128)S(1)}, f32[...) custom-call(s32[1]{0:T(128)} %bitcast.core_ref, bf16[512,512]{1,0:T(8,128)(2,1)S(1)} %after.5.refs_0_, ...), custom_call_target="tpu_custom_call" | custom-call | flops 1207959552 | tf_op jit(solution)/shard_map/forward/pallas_call | solution.py:52
  43.8 3.9 %forward.7 = (bf16[256,512]{1,0:T(8,128)(2,1)S(1)}, bf16[512,512]{1,0:T(8,128)(2,1)S(1)}, f32[256,3072]{1,0:T(8,128)S(1)}, f32[1280,512]{1,0:T(8,128)S(1)}, f32[...) custom-call(s32[1]{0:T(128)} %bitcast.core_ref, bf16[512,512]{1,0:T(8,128)(2,1)S(1)} %after.3.refs_0_, ...), custom_call_target="tpu_custom_call" | custom-call | flops 1476395008 | tf_op jit(solution)/shard_map/forward/pallas_call | solution.py:52
  48.1 0.8 collective-permute-done.15.got_ref
  49.0 1.1 %collective-permute-start.16 = (f32[32,128]{1,0:T(8,128)S(1)}, f32[32,128]{1,0:T(8,128)S(1)}, u32[]{:S(2)}, u32[]{:S(2)}) collective-permute-start(f32[32,128]{1,0:T(8,128)S(1)} %join.4.mine_ref), channel_id=1, source_target_pairs={{0,2},{1,7},{2,0},{3,5},{4,6},{5,3},{6,4},{7,1},{8,10},{9,15},{10,... | collective-permute-start | bytes 49160 | tf_op jit(solution)/shard_map/ppermute | solution.py:43
  50.1 2.8 %collective-permute-done.16.got_ref = f32[32,128]{1,0:T(8,128)S(1)} collective-permute-done((f32[32,128]{1,0:T(8,128)S(1)}, f32[32,128]{1,0:T(8,128)S(1)}, u32[]{:S(2)}, u32[]{:S(2)}) %collective-permute-start.16) | collective-permute-done | bytes 16416 | tf_op jit(solution)/shard_map/ppermute | solution.py:43
  52.9 2.7 %collective-permute-start.17 = (f32[32,128]{1,0:T(8,128)S(1)}, f32[32,128]{1,0:T(8,128)S(1)}, u32[]{:S(2)}, u32[]{:S(2)}) collective-permute-start(f32[32,128]{1,0:T(8,128)S(1)} %join.5.mine_ref), channel_id=1, source_target_pairs={{0,8},{1,25},{2,10},{3,27},{4,12},{5,29},{6,14},{7,31},{8,0},{9,17... | collective-permute-start | bytes 49160 | tf_op jit(solution)/shard_map/ppermute | solution.py:43
  55.6 1.2 %collective-permute-done.17.got_ref = f32[32,128]{1,0:T(8,128)S(1)} collective-permute-done((f32[32,128]{1,0:T(8,128)S(1)}, f32[32,128]{1,0:T(8,128)S(1)}, u32[]{:S(2)}, u32[]{:S(2)}) %collective-permute-start.17) | collective-permute-done | bytes 16416 | tf_op jit(solution)/shard_map/ppermute | solution.py:43
  56.8 1.4 %collective-permute-start.18 = (f32[32,128]{1,0:T(8,128)S(1)}, f32[32,128]{1,0:T(8,128)S(1)}, u32[]{:S(2)}, u32[]{:S(2)}) collective-permute-start(f32[32,128]{1,0:T(8,128)S(1)} %join.6.mine_ref), channel_id=1, source_target_pairs={{0,32},{1,97},{2,34},{3,99},{4,36},{5,101},{6,38},{7,103},{8,40},{... | collective-permute-start | bytes 49160 | tf_op jit(solution)/shard_map/ppermute | solution.py:43
  58.2 2.5 %collective-permute-done.18.got_ref = f32[32,128]{1,0:T(8,128)S(1)} collective-permute-done((f32[32,128]{1,0:T(8,128)S(1)}, f32[32,128]{1,0:T(8,128)S(1)}, u32[]{:S(2)}, u32[]{:S(2)}) %collective-permute-start.18) | collective-permute-done | bytes 16416 | tf_op jit(solution)/shard_map/ppermute | solution.py:43
  60.9 1.0 collective-permute-done.19.other_ref
  62.0 2.7 %far_grad.3 = (bf16[256,3072]{1,0:T(8,128)(2,1)S(1)}, bf16[1280,512]{1,0:T(8,128)(2,1)S(1)}, bf16[512,512]{1,0:T(8,128)(2,1)S(1)}, bf16[512,512]{1,0:T(8,128)(2,1)S(1)}, f32[8,128]{1,0:T(8,128)S(1)}) custom-call(s32[1]{0:T(128)} %bitcast.core_ref, f32[32,128]{1,0:T(8,128)S(1)} %join.7.mine_ref, f32[32,128]{1,0:T(8,128)S(1)} %collective-permute-done.19.other_ref, ...), custom_call_target="tpu_custom_call" | custom-call | flops 1610612736 | tf_op jit(solution)/shard_map/far_grad/pallas_call | solution.py:52
  64.9 2.5 %far_grad.4 = (bf16[256,2560]{1,0:T(8,128)(2,1)S(1)}, bf16[1024,512]{1,0:T(8,128)(2,1)S(1)}, bf16[512,512]{1,0:T(8,128)(2,1)S(1)}, bf16[512,512]{1,0:T(8,128)(2,1)S(1)}) custom-call(s32[1]{0:T(128)} %bitcast.core_ref, f32[32,128]{1,0:T(8,128)S(1)} %join.7.mine_ref, f32[32,128]{1,0:T(8,128)S(1)} %collective-permute-done.19.other_ref, ...), custom_call_target="tpu_custom_call" | custom-call | flops 1610612736 | tf_op jit(solution)/shard_map/far_grad/pallas_call | solution.py:52
  67.4 0.6 collective-permute-start.21
  68.1 2.3 %far_grad.5 = (bf16[256,2048]{1,0:T(8,128)(2,1)S(1)}, bf16[768,512]{1,0:T(8,128)(2,1)S(1)}, bf16[512,512]{1,0:T(8,128)(2,1)S(1)}, bf16[512,512]{1,0:T(8,128)(2,1)S(1)}) custom-call(s32[1]{0:T(128)} %bitcast.core_ref, f32[32,128]{1,0:T(8,128)S(1)} %join.7.mine_ref, f32[32,128]{1,0:T(8,128)S(1)} %collective-permute-done.19.other_ref, ...), custom_call_target="tpu_custom_call" | custom-call | flops 1610612736 | tf_op jit(solution)/shard_map/far_grad/pallas_call | solution.py:52
  70.8 2.7 %collective-permute-start.25 = (bf16[512,512]{1,0:T(8,128)(2,1)S(1)}, bf16[512,512]{1,0:T(8,128)(2,1)S(1)}, u32[]{:S(2)}, u32[]{:S(2)}) collective-permute-start(bf16[512,512]{1,0:T(8,128)(2,1)S(1)} %far_message.5.refs_17_), channel_id=1, source_target_pairs={{0,8},{1,25},{2,10},{3,27},{4,12},{5,29},{6,14},{7,31},{8,0},{9,17... | collective-permute-start | bytes 1572872 | tf_op jit(solution)/shard_map/ppermute | solution.py:43
  73.6 1.1 %collective-permute-start.24 = (bf16[512,512]{1,0:T(8,128)(2,1)S(1)}, bf16[512,512]{1,0:T(8,128)(2,1)S(1)}, u32[]{:S(2)}, u32[]{:S(2)}) collective-permute-start(bf16[512,512]{1,0:T(8,128)(2,1)S(1)} %far_message.4.refs_16_), channel_id=1, source_target_pairs={{0,2},{1,7},{2,0},{3,5},{4,6},{5,3},{6,4},{7,1},{8,10},{9,15},{10,... | collective-permute-start | bytes 1572872 | tf_op jit(solution)/shard_map/ppermute | solution.py:43
  74.9 2.7 %collective-permute-start.23 = (bf16[528,512]{1,0:T(8,128)(2,1)S(1)}, bf16[528,512]{1,0:T(8,128)(2,1)S(1)}, u32[]{:S(2)}, u32[]{:S(2)}) collective-permute-start(bf16[528,512]{1,0:T(8,128)(2,1)S(1)} %far_message.3.refs_15_), channel_id=1, source_target_pairs={{0,32},{1,97},{2,34},{3,99},{4,36},{5,101},{6,38},{7,103},{8,40},{... | collective-permute-start | bytes 1622024 | tf_op jit(solution)/shard_map/ppermute | solution.py:43
  77.5 2.8 %near_grad.3 = (f32[512,512]{1,0:T(8,128)S(1)}, bf16[512,512]{1,0:T(8,128)(2,1)S(1)}, f32[256,512]{1,0:T(8,128)S(1)}, bf16[768,1536]{1,0:T(8,128)(2,1)S(1)}) custom-call(s32[1]{0:T(128)} %bitcast.core_ref, f32[32,128]{1,0:T(8,128)S(1)} %join.7.mine_ref, f32[32,128]{1,0:T(8,128)S(1)} %collective-permute-done.19.other_ref, ...), custom_call_target="tpu_custom_call" | custom-call | flops 1610612736 | tf_op jit(solution)/shard_map/near_grad/pallas_call | solution.py:52
  80.4 1.8 %near_grad.5 = (f32[512,512]{1,0:T(8,128)S(1)}, bf16[512,512]{1,0:T(8,128)(2,1)S(1)}, f32[256,512]{1,0:T(8,128)S(1)}) custom-call(s32[1]{0:T(128)} %bitcast.core_ref, f32[32,128]{1,0:T(8,128)S(1)} %join.7.mine_ref, f32[32,128]{1,0:T(8,128)S(1)} %collective-permute-done.19.other_ref, bf16[768,1536]{1,0:T(8,128)(2,1)S(1)} %get-tuple-element.122.refs_0_, ...), custom_call_target="tpu_custom_call" | custom-call | flops 1610612736 | tf_op jit(solution)/shard_map/near_grad/pallas_call | solution.py:52
  82.8 1.8 %near_grad.4 = (f32[512,512]{1,0:T(8,128)S(1)}, bf16[512,512]{1,0:T(8,128)(2,1)S(1)}, f32[256,512]{1,0:T(8,128)S(1)}) custom-call(s32[1]{0:T(128)} %bitcast.core_ref, f32[32,128]{1,0:T(8,128)S(1)} %join.7.mine_ref, f32[32,128]{1,0:T(8,128)S(1)} %collective-permute-done.19.other_ref, bf16[768,1536]{1,0:T(8,128)(2,1)S(1)} %get-tuple-element.122.refs_0_, ...), custom_call_target="tpu_custom_call" | custom-call | flops 1610612736 | tf_op jit(solution)/shard_map/near_grad/pallas_call | solution.py:52
  85.0 1.6 %collective-permute-done.27.g1 = bf16[512,512]{1,0:T(8,128)(2,1)S(1)} collective-permute-done((bf16[512,512]{1,0:T(8,128)(2,1)S(1)}, bf16[512,512]{1,0:T(8,128)(2,1)S(1)}, u32[]{:S(2)}, u32[]{:S(2)}) %collective-permute-start.27) | collective-permute-done | bytes 524320 | tf_op jit(solution)/shard_map/ppermute | solution.py:47
  87.2 0.7 collective-permute-start.30
  87.9 1.2 %collective-permute-start.31 = (bf16[256,512]{1,0:T(8,128)(2,1)S(1)}, bf16[256,512]{1,0:T(8,128)(2,1)S(1)}, u32[]{:S(2)}, u32[]{:S(2)}) collective-permute-start(bf16[256,512]{1,0:T(8,128)(2,1)S(1)} %get-tuple-element.133), channel_id=1, source_target_pairs={{0,2},{1,7},{2,0},{3,5},{4,6},{5,3},{6,4},{7,1},{8,10},{9,15},{10,... | collective-permute-start | bytes 786440 | tf_op jit(solution)/shard_map/ppermute | solution.py:43
  89.0 4.6 %collective-permute-done.30.r1 = bf16[256,512]{1,0:T(8,128)(2,1)S(1)} collective-permute-done((bf16[256,512]{1,0:T(8,128)(2,1)S(1)}, bf16[256,512]{1,0:T(8,128)(2,1)S(1)}, u32[]{:S(2)}, u32[]{:S(2)}) %collective-permute-start.30) | collective-permute-done | bytes 262176 | tf_op jit(solution)/shard_map/ppermute | solution.py:43
  93.6 0.7 collective-permute-done.31.r2
  94.4 1.3 %collective-permute-start.32 = (bf16[144,512]{1,0:T(8,128)(2,1)S(1)}, bf16[144,512]{1,0:T(8,128)(2,1)S(1)}, u32[]{:S(2)}, u32[]{:S(2)}) collective-permute-start(bf16[144,512]{1,0:T(8,128)(2,1)S(1)} %get-tuple-element.135), channel_id=1, source_target_pairs={{0,2},{1,7},{2,0},{3,5},{4,6},{5,3},{6,4},{7,1},{8,10},{9,15},{10,... | collective-permute-start | bytes 442376 | tf_op jit(solution)/shard_map/ppermute | solution.py:43
  95.7 2.5 %collective-permute-start.33 = (bf16[128,512]{1,0:T(8,128)(2,1)S(1)}, bf16[128,512]{1,0:T(8,128)(2,1)S(1)}, u32[]{:S(2)}, u32[]{:S(2)}) collective-permute-start(bf16[128,512]{1,0:T(8,128)(2,1)S(1)} %get-tuple-element.136), channel_id=1, source_target_pairs={{0,8},{1,25},{2,10},{3,27},{4,12},{5,29},{6,14},{7,31},{8,0},{9,17... | collective-permute-start | bytes 393224 | tf_op jit(solution)/shard_map/ppermute | solution.py:43
  98.2 1.3 %collective-permute-start.34 = (bf16[128,512]{1,0:T(8,128)(2,1)S(1)}, bf16[128,512]{1,0:T(8,128)(2,1)S(1)}, u32[]{:S(2)}, u32[]{:S(2)}) collective-permute-start(bf16[128,512]{1,0:T(8,128)(2,1)S(1)} %get-tuple-element.137), channel_id=1, source_target_pairs={{0,32},{1,97},{2,34},{3,99},{4,36},{5,101},{6,38},{7,103},{8,40},{... | collective-permute-start | bytes 393224 | tf_op jit(solution)/shard_map/ppermute | solution.py:43
  99.5 1.3 %collective-permute-done.33.r1 = bf16[128,512]{1,0:T(8,128)(2,1)S(1)} collective-permute-done((bf16[128,512]{1,0:T(8,128)(2,1)S(1)}, bf16[128,512]{1,0:T(8,128)(2,1)S(1)}, u32[]{:S(2)}, u32[]{:S(2)}) %collective-permute-start.33) | collective-permute-done | bytes 131104 | tf_op jit(solution)/shard_map/ppermute | solution.py:43
  100.7 2.5 %collective-permute-done.34.r2 = bf16[128,512]{1,0:T(8,128)(2,1)S(1)} collective-permute-done((bf16[128,512]{1,0:T(8,128)(2,1)S(1)}, bf16[128,512]{1,0:T(8,128)(2,1)S(1)}, u32[]{:S(2)}, u32[]{:S(2)}) %collective-permute-start.34) | collective-permute-done | bytes 131104 | tf_op jit(solution)/shard_map/ppermute | solution.py:43
  103.5 2.3 %collective-permute-done.35.got_ref = f32[392,512]{1,0:T(8,128)S(1)} collective-permute-done((f32[392,512]{1,0:T(8,128)S(1)}, f32[392,512]{1,0:T(8,128)S(1)}, u32[]{:S(2)}, u32[]{:S(2)}) %collective-permute-start.35) | collective-permute-done | bytes 802848 | tf_op jit(solution)/shard_map/ppermute | solution.py:47
  105.8 1.0 finish.1
  (60 shorter events, 6.6 us)
Async XLA Ops:
  0.6 2.8 %collective-permute-start = (bf16[192,512]{1,0:T(8,128)(2,1)}, bf16[192,512]{1,0:T(8,128)(2,1)S(1)}, u32[]{:S(2)}, u32[]{:S(2)}) collective-permute-start(bf16[192,512]{1,0:T(8,128)(2,1)} %refs_10_.1), channel_id=1, source_target_pairs={{0,1},{1,0},{2,3},{3,2},{4,5},{5,4},{6,7},{7,6},{8,9},{9,8},{10,11... | collective-permute-start | bytes 589832 | tf_op jit(solution)/shard_map/ppermute | solution.py:47
  2.1 1.7 %collective-permute-start.1 = (bf16[192,512]{1,0:T(8,128)(2,1)}, bf16[192,512]{1,0:T(8,128)(2,1)S(1)}, u32[]{:S(2)}, u32[]{:S(2)}) collective-permute-start(bf16[192,512]{1,0:T(8,128)(2,1)} %refs_11_.1), channel_id=1, source_target_pairs={{0,1},{1,0},{2,3},{3,2},{4,5},{5,4},{6,7},{7,6},{8,9},{9,8},{10,11... | collective-permute-start | bytes 589832 | tf_op jit(solution)/shard_map/ppermute | solution.py:47
  3.8 0.9 copy-start
  4.7 0.9 copy-start.2
  5.7 9.1 %collective-permute-start.2 = (bf16[128,512]{1,0:T(8,128)(2,1)S(1)}, bf16[128,512]{1,0:T(8,128)(2,1)S(1)}, u32[]{:S(2)}, u32[]{:S(2)}) collective-permute-start(bf16[128,512]{1,0:T(8,128)(2,1)S(1)} %get-tuple-element.75.refs_0_), channel_id=1, source_target_pairs={{0,2},{1,7},{2,0},{3,5},{4,6},{5,3},{6,4},{7,1},{8,10},{9,15},{10,... | collective-permute-start | bytes 393224 | tf_op jit(solution)/shard_map/ppermute | solution.py:43
  8.3 6.5 %collective-permute-start.3 = (bf16[128,512]{1,0:T(8,128)(2,1)S(1)}, bf16[128,512]{1,0:T(8,128)(2,1)S(1)}, u32[]{:S(2)}, u32[]{:S(2)}) collective-permute-start(bf16[128,512]{1,0:T(8,128)(2,1)S(1)} %get-tuple-element.76.refs_1_), channel_id=1, source_target_pairs={{0,8},{1,25},{2,10},{3,27},{4,12},{5,29},{6,14},{7,31},{8,0},{9,17... | collective-permute-start | bytes 393224 | tf_op jit(solution)/shard_map/ppermute | solution.py:43
  11.1 6.1 %collective-permute-start.4 = (bf16[128,512]{1,0:T(8,128)(2,1)S(1)}, bf16[128,512]{1,0:T(8,128)(2,1)S(1)}, u32[]{:S(2)}, u32[]{:S(2)}) collective-permute-start(bf16[128,512]{1,0:T(8,128)(2,1)S(1)} %get-tuple-element.77.refs_2_), channel_id=1, source_target_pairs={{0,32},{1,97},{2,34},{3,99},{4,36},{5,101},{6,38},{7,103},{8,40},{... | collective-permute-start | bytes 393224 | tf_op jit(solution)/shard_map/ppermute | solution.py:43
  17.2 6.5 %collective-permute-start.5 = (bf16[256,512]{1,0:T(8,128)(2,1)S(1)}, bf16[256,512]{1,0:T(8,128)(2,1)S(1)}, u32[]{:S(2)}, u32[]{:S(2)}) collective-permute-start(bf16[256,512]{1,0:T(8,128)(2,1)S(1)} %get-tuple-element.78.refs_0_), channel_id=1, source_target_pairs={{0,8},{1,25},{2,10},{3,27},{4,12},{5,29},{6,14},{7,31},{8,0},{9,17... | collective-permute-start | bytes 786440 | tf_op jit(solution)/shard_map/ppermute | solution.py:43
  17.3 6.5 %collective-permute-start.6 = (bf16[256,512]{1,0:T(8,128)(2,1)S(1)}, bf16[256,512]{1,0:T(8,128)(2,1)S(1)}, u32[]{:S(2)}, u32[]{:S(2)}) collective-permute-start(bf16[256,512]{1,0:T(8,128)(2,1)S(1)} %get-tuple-element.79.refs_1_), channel_id=1, source_target_pairs={{0,32},{1,97},{2,34},{3,99},{4,36},{5,101},{6,38},{7,103},{8,40},{... | collective-permute-start | bytes 786440 | tf_op jit(solution)/shard_map/ppermute | solution.py:43
  20.1 6.4 %collective-permute-start.7 = (bf16[256,512]{1,0:T(8,128)(2,1)S(1)}, bf16[256,512]{1,0:T(8,128)(2,1)S(1)}, u32[]{:S(2)}, u32[]{:S(2)}) collective-permute-start(bf16[256,512]{1,0:T(8,128)(2,1)S(1)} %get-tuple-element.80.refs_2_), channel_id=1, source_target_pairs={{0,2},{1,7},{2,0},{3,5},{4,6},{5,3},{6,4},{7,1},{8,10},{9,15},{10,... | collective-permute-start | bytes 786440 | tf_op jit(solution)/shard_map/ppermute | solution.py:43
  26.7 3.5 %collective-permute-start.9 = (bf16[1536,512]{1,0:T(8,128)(2,1)S(1)}, bf16[1536,512]{1,0:T(8,128)(2,1)S(1)}, u32[]{:S(2)}, u32[]{:S(2)}) collective-permute-start(bf16[1536,512]{1,0:T(8,128)(2,1)S(1)} %get-tuple-element.84), channel_id=1, source_target_pairs={{0,1},{1,0},{2,3},{3,2},{4,5},{5,4},{6,7},{7,6},{8,9},{9,8},{10,11... | collective-permute-start | bytes 4718600 | tf_op jit(solution)/shard_map/ppermute | solution.py:47
  26.8 9.3 %collective-permute-start.11 = (bf16[512,512]{1,0:T(8,128)(2,1)S(1)}, bf16[512,512]{1,0:T(8,128)(2,1)S(1)}, u32[]{:S(2)}, u32[]{:S(2)}) collective-permute-start(bf16[512,512]{1,0:T(8,128)(2,1)S(1)} %get-tuple-element.82.refs_0_), channel_id=1, source_target_pairs={{0,32},{1,97},{2,34},{3,99},{4,36},{5,101},{6,38},{7,103},{8,40},{... | collective-permute-start | bytes 1572872 | tf_op jit(solution)/shard_map/ppermute | solution.py:43
  27.0 9.5 %collective-permute-start.13 = (bf16[512,512]{1,0:T(8,128)(2,1)S(1)}, bf16[512,512]{1,0:T(8,128)(2,1)S(1)}, u32[]{:S(2)}, u32[]{:S(2)}) collective-permute-start(bf16[512,512]{1,0:T(8,128)(2,1)S(1)} %get-tuple-element.83.refs_1_), channel_id=1, source_target_pairs={{0,2},{1,7},{2,0},{3,5},{4,6},{5,3},{6,4},{7,1},{8,10},{9,15},{10,... | collective-permute-start | bytes 1572872 | tf_op jit(solution)/shard_map/ppermute | solution.py:43
  27.4 9.3 %collective-permute-start.8 = (bf16[512,512]{1,0:T(8,128)(2,1)S(1)}, bf16[512,512]{1,0:T(8,128)(2,1)S(1)}, u32[]{:S(2)}, u32[]{:S(2)}) collective-permute-start(bf16[512,512]{1,0:T(8,128)(2,1)S(1)} %get-tuple-element.81.refs_2_), channel_id=1, source_target_pairs={{0,8},{1,25},{2,10},{3,27},{4,12},{5,29},{6,14},{7,31},{8,0},{9,17... | collective-permute-start | bytes 1572872 | tf_op jit(solution)/shard_map/ppermute | solution.py:43
  36.1 1.9 %collective-permute-start.12 = (bf16[512,512]{1,0:T(8,128)(2,1)S(1)}, bf16[512,512]{1,0:T(8,128)(2,1)S(1)}, u32[]{:S(2)}, u32[]{:S(2)}) collective-permute-start(bf16[512,512]{1,0:T(8,128)(2,1)S(1)} %after.4.refs_0_), channel_id=1, source_target_pairs={{0,1},{1,0},{2,3},{3,2},{4,5},{5,4},{6,7},{7,6},{8,9},{9,8},{10,11... | collective-permute-start | bytes 1572872 | tf_op jit(solution)/shard_map/ppermute | solution.py:47
  36.5 4.0 %collective-permute-start.14 = (bf16[512,512]{1,0:T(8,128)(2,1)S(1)}, bf16[512,512]{1,0:T(8,128)(2,1)S(1)}, u32[]{:S(2)}, u32[]{:S(2)}) collective-permute-start(bf16[512,512]{1,0:T(8,128)(2,1)S(1)} %after.5.refs_0_), channel_id=1, source_target_pairs={{0,1},{1,0},{2,3},{3,2},{4,5},{5,4},{6,7},{7,6},{8,9},{9,8},{10,11... | collective-permute-start | bytes 1572872 | tf_op jit(solution)/shard_map/ppermute | solution.py:47
  36.7 7.1 %collective-permute-start.10 = (bf16[512,512]{1,0:T(8,128)(2,1)S(1)}, bf16[512,512]{1,0:T(8,128)(2,1)S(1)}, u32[]{:S(2)}, u32[]{:S(2)}) collective-permute-start(bf16[512,512]{1,0:T(8,128)(2,1)S(1)} %after.3.refs_0_), channel_id=1, source_target_pairs={{0,1},{1,0},{2,3},{3,2},{4,5},{5,4},{6,7},{7,6},{8,9},{9,8},{10,11... | collective-permute-start | bytes 1572872 | tf_op jit(solution)/shard_map/ppermute | solution.py:47
  40.5 3.2 %copy-start.1 = (bf16[192,512]{1,0:T(8,128)(2,1)S(1)}, bf16[192,512]{1,0:T(8,128)(2,1)}, u32[]{:S(2)}) copy-start(bf16[192,512]{1,0:T(8,128)(2,1)} %refs_10_.1) | copy-start | bytes 589828
  40.5 3.2 %copy-start.3 = (bf16[192,512]{1,0:T(8,128)(2,1)S(1)}, bf16[192,512]{1,0:T(8,128)(2,1)}, u32[]{:S(2)}) copy-start(bf16[192,512]{1,0:T(8,128)(2,1)} %refs_11_.1) | copy-start | bytes 589828
  47.7 1.3 %collective-permute-start.15 = (f32[32,128]{1,0:T(8,128)S(1)}, f32[32,128]{1,0:T(8,128)S(1)}, u32[]{:S(2)}, u32[]{:S(2)}) collective-permute-start(f32[32,128]{1,0:T(8,128)S(1)} %get-tuple-element.98), channel_id=1, source_target_pairs={{0,1},{1,0},{2,3},{3,2},{4,5},{5,4},{6,7},{7,6},{8,9},{9,8},{10,11... | collective-permute-start | bytes 49160 | tf_op jit(solution)/shard_map/ppermute | solution.py:47
  49.0 3.9 %collective-permute-start.16 = (f32[32,128]{1,0:T(8,128)S(1)}, f32[32,128]{1,0:T(8,128)S(1)}, u32[]{:S(2)}, u32[]{:S(2)}) collective-permute-start(f32[32,128]{1,0:T(8,128)S(1)} %join.4.mine_ref), channel_id=1, source_target_pairs={{0,2},{1,7},{2,0},{3,5},{4,6},{5,3},{6,4},{7,1},{8,10},{9,15},{10,... | collective-permute-start | bytes 49160 | tf_op jit(solution)/shard_map/ppermute | solution.py:43
  52.9 3.9 %collective-permute-start.17 = (f32[32,128]{1,0:T(8,128)S(1)}, f32[32,128]{1,0:T(8,128)S(1)}, u32[]{:S(2)}, u32[]{:S(2)}) collective-permute-start(f32[32,128]{1,0:T(8,128)S(1)} %join.5.mine_ref), channel_id=1, source_target_pairs={{0,8},{1,25},{2,10},{3,27},{4,12},{5,29},{6,14},{7,31},{8,0},{9,17... | collective-permute-start | bytes 49160 | tf_op jit(solution)/shard_map/ppermute | solution.py:43
  56.8 3.9 %collective-permute-start.18 = (f32[32,128]{1,0:T(8,128)S(1)}, f32[32,128]{1,0:T(8,128)S(1)}, u32[]{:S(2)}, u32[]{:S(2)}) collective-permute-start(f32[32,128]{1,0:T(8,128)S(1)} %join.6.mine_ref), channel_id=1, source_target_pairs={{0,32},{1,97},{2,34},{3,99},{4,36},{5,101},{6,38},{7,103},{8,40},{... | collective-permute-start | bytes 49160 | tf_op jit(solution)/shard_map/ppermute | solution.py:43
  60.7 1.3 %collective-permute-start.19 = (f32[32,128]{1,0:T(8,128)S(1)}, f32[32,128]{1,0:T(8,128)S(1)}, u32[]{:S(2)}, u32[]{:S(2)}) collective-permute-start(f32[32,128]{1,0:T(8,128)S(1)} %join.7.mine_ref), channel_id=1, source_target_pairs={{0,1},{1,0},{2,3},{3,2},{4,5},{5,4},{6,7},{7,6},{8,9},{9,8},{10,11... | collective-permute-start | bytes 49160 | tf_op jit(solution)/shard_map/ppermute | solution.py:47
  64.7 5.9 %collective-permute-start.22 = (bf16[512,512]{1,0:T(8,128)(2,1)S(1)}, bf16[512,512]{1,0:T(8,128)(2,1)S(1)}, u32[]{:S(2)}, u32[]{:S(2)}) collective-permute-start(bf16[512,512]{1,0:T(8,128)(2,1)S(1)} %get-tuple-element.120), channel_id=1, source_target_pairs={{0,1},{1,0},{2,3},{3,2},{4,5},{5,4},{6,7},{7,6},{8,9},{9,8},{10,11... | collective-permute-start | bytes 1572872 | tf_op jit(solution)/shard_map/ppermute | solution.py:47
  67.4 6.0 %collective-permute-start.21 = (bf16[512,512]{1,0:T(8,128)(2,1)S(1)}, bf16[512,512]{1,0:T(8,128)(2,1)S(1)}, u32[]{:S(2)}, u32[]{:S(2)}) collective-permute-start(bf16[512,512]{1,0:T(8,128)(2,1)S(1)} %get-tuple-element.118), channel_id=1, source_target_pairs={{0,1},{1,0},{2,3},{3,2},{4,5},{5,4},{6,7},{7,6},{8,9},{9,8},{10,11... | collective-permute-start | bytes 1572872 | tf_op jit(solution)/shard_map/ppermute | solution.py:47
  70.4 4.3 %collective-permute-start.20 = (bf16[512,512]{1,0:T(8,128)(2,1)S(1)}, bf16[512,512]{1,0:T(8,128)(2,1)S(1)}, u32[]{:S(2)}, u32[]{:S(2)}) collective-permute-start(bf16[512,512]{1,0:T(8,128)(2,1)S(1)} %get-tuple-element.115), channel_id=1, source_target_pairs={{0,1},{1,0},{2,3},{3,2},{4,5},{5,4},{6,7},{7,6},{8,9},{9,8},{10,11... | collective-permute-start | bytes 1572872 | tf_op jit(solution)/shard_map/ppermute | solution.py:47
  70.8 13.8 %collective-permute-start.25 = (bf16[512,512]{1,0:T(8,128)(2,1)S(1)}, bf16[512,512]{1,0:T(8,128)(2,1)S(1)}, u32[]{:S(2)}, u32[]{:S(2)}) collective-permute-start(bf16[512,512]{1,0:T(8,128)(2,1)S(1)} %far_message.5.refs_17_), channel_id=1, source_target_pairs={{0,8},{1,25},{2,10},{3,27},{4,12},{5,29},{6,14},{7,31},{8,0},{9,17... | collective-permute-start | bytes 1572872 | tf_op jit(solution)/shard_map/ppermute | solution.py:43
  73.6 11.1 %collective-permute-start.24 = (bf16[512,512]{1,0:T(8,128)(2,1)S(1)}, bf16[512,512]{1,0:T(8,128)(2,1)S(1)}, u32[]{:S(2)}, u32[]{:S(2)}) collective-permute-start(bf16[512,512]{1,0:T(8,128)(2,1)S(1)} %far_message.4.refs_16_), channel_id=1, source_target_pairs={{0,2},{1,7},{2,0},{3,5},{4,6},{5,3},{6,4},{7,1},{8,10},{9,15},{10,... | collective-permute-start | bytes 1572872 | tf_op jit(solution)/shard_map/ppermute | solution.py:43
  74.9 9.8 %collective-permute-start.23 = (bf16[528,512]{1,0:T(8,128)(2,1)S(1)}, bf16[528,512]{1,0:T(8,128)(2,1)S(1)}, u32[]{:S(2)}, u32[]{:S(2)}) collective-permute-start(bf16[528,512]{1,0:T(8,128)(2,1)S(1)} %far_message.3.refs_15_), channel_id=1, source_target_pairs={{0,32},{1,97},{2,34},{3,99},{4,36},{5,101},{6,38},{7,103},{8,40},{... | collective-permute-start | bytes 1622024 | tf_op jit(solution)/shard_map/ppermute | solution.py:43
  80.3 4.7 %collective-permute-start.26 = (bf16[512,512]{1,0:T(8,128)(2,1)S(1)}, bf16[512,512]{1,0:T(8,128)(2,1)S(1)}, u32[]{:S(2)}, u32[]{:S(2)}) collective-permute-start(bf16[512,512]{1,0:T(8,128)(2,1)S(1)} %get-tuple-element.126), channel_id=1, source_target_pairs={{0,1},{1,0},{2,3},{3,2},{4,5},{5,4},{6,7},{7,6},{8,9},{9,8},{10,11... | collective-permute-start | bytes 1572872 | tf_op jit(solution)/shard_map/ppermute | solution.py:47
  82.2 2.8 %collective-permute-start.28 = (bf16[512,512]{1,0:T(8,128)(2,1)S(1)}, bf16[512,512]{1,0:T(8,128)(2,1)S(1)}, u32[]{:S(2)}, u32[]{:S(2)}) collective-permute-start(bf16[512,512]{1,0:T(8,128)(2,1)S(1)} %get-tuple-element.128), channel_id=1, source_target_pairs={{0,1},{1,0},{2,3},{3,2},{4,5},{5,4},{6,7},{7,6},{8,9},{9,8},{10,11... | collective-permute-start | bytes 1572872 | tf_op jit(solution)/shard_map/ppermute | solution.py:47
  84.6 2.0 %collective-permute-start.27 = (bf16[512,512]{1,0:T(8,128)(2,1)S(1)}, bf16[512,512]{1,0:T(8,128)(2,1)S(1)}, u32[]{:S(2)}, u32[]{:S(2)}) collective-permute-start(bf16[512,512]{1,0:T(8,128)(2,1)S(1)} %get-tuple-element.127), channel_id=1, source_target_pairs={{0,1},{1,0},{2,3},{3,2},{4,5},{5,4},{6,7},{7,6},{8,9},{9,8},{10,11... | collective-permute-start | bytes 1572872 | tf_op jit(solution)/shard_map/ppermute | solution.py:47
  87.0 7.3 %collective-permute-start.29 = (bf16[272,512]{1,0:T(8,128)(2,1)S(1)}, bf16[272,512]{1,0:T(8,128)(2,1)S(1)}, u32[]{:S(2)}, u32[]{:S(2)}) collective-permute-start(bf16[272,512]{1,0:T(8,128)(2,1)S(1)} %get-tuple-element.131), channel_id=1, source_target_pairs={{0,8},{1,25},{2,10},{3,27},{4,12},{5,29},{6,14},{7,31},{8,0},{9,17... | collective-permute-start | bytes 835592 | tf_op jit(solution)/shard_map/ppermute | solution.py:43
  87.2 6.4 %collective-permute-start.30 = (bf16[256,512]{1,0:T(8,128)(2,1)S(1)}, bf16[256,512]{1,0:T(8,128)(2,1)S(1)}, u32[]{:S(2)}, u32[]{:S(2)}) collective-permute-start(bf16[256,512]{1,0:T(8,128)(2,1)S(1)} %get-tuple-element.132), channel_id=1, source_target_pairs={{0,32},{1,97},{2,34},{3,99},{4,36},{5,101},{6,38},{7,103},{8,40},{... | collective-permute-start | bytes 786440 | tf_op jit(solution)/shard_map/ppermute | solution.py:43
  87.9 6.4 %collective-permute-start.31 = (bf16[256,512]{1,0:T(8,128)(2,1)S(1)}, bf16[256,512]{1,0:T(8,128)(2,1)S(1)}, u32[]{:S(2)}, u32[]{:S(2)}) collective-permute-start(bf16[256,512]{1,0:T(8,128)(2,1)S(1)} %get-tuple-element.133), channel_id=1, source_target_pairs={{0,2},{1,7},{2,0},{3,5},{4,6},{5,3},{6,4},{7,1},{8,10},{9,15},{10,... | collective-permute-start | bytes 786440 | tf_op jit(solution)/shard_map/ppermute | solution.py:43
  94.4 8.8 %collective-permute-start.32 = (bf16[144,512]{1,0:T(8,128)(2,1)S(1)}, bf16[144,512]{1,0:T(8,128)(2,1)S(1)}, u32[]{:S(2)}, u32[]{:S(2)}) collective-permute-start(bf16[144,512]{1,0:T(8,128)(2,1)S(1)} %get-tuple-element.135), channel_id=1, source_target_pairs={{0,2},{1,7},{2,0},{3,5},{4,6},{5,3},{6,4},{7,1},{8,10},{9,15},{10,... | collective-permute-start | bytes 442376 | tf_op jit(solution)/shard_map/ppermute | solution.py:43
  95.7 5.0 %collective-permute-start.33 = (bf16[128,512]{1,0:T(8,128)(2,1)S(1)}, bf16[128,512]{1,0:T(8,128)(2,1)S(1)}, u32[]{:S(2)}, u32[]{:S(2)}) collective-permute-start(bf16[128,512]{1,0:T(8,128)(2,1)S(1)} %get-tuple-element.136), channel_id=1, source_target_pairs={{0,8},{1,25},{2,10},{3,27},{4,12},{5,29},{6,14},{7,31},{8,0},{9,17... | collective-permute-start | bytes 393224 | tf_op jit(solution)/shard_map/ppermute | solution.py:43
  98.2 5.0 %collective-permute-start.34 = (bf16[128,512]{1,0:T(8,128)(2,1)S(1)}, bf16[128,512]{1,0:T(8,128)(2,1)S(1)}, u32[]{:S(2)}, u32[]{:S(2)}) collective-permute-start(bf16[128,512]{1,0:T(8,128)(2,1)S(1)} %get-tuple-element.137), channel_id=1, source_target_pairs={{0,32},{1,97},{2,34},{3,99},{4,36},{5,101},{6,38},{7,103},{8,40},{... | collective-permute-start | bytes 393224 | tf_op jit(solution)/shard_map/ppermute | solution.py:43
  103.4 2.4 %collective-permute-start.35 = (f32[392,512]{1,0:T(8,128)S(1)}, f32[392,512]{1,0:T(8,128)S(1)}, u32[]{:S(2)}, u32[]{:S(2)}) collective-permute-start(f32[392,512]{1,0:T(8,128)S(1)} %get-tuple-element.143), channel_id=1, source_target_pairs={{0,1},{1,0},{2,3},{3,2},{4,5},{5,4},{6,7},{7,6},{8,9},{9,8},{10,11... | collective-permute-start | bytes 2408456 | tf_op jit(solution)/shard_map/ppermute | solution.py:47

commit v8 on v7

--- a/solution.py
+++ b/solution.py
@@ -69,8 +69,6 @@
     return jax.ShapeDtypeStruct(dims, dtype)
 
 
-ROW_AT = (0, 768, 1024, 1280, 1536)
-COL_AT = (0, 1536, 2048, 2560, 3072)
 CONTRACT_LAST = (((1,), (1,)), ((), ()))
 CONTRACT_FIRST = (((0,), (0,)), ((), ()))
 
@@ -104,68 +102,62 @@
     return jnp.concatenate(lane_blocks(state[0] + jnp.log2(state[1])), 0)
 
 
-def forward_kernel(stage, core_ref, *refs):
-    refs = list(refs)
-    take = lambda n: [refs.pop(0) for _ in range(n)]
-    n = 3 if stage == 0 else 1
-    mine = take(n)
-    if stage == 0:
-        packed_ref = take(1)[0]
-        swapped = [packed_ref.at[k * 512 : k * 512 + 512] for k in range(3)]
-    else:
-        swapped = take(1)
-    rows, cols = take(stage), take(stage)
-    row_old, col_old = take(2) if stage else (None, None)
-    image_ref, text_ref = take(2) if stage == 3 else (None, None)
-    rows_ref, cols_ref, wide_ref = take(3)
-    tall_ref = take(1)[0] if stage else None
-    first = core_ref[0] == 0
-
+def product(a, b):
+    return lax.dot_general(a, b, CONTRACT_LAST, preferred_element_type=f32) * (logit_scale * log2e)
+
+
+def place(first, mine, swapped, rows_ref, cols_ref):
     @pl.when(first)
     def _():
-        for i in range(n):
-            rows_ref[i * 256 : i * 256 + 256, :] = mine[i][0:256, :]
-            cols_ref[i * 512 : i * 512 + 512, :] = swapped[i][...]
+        for q in range(3):
+            rows_ref[q * 256 : q * 256 + 256, :] = mine[q][0:256, :]
+            cols_ref[q * 512 : q * 512 + 512, :] = swapped[q][...]
 
     @pl.when(jnp.logical_not(first))
     def _():
-        for i in range(n):
-            rows_ref[i * 256 : i * 256 + 256, :] = swapped[i][256:512, :]
-            cols_ref[i * 512 : i * 512 + 512, :] = mine[i][...]
-
-    def product(a, b):
-        return lax.dot_general(a, b, CONTRACT_LAST, preferred_element_type=f32) * (logit_scale * log2e)
-
-    cols = cols + [cols_ref]
-    new_rows = []
-    state = None
-    for block in range(n):
-        part = slice(block * 256, block * 256 + 256)
-        for p in range(stage + 1):
-            wide_ref[part, COL_AT[p] : COL_AT[p + 1]] = product(rows_ref[part, :], cols[p][...])
-        logits = wide_ref[part, :]
-        new_rows.append(row_stat(logits))
+        for q in range(3):
+            rows_ref[q * 256 : q * 256 + 256, :] = swapped[q][256:512, :]
+            cols_ref[q * 512 : q * 512 + 512, :] = mine[q][...]
+
+
+def near_kernel(core_ref, m0, m1, m2, packed_ref, rows_ref, cols_ref, logit_ref, row_out, col_out):
+    swapped = [packed_ref.at[q * 512 : q * 512 + 512] for q in range(3)]
+    place(core_ref[0] == 0, (m0, m1, m2), swapped, rows_ref, cols_ref)
+    rows, state = [], None
+    for q in range(3):
+        part = slice(q * 256, q * 256 + 256)
+        logit_ref[part, :] = product(rows_ref[part, :], cols_ref[...])
+        logits = logit_ref[part, :]
+        rows.append(row_stat(logits))
         state = column_step(logits, state)
-    col = column_stat(state)
-    row = jnp.concatenate(new_rows, 0)
-    if stage:
-        state = None
-        old = []
-        for p in range(stage):
-            for start in range(0, rows[p].shape[0], 256):
-                part = slice(ROW_AT[p] + start, ROW_AT[p] + start + 256)
-                tall_ref[part, :] = product(rows[p][start : start + 256, :], cols_ref[...])
-                logits = tall_ref[part, :]
-                old.append(row_stat(logits))
-                state = column_step(logits, state)
-        row = jnp.concatenate([log_add(row_old[...], jnp.concatenate(old, 0)), row], 0)
-        col = log_add(col, jnp.concatenate([col_old[...], column_stat(state)], 0))
-    if stage < 3:
-        row_out, col_out = take(2)
-        row_out[...] = row
-        col_out[...] = col
-        return
-    send_ref, keep_ref = take(2)
+    row_out[...] = jnp.concatenate(rows, 0)
+    col_out[...] = column_stat(state)
+
+
+def far_kernel(core_ref, *refs):
+    mine, swapped = refs[0:3], refs[3:6]
+    near_rows, near_cols, row_old, col_old, image_ref, text_ref = refs[6:12]
+    rows_ref, cols_ref, *wide_refs = refs[12:17]
+    tall_ref, send_ref, keep_ref = refs[17:20]
+    first = core_ref[0] == 0
+    place(first, mine, swapped, rows_ref, cols_ref)
+    new, state = [], None
+    for q, wide in enumerate(wide_refs):
+        part = slice(q * 256, q * 256 + 256)
+        wide[:, 0:1536] = product(rows_ref[part, :], near_cols[...])
+        wide[:, 1536:3072] = product(rows_ref[part, :], cols_ref[...])
+        logits = wide[...]
+        new.append(row_stat(logits))
+        state = column_step(logits, state)
+    old, tall_state = [], None
+    for q in range(3):
+        part = slice(q * 256, q * 256 + 256)
+        tall_ref[part, :] = product(near_rows[part, :], cols_ref[...])
+        logits = tall_ref[part, :]
+        old.append(row_stat(logits))
+        tall_state = column_step(logits, tall_state)
+    row = jnp.concatenate([log_add(row_old[...], jnp.concatenate(old, 0))] + new, 0)
+    col = log_add(column_stat(state), jnp.concatenate([col_old[...], column_stat(tall_state)], 0))
     positive = logit_scale * jnp.sum(image_ref[...].astype(f32) * text_ref[...].astype(f32))
     extra = jnp.full((8, 128), positive, f32)
     blank = jnp.full((2, 128), lowest, f32)
@@ -253,79 +245,59 @@
     return lax.dot_general(a, b, CONTRACT_FIRST, preferred_element_type=f32)
 
 
-def far_grad_kernel(stage, core_ref, mine_ref, other_ref, *refs):
-    refs = list(refs)
-    take = lambda n: [refs.pop(0) for _ in range(n)]
-    wide_in, tall_in = take(2)
-    rows, cols = take(4), take(4)
-    wide = [None] * (stage + 1) + take(3 - stage)
-    tall = [None] * (stage + 1) + take(3 - stage)
-    wide[stage], tall[stage] = take(2)
-    kept_ref, send_ref = take(2)
+def coeff_kernel(core_ref, mine_ref, other_ref, *refs):
+    near_ref, tall_ref, *wide_refs = refs[0:5]
+    near_cols, far_cols = refs[5:7]
+    coeff_ref, *grad_refs = refs[7:14]
+    own_ref, loss_ref = refs[14:16]
     first = core_ref[0] == 0
     row, col = tile_lse(first, mine_ref, other_ref)
-    if stage == 3:
-        loss_ref = take(1)[0]
-        loss_ref[...] = jnp.sum(other_ref[0:24, :]) * ln2 - jnp.where(first, 0.0, 2.0) * other_ref[24:32, :]
-    wide[stage][...] = coefficients(
-        wide_in[...], row[:, ROW_AT[stage] : ROW_AT[stage + 1]], col[:, 0 : COL_AT[stage + 1]]
-    ).astype(bf16)
-    here = slice(ROW_AT[stage], ROW_AT[stage + 1])
-    image = [times(wide[stage][:, COL_AT[p] : COL_AT[p + 1]], cols[p][...]) for p in range(stage + 1)]
-    image += [times(tall[p][here, :], cols[p][...]) for p in range(stage + 1, 4)]
-    image = total_of(image).astype(bf16)
-    for start in range(0, ROW_AT[stage], 256):
-        part = slice(start, start + 256)
-        tall[stage][part, :] = coefficients(
-            tall_in[part, :], row[:, part], col[:, COL_AT[stage] : COL_AT[stage + 1]]
-        ).astype(bf16)
-    here = slice(COL_AT[stage], COL_AT[stage + 1])
-    text = [transposed_times(tall[stage][ROW_AT[p] : ROW_AT[p + 1], :], rows[p][...]) for p in range(stage)]
-    text += [transposed_times(wide[p][:, here], rows[p][...]) for p in range(stage, 4)]
-    text = total_of(text).astype(bf16)
+    loss_ref[...] = jnp.sum(other_ref[0:24, :]) * ln2 - jnp.where(first, 0.0, 2.0) * other_ref[24:32, :]
+    eye = lax.broadcasted_iota(jnp.int32, (128, 128), 0) == lax.broadcasted_iota(jnp.int32, (128, 128), 1)
+    positive = jnp.where(jnp.logical_and(eye, first), 1.0, 0.0)
+    for g in range(6):
+        part = slice(g * 256, g * 256 + 256)
+        if g < 3:
+            coeffs = coefficients(near_ref[part, :], row[:, part], col[:, 0:1536])
+            coeff_ref[part, 0:1536] = coeffs.astype(bf16)
+            own = slice(g * 512, g * 512 + 128)
+            coeff_ref[g * 256 : g * 256 + 128, own] = (coeffs[0:128, own] - positive).astype(bf16)
+            coeff_ref[part, 1536:3072] = coefficients(tall_ref[part, :], row[:, part], col[:, 1536:3072]).astype(bf16)
+        else:
+            coeff_ref[part, :] = coefficients(wide_refs[g - 3][...], row[:, part], col).astype(bf16)
+        grad = total_of(
+            [times(coeff_ref[part, 0:1536], near_cols[...]), times(coeff_ref[part, 1536:3072], far_cols[...])]
+        )
+        grad_refs[g][...] = grad.astype(bf16)
+        if g < 3:
+            own_ref[g * 128 : g * 128 + 128, :] = grad[0:128, :]
+
+
+def text_grad(coeff_ref, near_rows, far_rows, start):
+    here = slice(start, start + 512)
+    return total_of(
+        [
+            transposed_times(coeff_ref[0:768, here], near_rows[...]),
+            transposed_times(coeff_ref[768:1536, here], far_rows[...]),
+        ]
+    )
+
+
+def far_text_kernel(q, core_ref, coeff_ref, near_rows, far_rows, image_ref, kept_ref, send_ref):
+    first = core_ref[0] == 0
+    text = text_grad(coeff_ref, near_rows, far_rows, 1536 + q * 512).astype(bf16)
+    image = image_ref[...]
     kept_ref[0:256, :] = jnp.where(first, image, text[0:256])
     send_ref[0:256, :] = jnp.where(first, text[0:256], image)
     kept_ref[256:512, :] = text[256:512]
     send_ref[256:512, :] = text[256:512]
 
 
-def near_grad_kernel(q, core_ref, mine_ref, other_ref, *refs):
-    refs = list(refs)
-    take = lambda n: [refs.pop(0) for _ in range(n)]
-    source_ref = take(1)[0]
-    rows, cols = take(4), take(4)
-    wide, tall = [None] + take(3), [None] + take(3)
-    take(3)
-    base_ref, send_ref, own_ref = take(3)
-    first = core_ref[0] == 0
-    block_ref = source_ref
-    if q == 0:
-        block_ref = take(1)[0]
-        row, col = tile_lse(first, mine_ref, other_ref)
-        eye = lax.broadcasted_iota(jnp.int32, (128, 128), 0) == lax.broadcasted_iota(jnp.int32, (128, 128), 1)
-        positive = jnp.where(jnp.logical_and(eye, first), 1.0, 0.0)
-    def image_grad():
-        part = slice(q * 256, q * 256 + 256)
-        terms = [times(block_ref[part, :], cols[0][...])]
-        return total_of(terms + [times(tall[p][part, :], cols[p][...]) for p in range(1, 4)])
-
-    if q == 0:
-        for k in range(3):
-            part = slice(k * 256, k * 256 + 256)
-            coeffs = coefficients(source_ref[part, :], row[:, part], col[:, 0:1536])
-            block_ref[part, :] = coeffs.astype(bf16)
-            own = slice(k * 512, k * 512 + 128)
-            block_ref[k * 256 : k * 256 + 128, own] = (coeffs[0:128, own] - positive).astype(bf16)
-            if k == 0:
-                image = image_grad()
-    else:
-        image = image_grad()
-    here = slice(q * 512, q * 512 + 512)
-    text = total_of(
-        [transposed_times(block_ref[:, here], rows[0][...])]
-        + [transposed_times(wide[p][:, here], rows[p][...]) for p in range(1, 4)]
-    )
-    own_ref[0:128, :] = image[0:128]
+def near_text_kernel(q, core_ref, coeff_ref, near_rows, far_rows, image_ref, own_image, a0, a1, a2, base_ref, send_ref, own_ref):
+    first = core_ref[0] == 0
+    text = text_grad(coeff_ref, near_rows, far_rows, q * 512)
+    image = image_ref[...].astype(f32)
+    own_ref[0:128, :] = own_image[q * 128 : q * 128 + 128, :]
     own_ref[128:256, :] = text[0:128]
     base_ref[0:128, :] = jnp.where(first, 0.0, text[0:128])
     base_ref[128:256, :] = jnp.where(first, image[128:256], text[128:256])
@@ -408,12 +380,40 @@
     loss_out[...] = (keep_ref[384:385, 0:1] + got_ref[384:385, 0:1]) * (0.5 / count)
 
 
-def pair_kernel(core_ref, image_ref, text_ref, image_got, text_got, *out_refs):
-    first = core_ref[0] == 0
-    for q, out in enumerate(out_refs):
+def pair_kernel(core_ref, image_hbm, text_hbm, image_got, text_got, o0, o1, o2, image_ref, text_ref, sems):
+    copies = [
+        pltpu.make_async_copy(image_hbm, image_ref, sems.at[0]),
+        pltpu.make_async_copy(text_hbm, text_ref, sems.at[1]),
+    ]
+    for copy in copies:
+        copy.start()
+    for copy in copies:
+        copy.wait()
+    first = core_ref[0] == 0
+    for q, out in enumerate((o0, o1, o2)):
         rows = slice(q * 64, q * 64 + 64)
         out[0:64, :] = jnp.where(first, image_ref[rows, :], text_got[rows, :])
         out[64:128, :] = jnp.where(first, image_got[rows, :], text_ref[rows, :])
+
+
+def pair(core_id, image_emb, text_emb, image_got, text_got):
+    rows, width = image_emb.shape
+    anywhere = pl.BlockSpec(memory_space=pl.ANY)
+    return pl.pallas_call(
+        pair_kernel,
+        in_specs=[SMEM, anywhere, anywhere, VMEM, VMEM],
+        out_specs=[VMEM] * 3,
+        out_shape=[shape(128, width, dtype=bf16)] * 3,
+        scratch_shapes=[pltpu.VMEM((rows, width), bf16)] * 2 + [pltpu.SemaphoreType.DMA((2,))],
+        compiler_params=pltpu.CompilerParams(vmem_limit_bytes=4 << 20),
+        name="pair",
+    )(
+        core_id,
+        pltpu.with_memory_space_constraint(image_emb, pltpu.HBM),
+        pltpu.with_memory_space_constraint(text_emb, pltpu.HBM),
+        image_got,
+        text_got,
+    )
 
 
 def per_device(image_emb, text_emb):
@@ -422,9 +422,7 @@
     count = pair_rows * 128
 
     got = [core_swap(image_emb), core_swap(text_emb)]
-    near = call(
-        pair_kernel, "pair", [core_id, image_emb, text_emb, *got], [shape(128, width, dtype=bf16)] * 3, limit=4
-    )
+    near = pair(core_id, image_emb, text_emb, *got)
     for step in range(2):
         got = [flip_permute(near[q], q + step) for q in range(3)]
         outs = [shape(256 << step, width, dtype=bf16)] * 3 + [shape(1536, width, dtype=bf16)] * step
@@ -432,37 +430,29 @@
     *near, packed = near
     near_x = [core_swap(packed)]
     far = [flip_permute(near[q], q + 2) for q in range(3)]
-    far_x = [None] * 3
-
-    rows, cols, wide, tall = [], [], [], [None]
-    stat = []
-    for stage in range(4):
-        for q in {1: (0, 1, 2)}.get(stage, ()):
-            far[q] = after(far[q], stat[0])
-            far_x[q] = core_swap(far[q])
-        ins = [core_id] + (near + near_x if stage == 0 else [far[stage - 1], far_x[stage - 1]])
-        ins += [held(a) for a in rows + cols] + stat
-        if stage == 3:
-            ins += [image_emb, text_emb]
-        new_rows = 768 if stage == 0 else 256
-        new_cols = 1536 if stage == 0 else 512
-        outs = [pltpu.VMEM((new_rows, width), bf16), pltpu.VMEM((new_cols, width), bf16)]
-        outs.append(pltpu.VMEM((new_rows, COL_AT[stage + 1]), f32))
-        if stage:
-            outs.append(pltpu.VMEM((ROW_AT[stage], new_cols), f32))
-        if stage < 3:
-            outs += [shape(ROW_AT[stage + 1] // 128, 128), shape(COL_AT[stage + 1] // 128, 128)]
-        else:
-            outs += [shape(32, 128), shape(32, 128)]
-        area = new_rows * COL_AT[stage + 1] + ROW_AT[stage] * new_cols
-        got = call(functools.partial(forward_kernel, stage), "forward", ins, outs, limit=10, flops=2 * area * width)
-        rows.append(got[0])
-        cols.append(got[1])
-        wide.append(got[2])
-        if stage:
-            tall.append(got[3])
-        stat = list(got[-2:])
-    send, keep = stat
+
+    near_rows, near_cols, near_logits, row, col = call(
+        near_kernel,
+        "near",
+        [core_id, *near, *near_x],
+        [pltpu.VMEM((768, width), bf16), pltpu.VMEM((1536, width), bf16), pltpu.VMEM((768, 1536), f32)]
+        + [shape(6, 128), shape(12, 128)],
+        limit=10,
+        flops=2 * 768 * 1536 * width,
+    )
+    far = [after(a, row) for a in far]
+    far_x = [core_swap(a) for a in far]
+    far_rows, far_cols, *logits, send, keep = call(
+        far_kernel,
+        "far",
+        [core_id, *far, *far_x, held(near_rows), held(near_cols), row, col, image_emb, text_emb],
+        [pltpu.VMEM((768, width), bf16), pltpu.VMEM((1536, width), bf16)]
+        + [pltpu.VMEM((256, 3072), f32)] * 3
+        + [pltpu.VMEM((768, 1536), f32), shape(32, 128), shape(32, 128)],
+        limit=10,
+        flops=2 * 768 * 4608 * width,
+    )
+    *wide_logits, tall_logits = logits
 
     mine = call(functools.partial(join_kernel, list(range(24))), "join", [core_id, keep, core_swap(send)], [shape(32, 128)], limit=2)[0]
     for dim in range(3):
@@ -470,54 +460,43 @@
         mine = call(functools.partial(join_kernel, flip_order(dim)), "join", [core_id, mine, got], [shape(32, 128)], limit=2)[0]
     other = core_swap(mine)
 
-    held_rows, held_cols = [held(a) for a in rows], [held(a) for a in cols]
-    wide_coeffs, tall_coeffs = [], []
-    messages = [None] * 3
-    for stage in (3, 2, 1):
-        ins = [core_id, mine, other, held(wide[stage]), held(tall[stage]), *held_rows, *held_cols]
-        ins += [held(a) for a in wide_coeffs + tall_coeffs]
-        outs = [pltpu.VMEM((256, COL_AT[stage + 1]), bf16), pltpu.VMEM((ROW_AT[stage], 512), bf16)]
-        outs += [shape(512, width, dtype=bf16)] * 2
-        if stage == 3:
-            outs.append(shape(8, 128))
-        got = call(
-            functools.partial(far_grad_kernel, stage),
-            "far_grad",
-            ins,
-            outs,
-            limit=10,
-            flops=2 * (256 * 3072 + 1536 * 512) * width,
+    held_rows = [held(near_rows), held(far_rows)]
+    coeffs, *image_grads, own_image, loss = call(
+        coeff_kernel,
+        "coeffs",
+        [core_id, mine, other]
+        + [held(a) for a in (near_logits, tall_logits, *wide_logits, near_cols, far_cols)],
+        [pltpu.VMEM((1536, 3072), bf16)] + [shape(256, width, dtype=bf16)] * 6 + [shape(384, width), shape(8, 128)],
+        limit=10,
+        flops=2 * 1536 * 3072 * width,
+    )
+    messages = []
+    for q in range(3):
+        kept, send = call(
+            functools.partial(far_text_kernel, q),
+            "far_text",
+            [core_id, held(coeffs), *held_rows, image_grads[3 + q]],
+            [shape(512, width, dtype=bf16)] * 2,
+            limit=6,
+            flops=2 * 1536 * 512 * width,
         )
-        wide_coeffs.insert(0, got[0])
-        tall_coeffs.insert(0, got[1])
-        if stage == 3:
-            loss = got[4]
-        ins = [core_id, got[2], core_swap(got[3])]
-        if stage == 1:
-            ins.append(loss)
-        messages[stage - 1] = call(
-            far_message_kernel, "far_message", ins, [shape(528 if stage == 1 else 512, width, dtype=bf16)]
-        )[0]
+        ins = [core_id, kept, core_swap(send)] + ([loss] if q == 0 else [])
+        outs = [shape(528 if q == 0 else 512, width, dtype=bf16)]
+        messages.append(call(far_message_kernel, "far_message", ins, outs)[0])
     got = [flip_permute(messages[q], q + 2) for q in range(3)]
     bases, near_got, owns = [], [], []
-    source = wide[0]
     for q in range(3):
-        got_q = call(
-            functools.partial(near_grad_kernel, q),
-            "near_grad",
-            [core_id, mine, other, held(source), *held_rows, *held_cols]
-            + [held(a) for a in wide_coeffs + tall_coeffs]
-            + messages,
-            [shape(512, width), shape(512, width, dtype=bf16), shape(256, width)]
-            + ([pltpu.VMEM((768, 1536), bf16)] if q == 0 else []),
-            limit=10,
-            flops=2 * (256 * 3072 + 1536 * 512) * width,
+        base, send, own = call(
+            functools.partial(near_text_kernel, q),
+            "near_text",
+            [core_id, held(coeffs), *held_rows, image_grads[q], own_image, *messages],
+            [shape(512, width), shape(512, width, dtype=bf16), shape(256, width)],
+            limit=6,
+            flops=2 * 1536 * 512 * width,
         )
-        bases.append(got_q[0])
-        near_got.append(core_swap(got_q[1]))
-        owns.append(got_q[2])
-        if q == 0:
-            source = got_q[3]
+        bases.append(base)
+        near_got.append(core_swap(send))
+        owns.append(own)
     total, loss = call(far_sum_kernel, "far_sum", [core_id, *bases, *got, loss], [shape(1536, width), shape(8, 128)])
     low, *messages = call(
         near_sum_kernel,

time: 107 us -> 106 us (level)
  starting transfers between devices: 39.3 us -> 43 us
  Pallas kernels: 29.1 us -> 26.7 us
  local copies, waits for them, and re-layouts: 1.87 us -> 0.01 us
    ppermute x21, starting transfers between devices: 34.1 us -> 37.6 us  [flip_permute(): return lax.ppermute(x, AXES, ROLE_PAIRS[dim % 3])]
    pallas_call x25 -> x23, Pallas kernels: 29.1 us -> 25.7 us  [call(): pl.pallas_call(kernel, in_specs=in_specs, out_specs=[VMEM] * len(outs), o...]
    unnamed x8 -> x4, local copies, waits for them, and re-layouts: 1.87 us -> 0.01 us
    pallas_call x0 -> x1, Pallas kernels: none -> 1.08 us  [pair(): pl.pallas_call(pair_kernel, in_specs=[SMEM, anywhere, anywhere, VMEM, VME...]
  transfers between devices with their start and end apart: 36 -> 36, of which waited for: 20 -> 22; matrix products, arithmetic and copies ran while one was open for 0% -> 0% of each run, Pallas kernels for 19% -> 8%
where the time goes in v8:
time: 106 us
  starting transfers between devices  43 us (41%)
  waiting for transfers between devices  35.7 us (34%)
  Pallas kernels  26.7 us (25%)
    ppermute x21, starting transfers between devices, flip_permute(): return lax.ppermute(x, AXES, ROLE_PAIRS[dim % 3])  37.6 us
    ppermute x21, waiting for transfers between devices, flip_permute(): return lax.ppermute(x, AXES, ROLE_PAIRS[dim % 3])  27.3 us
    pallas_call x23, Pallas kernels, call(): pl.pallas_call(kernel, in_specs=in_specs, out_specs=[VMEM] * len(outs), o...  25.7 us
    ppermute x15, waiting for transfers between devices, core_swap(): return lax.ppermute(x, 'c', SWAP)  8.34 us
    ppermute x15, starting transfers between devices, core_swap(): return lax.ppermute(x, 'c', SWAP)  5.42 us
  transfers between devices with their start and end apart: 36, of which 22 were waited for; matrix products, arithmetic and copies ran while one was open for 0% of the time, Pallas kernels for 8%

profile of v8, /device:TPU:1, one launch (start us, length us, event | category | flops | bytes accessed | tf_op | source)
XLA Modules:
  0.0 106.2 jit_solution(5736659543723669963)
XLA Ops:
  0.6 1.5 %collective-permute-start = (bf16[192,512]{1,0:T(8,128)(2,1)}, bf16[192,512]{1,0:T(8,128)(2,1)S(1)}, u32[]{:S(2)}, u32[]{:S(2)}) collective-permute-start(bf16[192,512]{1,0:T(8,128)(2,1)} %refs_10_.1), channel_id=1, source_target_pairs={{0,1},{1,0},{2,3},{3,2},{4,5},{5,4},{6,7},{7,6},{8,9},{9,8},{10,11... | collective-permute-start | bytes 589832 | tf_op jit(solution)/shard_map/ppermute | solution.py:47
  2.2 1.2 %collective-permute-done.image_got = bf16[192,512]{1,0:T(8,128)(2,1)S(1)} collective-permute-done((bf16[192,512]{1,0:T(8,128)(2,1)}, bf16[192,512]{1,0:T(8,128)(2,1)S(1)}, u32[]{:S(2)}, u32[]{:S(2)}) %collective-permute-start) | collective-permute-done | bytes 196640 | tf_op jit(solution)/shard_map/ppermute | solution.py:47
  3.8 1.1 %pair.1 = (bf16[128,512]{1,0:T(8,128)(2,1)S(1)}, bf16[128,512]{1,0:T(8,128)(2,1)S(1)}, bf16[128,512]{1,0:T(8,128)(2,1)S(1)}) custom-call(s32[1]{0:T(128)} %bitcast.core_ref, bf16[192,512]{1,0:T(8,128)(2,1)} %refs_10_.1, bf16[192,512]{1,0:T(8,128)(2,1)} %refs_11_.1, bf16[192,512]{1,0:T(8,128)(2,1)S(1)} %collective-permute-done.image_got, ...), custom_call_target="tpu_custom_call" | custom-call | tf_op jit(solution)/shard_map/pair/pallas_call | solution.py:402
  4.9 2.6 %collective-permute-start.2 = (bf16[128,512]{1,0:T(8,128)(2,1)S(1)}, bf16[128,512]{1,0:T(8,128)(2,1)S(1)}, u32[]{:S(2)}, u32[]{:S(2)}) collective-permute-start(bf16[128,512]{1,0:T(8,128)(2,1)S(1)} %get-tuple-element.66.refs_0_), channel_id=1, source_target_pairs={{0,2},{1,7},{2,0},{3,5},{4,6},{5,3},{6,4},{7,1},{8,10},{9,15},{10,... | collective-permute-start | bytes 393224 | tf_op jit(solution)/shard_map/ppermute | solution.py:43
  7.5 2.7 %collective-permute-start.3 = (bf16[128,512]{1,0:T(8,128)(2,1)S(1)}, bf16[128,512]{1,0:T(8,128)(2,1)S(1)}, u32[]{:S(2)}, u32[]{:S(2)}) collective-permute-start(bf16[128,512]{1,0:T(8,128)(2,1)S(1)} %get-tuple-element.67.refs_1_), channel_id=1, source_target_pairs={{0,8},{1,25},{2,10},{3,27},{4,12},{5,29},{6,14},{7,31},{8,0},{9,17... | collective-permute-start | bytes 393224 | tf_op jit(solution)/shard_map/ppermute | solution.py:43
  10.2 3.8 %collective-permute-start.4 = (bf16[128,512]{1,0:T(8,128)(2,1)S(1)}, bf16[128,512]{1,0:T(8,128)(2,1)S(1)}, u32[]{:S(2)}, u32[]{:S(2)}) collective-permute-start(bf16[128,512]{1,0:T(8,128)(2,1)S(1)} %get-tuple-element.68.refs_2_), channel_id=1, source_target_pairs={{0,32},{1,97},{2,34},{3,99},{4,36},{5,101},{6,38},{7,103},{8,40},{... | collective-permute-start | bytes 393224 | tf_op jit(solution)/shard_map/ppermute | solution.py:43
  14.0 2.3 %collective-permute-done.4.refs_5_ = bf16[128,512]{1,0:T(8,128)(2,1)S(1)} collective-permute-done((bf16[128,512]{1,0:T(8,128)(2,1)S(1)}, bf16[128,512]{1,0:T(8,128)(2,1)S(1)}, u32[]{:S(2)}, u32[]{:S(2)}) %collective-permute-start.4) | collective-permute-done | bytes 131104 | tf_op jit(solution)/shard_map/ppermute | solution.py:43
  16.5 2.8 %collective-permute-start.6 = (bf16[256,512]{1,0:T(8,128)(2,1)S(1)}, bf16[256,512]{1,0:T(8,128)(2,1)S(1)}, u32[]{:S(2)}, u32[]{:S(2)}) collective-permute-start(bf16[256,512]{1,0:T(8,128)(2,1)S(1)} %get-tuple-element.70.refs_1_), channel_id=1, source_target_pairs={{0,32},{1,97},{2,34},{3,99},{4,36},{5,101},{6,38},{7,103},{8,40},{... | collective-permute-start | bytes 786440 | tf_op jit(solution)/shard_map/ppermute | solution.py:43
  19.5 3.5 %collective-permute-done.5.refs_3_ = bf16[256,512]{1,0:T(8,128)(2,1)S(1)} collective-permute-done((bf16[256,512]{1,0:T(8,128)(2,1)S(1)}, bf16[256,512]{1,0:T(8,128)(2,1)S(1)}, u32[]{:S(2)}, u32[]{:S(2)}) %collective-permute-start.5) | collective-permute-done | bytes 262176 | tf_op jit(solution)/shard_map/ppermute | solution.py:43
  23.0 2.7 %collective-permute-done.7.refs_5_ = bf16[256,512]{1,0:T(8,128)(2,1)S(1)} collective-permute-done((bf16[256,512]{1,0:T(8,128)(2,1)S(1)}, bf16[256,512]{1,0:T(8,128)(2,1)S(1)}, u32[]{:S(2)}, u32[]{:S(2)}) %collective-permute-start.7) | collective-permute-done | bytes 262176 | tf_op jit(solution)/shard_map/ppermute | solution.py:43
  26.6 2.7 %collective-permute-start.11 = (bf16[512,512]{1,0:T(8,128)(2,1)S(1)}, bf16[512,512]{1,0:T(8,128)(2,1)S(1)}, u32[]{:S(2)}, u32[]{:S(2)}) collective-permute-start(bf16[512,512]{1,0:T(8,128)(2,1)S(1)} %get-tuple-element.74.m2), channel_id=1, source_target_pairs={{0,8},{1,25},{2,10},{3,27},{4,12},{5,29},{6,14},{7,31},{8,0},{9,17... | collective-permute-start | bytes 1572872 | tf_op jit(solution)/shard_map/ppermute | solution.py:43
  29.4 2.8 %near.1 = (bf16[768,512]{1,0:T(8,128)(2,1)S(1)}, bf16[1536,512]{1,0:T(8,128)(2,1)S(1)}, f32[768,1536]{1,0:T(8,128)S(1)}, f32[6,128]{1,0:T(8,128)S(1)}, f32[12,128]{1,0:T(8,128)S(1)}) custom-call(s32[1]{0:T(128)} %bitcast.core_ref, bf16[512,512]{1,0:T(8,128)(2,1)S(1)} %get-tuple-element.72.m0, bf16[512,512]{1,0:T(8,128)(2,1)S(1)} %get-tuple-element.73.m1, ...), custom_call_target="tpu_custom_call" | custom-call | flops 1207959552 | tf_op jit(solution)/shard_map/near/pallas_call | solution.py:52
  32.2 3.1 %collective-permute-done.8.value_ref = bf16[512,512]{1,0:T(8,128)(2,1)S(1)} collective-permute-done((bf16[512,512]{1,0:T(8,128)(2,1)S(1)}, bf16[512,512]{1,0:T(8,128)(2,1)S(1)}, u32[]{:S(2)}, u32[]{:S(2)}) %collective-permute-start.8) | collective-permute-done | bytes 524320 | tf_op jit(solution)/shard_map/ppermute | solution.py:43
  36.2 1.0 collective-permute-done.12.refs_3_
  37.2 0.7 collective-permute-done.13.refs_4_
  38.0 0.7 collective-permute-done.14.refs_5_
  38.7 8.2 %far.1 = (bf16[768,512]{1,0:T(8,128)(2,1)S(1)}, bf16[1536,512]{1,0:T(8,128)(2,1)S(1)}, f32[256,3072]{1,0:T(8,128)S(1)}, f32[256,3072]{1,0:T(8,128)S(1)}, f32[256...) custom-call(s32[1]{0:T(128)} %bitcast.core_ref, ...), custom_call_target="tpu_custom_call" | custom-call | flops 3623878656 | tf_op jit(solution)/shard_map/far/pallas_call | solution.py:52
  47.4 0.8 collective-permute-done.15.got_ref
  48.2 1.4 %collective-permute-start.16 = (f32[32,128]{1,0:T(8,128)S(1)}, f32[32,128]{1,0:T(8,128)S(1)}, u32[]{:S(2)}, u32[]{:S(2)}) collective-permute-start(f32[32,128]{1,0:T(8,128)S(1)} %join.4.mine_ref), channel_id=1, source_target_pairs={{0,2},{1,7},{2,0},{3,5},{4,6},{5,3},{6,4},{7,1},{8,10},{9,15},{10,... | collective-permute-start | bytes 49160 | tf_op jit(solution)/shard_map/ppermute | solution.py:43
  49.6 2.5 %collective-permute-done.16.got_ref = f32[32,128]{1,0:T(8,128)S(1)} collective-permute-done((f32[32,128]{1,0:T(8,128)S(1)}, f32[32,128]{1,0:T(8,128)S(1)}, u32[]{:S(2)}, u32[]{:S(2)}) %collective-permute-start.16) | collective-permute-done | bytes 16416 | tf_op jit(solution)/shard_map/ppermute | solution.py:43
  52.1 2.7 %collective-permute-start.17 = (f32[32,128]{1,0:T(8,128)S(1)}, f32[32,128]{1,0:T(8,128)S(1)}, u32[]{:S(2)}, u32[]{:S(2)}) collective-permute-start(f32[32,128]{1,0:T(8,128)S(1)} %join.5.mine_ref), channel_id=1, source_target_pairs={{0,8},{1,25},{2,10},{3,27},{4,12},{5,29},{6,14},{7,31},{8,0},{9,17... | collective-permute-start | bytes 49160 | tf_op jit(solution)/shard_map/ppermute | solution.py:43
  54.8 1.2 %collective-permute-done.17.got_ref = f32[32,128]{1,0:T(8,128)S(1)} collective-permute-done((f32[32,128]{1,0:T(8,128)S(1)}, f32[32,128]{1,0:T(8,128)S(1)}, u32[]{:S(2)}, u32[]{:S(2)}) %collective-permute-start.17) | collective-permute-done | bytes 16416 | tf_op jit(solution)/shard_map/ppermute | solution.py:43
  56.0 2.0 %collective-permute-start.18 = (f32[32,128]{1,0:T(8,128)S(1)}, f32[32,128]{1,0:T(8,128)S(1)}, u32[]{:S(2)}, u32[]{:S(2)}) collective-permute-start(f32[32,128]{1,0:T(8,128)S(1)} %join.6.mine_ref), channel_id=1, source_target_pairs={{0,32},{1,97},{2,34},{3,99},{4,36},{5,101},{6,38},{7,103},{8,40},{... | collective-permute-start | bytes 49160 | tf_op jit(solution)/shard_map/ppermute | solution.py:43
  58.0 1.9 %collective-permute-done.18.got_ref = f32[32,128]{1,0:T(8,128)S(1)} collective-permute-done((f32[32,128]{1,0:T(8,128)S(1)}, f32[32,128]{1,0:T(8,128)S(1)}, u32[]{:S(2)}, u32[]{:S(2)}) %collective-permute-start.18) | collective-permute-done | bytes 16416 | tf_op jit(solution)/shard_map/ppermute | solution.py:43
  60.4 1.0 collective-permute-done.19.other_ref
  61.4 5.4 %coeffs.1 = (bf16[1536,3072]{1,0:T(8,128)(2,1)S(1)}, bf16[256,512]{1,0:T(8,128)(2,1)S(1)}, bf16[256,512]{1,0:T(8,128)(2,1)S(1)}, bf16[256,512]{1,0:T(8,128)(2,1)...) custom-call(s32[1]{0:T(128)} %bitcast.core_ref, ...), custom_call_target="tpu_custom_call" | custom-call | flops 4831838208 | tf_op jit(solution)/shard_map/coeffs/pallas_call | solution.py:52
  66.8 1.0 far_text.5
  68.1 1.0 far_text.3
  69.6 1.0 far_text.4
  71.0 2.7 %collective-permute-start.25 = (bf16[512,512]{1,0:T(8,128)(2,1)S(1)}, bf16[512,512]{1,0:T(8,128)(2,1)S(1)}, u32[]{:S(2)}, u32[]{:S(2)}) collective-permute-start(bf16[512,512]{1,0:T(8,128)(2,1)S(1)} %far_message.5.a2), channel_id=1, source_target_pairs={{0,8},{1,25},{2,10},{3,27},{4,12},{5,29},{6,14},{7,31},{8,0},{9,17... | collective-permute-start | bytes 1572872 | tf_op jit(solution)/shard_map/ppermute | solution.py:43
  73.9 2.0 %collective-permute-start.23 = (bf16[528,512]{1,0:T(8,128)(2,1)S(1)}, bf16[528,512]{1,0:T(8,128)(2,1)S(1)}, u32[]{:S(2)}, u32[]{:S(2)}) collective-permute-start(bf16[528,512]{1,0:T(8,128)(2,1)S(1)} %far_message.3.a0), channel_id=1, source_target_pairs={{0,32},{1,97},{2,34},{3,99},{4,36},{5,101},{6,38},{7,103},{8,40},{... | collective-permute-start | bytes 1622024 | tf_op jit(solution)/shard_map/ppermute | solution.py:43
  76.1 2.0 %collective-permute-start.24 = (bf16[512,512]{1,0:T(8,128)(2,1)S(1)}, bf16[512,512]{1,0:T(8,128)(2,1)S(1)}, u32[]{:S(2)}, u32[]{:S(2)}) collective-permute-start(bf16[512,512]{1,0:T(8,128)(2,1)S(1)} %far_message.4.a1), channel_id=1, source_target_pairs={{0,2},{1,7},{2,0},{3,5},{4,6},{5,3},{6,4},{7,1},{8,10},{9,15},{10,... | collective-permute-start | bytes 1572872 | tf_op jit(solution)/shard_map/ppermute | solution.py:43
  78.1 1.1 %near_text.5 = (f32[512,512]{1,0:T(8,128)S(1)}, bf16[512,512]{1,0:T(8,128)(2,1)S(1)}, f32[256,512]{1,0:T(8,128)S(1)}) custom-call(s32[1]{0:T(128)} %bitcast.core_ref, bf16[1536,3072]{1,0:T(8,128)(2,1)S(1)} %get-tuple-element.88.coeff_ref, bf16[768,512]{1,0:T(8,128)(2,1)S(1)} %get-tuple-element.77.refs_6_.near_rows, ...), custom_call_target="tpu_custom_call" | custom-call | flops 805306368 | tf_op jit(solution)/shard_map/near_text/pallas_call | solution.py:52
  79.5 1.1 %near_text.4 = (f32[512,512]{1,0:T(8,128)S(1)}, bf16[512,512]{1,0:T(8,128)(2,1)S(1)}, f32[256,512]{1,0:T(8,128)S(1)}) custom-call(s32[1]{0:T(128)} %bitcast.core_ref, bf16[1536,3072]{1,0:T(8,128)(2,1)S(1)} %get-tuple-element.88.coeff_ref, bf16[768,512]{1,0:T(8,128)(2,1)S(1)} %get-tuple-element.77.refs_6_.near_rows, ...), custom_call_target="tpu_custom_call" | custom-call | flops 805306368 | tf_op jit(solution)/shard_map/near_text/pallas_call | solution.py:52
  80.6 1.1 %near_text.3 = (f32[512,512]{1,0:T(8,128)S(1)}, bf16[512,512]{1,0:T(8,128)(2,1)S(1)}, f32[256,512]{1,0:T(8,128)S(1)}) custom-call(s32[1]{0:T(128)} %bitcast.core_ref, bf16[1536,3072]{1,0:T(8,128)(2,1)S(1)} %get-tuple-element.88.coeff_ref, bf16[768,512]{1,0:T(8,128)(2,1)S(1)} %get-tuple-element.77.refs_6_.near_rows, ...), custom_call_target="tpu_custom_call" | custom-call | flops 805306368 | tf_op jit(solution)/shard_map/near_text/pallas_call | solution.py:52
  81.7 0.6 collective-permute-start.27
  82.4 3.0 %collective-permute-done.24.r1 = bf16[512,512]{1,0:T(8,128)(2,1)S(1)} collective-permute-done((bf16[512,512]{1,0:T(8,128)(2,1)S(1)}, bf16[512,512]{1,0:T(8,128)(2,1)S(1)}, u32[]{:S(2)}, u32[]{:S(2)}) %collective-permute-start.24) | collective-permute-done | bytes 524320 | tf_op jit(solution)/shard_map/ppermute | solution.py:43
  86.4 1.1 %collective-permute-start.30 = (bf16[256,512]{1,0:T(8,128)(2,1)S(1)}, bf16[256,512]{1,0:T(8,128)(2,1)S(1)}, u32[]{:S(2)}, u32[]{:S(2)}) collective-permute-start(bf16[256,512]{1,0:T(8,128)(2,1)S(1)} %get-tuple-element.114), channel_id=1, source_target_pairs={{0,32},{1,97},{2,34},{3,99},{4,36},{5,101},{6,38},{7,103},{8,40},{... | collective-permute-start | bytes 786440 | tf_op jit(solution)/shard_map/ppermute | solution.py:43
  87.5 1.9 %collective-permute-start.31 = (bf16[256,512]{1,0:T(8,128)(2,1)S(1)}, bf16[256,512]{1,0:T(8,128)(2,1)S(1)}, u32[]{:S(2)}, u32[]{:S(2)}) collective-permute-start(bf16[256,512]{1,0:T(8,128)(2,1)S(1)} %get-tuple-element.115), channel_id=1, source_target_pairs={{0,2},{1,7},{2,0},{3,5},{4,6},{5,3},{6,4},{7,1},{8,10},{9,15},{10,... | collective-permute-start | bytes 786440 | tf_op jit(solution)/shard_map/ppermute | solution.py:43
  89.4 3.4 %collective-permute-done.30.r1 = bf16[256,512]{1,0:T(8,128)(2,1)S(1)} collective-permute-done((bf16[256,512]{1,0:T(8,128)(2,1)S(1)}, bf16[256,512]{1,0:T(8,128)(2,1)S(1)}, u32[]{:S(2)}, u32[]{:S(2)}) %collective-permute-start.30) | collective-permute-done | bytes 262176 | tf_op jit(solution)/shard_map/ppermute | solution.py:43
  92.8 1.1 %collective-permute-done.31.r2 = bf16[256,512]{1,0:T(8,128)(2,1)S(1)} collective-permute-done((bf16[256,512]{1,0:T(8,128)(2,1)S(1)}, bf16[256,512]{1,0:T(8,128)(2,1)S(1)}, u32[]{:S(2)}, u32[]{:S(2)}) %collective-permute-start.31) | collective-permute-done | bytes 262176 | tf_op jit(solution)/shard_map/ppermute | solution.py:43
  94.1 2.0 %collective-permute-start.32 = (bf16[144,512]{1,0:T(8,128)(2,1)S(1)}, bf16[144,512]{1,0:T(8,128)(2,1)S(1)}, u32[]{:S(2)}, u32[]{:S(2)}) collective-permute-start(bf16[144,512]{1,0:T(8,128)(2,1)S(1)} %get-tuple-element.117), channel_id=1, source_target_pairs={{0,2},{1,7},{2,0},{3,5},{4,6},{5,3},{6,4},{7,1},{8,10},{9,15},{10,... | collective-permute-start | bytes 442376 | tf_op jit(solution)/shard_map/ppermute | solution.py:43
  96.1 1.5 %collective-permute-start.33 = (bf16[128,512]{1,0:T(8,128)(2,1)S(1)}, bf16[128,512]{1,0:T(8,128)(2,1)S(1)}, u32[]{:S(2)}, u32[]{:S(2)}) collective-permute-start(bf16[128,512]{1,0:T(8,128)(2,1)S(1)} %get-tuple-element.118), channel_id=1, source_target_pairs={{0,8},{1,25},{2,10},{3,27},{4,12},{5,29},{6,14},{7,31},{8,0},{9,17... | collective-permute-start | bytes 393224 | tf_op jit(solution)/shard_map/ppermute | solution.py:43
  97.6 2.6 %collective-permute-start.34 = (bf16[128,512]{1,0:T(8,128)(2,1)S(1)}, bf16[128,512]{1,0:T(8,128)(2,1)S(1)}, u32[]{:S(2)}, u32[]{:S(2)}) collective-permute-start(bf16[128,512]{1,0:T(8,128)(2,1)S(1)} %get-tuple-element.119), channel_id=1, source_target_pairs={{0,32},{1,97},{2,34},{3,99},{4,36},{5,101},{6,38},{7,103},{8,40},{... | collective-permute-start | bytes 393224 | tf_op jit(solution)/shard_map/ppermute | solution.py:43
  100.2 0.9 collective-permute-done.33.r1
  101.1 1.5 %collective-permute-done.34.r2 = bf16[128,512]{1,0:T(8,128)(2,1)S(1)} collective-permute-done((bf16[128,512]{1,0:T(8,128)(2,1)S(1)}, bf16[128,512]{1,0:T(8,128)(2,1)S(1)}, u32[]{:S(2)}, u32[]{:S(2)}) %collective-permute-start.34) | collective-permute-done | bytes 131104 | tf_op jit(solution)/shard_map/ppermute | solution.py:43
  102.9 2.3 %collective-permute-done.35.got_ref = f32[392,512]{1,0:T(8,128)S(1)} collective-permute-done((f32[392,512]{1,0:T(8,128)S(1)}, f32[392,512]{1,0:T(8,128)S(1)}, u32[]{:S(2)}, u32[]{:S(2)}) %collective-permute-start.35) | collective-permute-done | bytes 802848 | tf_op jit(solution)/shard_map/ppermute | solution.py:47
  105.2 1.0 finish.1
  (55 shorter events, 6.9 us)
Async XLA Ops:
  0.6 2.8 %collective-permute-start = (bf16[192,512]{1,0:T(8,128)(2,1)}, bf16[192,512]{1,0:T(8,128)(2,1)S(1)}, u32[]{:S(2)}, u32[]{:S(2)}) collective-permute-start(bf16[192,512]{1,0:T(8,128)(2,1)} %refs_10_.1), channel_id=1, source_target_pairs={{0,1},{1,0},{2,3},{3,2},{4,5},{5,4},{6,7},{7,6},{8,9},{9,8},{10,11... | collective-permute-start | bytes 589832 | tf_op jit(solution)/shard_map/ppermute | solution.py:47
  2.1 1.7 %collective-permute-start.1 = (bf16[192,512]{1,0:T(8,128)(2,1)}, bf16[192,512]{1,0:T(8,128)(2,1)S(1)}, u32[]{:S(2)}, u32[]{:S(2)}) collective-permute-start(bf16[192,512]{1,0:T(8,128)(2,1)} %refs_11_.1), channel_id=1, source_target_pairs={{0,1},{1,0},{2,3},{3,2},{4,5},{5,4},{6,7},{7,6},{8,9},{9,8},{10,11... | collective-permute-start | bytes 589832 | tf_op jit(solution)/shard_map/ppermute | solution.py:47
  4.9 9.1 %collective-permute-start.2 = (bf16[128,512]{1,0:T(8,128)(2,1)S(1)}, bf16[128,512]{1,0:T(8,128)(2,1)S(1)}, u32[]{:S(2)}, u32[]{:S(2)}) collective-permute-start(bf16[128,512]{1,0:T(8,128)(2,1)S(1)} %get-tuple-element.66.refs_0_), channel_id=1, source_target_pairs={{0,2},{1,7},{2,0},{3,5},{4,6},{5,3},{6,4},{7,1},{8,10},{9,15},{10,... | collective-permute-start | bytes 393224 | tf_op jit(solution)/shard_map/ppermute | solution.py:43
  7.5 6.5 %collective-permute-start.3 = (bf16[128,512]{1,0:T(8,128)(2,1)S(1)}, bf16[128,512]{1,0:T(8,128)(2,1)S(1)}, u32[]{:S(2)}, u32[]{:S(2)}) collective-permute-start(bf16[128,512]{1,0:T(8,128)(2,1)S(1)} %get-tuple-element.67.refs_1_), channel_id=1, source_target_pairs={{0,8},{1,25},{2,10},{3,27},{4,12},{5,29},{6,14},{7,31},{8,0},{9,17... | collective-permute-start | bytes 393224 | tf_op jit(solution)/shard_map/ppermute | solution.py:43
  10.2 6.1 %collective-permute-start.4 = (bf16[128,512]{1,0:T(8,128)(2,1)S(1)}, bf16[128,512]{1,0:T(8,128)(2,1)S(1)}, u32[]{:S(2)}, u32[]{:S(2)}) collective-permute-start(bf16[128,512]{1,0:T(8,128)(2,1)S(1)} %get-tuple-element.68.refs_2_), channel_id=1, source_target_pairs={{0,32},{1,97},{2,34},{3,99},{4,36},{5,101},{6,38},{7,103},{8,40},{... | collective-permute-start | bytes 393224 | tf_op jit(solution)/shard_map/ppermute | solution.py:43
  16.4 6.5 %collective-permute-start.5 = (bf16[256,512]{1,0:T(8,128)(2,1)S(1)}, bf16[256,512]{1,0:T(8,128)(2,1)S(1)}, u32[]{:S(2)}, u32[]{:S(2)}) collective-permute-start(bf16[256,512]{1,0:T(8,128)(2,1)S(1)} %get-tuple-element.69.refs_0_), channel_id=1, source_target_pairs={{0,8},{1,25},{2,10},{3,27},{4,12},{5,29},{6,14},{7,31},{8,0},{9,17... | collective-permute-start | bytes 786440 | tf_op jit(solution)/shard_map/ppermute | solution.py:43
  16.5 6.5 %collective-permute-start.6 = (bf16[256,512]{1,0:T(8,128)(2,1)S(1)}, bf16[256,512]{1,0:T(8,128)(2,1)S(1)}, u32[]{:S(2)}, u32[]{:S(2)}) collective-permute-start(bf16[256,512]{1,0:T(8,128)(2,1)S(1)} %get-tuple-element.70.refs_1_), channel_id=1, source_target_pairs={{0,32},{1,97},{2,34},{3,99},{4,36},{5,101},{6,38},{7,103},{8,40},{... | collective-permute-start | bytes 786440 | tf_op jit(solution)/shard_map/ppermute | solution.py:43
  19.3 6.4 %collective-permute-start.7 = (bf16[256,512]{1,0:T(8,128)(2,1)S(1)}, bf16[256,512]{1,0:T(8,128)(2,1)S(1)}, u32[]{:S(2)}, u32[]{:S(2)}) collective-permute-start(bf16[256,512]{1,0:T(8,128)(2,1)S(1)} %get-tuple-element.71.refs_2_), channel_id=1, source_target_pairs={{0,2},{1,7},{2,0},{3,5},{4,6},{5,3},{6,4},{7,1},{8,10},{9,15},{10,... | collective-permute-start | bytes 786440 | tf_op jit(solution)/shard_map/ppermute | solution.py:43
  25.9 3.5 %collective-permute-start.9 = (bf16[1536,512]{1,0:T(8,128)(2,1)S(1)}, bf16[1536,512]{1,0:T(8,128)(2,1)S(1)}, u32[]{:S(2)}, u32[]{:S(2)}) collective-permute-start(bf16[1536,512]{1,0:T(8,128)(2,1)S(1)} %get-tuple-element.75), channel_id=1, source_target_pairs={{0,1},{1,0},{2,3},{3,2},{4,5},{5,4},{6,7},{7,6},{8,9},{9,8},{10,11... | collective-permute-start | bytes 4718600 | tf_op jit(solution)/shard_map/ppermute | solution.py:47
  26.0 9.3 %collective-permute-start.8 = (bf16[512,512]{1,0:T(8,128)(2,1)S(1)}, bf16[512,512]{1,0:T(8,128)(2,1)S(1)}, u32[]{:S(2)}, u32[]{:S(2)}) collective-permute-start(bf16[512,512]{1,0:T(8,128)(2,1)S(1)} %get-tuple-element.72.m0), channel_id=1, source_target_pairs={{0,32},{1,97},{2,34},{3,99},{4,36},{5,101},{6,38},{7,103},{8,40},{... | collective-permute-start | bytes 1572872 | tf_op jit(solution)/shard_map/ppermute | solution.py:43
  26.2 9.5 %collective-permute-start.10 = (bf16[512,512]{1,0:T(8,128)(2,1)S(1)}, bf16[512,512]{1,0:T(8,128)(2,1)S(1)}, u32[]{:S(2)}, u32[]{:S(2)}) collective-permute-start(bf16[512,512]{1,0:T(8,128)(2,1)S(1)} %get-tuple-element.73.m1), channel_id=1, source_target_pairs={{0,2},{1,7},{2,0},{3,5},{4,6},{5,3},{6,4},{7,1},{8,10},{9,15},{10,... | collective-permute-start | bytes 1572872 | tf_op jit(solution)/shard_map/ppermute | solution.py:43
  26.6 12.2 %copy-start = (bf16[192,512]{1,0:T(8,128)(2,1)S(1)}, bf16[192,512]{1,0:T(8,128)(2,1)}, u32[]{:S(2)}) copy-start(bf16[192,512]{1,0:T(8,128)(2,1)} %refs_10_.1) | copy-start | bytes 589828
  26.6 12.2 %copy-start.1 = (bf16[192,512]{1,0:T(8,128)(2,1)S(1)}, bf16[192,512]{1,0:T(8,128)(2,1)}, u32[]{:S(2)}) copy-start(bf16[192,512]{1,0:T(8,128)(2,1)} %refs_11_.1) | copy-start | bytes 589828
  26.6 9.3 %collective-permute-start.11 = (bf16[512,512]{1,0:T(8,128)(2,1)S(1)}, bf16[512,512]{1,0:T(8,128)(2,1)S(1)}, u32[]{:S(2)}, u32[]{:S(2)}) collective-permute-start(bf16[512,512]{1,0:T(8,128)(2,1)S(1)} %get-tuple-element.74.m2), channel_id=1, source_target_pairs={{0,8},{1,25},{2,10},{3,27},{4,12},{5,29},{6,14},{7,31},{8,0},{9,17... | collective-permute-start | bytes 1572872 | tf_op jit(solution)/shard_map/ppermute | solution.py:43
  35.3 1.9 %collective-permute-start.12 = (bf16[512,512]{1,0:T(8,128)(2,1)S(1)}, bf16[512,512]{1,0:T(8,128)(2,1)S(1)}, u32[]{:S(2)}, u32[]{:S(2)}) collective-permute-start(bf16[512,512]{1,0:T(8,128)(2,1)S(1)} %after.3.refs_0_), channel_id=1, source_target_pairs={{0,1},{1,0},{2,3},{3,2},{4,5},{5,4},{6,7},{7,6},{8,9},{9,8},{10,11... | collective-permute-start | bytes 1572872 | tf_op jit(solution)/shard_map/ppermute | solution.py:47
  35.7 2.3 %collective-permute-start.13 = (bf16[512,512]{1,0:T(8,128)(2,1)S(1)}, bf16[512,512]{1,0:T(8,128)(2,1)S(1)}, u32[]{:S(2)}, u32[]{:S(2)}) collective-permute-start(bf16[512,512]{1,0:T(8,128)(2,1)S(1)} %after.4.refs_1_), channel_id=1, source_target_pairs={{0,1},{1,0},{2,3},{3,2},{4,5},{5,4},{6,7},{7,6},{8,9},{9,8},{10,11... | collective-permute-start | bytes 1572872 | tf_op jit(solution)/shard_map/ppermute | solution.py:47
  35.9 2.8 %collective-permute-start.14 = (bf16[512,512]{1,0:T(8,128)(2,1)S(1)}, bf16[512,512]{1,0:T(8,128)(2,1)S(1)}, u32[]{:S(2)}, u32[]{:S(2)}) collective-permute-start(bf16[512,512]{1,0:T(8,128)(2,1)S(1)} %after.5.refs_2_), channel_id=1, source_target_pairs={{0,1},{1,0},{2,3},{3,2},{4,5},{5,4},{6,7},{7,6},{8,9},{9,8},{10,11... | collective-permute-start | bytes 1572872 | tf_op jit(solution)/shard_map/ppermute | solution.py:47
  47.0 1.3 %collective-permute-start.15 = (f32[32,128]{1,0:T(8,128)S(1)}, f32[32,128]{1,0:T(8,128)S(1)}, u32[]{:S(2)}, u32[]{:S(2)}) collective-permute-start(f32[32,128]{1,0:T(8,128)S(1)} %get-tuple-element.81), channel_id=1, source_target_pairs={{0,1},{1,0},{2,3},{3,2},{4,5},{5,4},{6,7},{7,6},{8,9},{9,8},{10,11... | collective-permute-start | bytes 49160 | tf_op jit(solution)/shard_map/ppermute | solution.py:47
  48.2 3.9 %collective-permute-start.16 = (f32[32,128]{1,0:T(8,128)S(1)}, f32[32,128]{1,0:T(8,128)S(1)}, u32[]{:S(2)}, u32[]{:S(2)}) collective-permute-start(f32[32,128]{1,0:T(8,128)S(1)} %join.4.mine_ref), channel_id=1, source_target_pairs={{0,2},{1,7},{2,0},{3,5},{4,6},{5,3},{6,4},{7,1},{8,10},{9,15},{10,... | collective-permute-start | bytes 49160 | tf_op jit(solution)/shard_map/ppermute | solution.py:43
  52.1 3.9 %collective-permute-start.17 = (f32[32,128]{1,0:T(8,128)S(1)}, f32[32,128]{1,0:T(8,128)S(1)}, u32[]{:S(2)}, u32[]{:S(2)}) collective-permute-start(f32[32,128]{1,0:T(8,128)S(1)} %join.5.mine_ref), channel_id=1, source_target_pairs={{0,8},{1,25},{2,10},{3,27},{4,12},{5,29},{6,14},{7,31},{8,0},{9,17... | collective-permute-start | bytes 49160 | tf_op jit(solution)/shard_map/ppermute | solution.py:43
  56.0 3.9 %collective-permute-start.18 = (f32[32,128]{1,0:T(8,128)S(1)}, f32[32,128]{1,0:T(8,128)S(1)}, u32[]{:S(2)}, u32[]{:S(2)}) collective-permute-start(f32[32,128]{1,0:T(8,128)S(1)} %join.6.mine_ref), channel_id=1, source_target_pairs={{0,32},{1,97},{2,34},{3,99},{4,36},{5,101},{6,38},{7,103},{8,40},{... | collective-permute-start | bytes 49160 | tf_op jit(solution)/shard_map/ppermute | solution.py:43
  59.9 1.5 %collective-permute-start.19 = (f32[32,128]{1,0:T(8,128)S(1)}, f32[32,128]{1,0:T(8,128)S(1)}, u32[]{:S(2)}, u32[]{:S(2)}) collective-permute-start(f32[32,128]{1,0:T(8,128)S(1)} %join.7.mine_ref), channel_id=1, source_target_pairs={{0,1},{1,0},{2,3},{3,2},{4,5},{5,4},{6,7},{7,6},{8,9},{9,8},{10,11... | collective-permute-start | bytes 49160 | tf_op jit(solution)/shard_map/ppermute | solution.py:47
  67.9 3.0 %collective-permute-start.22 = (bf16[512,512]{1,0:T(8,128)(2,1)S(1)}, bf16[512,512]{1,0:T(8,128)(2,1)S(1)}, u32[]{:S(2)}, u32[]{:S(2)}) collective-permute-start(bf16[512,512]{1,0:T(8,128)(2,1)S(1)} %get-tuple-element.101), channel_id=1, source_target_pairs={{0,1},{1,0},{2,3},{3,2},{4,5},{5,4},{6,7},{7,6},{8,9},{9,8},{10,11... | collective-permute-start | bytes 1572872 | tf_op jit(solution)/shard_map/ppermute | solution.py:47
  69.2 4.5 %collective-permute-start.20 = (bf16[512,512]{1,0:T(8,128)(2,1)S(1)}, bf16[512,512]{1,0:T(8,128)(2,1)S(1)}, u32[]{:S(2)}, u32[]{:S(2)}) collective-permute-start(bf16[512,512]{1,0:T(8,128)(2,1)S(1)} %get-tuple-element.94), channel_id=1, source_target_pairs={{0,1},{1,0},{2,3},{3,2},{4,5},{5,4},{6,7},{7,6},{8,9},{9,8},{10,11... | collective-permute-start | bytes 1572872 | tf_op jit(solution)/shard_map/ppermute | solution.py:47
  70.6 5.3 %collective-permute-start.21 = (bf16[512,512]{1,0:T(8,128)(2,1)S(1)}, bf16[512,512]{1,0:T(8,128)(2,1)S(1)}, u32[]{:S(2)}, u32[]{:S(2)}) collective-permute-start(bf16[512,512]{1,0:T(8,128)(2,1)S(1)} %get-tuple-element.98), channel_id=1, source_target_pairs={{0,1},{1,0},{2,3},{3,2},{4,5},{5,4},{6,7},{7,6},{8,9},{9,8},{10,11... | collective-permute-start | bytes 1572872 | tf_op jit(solution)/shard_map/ppermute | solution.py:47
  71.0 11.2 %collective-permute-start.25 = (bf16[512,512]{1,0:T(8,128)(2,1)S(1)}, bf16[512,512]{1,0:T(8,128)(2,1)S(1)}, u32[]{:S(2)}, u32[]{:S(2)}) collective-permute-start(bf16[512,512]{1,0:T(8,128)(2,1)S(1)} %far_message.5.a2), channel_id=1, source_target_pairs={{0,8},{1,25},{2,10},{3,27},{4,12},{5,29},{6,14},{7,31},{8,0},{9,17... | collective-permute-start | bytes 1572872 | tf_op jit(solution)/shard_map/ppermute | solution.py:43
  73.9 11.5 %collective-permute-start.23 = (bf16[528,512]{1,0:T(8,128)(2,1)S(1)}, bf16[528,512]{1,0:T(8,128)(2,1)S(1)}, u32[]{:S(2)}, u32[]{:S(2)}) collective-permute-start(bf16[528,512]{1,0:T(8,128)(2,1)S(1)} %far_message.3.a0), channel_id=1, source_target_pairs={{0,32},{1,97},{2,34},{3,99},{4,36},{5,101},{6,38},{7,103},{8,40},{... | collective-permute-start | bytes 1622024 | tf_op jit(solution)/shard_map/ppermute | solution.py:43
  76.1 9.3 %collective-permute-start.24 = (bf16[512,512]{1,0:T(8,128)(2,1)S(1)}, bf16[512,512]{1,0:T(8,128)(2,1)S(1)}, u32[]{:S(2)}, u32[]{:S(2)}) collective-permute-start(bf16[512,512]{1,0:T(8,128)(2,1)S(1)} %far_message.4.a1), channel_id=1, source_target_pairs={{0,2},{1,7},{2,0},{3,5},{4,6},{5,3},{6,4},{7,1},{8,10},{9,15},{10,... | collective-permute-start | bytes 1572872 | tf_op jit(solution)/shard_map/ppermute | solution.py:43
  79.2 6.5 %collective-permute-start.28 = (bf16[512,512]{1,0:T(8,128)(2,1)S(1)}, bf16[512,512]{1,0:T(8,128)(2,1)S(1)}, u32[]{:S(2)}, u32[]{:S(2)}) collective-permute-start(bf16[512,512]{1,0:T(8,128)(2,1)S(1)} %get-tuple-element.110), channel_id=1, source_target_pairs={{0,1},{1,0},{2,3},{3,2},{4,5},{5,4},{6,7},{7,6},{8,9},{9,8},{10,11... | collective-permute-start | bytes 1572872 | tf_op jit(solution)/shard_map/ppermute | solution.py:47
  81.7 4.0 %collective-permute-start.27 = (bf16[512,512]{1,0:T(8,128)(2,1)S(1)}, bf16[512,512]{1,0:T(8,128)(2,1)S(1)}, u32[]{:S(2)}, u32[]{:S(2)}) collective-permute-start(bf16[512,512]{1,0:T(8,128)(2,1)S(1)} %get-tuple-element.109), channel_id=1, source_target_pairs={{0,1},{1,0},{2,3},{3,2},{4,5},{5,4},{6,7},{7,6},{8,9},{9,8},{10,11... | collective-permute-start | bytes 1572872 | tf_op jit(solution)/shard_map/ppermute | solution.py:47
  82.3 3.5 %collective-permute-start.26 = (bf16[512,512]{1,0:T(8,128)(2,1)S(1)}, bf16[512,512]{1,0:T(8,128)(2,1)S(1)}, u32[]{:S(2)}, u32[]{:S(2)}) collective-permute-start(bf16[512,512]{1,0:T(8,128)(2,1)S(1)} %get-tuple-element.108), channel_id=1, source_target_pairs={{0,1},{1,0},{2,3},{3,2},{4,5},{5,4},{6,7},{7,6},{8,9},{9,8},{10,11... | collective-permute-start | bytes 1572872 | tf_op jit(solution)/shard_map/ppermute | solution.py:47
  86.2 7.8 %collective-permute-start.29 = (bf16[272,512]{1,0:T(8,128)(2,1)S(1)}, bf16[272,512]{1,0:T(8,128)(2,1)S(1)}, u32[]{:S(2)}, u32[]{:S(2)}) collective-permute-start(bf16[272,512]{1,0:T(8,128)(2,1)S(1)} %get-tuple-element.113), channel_id=1, source_target_pairs={{0,8},{1,25},{2,10},{3,27},{4,12},{5,29},{6,14},{7,31},{8,0},{9,17... | collective-permute-start | bytes 835592 | tf_op jit(solution)/shard_map/ppermute | solution.py:43
  86.4 6.4 %collective-permute-start.30 = (bf16[256,512]{1,0:T(8,128)(2,1)S(1)}, bf16[256,512]{1,0:T(8,128)(2,1)S(1)}, u32[]{:S(2)}, u32[]{:S(2)}) collective-permute-start(bf16[256,512]{1,0:T(8,128)(2,1)S(1)} %get-tuple-element.114), channel_id=1, source_target_pairs={{0,32},{1,97},{2,34},{3,99},{4,36},{5,101},{6,38},{7,103},{8,40},{... | collective-permute-start | bytes 786440 | tf_op jit(solution)/shard_map/ppermute | solution.py:43
  87.5 6.4 %collective-permute-start.31 = (bf16[256,512]{1,0:T(8,128)(2,1)S(1)}, bf16[256,512]{1,0:T(8,128)(2,1)S(1)}, u32[]{:S(2)}, u32[]{:S(2)}) collective-permute-start(bf16[256,512]{1,0:T(8,128)(2,1)S(1)} %get-tuple-element.115), channel_id=1, source_target_pairs={{0,2},{1,7},{2,0},{3,5},{4,6},{5,3},{6,4},{7,1},{8,10},{9,15},{10,... | collective-permute-start | bytes 786440 | tf_op jit(solution)/shard_map/ppermute | solution.py:43
  94.1 8.6 %collective-permute-start.32 = (bf16[144,512]{1,0:T(8,128)(2,1)S(1)}, bf16[144,512]{1,0:T(8,128)(2,1)S(1)}, u32[]{:S(2)}, u32[]{:S(2)}) collective-permute-start(bf16[144,512]{1,0:T(8,128)(2,1)S(1)} %get-tuple-element.117), channel_id=1, source_target_pairs={{0,2},{1,7},{2,0},{3,5},{4,6},{5,3},{6,4},{7,1},{8,10},{9,15},{10,... | collective-permute-start | bytes 442376 | tf_op jit(solution)/shard_map/ppermute | solution.py:43
  96.1 5.0 %collective-permute-start.33 = (bf16[128,512]{1,0:T(8,128)(2,1)S(1)}, bf16[128,512]{1,0:T(8,128)(2,1)S(1)}, u32[]{:S(2)}, u32[]{:S(2)}) collective-permute-start(bf16[128,512]{1,0:T(8,128)(2,1)S(1)} %get-tuple-element.118), channel_id=1, source_target_pairs={{0,8},{1,25},{2,10},{3,27},{4,12},{5,29},{6,14},{7,31},{8,0},{9,17... | collective-permute-start | bytes 393224 | tf_op jit(solution)/shard_map/ppermute | solution.py:43
  97.6 5.0 %collective-permute-start.34 = (bf16[128,512]{1,0:T(8,128)(2,1)S(1)}, bf16[128,512]{1,0:T(8,128)(2,1)S(1)}, u32[]{:S(2)}, u32[]{:S(2)}) collective-permute-start(bf16[128,512]{1,0:T(8,128)(2,1)S(1)} %get-tuple-element.119), channel_id=1, source_target_pairs={{0,32},{1,97},{2,34},{3,99},{4,36},{5,101},{6,38},{7,103},{8,40},{... | collective-permute-start | bytes 393224 | tf_op jit(solution)/shard_map/ppermute | solution.py:43
  102.8 2.4 %collective-permute-start.35 = (f32[392,512]{1,0:T(8,128)S(1)}, f32[392,512]{1,0:T(8,128)S(1)}, u32[]{:S(2)}, u32[]{:S(2)}) collective-permute-start(f32[392,512]{1,0:T(8,128)S(1)} %get-tuple-element.125), channel_id=1, source_target_pairs={{0,1},{1,0},{2,3},{3,2},{4,5},{5,4},{6,7},{7,6},{8,9},{9,8},{10,11... | collective-permute-start | bytes 2408456 | tf_op jit(solution)/shard_map/ppermute | solution.py:47

commit v9 on v8

--- a/solution.py
+++ b/solution.py
@@ -19,8 +19,9 @@
 AXES = ("z", "y", "x", "c")
 SWAP = ((0, 1), (1, 0))
 FLIPS = ((0, 0, 1), (0, 1, 0), (1, 0, 0))
-IMAGE_PAIR = (1, 0, 3, 2)
-TEXT_PAIR = (3, 2, 1, 0)
+INNER, OUTER = (1, 0, 3, 2), (3, 2, 1, 0)
+IMAGE_PAIRS = (INNER, OUTER, INNER)
+TEXT_PAIRS = (OUTER, INNER, OUTER)
 VMEM = pl.BlockSpec(memory_space=pltpu.VMEM)
 SMEM = pl.BlockSpec(memory_space=pltpu.SMEM)
 
@@ -28,8 +29,8 @@
 def role_pairs(flip):
     pairs = []
     for z, y, x in itertools.product(range(4), repeat=3):
-        for core, pair in ((0, IMAGE_PAIR), (1, TEXT_PAIR)):
-            target = [pair[v] if f else v for v, f in zip((z, y, x), flip)]
+        for core, pairs_of in ((0, IMAGE_PAIRS), (1, TEXT_PAIRS)):
+            target = [pair[v] if f else v for v, f, pair in zip((z, y, x), flip, pairs_of)]
             source_id = ((z * 4 + y) * 4 + x) * 2 + core
             target_id = ((target[0] * 4 + target[1]) * 4 + target[2]) * 2 + core
             pairs.append((source_id, target_id))

time: 106 us -> 107 us (level)
  waiting for transfers between devices: 35.7 us -> 37 us
    ppermute x21, starting transfers between devices: 37.6 us -> 34 us  [flip_permute(): return lax.ppermute(x, AXES, ROLE_PAIRS[dim % 3])]
    ppermute x15, starting transfers between devices: 5.42 us -> 8.11 us  [core_swap(): return lax.ppermute(x, 'c', SWAP)]
    ppermute x21, waiting for transfers between devices: 27.3 us -> 29.6 us  [flip_permute(): return lax.ppermute(x, AXES, ROLE_PAIRS[dim % 3])]
where the time goes in v9:
time: 107 us
  starting transfers between devices  42.1 us (39%)
  waiting for transfers between devices  37 us (35%)
  Pallas kernels  26.8 us (25%)
    ppermute x21, starting transfers between devices, flip_permute(): return lax.ppermute(x, AXES, ROLE_PAIRS[dim % 3])  34 us
    ppermute x21, waiting for transfers between devices, flip_permute(): return lax.ppermute(x, AXES, ROLE_PAIRS[dim % 3])  29.6 us
    pallas_call x23, Pallas kernels, call(): pl.pallas_call(kernel, in_specs=in_specs, out_specs=[VMEM] * len(outs), o...  25.7 us
    ppermute x15, starting transfers between devices, core_swap(): return lax.ppermute(x, 'c', SWAP)  8.11 us
    ppermute x15, waiting for transfers between devices, core_swap(): return lax.ppermute(x, 'c', SWAP)  7.46 us
  transfers between devices with their start and end apart: 36, of which 22 were waited for; matrix products, arithmetic and copies ran while one was open for 0% of the time, Pallas kernels for 8%

profile of v9, /device:TPU:1, one launch (start us, length us, event | category | flops | bytes accessed | tf_op | source)
XLA Modules:
  0.0 106.7 jit_solution(1020441977987835797)
XLA Ops:
  0.6 1.5 %collective-permute-start = (bf16[192,512]{1,0:T(8,128)(2,1)}, bf16[192,512]{1,0:T(8,128)(2,1)S(1)}, u32[]{:S(2)}, u32[]{:S(2)}) collective-permute-start(bf16[192,512]{1,0:T(8,128)(2,1)} %refs_10_.1), channel_id=1, source_target_pairs={{0,1},{1,0},{2,3},{3,2},{4,5},{5,4},{6,7},{7,6},{8,9},{9,8},{10,11... | collective-permute-start | bytes 589832 | tf_op jit(solution)/shard_map/ppermute | solution.py:48
  2.2 1.2 %collective-permute-done.image_got = bf16[192,512]{1,0:T(8,128)(2,1)S(1)} collective-permute-done((bf16[192,512]{1,0:T(8,128)(2,1)}, bf16[192,512]{1,0:T(8,128)(2,1)S(1)}, u32[]{:S(2)}, u32[]{:S(2)}) %collective-permute-start) | collective-permute-done | bytes 196640 | tf_op jit(solution)/shard_map/ppermute | solution.py:48
  3.8 1.1 %pair.1 = (bf16[128,512]{1,0:T(8,128)(2,1)S(1)}, bf16[128,512]{1,0:T(8,128)(2,1)S(1)}, bf16[128,512]{1,0:T(8,128)(2,1)S(1)}) custom-call(s32[1]{0:T(128)} %bitcast.core_ref, bf16[192,512]{1,0:T(8,128)(2,1)} %refs_10_.1, bf16[192,512]{1,0:T(8,128)(2,1)} %refs_11_.1, bf16[192,512]{1,0:T(8,128)(2,1)S(1)} %collective-permute-done.image_got, ...), custom_call_target="tpu_custom_call" | custom-call | tf_op jit(solution)/shard_map/pair/pallas_call | solution.py:403
  4.9 2.6 %collective-permute-start.2 = (bf16[128,512]{1,0:T(8,128)(2,1)S(1)}, bf16[128,512]{1,0:T(8,128)(2,1)S(1)}, u32[]{:S(2)}, u32[]{:S(2)}) collective-permute-start(bf16[128,512]{1,0:T(8,128)(2,1)S(1)} %get-tuple-element.66.refs_0_), channel_id=1, source_target_pairs={{0,2},{1,7},{2,0},{3,5},{4,6},{5,3},{6,4},{7,1},{8,10},{9,15},{10,... | collective-permute-start | bytes 393224 | tf_op jit(solution)/shard_map/ppermute | solution.py:44
  7.5 1.3 %collective-permute-start.3 = (bf16[128,512]{1,0:T(8,128)(2,1)S(1)}, bf16[128,512]{1,0:T(8,128)(2,1)S(1)}, u32[]{:S(2)}, u32[]{:S(2)}) collective-permute-start(bf16[128,512]{1,0:T(8,128)(2,1)S(1)} %get-tuple-element.67.refs_1_), channel_id=1, source_target_pairs={{0,24},{1,9},{2,26},{3,11},{4,28},{5,13},{6,30},{7,15},{8,16},{9,1... | collective-permute-start | bytes 393224 | tf_op jit(solution)/shard_map/ppermute | solution.py:44
  8.8 3.8 %collective-permute-start.4 = (bf16[128,512]{1,0:T(8,128)(2,1)S(1)}, bf16[128,512]{1,0:T(8,128)(2,1)S(1)}, u32[]{:S(2)}, u32[]{:S(2)}) collective-permute-start(bf16[128,512]{1,0:T(8,128)(2,1)S(1)} %get-tuple-element.68.refs_2_), channel_id=1, source_target_pairs={{0,32},{1,97},{2,34},{3,99},{4,36},{5,101},{6,38},{7,103},{8,40},{... | collective-permute-start | bytes 393224 | tf_op jit(solution)/shard_map/ppermute | solution.py:44
  12.6 2.3 %collective-permute-done.4.refs_5_ = bf16[128,512]{1,0:T(8,128)(2,1)S(1)} collective-permute-done((bf16[128,512]{1,0:T(8,128)(2,1)S(1)}, bf16[128,512]{1,0:T(8,128)(2,1)S(1)}, u32[]{:S(2)}, u32[]{:S(2)}) %collective-permute-start.4) | collective-permute-done | bytes 131104 | tf_op jit(solution)/shard_map/ppermute | solution.py:44
  15.2 2.7 %collective-permute-start.6 = (bf16[256,512]{1,0:T(8,128)(2,1)S(1)}, bf16[256,512]{1,0:T(8,128)(2,1)S(1)}, u32[]{:S(2)}, u32[]{:S(2)}) collective-permute-start(bf16[256,512]{1,0:T(8,128)(2,1)S(1)} %get-tuple-element.70.refs_1_), channel_id=1, source_target_pairs={{0,32},{1,97},{2,34},{3,99},{4,36},{5,101},{6,38},{7,103},{8,40},{... | collective-permute-start | bytes 786440 | tf_op jit(solution)/shard_map/ppermute | solution.py:44
  18.3 2.3 %collective-permute-done.5.refs_3_ = bf16[256,512]{1,0:T(8,128)(2,1)S(1)} collective-permute-done((bf16[256,512]{1,0:T(8,128)(2,1)S(1)}, bf16[256,512]{1,0:T(8,128)(2,1)S(1)}, u32[]{:S(2)}, u32[]{:S(2)}) %collective-permute-start.5) | collective-permute-done | bytes 262176 | tf_op jit(solution)/shard_map/ppermute | solution.py:44
  20.6 1.4 %collective-permute-done.6.refs_4_ = bf16[256,512]{1,0:T(8,128)(2,1)S(1)} collective-permute-done((bf16[256,512]{1,0:T(8,128)(2,1)S(1)}, bf16[256,512]{1,0:T(8,128)(2,1)S(1)}, u32[]{:S(2)}, u32[]{:S(2)}) %collective-permute-start.6) | collective-permute-done | bytes 262176 | tf_op jit(solution)/shard_map/ppermute | solution.py:44
  22.0 2.4 %collective-permute-done.7.refs_5_ = bf16[256,512]{1,0:T(8,128)(2,1)S(1)} collective-permute-done((bf16[256,512]{1,0:T(8,128)(2,1)S(1)}, bf16[256,512]{1,0:T(8,128)(2,1)S(1)}, u32[]{:S(2)}, u32[]{:S(2)}) %collective-permute-start.7) | collective-permute-done | bytes 262176 | tf_op jit(solution)/shard_map/ppermute | solution.py:44
  24.7 2.2 %collective-permute-start.8 = (bf16[512,512]{1,0:T(8,128)(2,1)S(1)}, bf16[512,512]{1,0:T(8,128)(2,1)S(1)}, u32[]{:S(2)}, u32[]{:S(2)}) collective-permute-start(bf16[512,512]{1,0:T(8,128)(2,1)S(1)} %get-tuple-element.72.m0), channel_id=1, source_target_pairs={{0,32},{1,97},{2,34},{3,99},{4,36},{5,101},{6,38},{7,103},{8,40},{... | collective-permute-start | bytes 1572872 | tf_op jit(solution)/shard_map/ppermute | solution.py:44
  27.0 1.8 %collective-permute-start.10 = (bf16[512,512]{1,0:T(8,128)(2,1)S(1)}, bf16[512,512]{1,0:T(8,128)(2,1)S(1)}, u32[]{:S(2)}, u32[]{:S(2)}) collective-permute-start(bf16[512,512]{1,0:T(8,128)(2,1)S(1)} %get-tuple-element.73.m1), channel_id=1, source_target_pairs={{0,2},{1,7},{2,0},{3,5},{4,6},{5,3},{6,4},{7,1},{8,10},{9,15},{10,... | collective-permute-start | bytes 1572872 | tf_op jit(solution)/shard_map/ppermute | solution.py:44
  28.8 2.9 %near.1 = (bf16[768,512]{1,0:T(8,128)(2,1)S(1)}, bf16[1536,512]{1,0:T(8,128)(2,1)S(1)}, f32[768,1536]{1,0:T(8,128)S(1)}, f32[6,128]{1,0:T(8,128)S(1)}, f32[12,128]{1,0:T(8,128)S(1)}) custom-call(s32[1]{0:T(128)} %bitcast.core_ref, bf16[512,512]{1,0:T(8,128)(2,1)S(1)} %get-tuple-element.72.m0, bf16[512,512]{1,0:T(8,128)(2,1)S(1)} %get-tuple-element.73.m1, ...), custom_call_target="tpu_custom_call" | custom-call | flops 1207959552 | tf_op jit(solution)/shard_map/near/pallas_call | solution.py:53
  31.6 2.6 %collective-permute-done.8.value_ref = bf16[512,512]{1,0:T(8,128)(2,1)S(1)} collective-permute-done((bf16[512,512]{1,0:T(8,128)(2,1)S(1)}, bf16[512,512]{1,0:T(8,128)(2,1)S(1)}, u32[]{:S(2)}, u32[]{:S(2)}) %collective-permute-start.8) | collective-permute-done | bytes 524320 | tf_op jit(solution)/shard_map/ppermute | solution.py:44
  34.3 1.9 %collective-permute-done.10.value_ref = bf16[512,512]{1,0:T(8,128)(2,1)S(1)} collective-permute-done((bf16[512,512]{1,0:T(8,128)(2,1)S(1)}, bf16[512,512]{1,0:T(8,128)(2,1)S(1)}, u32[]{:S(2)}, u32[]{:S(2)}) %collective-permute-start.10) | collective-permute-done | bytes 524320 | tf_op jit(solution)/shard_map/ppermute | solution.py:44
  36.8 1.3 %collective-permute-done.13.refs_4_ = bf16[512,512]{1,0:T(8,128)(2,1)S(1)} collective-permute-done((bf16[512,512]{1,0:T(8,128)(2,1)S(1)}, bf16[512,512]{1,0:T(8,128)(2,1)S(1)}, u32[]{:S(2)}, u32[]{:S(2)}) %collective-permute-start.13) | collective-permute-done | bytes 524320 | tf_op jit(solution)/shard_map/ppermute | solution.py:48
  38.1 0.7 collective-permute-done.14.refs_5_
  38.9 8.2 %far.1 = (bf16[768,512]{1,0:T(8,128)(2,1)S(1)}, bf16[1536,512]{1,0:T(8,128)(2,1)S(1)}, f32[256,3072]{1,0:T(8,128)S(1)}, f32[256,3072]{1,0:T(8,128)S(1)}, f32[256...) custom-call(s32[1]{0:T(128)} %bitcast.core_ref, ...), custom_call_target="tpu_custom_call" | custom-call | flops 3623878656 | tf_op jit(solution)/shard_map/far/pallas_call | solution.py:53
  47.3 1.0 collective-permute-done.15.got_ref
  48.4 1.9 %collective-permute-start.16 = (f32[32,128]{1,0:T(8,128)S(1)}, f32[32,128]{1,0:T(8,128)S(1)}, u32[]{:S(2)}, u32[]{:S(2)}) collective-permute-start(f32[32,128]{1,0:T(8,128)S(1)} %join.4.mine_ref), channel_id=1, source_target_pairs={{0,2},{1,7},{2,0},{3,5},{4,6},{5,3},{6,4},{7,1},{8,10},{9,15},{10,... | collective-permute-start | bytes 49160 | tf_op jit(solution)/shard_map/ppermute | solution.py:44
  50.3 2.0 %collective-permute-done.16.got_ref = f32[32,128]{1,0:T(8,128)S(1)} collective-permute-done((f32[32,128]{1,0:T(8,128)S(1)}, f32[32,128]{1,0:T(8,128)S(1)}, u32[]{:S(2)}, u32[]{:S(2)}) %collective-permute-start.16) | collective-permute-done | bytes 16416 | tf_op jit(solution)/shard_map/ppermute | solution.py:44
  52.4 2.6 %collective-permute-done.17.got_ref = f32[32,128]{1,0:T(8,128)S(1)} collective-permute-done((f32[32,128]{1,0:T(8,128)S(1)}, f32[32,128]{1,0:T(8,128)S(1)}, u32[]{:S(2)}, u32[]{:S(2)}) %collective-permute-start.17) | collective-permute-done | bytes 16416 | tf_op jit(solution)/shard_map/ppermute | solution.py:44
  55.0 2.4 %collective-permute-start.18 = (f32[32,128]{1,0:T(8,128)S(1)}, f32[32,128]{1,0:T(8,128)S(1)}, u32[]{:S(2)}, u32[]{:S(2)}) collective-permute-start(f32[32,128]{1,0:T(8,128)S(1)} %join.6.mine_ref), channel_id=1, source_target_pairs={{0,32},{1,97},{2,34},{3,99},{4,36},{5,101},{6,38},{7,103},{8,40},{... | collective-permute-start | bytes 49160 | tf_op jit(solution)/shard_map/ppermute | solution.py:44
  57.4 1.5 %collective-permute-done.18.got_ref = f32[32,128]{1,0:T(8,128)S(1)} collective-permute-done((f32[32,128]{1,0:T(8,128)S(1)}, f32[32,128]{1,0:T(8,128)S(1)}, u32[]{:S(2)}, u32[]{:S(2)}) %collective-permute-start.18) | collective-permute-done | bytes 16416 | tf_op jit(solution)/shard_map/ppermute | solution.py:44
  58.9 2.7 %collective-permute-start.19 = (f32[32,128]{1,0:T(8,128)S(1)}, f32[32,128]{1,0:T(8,128)S(1)}, u32[]{:S(2)}, u32[]{:S(2)}) collective-permute-start(f32[32,128]{1,0:T(8,128)S(1)} %join.7.mine_ref), channel_id=1, source_target_pairs={{0,1},{1,0},{2,3},{3,2},{4,5},{5,4},{6,7},{7,6},{8,9},{9,8},{10,11... | collective-permute-start | bytes 49160 | tf_op jit(solution)/shard_map/ppermute | solution.py:48
  61.6 0.8 collective-permute-done.19.other_ref
  62.4 5.4 %coeffs.1 = (bf16[1536,3072]{1,0:T(8,128)(2,1)S(1)}, bf16[256,512]{1,0:T(8,128)(2,1)S(1)}, bf16[256,512]{1,0:T(8,128)(2,1)S(1)}, bf16[256,512]{1,0:T(8,128)(2,1)...) custom-call(s32[1]{0:T(128)} %bitcast.core_ref, ...), custom_call_target="tpu_custom_call" | custom-call | flops 4831838208 | tf_op jit(solution)/shard_map/coeffs/pallas_call | solution.py:53
  67.8 1.1 far_text.5
  69.3 1.0 far_text.3
  70.6 1.0 far_text.4
  72.5 2.6 %collective-permute-start.23 = (bf16[528,512]{1,0:T(8,128)(2,1)S(1)}, bf16[528,512]{1,0:T(8,128)(2,1)S(1)}, u32[]{:S(2)}, u32[]{:S(2)}) collective-permute-start(bf16[528,512]{1,0:T(8,128)(2,1)S(1)} %far_message.3.a0), channel_id=1, source_target_pairs={{0,32},{1,97},{2,34},{3,99},{4,36},{5,101},{6,38},{7,103},{8,40},{... | collective-permute-start | bytes 1622024 | tf_op jit(solution)/shard_map/ppermute | solution.py:44
  75.3 2.6 %collective-permute-start.24 = (bf16[512,512]{1,0:T(8,128)(2,1)S(1)}, bf16[512,512]{1,0:T(8,128)(2,1)S(1)}, u32[]{:S(2)}, u32[]{:S(2)}) collective-permute-start(bf16[512,512]{1,0:T(8,128)(2,1)S(1)} %far_message.4.a1), channel_id=1, source_target_pairs={{0,2},{1,7},{2,0},{3,5},{4,6},{5,3},{6,4},{7,1},{8,10},{9,15},{10,... | collective-permute-start | bytes 1572872 | tf_op jit(solution)/shard_map/ppermute | solution.py:44
  77.8 1.1 %near_text.5 = (f32[512,512]{1,0:T(8,128)S(1)}, bf16[512,512]{1,0:T(8,128)(2,1)S(1)}, f32[256,512]{1,0:T(8,128)S(1)}) custom-call(s32[1]{0:T(128)} %bitcast.core_ref, bf16[1536,3072]{1,0:T(8,128)(2,1)S(1)} %get-tuple-element.88.coeff_ref, bf16[768,512]{1,0:T(8,128)(2,1)S(1)} %get-tuple-element.77.refs_6_.near_rows, ...), custom_call_target="tpu_custom_call" | custom-call | flops 805306368 | tf_op jit(solution)/shard_map/near_text/pallas_call | solution.py:53
  78.9 1.0 collective-permute-start.28
  79.9 1.1 near_text.4
  80.9 1.1 %near_text.3 = (f32[512,512]{1,0:T(8,128)S(1)}, bf16[512,512]{1,0:T(8,128)(2,1)S(1)}, f32[256,512]{1,0:T(8,128)S(1)}) custom-call(s32[1]{0:T(128)} %bitcast.core_ref, bf16[1536,3072]{1,0:T(8,128)(2,1)S(1)} %get-tuple-element.88.coeff_ref, bf16[768,512]{1,0:T(8,128)(2,1)S(1)} %get-tuple-element.77.refs_6_.near_rows, ...), custom_call_target="tpu_custom_call" | custom-call | flops 805306368 | tf_op jit(solution)/shard_map/near_text/pallas_call | solution.py:53
  82.8 1.8 %collective-permute-done.24.r1 = bf16[512,512]{1,0:T(8,128)(2,1)S(1)} collective-permute-done((bf16[512,512]{1,0:T(8,128)(2,1)S(1)}, bf16[512,512]{1,0:T(8,128)(2,1)S(1)}, u32[]{:S(2)}, u32[]{:S(2)}) %collective-permute-start.24) | collective-permute-done | bytes 524320 | tf_op jit(solution)/shard_map/ppermute | solution.py:44
  85.4 1.5 %collective-permute-start.29 = (bf16[272,512]{1,0:T(8,128)(2,1)S(1)}, bf16[272,512]{1,0:T(8,128)(2,1)S(1)}, u32[]{:S(2)}, u32[]{:S(2)}) collective-permute-start(bf16[272,512]{1,0:T(8,128)(2,1)S(1)} %get-tuple-element.113), channel_id=1, source_target_pairs={{0,24},{1,9},{2,26},{3,11},{4,28},{5,13},{6,30},{7,15},{8,16},{9,1... | collective-permute-start | bytes 835592 | tf_op jit(solution)/shard_map/ppermute | solution.py:44
  87.5 2.5 %collective-permute-start.31 = (bf16[256,512]{1,0:T(8,128)(2,1)S(1)}, bf16[256,512]{1,0:T(8,128)(2,1)S(1)}, u32[]{:S(2)}, u32[]{:S(2)}) collective-permute-start(bf16[256,512]{1,0:T(8,128)(2,1)S(1)} %get-tuple-element.115), channel_id=1, source_target_pairs={{0,2},{1,7},{2,0},{3,5},{4,6},{5,3},{6,4},{7,1},{8,10},{9,15},{10,... | collective-permute-start | bytes 786440 | tf_op jit(solution)/shard_map/ppermute | solution.py:44
  90.0 3.6 %collective-permute-done.30.r1 = bf16[256,512]{1,0:T(8,128)(2,1)S(1)} collective-permute-done((bf16[256,512]{1,0:T(8,128)(2,1)S(1)}, bf16[256,512]{1,0:T(8,128)(2,1)S(1)}, u32[]{:S(2)}, u32[]{:S(2)}) %collective-permute-start.30) | collective-permute-done | bytes 262176 | tf_op jit(solution)/shard_map/ppermute | solution.py:44
  94.1 2.6 %collective-permute-start.32 = (bf16[144,512]{1,0:T(8,128)(2,1)S(1)}, bf16[144,512]{1,0:T(8,128)(2,1)S(1)}, u32[]{:S(2)}, u32[]{:S(2)}) collective-permute-start(bf16[144,512]{1,0:T(8,128)(2,1)S(1)} %get-tuple-element.117), channel_id=1, source_target_pairs={{0,2},{1,7},{2,0},{3,5},{4,6},{5,3},{6,4},{7,1},{8,10},{9,15},{10,... | collective-permute-start | bytes 442376 | tf_op jit(solution)/shard_map/ppermute | solution.py:44
  96.6 1.4 %collective-permute-start.33 = (bf16[128,512]{1,0:T(8,128)(2,1)S(1)}, bf16[128,512]{1,0:T(8,128)(2,1)S(1)}, u32[]{:S(2)}, u32[]{:S(2)}) collective-permute-start(bf16[128,512]{1,0:T(8,128)(2,1)S(1)} %get-tuple-element.118), channel_id=1, source_target_pairs={{0,24},{1,9},{2,26},{3,11},{4,28},{5,13},{6,30},{7,15},{8,16},{9,1... | collective-permute-start | bytes 393224 | tf_op jit(solution)/shard_map/ppermute | solution.py:44
  98.0 0.8 collective-permute-start.34
  98.8 1.7 %collective-permute-done.33.r1 = bf16[128,512]{1,0:T(8,128)(2,1)S(1)} collective-permute-done((bf16[128,512]{1,0:T(8,128)(2,1)S(1)}, bf16[128,512]{1,0:T(8,128)(2,1)S(1)}, u32[]{:S(2)}, u32[]{:S(2)}) %collective-permute-start.33) | collective-permute-done | bytes 131104 | tf_op jit(solution)/shard_map/ppermute | solution.py:44
  100.4 2.7 %collective-permute-done.34.r2 = bf16[128,512]{1,0:T(8,128)(2,1)S(1)} collective-permute-done((bf16[128,512]{1,0:T(8,128)(2,1)S(1)}, bf16[128,512]{1,0:T(8,128)(2,1)S(1)}, u32[]{:S(2)}, u32[]{:S(2)}) %collective-permute-start.34) | collective-permute-done | bytes 131104 | tf_op jit(solution)/shard_map/ppermute | solution.py:44
  103.8 1.9 %collective-permute-done.35.got_ref = f32[392,512]{1,0:T(8,128)S(1)} collective-permute-done((f32[392,512]{1,0:T(8,128)S(1)}, f32[392,512]{1,0:T(8,128)S(1)}, u32[]{:S(2)}, u32[]{:S(2)}) %collective-permute-start.35) | collective-permute-done | bytes 802848 | tf_op jit(solution)/shard_map/ppermute | solution.py:48
  105.7 1.0 finish.1
  (55 shorter events, 7.6 us)
Async XLA Ops:
  0.6 2.8 %collective-permute-start = (bf16[192,512]{1,0:T(8,128)(2,1)}, bf16[192,512]{1,0:T(8,128)(2,1)S(1)}, u32[]{:S(2)}, u32[]{:S(2)}) collective-permute-start(bf16[192,512]{1,0:T(8,128)(2,1)} %refs_10_.1), channel_id=1, source_target_pairs={{0,1},{1,0},{2,3},{3,2},{4,5},{5,4},{6,7},{7,6},{8,9},{9,8},{10,11... | collective-permute-start | bytes 589832 | tf_op jit(solution)/shard_map/ppermute | solution.py:48
  2.1 1.7 %collective-permute-start.1 = (bf16[192,512]{1,0:T(8,128)(2,1)}, bf16[192,512]{1,0:T(8,128)(2,1)S(1)}, u32[]{:S(2)}, u32[]{:S(2)}) collective-permute-start(bf16[192,512]{1,0:T(8,128)(2,1)} %refs_11_.1), channel_id=1, source_target_pairs={{0,1},{1,0},{2,3},{3,2},{4,5},{5,4},{6,7},{7,6},{8,9},{9,8},{10,11... | collective-permute-start | bytes 589832 | tf_op jit(solution)/shard_map/ppermute | solution.py:48
  4.9 7.7 %collective-permute-start.2 = (bf16[128,512]{1,0:T(8,128)(2,1)S(1)}, bf16[128,512]{1,0:T(8,128)(2,1)S(1)}, u32[]{:S(2)}, u32[]{:S(2)}) collective-permute-start(bf16[128,512]{1,0:T(8,128)(2,1)S(1)} %get-tuple-element.66.refs_0_), channel_id=1, source_target_pairs={{0,2},{1,7},{2,0},{3,5},{4,6},{5,3},{6,4},{7,1},{8,10},{9,15},{10,... | collective-permute-start | bytes 393224 | tf_op jit(solution)/shard_map/ppermute | solution.py:44
  7.5 5.1 %collective-permute-start.3 = (bf16[128,512]{1,0:T(8,128)(2,1)S(1)}, bf16[128,512]{1,0:T(8,128)(2,1)S(1)}, u32[]{:S(2)}, u32[]{:S(2)}) collective-permute-start(bf16[128,512]{1,0:T(8,128)(2,1)S(1)} %get-tuple-element.67.refs_1_), channel_id=1, source_target_pairs={{0,24},{1,9},{2,26},{3,11},{4,28},{5,13},{6,30},{7,15},{8,16},{9,1... | collective-permute-start | bytes 393224 | tf_op jit(solution)/shard_map/ppermute | solution.py:44
  8.8 6.1 %collective-permute-start.4 = (bf16[128,512]{1,0:T(8,128)(2,1)S(1)}, bf16[128,512]{1,0:T(8,128)(2,1)S(1)}, u32[]{:S(2)}, u32[]{:S(2)}) collective-permute-start(bf16[128,512]{1,0:T(8,128)(2,1)S(1)} %get-tuple-element.68.refs_2_), channel_id=1, source_target_pairs={{0,32},{1,97},{2,34},{3,99},{4,36},{5,101},{6,38},{7,103},{8,40},{... | collective-permute-start | bytes 393224 | tf_op jit(solution)/shard_map/ppermute | solution.py:44
  15.0 5.6 %collective-permute-start.5 = (bf16[256,512]{1,0:T(8,128)(2,1)S(1)}, bf16[256,512]{1,0:T(8,128)(2,1)S(1)}, u32[]{:S(2)}, u32[]{:S(2)}) collective-permute-start(bf16[256,512]{1,0:T(8,128)(2,1)S(1)} %get-tuple-element.69.refs_0_), channel_id=1, source_target_pairs={{0,24},{1,9},{2,26},{3,11},{4,28},{5,13},{6,30},{7,15},{8,16},{9,1... | collective-permute-start | bytes 786440 | tf_op jit(solution)/shard_map/ppermute | solution.py:44
  15.2 6.7 %collective-permute-start.6 = (bf16[256,512]{1,0:T(8,128)(2,1)S(1)}, bf16[256,512]{1,0:T(8,128)(2,1)S(1)}, u32[]{:S(2)}, u32[]{:S(2)}) collective-permute-start(bf16[256,512]{1,0:T(8,128)(2,1)S(1)} %get-tuple-element.70.refs_1_), channel_id=1, source_target_pairs={{0,32},{1,97},{2,34},{3,99},{4,36},{5,101},{6,38},{7,103},{8,40},{... | collective-permute-start | bytes 786440 | tf_op jit(solution)/shard_map/ppermute | solution.py:44
  17.9 6.4 %collective-permute-start.7 = (bf16[256,512]{1,0:T(8,128)(2,1)S(1)}, bf16[256,512]{1,0:T(8,128)(2,1)S(1)}, u32[]{:S(2)}, u32[]{:S(2)}) collective-permute-start(bf16[256,512]{1,0:T(8,128)(2,1)S(1)} %get-tuple-element.71.refs_2_), channel_id=1, source_target_pairs={{0,2},{1,7},{2,0},{3,5},{4,6},{5,3},{6,4},{7,1},{8,10},{9,15},{10,... | collective-permute-start | bytes 786440 | tf_op jit(solution)/shard_map/ppermute | solution.py:44
  24.5 4.2 %collective-permute-start.9 = (bf16[1536,512]{1,0:T(8,128)(2,1)S(1)}, bf16[1536,512]{1,0:T(8,128)(2,1)S(1)}, u32[]{:S(2)}, u32[]{:S(2)}) collective-permute-start(bf16[1536,512]{1,0:T(8,128)(2,1)S(1)} %get-tuple-element.75), channel_id=1, source_target_pairs={{0,1},{1,0},{2,3},{3,2},{4,5},{5,4},{6,7},{7,6},{8,9},{9,8},{10,11... | collective-permute-start | bytes 4718600 | tf_op jit(solution)/shard_map/ppermute | solution.py:48
  24.7 9.5 %collective-permute-start.8 = (bf16[512,512]{1,0:T(8,128)(2,1)S(1)}, bf16[512,512]{1,0:T(8,128)(2,1)S(1)}, u32[]{:S(2)}, u32[]{:S(2)}) collective-permute-start(bf16[512,512]{1,0:T(8,128)(2,1)S(1)} %get-tuple-element.72.m0), channel_id=1, source_target_pairs={{0,32},{1,97},{2,34},{3,99},{4,36},{5,101},{6,38},{7,103},{8,40},{... | collective-permute-start | bytes 1572872 | tf_op jit(solution)/shard_map/ppermute | solution.py:44
  27.0 9.2 %collective-permute-start.10 = (bf16[512,512]{1,0:T(8,128)(2,1)S(1)}, bf16[512,512]{1,0:T(8,128)(2,1)S(1)}, u32[]{:S(2)}, u32[]{:S(2)}) collective-permute-start(bf16[512,512]{1,0:T(8,128)(2,1)S(1)} %get-tuple-element.73.m1), channel_id=1, source_target_pairs={{0,2},{1,7},{2,0},{3,5},{4,6},{5,3},{6,4},{7,1},{8,10},{9,15},{10,... | collective-permute-start | bytes 1572872 | tf_op jit(solution)/shard_map/ppermute | solution.py:44
  28.8 10.1 %copy-start = (bf16[192,512]{1,0:T(8,128)(2,1)S(1)}, bf16[192,512]{1,0:T(8,128)(2,1)}, u32[]{:S(2)}) copy-start(bf16[192,512]{1,0:T(8,128)(2,1)} %refs_10_.1) | copy-start | bytes 589828
  28.8 10.1 %copy-start.1 = (bf16[192,512]{1,0:T(8,128)(2,1)S(1)}, bf16[192,512]{1,0:T(8,128)(2,1)}, u32[]{:S(2)}) copy-start(bf16[192,512]{1,0:T(8,128)(2,1)} %refs_11_.1) | copy-start | bytes 589828
  28.8 8.0 %collective-permute-start.11 = (bf16[512,512]{1,0:T(8,128)(2,1)S(1)}, bf16[512,512]{1,0:T(8,128)(2,1)S(1)}, u32[]{:S(2)}, u32[]{:S(2)}) collective-permute-start(bf16[512,512]{1,0:T(8,128)(2,1)S(1)} %get-tuple-element.74.m2), channel_id=1, source_target_pairs={{0,24},{1,9},{2,26},{3,11},{4,28},{5,13},{6,30},{7,15},{8,16},{9,1... | collective-permute-start | bytes 1572872 | tf_op jit(solution)/shard_map/ppermute | solution.py:44
  34.3 2.6 %collective-permute-start.12 = (bf16[512,512]{1,0:T(8,128)(2,1)S(1)}, bf16[512,512]{1,0:T(8,128)(2,1)S(1)}, u32[]{:S(2)}, u32[]{:S(2)}) collective-permute-start(bf16[512,512]{1,0:T(8,128)(2,1)S(1)} %after.3.refs_0_), channel_id=1, source_target_pairs={{0,1},{1,0},{2,3},{3,2},{4,5},{5,4},{6,7},{7,6},{8,9},{9,8},{10,11... | collective-permute-start | bytes 1572872 | tf_op jit(solution)/shard_map/ppermute | solution.py:48
  36.2 1.9 %collective-permute-start.13 = (bf16[512,512]{1,0:T(8,128)(2,1)S(1)}, bf16[512,512]{1,0:T(8,128)(2,1)S(1)}, u32[]{:S(2)}, u32[]{:S(2)}) collective-permute-start(bf16[512,512]{1,0:T(8,128)(2,1)S(1)} %after.4.refs_1_), channel_id=1, source_target_pairs={{0,1},{1,0},{2,3},{3,2},{4,5},{5,4},{6,7},{7,6},{8,9},{9,8},{10,11... | collective-permute-start | bytes 1572872 | tf_op jit(solution)/shard_map/ppermute | solution.py:48
  36.8 2.1 %collective-permute-start.14 = (bf16[512,512]{1,0:T(8,128)(2,1)S(1)}, bf16[512,512]{1,0:T(8,128)(2,1)S(1)}, u32[]{:S(2)}, u32[]{:S(2)}) collective-permute-start(bf16[512,512]{1,0:T(8,128)(2,1)S(1)} %after.5.refs_2_), channel_id=1, source_target_pairs={{0,1},{1,0},{2,3},{3,2},{4,5},{5,4},{6,7},{7,6},{8,9},{9,8},{10,11... | collective-permute-start | bytes 1572872 | tf_op jit(solution)/shard_map/ppermute | solution.py:48
  47.1 1.3 %collective-permute-start.15 = (f32[32,128]{1,0:T(8,128)S(1)}, f32[32,128]{1,0:T(8,128)S(1)}, u32[]{:S(2)}, u32[]{:S(2)}) collective-permute-start(f32[32,128]{1,0:T(8,128)S(1)} %get-tuple-element.81), channel_id=1, source_target_pairs={{0,1},{1,0},{2,3},{3,2},{4,5},{5,4},{6,7},{7,6},{8,9},{9,8},{10,11... | collective-permute-start | bytes 49160 | tf_op jit(solution)/shard_map/ppermute | solution.py:48
  48.4 3.9 %collective-permute-start.16 = (f32[32,128]{1,0:T(8,128)S(1)}, f32[32,128]{1,0:T(8,128)S(1)}, u32[]{:S(2)}, u32[]{:S(2)}) collective-permute-start(f32[32,128]{1,0:T(8,128)S(1)} %join.4.mine_ref), channel_id=1, source_target_pairs={{0,2},{1,7},{2,0},{3,5},{4,6},{5,3},{6,4},{7,1},{8,10},{9,15},{10,... | collective-permute-start | bytes 49160 | tf_op jit(solution)/shard_map/ppermute | solution.py:44
  52.3 2.7 %collective-permute-start.17 = (f32[32,128]{1,0:T(8,128)S(1)}, f32[32,128]{1,0:T(8,128)S(1)}, u32[]{:S(2)}, u32[]{:S(2)}) collective-permute-start(f32[32,128]{1,0:T(8,128)S(1)} %join.5.mine_ref), channel_id=1, source_target_pairs={{0,24},{1,9},{2,26},{3,11},{4,28},{5,13},{6,30},{7,15},{8,16},{9,1... | collective-permute-start | bytes 49160 | tf_op jit(solution)/shard_map/ppermute | solution.py:44
  55.0 3.9 %collective-permute-start.18 = (f32[32,128]{1,0:T(8,128)S(1)}, f32[32,128]{1,0:T(8,128)S(1)}, u32[]{:S(2)}, u32[]{:S(2)}) collective-permute-start(f32[32,128]{1,0:T(8,128)S(1)} %join.6.mine_ref), channel_id=1, source_target_pairs={{0,32},{1,97},{2,34},{3,99},{4,36},{5,101},{6,38},{7,103},{8,40},{... | collective-permute-start | bytes 49160 | tf_op jit(solution)/shard_map/ppermute | solution.py:44
  58.9 3.5 %collective-permute-start.19 = (f32[32,128]{1,0:T(8,128)S(1)}, f32[32,128]{1,0:T(8,128)S(1)}, u32[]{:S(2)}, u32[]{:S(2)}) collective-permute-start(f32[32,128]{1,0:T(8,128)S(1)} %join.7.mine_ref), channel_id=1, source_target_pairs={{0,1},{1,0},{2,3},{3,2},{4,5},{5,4},{6,7},{7,6},{8,9},{9,8},{10,11... | collective-permute-start | bytes 49160 | tf_op jit(solution)/shard_map/ppermute | solution.py:48
  68.8 3.2 %collective-permute-start.22 = (bf16[512,512]{1,0:T(8,128)(2,1)S(1)}, bf16[512,512]{1,0:T(8,128)(2,1)S(1)}, u32[]{:S(2)}, u32[]{:S(2)}) collective-permute-start(bf16[512,512]{1,0:T(8,128)(2,1)S(1)} %get-tuple-element.101), channel_id=1, source_target_pairs={{0,1},{1,0},{2,3},{3,2},{4,5},{5,4},{6,7},{7,6},{8,9},{9,8},{10,11... | collective-permute-start | bytes 1572872 | tf_op jit(solution)/shard_map/ppermute | solution.py:48
  70.3 2.0 %collective-permute-start.20 = (bf16[512,512]{1,0:T(8,128)(2,1)S(1)}, bf16[512,512]{1,0:T(8,128)(2,1)S(1)}, u32[]{:S(2)}, u32[]{:S(2)}) collective-permute-start(bf16[512,512]{1,0:T(8,128)(2,1)S(1)} %get-tuple-element.94), channel_id=1, source_target_pairs={{0,1},{1,0},{2,3},{3,2},{4,5},{5,4},{6,7},{7,6},{8,9},{9,8},{10,11... | collective-permute-start | bytes 1572872 | tf_op jit(solution)/shard_map/ppermute | solution.py:48
  71.6 3.5 %collective-permute-start.21 = (bf16[512,512]{1,0:T(8,128)(2,1)S(1)}, bf16[512,512]{1,0:T(8,128)(2,1)S(1)}, u32[]{:S(2)}, u32[]{:S(2)}) collective-permute-start(bf16[512,512]{1,0:T(8,128)(2,1)S(1)} %get-tuple-element.98), channel_id=1, source_target_pairs={{0,1},{1,0},{2,3},{3,2},{4,5},{5,4},{6,7},{7,6},{8,9},{9,8},{10,11... | collective-permute-start | bytes 1572872 | tf_op jit(solution)/shard_map/ppermute | solution.py:48
  72.2 9.9 %collective-permute-start.25 = (bf16[512,512]{1,0:T(8,128)(2,1)S(1)}, bf16[512,512]{1,0:T(8,128)(2,1)S(1)}, u32[]{:S(2)}, u32[]{:S(2)}) collective-permute-start(bf16[512,512]{1,0:T(8,128)(2,1)S(1)} %far_message.5.a2), channel_id=1, source_target_pairs={{0,24},{1,9},{2,26},{3,11},{4,28},{5,13},{6,30},{7,15},{8,16},{9,1... | collective-permute-start | bytes 1572872 | tf_op jit(solution)/shard_map/ppermute | solution.py:44
  72.5 12.1 %collective-permute-start.23 = (bf16[528,512]{1,0:T(8,128)(2,1)S(1)}, bf16[528,512]{1,0:T(8,128)(2,1)S(1)}, u32[]{:S(2)}, u32[]{:S(2)}) collective-permute-start(bf16[528,512]{1,0:T(8,128)(2,1)S(1)} %far_message.3.a0), channel_id=1, source_target_pairs={{0,32},{1,97},{2,34},{3,99},{4,36},{5,101},{6,38},{7,103},{8,40},{... | collective-permute-start | bytes 1622024 | tf_op jit(solution)/shard_map/ppermute | solution.py:44
  75.3 9.3 %collective-permute-start.24 = (bf16[512,512]{1,0:T(8,128)(2,1)S(1)}, bf16[512,512]{1,0:T(8,128)(2,1)S(1)}, u32[]{:S(2)}, u32[]{:S(2)}) collective-permute-start(bf16[512,512]{1,0:T(8,128)(2,1)S(1)} %far_message.4.a1), channel_id=1, source_target_pairs={{0,2},{1,7},{2,0},{3,5},{4,6},{5,3},{6,4},{7,1},{8,10},{9,15},{10,... | collective-permute-start | bytes 1572872 | tf_op jit(solution)/shard_map/ppermute | solution.py:44
  78.9 6.0 %collective-permute-start.28 = (bf16[512,512]{1,0:T(8,128)(2,1)S(1)}, bf16[512,512]{1,0:T(8,128)(2,1)S(1)}, u32[]{:S(2)}, u32[]{:S(2)}) collective-permute-start(bf16[512,512]{1,0:T(8,128)(2,1)S(1)} %get-tuple-element.110), channel_id=1, source_target_pairs={{0,1},{1,0},{2,3},{3,2},{4,5},{5,4},{6,7},{7,6},{8,9},{9,8},{10,11... | collective-permute-start | bytes 1572872 | tf_op jit(solution)/shard_map/ppermute | solution.py:48
  82.0 2.9 %collective-permute-start.27 = (bf16[512,512]{1,0:T(8,128)(2,1)S(1)}, bf16[512,512]{1,0:T(8,128)(2,1)S(1)}, u32[]{:S(2)}, u32[]{:S(2)}) collective-permute-start(bf16[512,512]{1,0:T(8,128)(2,1)S(1)} %get-tuple-element.109), channel_id=1, source_target_pairs={{0,1},{1,0},{2,3},{3,2},{4,5},{5,4},{6,7},{7,6},{8,9},{9,8},{10,11... | collective-permute-start | bytes 1572872 | tf_op jit(solution)/shard_map/ppermute | solution.py:48
  82.1 2.8 %collective-permute-start.26 = (bf16[512,512]{1,0:T(8,128)(2,1)S(1)}, bf16[512,512]{1,0:T(8,128)(2,1)S(1)}, u32[]{:S(2)}, u32[]{:S(2)}) collective-permute-start(bf16[512,512]{1,0:T(8,128)(2,1)S(1)} %get-tuple-element.108), channel_id=1, source_target_pairs={{0,1},{1,0},{2,3},{3,2},{4,5},{5,4},{6,7},{7,6},{8,9},{9,8},{10,11... | collective-permute-start | bytes 1572872 | tf_op jit(solution)/shard_map/ppermute | solution.py:48
  85.4 8.6 %collective-permute-start.29 = (bf16[272,512]{1,0:T(8,128)(2,1)S(1)}, bf16[272,512]{1,0:T(8,128)(2,1)S(1)}, u32[]{:S(2)}, u32[]{:S(2)}) collective-permute-start(bf16[272,512]{1,0:T(8,128)(2,1)S(1)} %get-tuple-element.113), channel_id=1, source_target_pairs={{0,24},{1,9},{2,26},{3,11},{4,28},{5,13},{6,30},{7,15},{8,16},{9,1... | collective-permute-start | bytes 835592 | tf_op jit(solution)/shard_map/ppermute | solution.py:44
  86.9 6.7 %collective-permute-start.30 = (bf16[256,512]{1,0:T(8,128)(2,1)S(1)}, bf16[256,512]{1,0:T(8,128)(2,1)S(1)}, u32[]{:S(2)}, u32[]{:S(2)}) collective-permute-start(bf16[256,512]{1,0:T(8,128)(2,1)S(1)} %get-tuple-element.114), channel_id=1, source_target_pairs={{0,32},{1,97},{2,34},{3,99},{4,36},{5,101},{6,38},{7,103},{8,40},{... | collective-permute-start | bytes 786440 | tf_op jit(solution)/shard_map/ppermute | solution.py:44
  87.5 6.4 %collective-permute-start.31 = (bf16[256,512]{1,0:T(8,128)(2,1)S(1)}, bf16[256,512]{1,0:T(8,128)(2,1)S(1)}, u32[]{:S(2)}, u32[]{:S(2)}) collective-permute-start(bf16[256,512]{1,0:T(8,128)(2,1)S(1)} %get-tuple-element.115), channel_id=1, source_target_pairs={{0,2},{1,7},{2,0},{3,5},{4,6},{5,3},{6,4},{7,1},{8,10},{9,15},{10,... | collective-permute-start | bytes 786440 | tf_op jit(solution)/shard_map/ppermute | solution.py:44
  94.1 9.1 %collective-permute-start.32 = (bf16[144,512]{1,0:T(8,128)(2,1)S(1)}, bf16[144,512]{1,0:T(8,128)(2,1)S(1)}, u32[]{:S(2)}, u32[]{:S(2)}) collective-permute-start(bf16[144,512]{1,0:T(8,128)(2,1)S(1)} %get-tuple-element.117), channel_id=1, source_target_pairs={{0,2},{1,7},{2,0},{3,5},{4,6},{5,3},{6,4},{7,1},{8,10},{9,15},{10,... | collective-permute-start | bytes 442376 | tf_op jit(solution)/shard_map/ppermute | solution.py:44
  96.6 3.8 %collective-permute-start.33 = (bf16[128,512]{1,0:T(8,128)(2,1)S(1)}, bf16[128,512]{1,0:T(8,128)(2,1)S(1)}, u32[]{:S(2)}, u32[]{:S(2)}) collective-permute-start(bf16[128,512]{1,0:T(8,128)(2,1)S(1)} %get-tuple-element.118), channel_id=1, source_target_pairs={{0,24},{1,9},{2,26},{3,11},{4,28},{5,13},{6,30},{7,15},{8,16},{9,1... | collective-permute-start | bytes 393224 | tf_op jit(solution)/shard_map/ppermute | solution.py:44
  98.0 5.1 %collective-permute-start.34 = (bf16[128,512]{1,0:T(8,128)(2,1)S(1)}, bf16[128,512]{1,0:T(8,128)(2,1)S(1)}, u32[]{:S(2)}, u32[]{:S(2)}) collective-permute-start(bf16[128,512]{1,0:T(8,128)(2,1)S(1)} %get-tuple-element.119), channel_id=1, source_target_pairs={{0,32},{1,97},{2,34},{3,99},{4,36},{5,101},{6,38},{7,103},{8,40},{... | collective-permute-start | bytes 393224 | tf_op jit(solution)/shard_map/ppermute | solution.py:44
  103.3 2.4 %collective-permute-start.35 = (f32[392,512]{1,0:T(8,128)S(1)}, f32[392,512]{1,0:T(8,128)S(1)}, u32[]{:S(2)}, u32[]{:S(2)}) collective-permute-start(f32[392,512]{1,0:T(8,128)S(1)} %get-tuple-element.125), channel_id=1, source_target_pairs={{0,1},{1,0},{2,3},{3,2},{4,5},{5,4},{6,7},{7,6},{8,9},{9,8},{10,11... | collective-permute-start | bytes 2408456 | tf_op jit(solution)/shard_map/ppermute | solution.py:48

commit v10 on v8

--- a/solution.py
+++ b/solution.py
@@ -245,47 +245,50 @@
     return lax.dot_general(a, b, CONTRACT_FIRST, preferred_element_type=f32)
 
 
-def coeff_kernel(core_ref, mine_ref, other_ref, *refs):
-    near_ref, tall_ref, *wide_refs = refs[0:5]
-    near_cols, far_cols = refs[5:7]
-    coeff_ref, *grad_refs = refs[7:14]
-    own_ref, loss_ref = refs[14:16]
+def far_coeff_kernel(core_ref, mine_ref, other_ref, *refs):
+    tall_ref, *wide_refs = refs[0:4]
+    near_cols, far_cols = refs[4:6]
+    coeff_ref, *grad_refs = refs[6:10]
+    loss_ref = refs[10]
     first = core_ref[0] == 0
     row, col = tile_lse(first, mine_ref, other_ref)
     loss_ref[...] = jnp.sum(other_ref[0:24, :]) * ln2 - jnp.where(first, 0.0, 2.0) * other_ref[24:32, :]
+    for q in range(3):
+        part = slice(768 + q * 256, 768 + q * 256 + 256)
+        coeff_ref[part, :] = coefficients(wide_refs[q][...], row[:, part], col).astype(bf16)
+        grad = [times(coeff_ref[part, 0:1536], near_cols[...]), times(coeff_ref[part, 1536:3072], far_cols[...])]
+        grad_refs[q][...] = total_of(grad).astype(bf16)
+        part = slice(q * 256, q * 256 + 256)
+        coeff_ref[part, 1536:3072] = coefficients(tall_ref[part, :], row[:, part], col[:, 1536:3072]).astype(bf16)
+
+
+def near_coeff_kernel(core_ref, mine_ref, other_ref, *refs):
+    logit_ref, coeff_ref, near_cols, far_cols = refs[0:4]
+    block_ref, *grad_refs = refs[7:11]
+    own_ref = refs[11]
+    first = core_ref[0] == 0
+    row, col = tile_lse(first, mine_ref, other_ref)
     eye = lax.broadcasted_iota(jnp.int32, (128, 128), 0) == lax.broadcasted_iota(jnp.int32, (128, 128), 1)
     positive = jnp.where(jnp.logical_and(eye, first), 1.0, 0.0)
-    for g in range(6):
-        part = slice(g * 256, g * 256 + 256)
-        if g < 3:
-            coeffs = coefficients(near_ref[part, :], row[:, part], col[:, 0:1536])
-            coeff_ref[part, 0:1536] = coeffs.astype(bf16)
-            own = slice(g * 512, g * 512 + 128)
-            coeff_ref[g * 256 : g * 256 + 128, own] = (coeffs[0:128, own] - positive).astype(bf16)
-            coeff_ref[part, 1536:3072] = coefficients(tall_ref[part, :], row[:, part], col[:, 1536:3072]).astype(bf16)
-        else:
-            coeff_ref[part, :] = coefficients(wide_refs[g - 3][...], row[:, part], col).astype(bf16)
-        grad = total_of(
-            [times(coeff_ref[part, 0:1536], near_cols[...]), times(coeff_ref[part, 1536:3072], far_cols[...])]
-        )
-        grad_refs[g][...] = grad.astype(bf16)
-        if g < 3:
-            own_ref[g * 128 : g * 128 + 128, :] = grad[0:128, :]
-
-
-def text_grad(coeff_ref, near_rows, far_rows, start):
-    here = slice(start, start + 512)
-    return total_of(
-        [
-            transposed_times(coeff_ref[0:768, here], near_rows[...]),
-            transposed_times(coeff_ref[768:1536, here], far_rows[...]),
-        ]
-    )
+    for q in range(3):
+        part = slice(q * 256, q * 256 + 256)
+        coeffs = coefficients(logit_ref[part, :], row[:, part], col[:, 0:1536])
+        block_ref[part, :] = coeffs.astype(bf16)
+        own = slice(q * 512, q * 512 + 128)
+        block_ref[q * 256 : q * 256 + 128, own] = (coeffs[0:128, own] - positive).astype(bf16)
+        grad = total_of([times(block_ref[part, :], near_cols[...]), times(coeff_ref[part, 1536:3072], far_cols[...])])
+        grad_refs[q][...] = grad.astype(bf16)
+        own_ref[q * 128 : q * 128 + 128, :] = grad[0:128, :]
+
+
+def text_grad(near_coeffs, far_coeffs, near_rows, far_rows):
+    return total_of([transposed_times(near_coeffs, near_rows[...]), transposed_times(far_coeffs, far_rows[...])])
 
 
 def far_text_kernel(q, core_ref, coeff_ref, near_rows, far_rows, image_ref, kept_ref, send_ref):
     first = core_ref[0] == 0
-    text = text_grad(coeff_ref, near_rows, far_rows, 1536 + q * 512).astype(bf16)
+    here = slice(1536 + q * 512, 2048 + q * 512)
+    text = text_grad(coeff_ref[0:768, here], coeff_ref[768:1536, here], near_rows, far_rows).astype(bf16)
     image = image_ref[...]
     kept_ref[0:256, :] = jnp.where(first, image, text[0:256])
     send_ref[0:256, :] = jnp.where(first, text[0:256], image)
@@ -293,18 +296,27 @@
     send_ref[256:512, :] = text[256:512]
 
 
-def near_text_kernel(q, core_ref, coeff_ref, near_rows, far_rows, image_ref, own_image, a0, a1, a2, base_ref, send_ref, own_ref):
-    first = core_ref[0] == 0
-    text = text_grad(coeff_ref, near_rows, far_rows, q * 512)
+def near_text_kernel(q, core_ref, block_ref, coeff_ref, near_rows, far_rows, image_ref, base_ref, send_ref, own_ref):
+    first = core_ref[0] == 0
+    here = slice(q * 512, q * 512 + 512)
+    text = text_grad(block_ref[:, here], coeff_ref[768:1536, here], near_rows, far_rows)
     image = image_ref[...].astype(f32)
-    own_ref[0:128, :] = own_image[q * 128 : q * 128 + 128, :]
-    own_ref[128:256, :] = text[0:128]
+    own_ref[...] = text[0:128]
     base_ref[0:128, :] = jnp.where(first, 0.0, text[0:128])
     base_ref[128:256, :] = jnp.where(first, image[128:256], text[128:256])
     base_ref[256:512, :] = jnp.where(first, 0.0, text[256:512])
     send_ref[0:128, :] = jnp.where(first, 0.0, image[0:128]).astype(bf16)
     send_ref[128:256, :] = jnp.where(first, text[128:256], image[128:256]).astype(bf16)
     send_ref[256:512, :] = text[256:512].astype(bf16)
+
+
+def own_kernel(core_ref, image_ref, t0, t1, t2, early_image, early_text, kept_ref):
+    for q, t in enumerate((t0, t1, t2)):
+        rows, text_rows = slice(q * 64, q * 64 + 64), slice(192 + q * 64, 192 + q * 64 + 64)
+        kept_ref[rows, :] = image_ref[q * 128 : q * 128 + 64, :]
+        early_image[rows, :] = image_ref[q * 128 + 64 : q * 128 + 128, :]
+        kept_ref[text_rows, :] = t[0:64, :]
+        early_text[rows, :] = t[64:128, :]
 
 
 def split_terms(x):
@@ -337,7 +349,7 @@
         total_ref[q * 512 : q * 512 + 512, :] = b[...] + r[0:512, :].astype(f32)
 
 
-def near_sum_kernel(core_ref, total_ref, g0, g1, g2, loss_ref, low_ref, s0, s1, s2):
+def near_sum_kernel(core_ref, total_ref, g0, g1, g2, loss_ref, e0, e1, low_ref, s0, s1, s2):
     first = core_ref[0] == 0
     s0[256:272, :] = split_terms(loss_ref[...])
     for q, (g, s) in enumerate(((g0, s0), (g1, s1), (g2, s2))):
@@ -357,27 +369,24 @@
         s[0:128, :] = total[128:256].astype(bf16)
 
 
-def last_sum_kernel(core_ref, low_ref, r0, r1, r2, o0, o1, o2, loss_ref, keep_ref, send_ref):
+def last_sum_kernel(core_ref, low_ref, r0, r1, r2, loss_ref, keep_ref, send_ref):
     first = core_ref[0] == 0
     loss = loss_ref[...] + join_terms(r0, 128)
-    keep_ref[384:392, :] = jnp.concatenate([loss] * 4, 1)
-    send_ref[384:392, :] = jnp.concatenate([loss] * 4, 1)
-    for q, (r, own) in enumerate(((r0, o0), (r1, o1), (r2, o2))):
-        rows, text_rows = slice(q * 64, q * 64 + 64), slice(192 + q * 64, 192 + q * 64 + 64)
+    keep_ref[192:200, :] = jnp.concatenate([loss] * 4, 1)
+    send_ref[192:200, :] = jnp.concatenate([loss] * 4, 1)
+    for q, r in enumerate((r0, r1, r2)):
+        rows = slice(q * 64, q * 64 + 64)
         total = low_ref[q * 128 : q * 128 + 128, :] + r[0:128, :].astype(f32)
-        keep_ref[rows, :] = jnp.where(first, total[0:64] + own[0:64, :], total[64:128])
-        keep_ref[text_rows, :] = own[128:192, :]
-        send_ref[rows, :] = jnp.where(first, total[64:128] + own[64:128, :], total[0:64])
-        send_ref[text_rows, :] = own[192:256, :]
-
-
-def finish_kernel(count, core_ref, keep_ref, got_ref, image_out, text_out, loss_out):
-    first = core_ref[0] == 0
-    image_out[...] = jnp.where(first, keep_ref[0:192, :], got_ref[0:192, :])
-    text_out[...] = jnp.where(
-        first, got_ref[0:192, :] + keep_ref[192:384, :], keep_ref[0:192, :] + got_ref[192:384, :]
-    )
-    loss_out[...] = (keep_ref[384:385, 0:1] + got_ref[384:385, 0:1]) * (0.5 / count)
+        keep_ref[rows, :] = jnp.where(first, total[0:64], total[64:128])
+        send_ref[rows, :] = jnp.where(first, total[64:128], total[0:64])
+
+
+def finish_kernel(count, core_ref, keep_ref, got_ref, kept_ref, early_image, early_text, image_out, text_out, loss_out):
+    first = core_ref[0] == 0
+    keep, got = keep_ref[0:192, :], got_ref[0:192, :]
+    image_out[...] = jnp.where(first, keep, got) + jnp.where(first, kept_ref[0:192, :], early_image[...])
+    text_out[...] = jnp.where(first, got, keep) + jnp.where(first, kept_ref[192:384, :], early_text[...])
+    loss_out[...] = (keep_ref[192:193, 0:1] + got_ref[192:193, 0:1]) * (0.5 / count)
 
 
 def pair_kernel(core_ref, image_hbm, text_hbm, image_got, text_got, o0, o1, o2, image_ref, text_ref, sems):
@@ -461,21 +470,21 @@
     other = core_swap(mine)
 
     held_rows = [held(near_rows), held(far_rows)]
-    coeffs, *image_grads, own_image, loss = call(
-        coeff_kernel,
-        "coeffs",
-        [core_id, mine, other]
-        + [held(a) for a in (near_logits, tall_logits, *wide_logits, near_cols, far_cols)],
-        [pltpu.VMEM((1536, 3072), bf16)] + [shape(256, width, dtype=bf16)] * 6 + [shape(384, width), shape(8, 128)],
+    held_cols = [held(near_cols), held(far_cols)]
+    coeffs, *far_images, loss = call(
+        far_coeff_kernel,
+        "far_coeffs",
+        [core_id, mine, other, held(tall_logits), *[held(a) for a in wide_logits], *held_cols],
+        [pltpu.VMEM((1536, 3072), bf16)] + [shape(256, width, dtype=bf16)] * 3 + [shape(8, 128)],
         limit=10,
-        flops=2 * 1536 * 3072 * width,
+        flops=2 * 768 * 3072 * width,
     )
     messages = []
     for q in range(3):
         kept, send = call(
             functools.partial(far_text_kernel, q),
             "far_text",
-            [core_id, held(coeffs), *held_rows, image_grads[3 + q]],
+            [core_id, held(coeffs), *held_rows, far_images[q]],
             [shape(512, width, dtype=bf16)] * 2,
             limit=6,
             flops=2 * 1536 * 512 * width,
@@ -484,24 +493,36 @@
         outs = [shape(528 if q == 0 else 512, width, dtype=bf16)]
         messages.append(call(far_message_kernel, "far_message", ins, outs)[0])
     got = [flip_permute(messages[q], q + 2) for q in range(3)]
+    block, *near_images, own_image = call(
+        near_coeff_kernel,
+        "near_coeffs",
+        [core_id, mine, other, held(near_logits), held(coeffs), *held_cols, *messages],
+        [pltpu.VMEM((768, 1536), bf16)] + [shape(256, width, dtype=bf16)] * 3 + [shape(384, width)],
+        limit=10,
+        flops=2 * 768 * 3072 * width,
+    )
     bases, near_got, owns = [], [], []
     for q in range(3):
         base, send, own = call(
             functools.partial(near_text_kernel, q),
             "near_text",
-            [core_id, held(coeffs), *held_rows, image_grads[q], own_image, *messages],
-            [shape(512, width), shape(512, width, dtype=bf16), shape(256, width)],
+            [core_id, held(block), held(coeffs), *held_rows, near_images[q]],
+            [shape(512, width), shape(512, width, dtype=bf16), shape(128, width)],
             limit=6,
             flops=2 * 1536 * 512 * width,
         )
         bases.append(base)
         near_got.append(core_swap(send))
         owns.append(own)
+    *early, kept = call(
+        own_kernel, "own", [core_id, own_image, *owns], [shape(192, width), shape(192, width), shape(384, width)]
+    )
+    early_got = [core_swap(a) for a in early]
     total, loss = call(far_sum_kernel, "far_sum", [core_id, *bases, *got, loss], [shape(1536, width), shape(8, 128)])
     low, *messages = call(
         near_sum_kernel,
         "near_sum",
-        [core_id, total, *near_got, loss],
+        [core_id, total, *near_got, loss, *early_got],
         [shape(768, width)] + [shape(272 if q == 0 else 256, width, dtype=bf16) for q in range(3)],
     )
     got = [flip_permute(messages[q], q + 1) for q in range(3)]
@@ -513,12 +534,12 @@
     )
     got = [flip_permute(messages[q], q) for q in range(3)]
     keep, send = call(
-        last_sum_kernel, "last_sum", [core_id, low, *got, *owns, loss], [shape(392, width), shape(392, width)]
+        last_sum_kernel, "last_sum", [core_id, low, *got, loss], [shape(200, width), shape(200, width)]
     )
     grad_image, grad_text, loss = call(
         functools.partial(finish_kernel, count),
         "finish",
-        [core_id, keep, core_swap(send)],
+        [core_id, keep, core_swap(send), kept, *early_got],
         [shape(192, width), shape(192, width), shape(1, 1)],
     )
     return loss.reshape(()), grad_image, grad_text

time: 106 us -> 108 us (1.019)
  Pallas kernels: 26.7 us -> 29.8 us
  starting transfers between devices: 43 us -> 41.2 us
    pallas_call x23 -> x25, Pallas kernels: 25.7 us -> 28.7 us  [call(): pl.pallas_call(kernel, in_specs=in_specs, out_specs=[VMEM] * len(outs), o...]
    ppermute x21, starting transfers between devices: 37.6 us -> 35.1 us  [flip_permute(): return lax.ppermute(x, AXES, ROLE_PAIRS[dim % 3])]
    ppermute x15 -> x17, waiting for transfers between devices: 8.34 us -> 9.93 us  [core_swap(): return lax.ppermute(x, 'c', SWAP)]
    ppermute x21, waiting for transfers between devices: 27.3 us -> 26 us  [flip_permute(): return lax.ppermute(x, AXES, ROLE_PAIRS[dim % 3])]
    ppermute x15 -> x17, starting transfers between devices: 5.42 us -> 6.11 us  [core_swap(): return lax.ppermute(x, 'c', SWAP)]
  transfers between devices with their start and end apart: 36 -> 38, of which waited for: 22 -> 24; matrix products, arithmetic and copies ran while one was open for 0% -> 0% of each run, Pallas kernels for 8% -> 12%
where the time goes in v10:
time: 108 us
  starting transfers between devices  41.2 us (38%)
  waiting for transfers between devices  36 us (33%)
  Pallas kernels  29.8 us (28%)
    ppermute x21, starting transfers between devices, flip_permute(): return lax.ppermute(x, AXES, ROLE_PAIRS[dim % 3])  35.1 us
    pallas_call x25, Pallas kernels, call(): pl.pallas_call(kernel, in_specs=in_specs, out_specs=[VMEM] * len(outs), o...  28.7 us
    ppermute x21, waiting for transfers between devices, flip_permute(): return lax.ppermute(x, AXES, ROLE_PAIRS[dim % 3])  26 us
    ppermute x17, waiting for transfers between devices, core_swap(): return lax.ppermute(x, 'c', SWAP)  9.93 us
    ppermute x17, starting transfers between devices, core_swap(): return lax.ppermute(x, 'c', SWAP)  6.11 us
  transfers between devices with their start and end apart: 38, of which 24 were waited for; matrix products, arithmetic and copies ran while one was open for 0% of the time, Pallas kernels for 12%

profile of v10, /device:TPU:1, one launch (start us, length us, event | category | flops | bytes accessed | tf_op | source)
XLA Modules:
  0.0 107.8 jit_solution(2004408268579802662)
XLA Ops:
  0.6 1.5 %collective-permute-start = (bf16[192,512]{1,0:T(8,128)(2,1)}, bf16[192,512]{1,0:T(8,128)(2,1)S(1)}, u32[]{:S(2)}, u32[]{:S(2)}) collective-permute-start(bf16[192,512]{1,0:T(8,128)(2,1)} %refs_10_.1), channel_id=1, source_target_pairs={{0,1},{1,0},{2,3},{3,2},{4,5},{5,4},{6,7},{7,6},{8,9},{9,8},{10,11... | collective-permute-start | bytes 589832 | tf_op jit(solution)/shard_map/ppermute | solution.py:47
  2.2 1.2 %collective-permute-done.image_got = bf16[192,512]{1,0:T(8,128)(2,1)S(1)} collective-permute-done((bf16[192,512]{1,0:T(8,128)(2,1)}, bf16[192,512]{1,0:T(8,128)(2,1)S(1)}, u32[]{:S(2)}, u32[]{:S(2)}) %collective-permute-start) | collective-permute-done | bytes 196640 | tf_op jit(solution)/shard_map/ppermute | solution.py:47
  3.8 1.1 %pair.1 = (bf16[128,512]{1,0:T(8,128)(2,1)S(1)}, bf16[128,512]{1,0:T(8,128)(2,1)S(1)}, bf16[128,512]{1,0:T(8,128)(2,1)S(1)}) custom-call(s32[1]{0:T(128)} %bitcast.core_ref, bf16[192,512]{1,0:T(8,128)(2,1)} %refs_10_.1, bf16[192,512]{1,0:T(8,128)(2,1)} %refs_11_.1, bf16[192,512]{1,0:T(8,128)(2,1)S(1)} %collective-permute-done.image_got, ...), custom_call_target="tpu_custom_call" | custom-call | tf_op jit(solution)/shard_map/pair/pallas_call | solution.py:411
  4.9 2.6 %collective-permute-start.2 = (bf16[128,512]{1,0:T(8,128)(2,1)S(1)}, bf16[128,512]{1,0:T(8,128)(2,1)S(1)}, u32[]{:S(2)}, u32[]{:S(2)}) collective-permute-start(bf16[128,512]{1,0:T(8,128)(2,1)S(1)} %get-tuple-element.70.refs_0_), channel_id=1, source_target_pairs={{0,2},{1,7},{2,0},{3,5},{4,6},{5,3},{6,4},{7,1},{8,10},{9,15},{10,... | collective-permute-start | bytes 393224 | tf_op jit(solution)/shard_map/ppermute | solution.py:43
  7.5 2.7 %collective-permute-start.3 = (bf16[128,512]{1,0:T(8,128)(2,1)S(1)}, bf16[128,512]{1,0:T(8,128)(2,1)S(1)}, u32[]{:S(2)}, u32[]{:S(2)}) collective-permute-start(bf16[128,512]{1,0:T(8,128)(2,1)S(1)} %get-tuple-element.71.refs_1_), channel_id=1, source_target_pairs={{0,8},{1,25},{2,10},{3,27},{4,12},{5,29},{6,14},{7,31},{8,0},{9,17... | collective-permute-start | bytes 393224 | tf_op jit(solution)/shard_map/ppermute | solution.py:43
  10.2 3.8 %collective-permute-start.4 = (bf16[128,512]{1,0:T(8,128)(2,1)S(1)}, bf16[128,512]{1,0:T(8,128)(2,1)S(1)}, u32[]{:S(2)}, u32[]{:S(2)}) collective-permute-start(bf16[128,512]{1,0:T(8,128)(2,1)S(1)} %get-tuple-element.72.refs_2_), channel_id=1, source_target_pairs={{0,32},{1,97},{2,34},{3,99},{4,36},{5,101},{6,38},{7,103},{8,40},{... | collective-permute-start | bytes 393224 | tf_op jit(solution)/shard_map/ppermute | solution.py:43
  14.0 2.3 %collective-permute-done.4.refs_5_ = bf16[128,512]{1,0:T(8,128)(2,1)S(1)} collective-permute-done((bf16[128,512]{1,0:T(8,128)(2,1)S(1)}, bf16[128,512]{1,0:T(8,128)(2,1)S(1)}, u32[]{:S(2)}, u32[]{:S(2)}) %collective-permute-start.4) | collective-permute-done | bytes 131104 | tf_op jit(solution)/shard_map/ppermute | solution.py:43
  16.5 2.8 %collective-permute-start.6 = (bf16[256,512]{1,0:T(8,128)(2,1)S(1)}, bf16[256,512]{1,0:T(8,128)(2,1)S(1)}, u32[]{:S(2)}, u32[]{:S(2)}) collective-permute-start(bf16[256,512]{1,0:T(8,128)(2,1)S(1)} %get-tuple-element.74.refs_1_), channel_id=1, source_target_pairs={{0,32},{1,97},{2,34},{3,99},{4,36},{5,101},{6,38},{7,103},{8,40},{... | collective-permute-start | bytes 786440 | tf_op jit(solution)/shard_map/ppermute | solution.py:43
  19.5 3.5 %collective-permute-done.5.refs_3_ = bf16[256,512]{1,0:T(8,128)(2,1)S(1)} collective-permute-done((bf16[256,512]{1,0:T(8,128)(2,1)S(1)}, bf16[256,512]{1,0:T(8,128)(2,1)S(1)}, u32[]{:S(2)}, u32[]{:S(2)}) %collective-permute-start.5) | collective-permute-done | bytes 262176 | tf_op jit(solution)/shard_map/ppermute | solution.py:43
  23.0 2.7 %collective-permute-done.7.refs_5_ = bf16[256,512]{1,0:T(8,128)(2,1)S(1)} collective-permute-done((bf16[256,512]{1,0:T(8,128)(2,1)S(1)}, bf16[256,512]{1,0:T(8,128)(2,1)S(1)}, u32[]{:S(2)}, u32[]{:S(2)}) %collective-permute-start.7) | collective-permute-done | bytes 262176 | tf_op jit(solution)/shard_map/ppermute | solution.py:43
  26.6 2.7 %collective-permute-start.11 = (bf16[512,512]{1,0:T(8,128)(2,1)S(1)}, bf16[512,512]{1,0:T(8,128)(2,1)S(1)}, u32[]{:S(2)}, u32[]{:S(2)}) collective-permute-start(bf16[512,512]{1,0:T(8,128)(2,1)S(1)} %get-tuple-element.78.m2), channel_id=1, source_target_pairs={{0,8},{1,25},{2,10},{3,27},{4,12},{5,29},{6,14},{7,31},{8,0},{9,17... | collective-permute-start | bytes 1572872 | tf_op jit(solution)/shard_map/ppermute | solution.py:43
  29.4 3.0 %near.1 = (bf16[768,512]{1,0:T(8,128)(2,1)S(1)}, bf16[1536,512]{1,0:T(8,128)(2,1)S(1)}, f32[768,1536]{1,0:T(8,128)S(1)}, f32[6,128]{1,0:T(8,128)S(1)}, f32[12,128]{1,0:T(8,128)S(1)}) custom-call(s32[1]{0:T(128)} %bitcast.core_ref, bf16[512,512]{1,0:T(8,128)(2,1)S(1)} %get-tuple-element.76.m0, bf16[512,512]{1,0:T(8,128)(2,1)S(1)} %get-tuple-element.77.m1, ...), custom_call_target="tpu_custom_call" | custom-call | flops 1207959552 | tf_op jit(solution)/shard_map/near/pallas_call | solution.py:52
  32.4 2.9 %collective-permute-done.8.value_ref = bf16[512,512]{1,0:T(8,128)(2,1)S(1)} collective-permute-done((bf16[512,512]{1,0:T(8,128)(2,1)S(1)}, bf16[512,512]{1,0:T(8,128)(2,1)S(1)}, u32[]{:S(2)}, u32[]{:S(2)}) %collective-permute-start.8) | collective-permute-done | bytes 524320 | tf_op jit(solution)/shard_map/ppermute | solution.py:43
  36.2 1.0 collective-permute-done.12.refs_3_
  37.2 0.7 collective-permute-done.13.refs_4_
  38.0 0.7 collective-permute-done.14.refs_5_
  38.7 8.7 %far.1 = (bf16[768,512]{1,0:T(8,128)(2,1)S(1)}, bf16[1536,512]{1,0:T(8,128)(2,1)S(1)}, f32[256,3072]{1,0:T(8,128)S(1)}, f32[256,3072]{1,0:T(8,128)S(1)}, f32[256...) custom-call(s32[1]{0:T(128)} %bitcast.core_ref, ...), custom_call_target="tpu_custom_call" | custom-call | flops 3623878656 | tf_op jit(solution)/shard_map/far/pallas_call | solution.py:52
  47.9 0.8 collective-permute-done.15.got_ref
  48.7 1.3 %collective-permute-start.16 = (f32[32,128]{1,0:T(8,128)S(1)}, f32[32,128]{1,0:T(8,128)S(1)}, u32[]{:S(2)}, u32[]{:S(2)}) collective-permute-start(f32[32,128]{1,0:T(8,128)S(1)} %join.4.mine_ref), channel_id=1, source_target_pairs={{0,2},{1,7},{2,0},{3,5},{4,6},{5,3},{6,4},{7,1},{8,10},{9,15},{10,... | collective-permute-start | bytes 49160 | tf_op jit(solution)/shard_map/ppermute | solution.py:43
  50.0 2.5 %collective-permute-done.16.got_ref = f32[32,128]{1,0:T(8,128)S(1)} collective-permute-done((f32[32,128]{1,0:T(8,128)S(1)}, f32[32,128]{1,0:T(8,128)S(1)}, u32[]{:S(2)}, u32[]{:S(2)}) %collective-permute-start.16) | collective-permute-done | bytes 16416 | tf_op jit(solution)/shard_map/ppermute | solution.py:43
  52.6 2.7 %collective-permute-start.17 = (f32[32,128]{1,0:T(8,128)S(1)}, f32[32,128]{1,0:T(8,128)S(1)}, u32[]{:S(2)}, u32[]{:S(2)}) collective-permute-start(f32[32,128]{1,0:T(8,128)S(1)} %join.5.mine_ref), channel_id=1, source_target_pairs={{0,8},{1,25},{2,10},{3,27},{4,12},{5,29},{6,14},{7,31},{8,0},{9,17... | collective-permute-start | bytes 49160 | tf_op jit(solution)/shard_map/ppermute | solution.py:43
  55.3 1.2 %collective-permute-done.17.got_ref = f32[32,128]{1,0:T(8,128)S(1)} collective-permute-done((f32[32,128]{1,0:T(8,128)S(1)}, f32[32,128]{1,0:T(8,128)S(1)}, u32[]{:S(2)}, u32[]{:S(2)}) %collective-permute-start.17) | collective-permute-done | bytes 16416 | tf_op jit(solution)/shard_map/ppermute | solution.py:43
  56.5 2.0 %collective-permute-start.18 = (f32[32,128]{1,0:T(8,128)S(1)}, f32[32,128]{1,0:T(8,128)S(1)}, u32[]{:S(2)}, u32[]{:S(2)}) collective-permute-start(f32[32,128]{1,0:T(8,128)S(1)} %join.6.mine_ref), channel_id=1, source_target_pairs={{0,32},{1,97},{2,34},{3,99},{4,36},{5,101},{6,38},{7,103},{8,40},{... | collective-permute-start | bytes 49160 | tf_op jit(solution)/shard_map/ppermute | solution.py:43
  58.5 1.9 %collective-permute-done.18.got_ref = f32[32,128]{1,0:T(8,128)S(1)} collective-permute-done((f32[32,128]{1,0:T(8,128)S(1)}, f32[32,128]{1,0:T(8,128)S(1)}, u32[]{:S(2)}, u32[]{:S(2)}) %collective-permute-start.18) | collective-permute-done | bytes 16416 | tf_op jit(solution)/shard_map/ppermute | solution.py:43
  60.9 1.0 collective-permute-done.19.other_ref
  61.9 4.2 %far_coeffs.1 = (bf16[1536,3072]{1,0:T(8,128)(2,1)S(1)}, bf16[256,512]{1,0:T(8,128)(2,1)S(1)}, bf16[256,512]{1,0:T(8,128)(2,1)S(1)}, bf16[256,512]{1,0:T(8,128)(2,1)S(1)}, f32[8,128]{1,0:T(8,128)S(1)}) custom-call(s32[1]{0:T(128)} %bitcast.core_ref, f32[32,128]{1,0:T(8,128)S(1)} %join.7.mine_ref, f32[32,128]{1,0:T(8,128)S(1)} %collective-permute-done.19.other_ref, ...), custom_call_target="tpu_custom_call" | custom-call | flops 2415919104 | tf_op jit(solution)/shard_map/far_coeffs/pallas_call | solution.py:52
  66.1 1.1 far_text.3
  67.4 1.0 far_text.5
  68.9 1.0 far_text.4
  70.6 2.7 %collective-permute-start.25 = (bf16[512,512]{1,0:T(8,128)(2,1)S(1)}, bf16[512,512]{1,0:T(8,128)(2,1)S(1)}, u32[]{:S(2)}, u32[]{:S(2)}) collective-permute-start(bf16[512,512]{1,0:T(8,128)(2,1)S(1)} %far_message.5.refs_6_), channel_id=1, source_target_pairs={{0,8},{1,25},{2,10},{3,27},{4,12},{5,29},{6,14},{7,31},{8,0},{9,17... | collective-permute-start | bytes 1572872 | tf_op jit(solution)/shard_map/ppermute | solution.py:43
  73.4 2.0 %collective-permute-start.23 = (bf16[528,512]{1,0:T(8,128)(2,1)S(1)}, bf16[528,512]{1,0:T(8,128)(2,1)S(1)}, u32[]{:S(2)}, u32[]{:S(2)}) collective-permute-start(bf16[528,512]{1,0:T(8,128)(2,1)S(1)} %far_message.3.refs_4_), channel_id=1, source_target_pairs={{0,32},{1,97},{2,34},{3,99},{4,36},{5,101},{6,38},{7,103},{8,40},{... | collective-permute-start | bytes 1622024 | tf_op jit(solution)/shard_map/ppermute | solution.py:43
  75.5 2.0 %collective-permute-start.24 = (bf16[512,512]{1,0:T(8,128)(2,1)S(1)}, bf16[512,512]{1,0:T(8,128)(2,1)S(1)}, u32[]{:S(2)}, u32[]{:S(2)}) collective-permute-start(bf16[512,512]{1,0:T(8,128)(2,1)S(1)} %far_message.4.refs_5_), channel_id=1, source_target_pairs={{0,2},{1,7},{2,0},{3,5},{4,6},{5,3},{6,4},{7,1},{8,10},{9,15},{10,... | collective-permute-start | bytes 1572872 | tf_op jit(solution)/shard_map/ppermute | solution.py:43
  77.5 3.6 %near_coeffs.1 = (bf16[768,1536]{1,0:T(8,128)(2,1)S(1)}, bf16[256,512]{1,0:T(8,128)(2,1)S(1)}, bf16[256,512]{1,0:T(8,128)(2,1)S(1)}, bf16[256,512]{1,0:T(8,128)(2,1)S(1)}, f32[384,512]{1,0:T(8,128)S(1)}) custom-call(s32[1]{0:T(128)} %bitcast.core_ref, f32[32,128]{1,0:T(8,128)S(1)} %join.7.mine_ref, f32[32,128]{1,0:T(8,128)S(1)} %collective-permute-done.19.other_ref, ...), custom_call_target="tpu_custom_call" | custom-call | flops 2415919104 | tf_op jit(solution)/shard_map/near_coeffs/pallas_call | solution.py:52
  81.2 1.1 near_text.3
  82.6 1.1 near_text.4
  84.2 1.0 near_text.5
  86.5 1.3 %collective-permute-done.29.e0.early_image = f32[192,512]{1,0:T(8,128)S(1)} collective-permute-done((f32[192,512]{1,0:T(8,128)S(1)}, f32[192,512]{1,0:T(8,128)S(1)}, u32[]{:S(2)}, u32[]{:S(2)}) %collective-permute-start.29) | collective-permute-done | bytes 393248 | tf_op jit(solution)/shard_map/ppermute | solution.py:47
  89.0 0.9 collective-permute-start.32
  90.0 0.7 collective-permute-start.33
  90.7 4.8 %collective-permute-done.32.r1 = bf16[256,512]{1,0:T(8,128)(2,1)S(1)} collective-permute-done((bf16[256,512]{1,0:T(8,128)(2,1)S(1)}, bf16[256,512]{1,0:T(8,128)(2,1)S(1)}, u32[]{:S(2)}, u32[]{:S(2)}) %collective-permute-start.32) | collective-permute-done | bytes 262176 | tf_op jit(solution)/shard_map/ppermute | solution.py:43
  95.5 0.9 collective-permute-done.33.r2
  96.6 0.8 collective-permute-start.34
  97.4 2.4 %collective-permute-start.35 = (bf16[128,512]{1,0:T(8,128)(2,1)S(1)}, bf16[128,512]{1,0:T(8,128)(2,1)S(1)}, u32[]{:S(2)}, u32[]{:S(2)}) collective-permute-start(bf16[128,512]{1,0:T(8,128)(2,1)S(1)} %get-tuple-element.128), channel_id=1, source_target_pairs={{0,8},{1,25},{2,10},{3,27},{4,12},{5,29},{6,14},{7,31},{8,0},{9,17... | collective-permute-start | bytes 393224 | tf_op jit(solution)/shard_map/ppermute | solution.py:43
  99.8 1.9 %collective-permute-start.36 = (bf16[128,512]{1,0:T(8,128)(2,1)S(1)}, bf16[128,512]{1,0:T(8,128)(2,1)S(1)}, u32[]{:S(2)}, u32[]{:S(2)}) collective-permute-start(bf16[128,512]{1,0:T(8,128)(2,1)S(1)} %get-tuple-element.129), channel_id=1, source_target_pairs={{0,32},{1,97},{2,34},{3,99},{4,36},{5,101},{6,38},{7,103},{8,40},{... | collective-permute-start | bytes 393224 | tf_op jit(solution)/shard_map/ppermute | solution.py:43
  101.7 0.7 collective-permute-done.35.r1
  102.4 2.4 %collective-permute-done.36.r2 = bf16[128,512]{1,0:T(8,128)(2,1)S(1)} collective-permute-done((bf16[128,512]{1,0:T(8,128)(2,1)S(1)}, bf16[128,512]{1,0:T(8,128)(2,1)S(1)}, u32[]{:S(2)}, u32[]{:S(2)}) %collective-permute-start.36) | collective-permute-done | bytes 131104 | tf_op jit(solution)/shard_map/ppermute | solution.py:43
  105.0 1.7 %collective-permute-done.37.got_ref = f32[200,512]{1,0:T(8,128)S(1)} collective-permute-done((f32[200,512]{1,0:T(8,128)S(1)}, f32[200,512]{1,0:T(8,128)S(1)}, u32[]{:S(2)}, u32[]{:S(2)}) %collective-permute-start.37) | collective-permute-done | bytes 409632 | tf_op jit(solution)/shard_map/ppermute | solution.py:47
  106.8 1.1 %finish.1 = (f32[192,512]{1,0:T(8,128)}, f32[192,512]{1,0:T(8,128)}, f32[1,1]{1,0:T(1,128)}) custom-call(s32[1]{0:T(128)} %bitcast.core_ref, f32[200,512]{1,0:T(8,128)S(1)} %get-tuple-element.131.keep_ref, f32[200,512]{1,0:T(8,128)S(1)} %collective-permute-done.37.got_ref, f32[384,512]{1,0:T(8,128)S(1)} %get-tuple-element.133.kept_ref, ...), custom_call_target="tpu_custom_call" | custom-call | tf_op jit(solution)/shard_map/finish/pallas_call | solution.py:52
  (61 shorter events, 9.0 us)
Async XLA Ops:
  0.6 2.8 %collective-permute-start = (bf16[192,512]{1,0:T(8,128)(2,1)}, bf16[192,512]{1,0:T(8,128)(2,1)S(1)}, u32[]{:S(2)}, u32[]{:S(2)}) collective-permute-start(bf16[192,512]{1,0:T(8,128)(2,1)} %refs_10_.1), channel_id=1, source_target_pairs={{0,1},{1,0},{2,3},{3,2},{4,5},{5,4},{6,7},{7,6},{8,9},{9,8},{10,11... | collective-permute-start | bytes 589832 | tf_op jit(solution)/shard_map/ppermute | solution.py:47
  2.1 1.7 %collective-permute-start.1 = (bf16[192,512]{1,0:T(8,128)(2,1)}, bf16[192,512]{1,0:T(8,128)(2,1)S(1)}, u32[]{:S(2)}, u32[]{:S(2)}) collective-permute-start(bf16[192,512]{1,0:T(8,128)(2,1)} %refs_11_.1), channel_id=1, source_target_pairs={{0,1},{1,0},{2,3},{3,2},{4,5},{5,4},{6,7},{7,6},{8,9},{9,8},{10,11... | collective-permute-start | bytes 589832 | tf_op jit(solution)/shard_map/ppermute | solution.py:47
  4.9 9.1 %collective-permute-start.2 = (bf16[128,512]{1,0:T(8,128)(2,1)S(1)}, bf16[128,512]{1,0:T(8,128)(2,1)S(1)}, u32[]{:S(2)}, u32[]{:S(2)}) collective-permute-start(bf16[128,512]{1,0:T(8,128)(2,1)S(1)} %get-tuple-element.70.refs_0_), channel_id=1, source_target_pairs={{0,2},{1,7},{2,0},{3,5},{4,6},{5,3},{6,4},{7,1},{8,10},{9,15},{10,... | collective-permute-start | bytes 393224 | tf_op jit(solution)/shard_map/ppermute | solution.py:43
  7.5 6.5 %collective-permute-start.3 = (bf16[128,512]{1,0:T(8,128)(2,1)S(1)}, bf16[128,512]{1,0:T(8,128)(2,1)S(1)}, u32[]{:S(2)}, u32[]{:S(2)}) collective-permute-start(bf16[128,512]{1,0:T(8,128)(2,1)S(1)} %get-tuple-element.71.refs_1_), channel_id=1, source_target_pairs={{0,8},{1,25},{2,10},{3,27},{4,12},{5,29},{6,14},{7,31},{8,0},{9,17... | collective-permute-start | bytes 393224 | tf_op jit(solution)/shard_map/ppermute | solution.py:43
  10.2 6.1 %collective-permute-start.4 = (bf16[128,512]{1,0:T(8,128)(2,1)S(1)}, bf16[128,512]{1,0:T(8,128)(2,1)S(1)}, u32[]{:S(2)}, u32[]{:S(2)}) collective-permute-start(bf16[128,512]{1,0:T(8,128)(2,1)S(1)} %get-tuple-element.72.refs_2_), channel_id=1, source_target_pairs={{0,32},{1,97},{2,34},{3,99},{4,36},{5,101},{6,38},{7,103},{8,40},{... | collective-permute-start | bytes 393224 | tf_op jit(solution)/shard_map/ppermute | solution.py:43
  16.4 6.5 %collective-permute-start.5 = (bf16[256,512]{1,0:T(8,128)(2,1)S(1)}, bf16[256,512]{1,0:T(8,128)(2,1)S(1)}, u32[]{:S(2)}, u32[]{:S(2)}) collective-permute-start(bf16[256,512]{1,0:T(8,128)(2,1)S(1)} %get-tuple-element.73.refs_0_), channel_id=1, source_target_pairs={{0,8},{1,25},{2,10},{3,27},{4,12},{5,29},{6,14},{7,31},{8,0},{9,17... | collective-permute-start | bytes 786440 | tf_op jit(solution)/shard_map/ppermute | solution.py:43
  16.5 6.5 %collective-permute-start.6 = (bf16[256,512]{1,0:T(8,128)(2,1)S(1)}, bf16[256,512]{1,0:T(8,128)(2,1)S(1)}, u32[]{:S(2)}, u32[]{:S(2)}) collective-permute-start(bf16[256,512]{1,0:T(8,128)(2,1)S(1)} %get-tuple-element.74.refs_1_), channel_id=1, source_target_pairs={{0,32},{1,97},{2,34},{3,99},{4,36},{5,101},{6,38},{7,103},{8,40},{... | collective-permute-start | bytes 786440 | tf_op jit(solution)/shard_map/ppermute | solution.py:43
  19.3 6.4 %collective-permute-start.7 = (bf16[256,512]{1,0:T(8,128)(2,1)S(1)}, bf16[256,512]{1,0:T(8,128)(2,1)S(1)}, u32[]{:S(2)}, u32[]{:S(2)}) collective-permute-start(bf16[256,512]{1,0:T(8,128)(2,1)S(1)} %get-tuple-element.75.refs_2_), channel_id=1, source_target_pairs={{0,2},{1,7},{2,0},{3,5},{4,6},{5,3},{6,4},{7,1},{8,10},{9,15},{10,... | collective-permute-start | bytes 786440 | tf_op jit(solution)/shard_map/ppermute | solution.py:43
  25.9 3.5 %collective-permute-start.9 = (bf16[1536,512]{1,0:T(8,128)(2,1)S(1)}, bf16[1536,512]{1,0:T(8,128)(2,1)S(1)}, u32[]{:S(2)}, u32[]{:S(2)}) collective-permute-start(bf16[1536,512]{1,0:T(8,128)(2,1)S(1)} %get-tuple-element.79), channel_id=1, source_target_pairs={{0,1},{1,0},{2,3},{3,2},{4,5},{5,4},{6,7},{7,6},{8,9},{9,8},{10,11... | collective-permute-start | bytes 4718600 | tf_op jit(solution)/shard_map/ppermute | solution.py:47
  26.0 9.3 %collective-permute-start.8 = (bf16[512,512]{1,0:T(8,128)(2,1)S(1)}, bf16[512,512]{1,0:T(8,128)(2,1)S(1)}, u32[]{:S(2)}, u32[]{:S(2)}) collective-permute-start(bf16[512,512]{1,0:T(8,128)(2,1)S(1)} %get-tuple-element.76.m0), channel_id=1, source_target_pairs={{0,32},{1,97},{2,34},{3,99},{4,36},{5,101},{6,38},{7,103},{8,40},{... | collective-permute-start | bytes 1572872 | tf_op jit(solution)/shard_map/ppermute | solution.py:43
  26.2 9.5 %collective-permute-start.10 = (bf16[512,512]{1,0:T(8,128)(2,1)S(1)}, bf16[512,512]{1,0:T(8,128)(2,1)S(1)}, u32[]{:S(2)}, u32[]{:S(2)}) collective-permute-start(bf16[512,512]{1,0:T(8,128)(2,1)S(1)} %get-tuple-element.77.m1), channel_id=1, source_target_pairs={{0,2},{1,7},{2,0},{3,5},{4,6},{5,3},{6,4},{7,1},{8,10},{9,15},{10,... | collective-permute-start | bytes 1572872 | tf_op jit(solution)/shard_map/ppermute | solution.py:43
  26.6 12.2 %copy-start = (bf16[192,512]{1,0:T(8,128)(2,1)S(1)}, bf16[192,512]{1,0:T(8,128)(2,1)}, u32[]{:S(2)}) copy-start(bf16[192,512]{1,0:T(8,128)(2,1)} %refs_10_.1) | copy-start | bytes 589828
  26.6 12.2 %copy-start.1 = (bf16[192,512]{1,0:T(8,128)(2,1)S(1)}, bf16[192,512]{1,0:T(8,128)(2,1)}, u32[]{:S(2)}) copy-start(bf16[192,512]{1,0:T(8,128)(2,1)} %refs_11_.1) | copy-start | bytes 589828
  26.6 9.3 %collective-permute-start.11 = (bf16[512,512]{1,0:T(8,128)(2,1)S(1)}, bf16[512,512]{1,0:T(8,128)(2,1)S(1)}, u32[]{:S(2)}, u32[]{:S(2)}) collective-permute-start(bf16[512,512]{1,0:T(8,128)(2,1)S(1)} %get-tuple-element.78.m2), channel_id=1, source_target_pairs={{0,8},{1,25},{2,10},{3,27},{4,12},{5,29},{6,14},{7,31},{8,0},{9,17... | collective-permute-start | bytes 1572872 | tf_op jit(solution)/shard_map/ppermute | solution.py:43
  35.3 1.9 %collective-permute-start.12 = (bf16[512,512]{1,0:T(8,128)(2,1)S(1)}, bf16[512,512]{1,0:T(8,128)(2,1)S(1)}, u32[]{:S(2)}, u32[]{:S(2)}) collective-permute-start(bf16[512,512]{1,0:T(8,128)(2,1)S(1)} %after.3.refs_0_), channel_id=1, source_target_pairs={{0,1},{1,0},{2,3},{3,2},{4,5},{5,4},{6,7},{7,6},{8,9},{9,8},{10,11... | collective-permute-start | bytes 1572872 | tf_op jit(solution)/shard_map/ppermute | solution.py:47
  35.7 2.3 %collective-permute-start.13 = (bf16[512,512]{1,0:T(8,128)(2,1)S(1)}, bf16[512,512]{1,0:T(8,128)(2,1)S(1)}, u32[]{:S(2)}, u32[]{:S(2)}) collective-permute-start(bf16[512,512]{1,0:T(8,128)(2,1)S(1)} %after.4.refs_1_), channel_id=1, source_target_pairs={{0,1},{1,0},{2,3},{3,2},{4,5},{5,4},{6,7},{7,6},{8,9},{9,8},{10,11... | collective-permute-start | bytes 1572872 | tf_op jit(solution)/shard_map/ppermute | solution.py:47
  35.9 2.8 %collective-permute-start.14 = (bf16[512,512]{1,0:T(8,128)(2,1)S(1)}, bf16[512,512]{1,0:T(8,128)(2,1)S(1)}, u32[]{:S(2)}, u32[]{:S(2)}) collective-permute-start(bf16[512,512]{1,0:T(8,128)(2,1)S(1)} %after.5.refs_2_), channel_id=1, source_target_pairs={{0,1},{1,0},{2,3},{3,2},{4,5},{5,4},{6,7},{7,6},{8,9},{9,8},{10,11... | collective-permute-start | bytes 1572872 | tf_op jit(solution)/shard_map/ppermute | solution.py:47
  47.4 1.3 %collective-permute-start.15 = (f32[32,128]{1,0:T(8,128)S(1)}, f32[32,128]{1,0:T(8,128)S(1)}, u32[]{:S(2)}, u32[]{:S(2)}) collective-permute-start(f32[32,128]{1,0:T(8,128)S(1)} %get-tuple-element.85), channel_id=1, source_target_pairs={{0,1},{1,0},{2,3},{3,2},{4,5},{5,4},{6,7},{7,6},{8,9},{9,8},{10,11... | collective-permute-start | bytes 49160 | tf_op jit(solution)/shard_map/ppermute | solution.py:47
  48.7 3.9 %collective-permute-start.16 = (f32[32,128]{1,0:T(8,128)S(1)}, f32[32,128]{1,0:T(8,128)S(1)}, u32[]{:S(2)}, u32[]{:S(2)}) collective-permute-start(f32[32,128]{1,0:T(8,128)S(1)} %join.4.mine_ref), channel_id=1, source_target_pairs={{0,2},{1,7},{2,0},{3,5},{4,6},{5,3},{6,4},{7,1},{8,10},{9,15},{10,... | collective-permute-start | bytes 49160 | tf_op jit(solution)/shard_map/ppermute | solution.py:43
  52.6 3.9 %collective-permute-start.17 = (f32[32,128]{1,0:T(8,128)S(1)}, f32[32,128]{1,0:T(8,128)S(1)}, u32[]{:S(2)}, u32[]{:S(2)}) collective-permute-start(f32[32,128]{1,0:T(8,128)S(1)} %join.5.mine_ref), channel_id=1, source_target_pairs={{0,8},{1,25},{2,10},{3,27},{4,12},{5,29},{6,14},{7,31},{8,0},{9,17... | collective-permute-start | bytes 49160 | tf_op jit(solution)/shard_map/ppermute | solution.py:43
  56.5 3.9 %collective-permute-start.18 = (f32[32,128]{1,0:T(8,128)S(1)}, f32[32,128]{1,0:T(8,128)S(1)}, u32[]{:S(2)}, u32[]{:S(2)}) collective-permute-start(f32[32,128]{1,0:T(8,128)S(1)} %join.6.mine_ref), channel_id=1, source_target_pairs={{0,32},{1,97},{2,34},{3,99},{4,36},{5,101},{6,38},{7,103},{8,40},{... | collective-permute-start | bytes 49160 | tf_op jit(solution)/shard_map/ppermute | solution.py:43
  60.4 1.5 %collective-permute-start.19 = (f32[32,128]{1,0:T(8,128)S(1)}, f32[32,128]{1,0:T(8,128)S(1)}, u32[]{:S(2)}, u32[]{:S(2)}) collective-permute-start(f32[32,128]{1,0:T(8,128)S(1)} %join.7.mine_ref), channel_id=1, source_target_pairs={{0,1},{1,0},{2,3},{3,2},{4,5},{5,4},{6,7},{7,6},{8,9},{9,8},{10,11... | collective-permute-start | bytes 49160 | tf_op jit(solution)/shard_map/ppermute | solution.py:47
  67.2 6.1 %collective-permute-start.20 = (bf16[512,512]{1,0:T(8,128)(2,1)S(1)}, bf16[512,512]{1,0:T(8,128)(2,1)S(1)}, u32[]{:S(2)}, u32[]{:S(2)}) collective-permute-start(bf16[512,512]{1,0:T(8,128)(2,1)S(1)} %get-tuple-element.96), channel_id=1, source_target_pairs={{0,1},{1,0},{2,3},{3,2},{4,5},{5,4},{6,7},{7,6},{8,9},{9,8},{10,11... | collective-permute-start | bytes 1572872 | tf_op jit(solution)/shard_map/ppermute | solution.py:47
  68.5 2.0 %collective-permute-start.22 = (bf16[512,512]{1,0:T(8,128)(2,1)S(1)}, bf16[512,512]{1,0:T(8,128)(2,1)S(1)}, u32[]{:S(2)}, u32[]{:S(2)}) collective-permute-start(bf16[512,512]{1,0:T(8,128)(2,1)S(1)} %get-tuple-element.103), channel_id=1, source_target_pairs={{0,1},{1,0},{2,3},{3,2},{4,5},{5,4},{6,7},{7,6},{8,9},{9,8},{10,11... | collective-permute-start | bytes 1572872 | tf_op jit(solution)/shard_map/ppermute | solution.py:47
  69.9 5.5 %collective-permute-start.21 = (bf16[512,512]{1,0:T(8,128)(2,1)S(1)}, bf16[512,512]{1,0:T(8,128)(2,1)S(1)}, u32[]{:S(2)}, u32[]{:S(2)}) collective-permute-start(bf16[512,512]{1,0:T(8,128)(2,1)S(1)} %get-tuple-element.100), channel_id=1, source_target_pairs={{0,1},{1,0},{2,3},{3,2},{4,5},{5,4},{6,7},{7,6},{8,9},{9,8},{10,11... | collective-permute-start | bytes 1572872 | tf_op jit(solution)/shard_map/ppermute | solution.py:47
  70.6 14.7 %collective-permute-start.25 = (bf16[512,512]{1,0:T(8,128)(2,1)S(1)}, bf16[512,512]{1,0:T(8,128)(2,1)S(1)}, u32[]{:S(2)}, u32[]{:S(2)}) collective-permute-start(bf16[512,512]{1,0:T(8,128)(2,1)S(1)} %far_message.5.refs_6_), channel_id=1, source_target_pairs={{0,8},{1,25},{2,10},{3,27},{4,12},{5,29},{6,14},{7,31},{8,0},{9,17... | collective-permute-start | bytes 1572872 | tf_op jit(solution)/shard_map/ppermute | solution.py:43
  73.4 12.7 %collective-permute-start.23 = (bf16[528,512]{1,0:T(8,128)(2,1)S(1)}, bf16[528,512]{1,0:T(8,128)(2,1)S(1)}, u32[]{:S(2)}, u32[]{:S(2)}) collective-permute-start(bf16[528,512]{1,0:T(8,128)(2,1)S(1)} %far_message.3.refs_4_), channel_id=1, source_target_pairs={{0,32},{1,97},{2,34},{3,99},{4,36},{5,101},{6,38},{7,103},{8,40},{... | collective-permute-start | bytes 1622024 | tf_op jit(solution)/shard_map/ppermute | solution.py:43
  75.5 9.9 %collective-permute-start.24 = (bf16[512,512]{1,0:T(8,128)(2,1)S(1)}, bf16[512,512]{1,0:T(8,128)(2,1)S(1)}, u32[]{:S(2)}, u32[]{:S(2)}) collective-permute-start(bf16[512,512]{1,0:T(8,128)(2,1)S(1)} %far_message.4.refs_5_), channel_id=1, source_target_pairs={{0,2},{1,7},{2,0},{3,5},{4,6},{5,3},{6,4},{7,1},{8,10},{9,15},{10,... | collective-permute-start | bytes 1572872 | tf_op jit(solution)/shard_map/ppermute | solution.py:43
  82.2 6.2 %collective-permute-start.26 = (bf16[512,512]{1,0:T(8,128)(2,1)S(1)}, bf16[512,512]{1,0:T(8,128)(2,1)S(1)}, u32[]{:S(2)}, u32[]{:S(2)}) collective-permute-start(bf16[512,512]{1,0:T(8,128)(2,1)S(1)} %get-tuple-element.112), channel_id=1, source_target_pairs={{0,1},{1,0},{2,3},{3,2},{4,5},{5,4},{6,7},{7,6},{8,9},{9,8},{10,11... | collective-permute-start | bytes 1572872 | tf_op jit(solution)/shard_map/ppermute | solution.py:47
  83.6 4.8 %collective-permute-start.27 = (bf16[512,512]{1,0:T(8,128)(2,1)S(1)}, bf16[512,512]{1,0:T(8,128)(2,1)S(1)}, u32[]{:S(2)}, u32[]{:S(2)}) collective-permute-start(bf16[512,512]{1,0:T(8,128)(2,1)S(1)} %get-tuple-element.113), channel_id=1, source_target_pairs={{0,1},{1,0},{2,3},{3,2},{4,5},{5,4},{6,7},{7,6},{8,9},{9,8},{10,11... | collective-permute-start | bytes 1572872 | tf_op jit(solution)/shard_map/ppermute | solution.py:47
  85.3 3.1 %collective-permute-start.28 = (bf16[512,512]{1,0:T(8,128)(2,1)S(1)}, bf16[512,512]{1,0:T(8,128)(2,1)S(1)}, u32[]{:S(2)}, u32[]{:S(2)}) collective-permute-start(bf16[512,512]{1,0:T(8,128)(2,1)S(1)} %get-tuple-element.114), channel_id=1, source_target_pairs={{0,1},{1,0},{2,3},{3,2},{4,5},{5,4},{6,7},{7,6},{8,9},{9,8},{10,11... | collective-permute-start | bytes 1572872 | tf_op jit(solution)/shard_map/ppermute | solution.py:47
  85.5 2.3 %collective-permute-start.29 = (f32[192,512]{1,0:T(8,128)S(1)}, f32[192,512]{1,0:T(8,128)S(1)}, u32[]{:S(2)}, u32[]{:S(2)}) collective-permute-start(f32[192,512]{1,0:T(8,128)S(1)} %get-tuple-element.120), channel_id=1, source_target_pairs={{0,1},{1,0},{2,3},{3,2},{4,5},{5,4},{6,7},{7,6},{8,9},{9,8},{10,11... | collective-permute-start | bytes 1179656 | tf_op jit(solution)/shard_map/ppermute | solution.py:47
  86.1 2.3 %collective-permute-start.30 = (f32[192,512]{1,0:T(8,128)S(1)}, f32[192,512]{1,0:T(8,128)S(1)}, u32[]{:S(2)}, u32[]{:S(2)}) collective-permute-start(f32[192,512]{1,0:T(8,128)S(1)} %get-tuple-element.121), channel_id=1, source_target_pairs={{0,1},{1,0},{2,3},{3,2},{4,5},{5,4},{6,7},{7,6},{8,9},{9,8},{10,11... | collective-permute-start | bytes 1179656 | tf_op jit(solution)/shard_map/ppermute | solution.py:47
  88.9 7.5 %collective-permute-start.31 = (bf16[272,512]{1,0:T(8,128)(2,1)S(1)}, bf16[272,512]{1,0:T(8,128)(2,1)S(1)}, u32[]{:S(2)}, u32[]{:S(2)}) collective-permute-start(bf16[272,512]{1,0:T(8,128)(2,1)S(1)} %get-tuple-element.123), channel_id=1, source_target_pairs={{0,8},{1,25},{2,10},{3,27},{4,12},{5,29},{6,14},{7,31},{8,0},{9,17... | collective-permute-start | bytes 835592 | tf_op jit(solution)/shard_map/ppermute | solution.py:43
  89.0 6.4 %collective-permute-start.32 = (bf16[256,512]{1,0:T(8,128)(2,1)S(1)}, bf16[256,512]{1,0:T(8,128)(2,1)S(1)}, u32[]{:S(2)}, u32[]{:S(2)}) collective-permute-start(bf16[256,512]{1,0:T(8,128)(2,1)S(1)} %get-tuple-element.124), channel_id=1, source_target_pairs={{0,32},{1,97},{2,34},{3,99},{4,36},{5,101},{6,38},{7,103},{8,40},{... | collective-permute-start | bytes 786440 | tf_op jit(solution)/shard_map/ppermute | solution.py:43
  90.0 6.4 %collective-permute-start.33 = (bf16[256,512]{1,0:T(8,128)(2,1)S(1)}, bf16[256,512]{1,0:T(8,128)(2,1)S(1)}, u32[]{:S(2)}, u32[]{:S(2)}) collective-permute-start(bf16[256,512]{1,0:T(8,128)(2,1)S(1)} %get-tuple-element.125), channel_id=1, source_target_pairs={{0,2},{1,7},{2,0},{3,5},{4,6},{5,3},{6,4},{7,1},{8,10},{9,15},{10,... | collective-permute-start | bytes 786440 | tf_op jit(solution)/shard_map/ppermute | solution.py:43
  96.6 8.3 %collective-permute-start.34 = (bf16[144,512]{1,0:T(8,128)(2,1)S(1)}, bf16[144,512]{1,0:T(8,128)(2,1)S(1)}, u32[]{:S(2)}, u32[]{:S(2)}) collective-permute-start(bf16[144,512]{1,0:T(8,128)(2,1)S(1)} %get-tuple-element.127), channel_id=1, source_target_pairs={{0,2},{1,7},{2,0},{3,5},{4,6},{5,3},{6,4},{7,1},{8,10},{9,15},{10,... | collective-permute-start | bytes 442376 | tf_op jit(solution)/shard_map/ppermute | solution.py:43
  97.4 5.0 %collective-permute-start.35 = (bf16[128,512]{1,0:T(8,128)(2,1)S(1)}, bf16[128,512]{1,0:T(8,128)(2,1)S(1)}, u32[]{:S(2)}, u32[]{:S(2)}) collective-permute-start(bf16[128,512]{1,0:T(8,128)(2,1)S(1)} %get-tuple-element.128), channel_id=1, source_target_pairs={{0,8},{1,25},{2,10},{3,27},{4,12},{5,29},{6,14},{7,31},{8,0},{9,17... | collective-permute-start | bytes 393224 | tf_op jit(solution)/shard_map/ppermute | solution.py:43
  99.8 5.0 %collective-permute-start.36 = (bf16[128,512]{1,0:T(8,128)(2,1)S(1)}, bf16[128,512]{1,0:T(8,128)(2,1)S(1)}, u32[]{:S(2)}, u32[]{:S(2)}) collective-permute-start(bf16[128,512]{1,0:T(8,128)(2,1)S(1)} %get-tuple-element.129), channel_id=1, source_target_pairs={{0,32},{1,97},{2,34},{3,99},{4,36},{5,101},{6,38},{7,103},{8,40},{... | collective-permute-start | bytes 393224 | tf_op jit(solution)/shard_map/ppermute | solution.py:43
  104.9 1.8 %collective-permute-start.37 = (f32[200,512]{1,0:T(8,128)S(1)}, f32[200,512]{1,0:T(8,128)S(1)}, u32[]{:S(2)}, u32[]{:S(2)}) collective-permute-start(f32[200,512]{1,0:T(8,128)S(1)} %get-tuple-element.132), channel_id=1, source_target_pairs={{0,1},{1,0},{2,3},{3,2},{4,5},{5,4},{6,7},{7,6},{8,9},{9,8},{10,11... | collective-permute-start | bytes 1228808 | tf_op jit(solution)/shard_map/ppermute | solution.py:47

commit v11 on v8

--- a/solution.py
+++ b/solution.py
@@ -331,40 +331,45 @@
         refs[-1][512:528, :] = split_terms(refs[0][...])
 
 
-def far_sum_kernel(core_ref, b0, b1, b2, r0, r1, r2, loss_ref, total_ref, loss_out):
-    loss_out[...] = loss_ref[...] + join_terms(r0, 512)
-    for q, (b, r) in enumerate(((b0, r0), (b1, r1), (b2, r2))):
-        total_ref[q * 512 : q * 512 + 512, :] = b[...] + r[0:512, :].astype(f32)
-
-
-def near_sum_kernel(core_ref, total_ref, g0, g1, g2, loss_ref, low_ref, s0, s1, s2):
-    first = core_ref[0] == 0
-    s0[256:272, :] = split_terms(loss_ref[...])
-    for q, (g, s) in enumerate(((g0, s0), (g1, s1), (g2, s2))):
-        at = q * 512
-        got = g[...].astype(f32)
-        low_ref[q * 256 : q * 256 + 256, :] = total_ref[at : at + 256, :] + jnp.where(first, 0.0, got[0:256])
-        s[0:256, :] = (total_ref[at + 256 : at + 512, :] + jnp.where(first, got[0:256], got[256:512])).astype(bf16)
-
-
-def half_sum_kernel(core_ref, low_ref, r0, r1, r2, loss_ref, out_ref, s0, s1, s2, loss_out):
-    loss = loss_ref[...] + join_terms(r0, 256)
-    loss_out[...] = loss
-    s0[128:144, :] = split_terms(loss)
-    for q, (r, s) in enumerate(((r0, s0), (r1, s1), (r2, s2))):
-        total = low_ref[q * 256 : q * 256 + 256, :] + r[0:256, :].astype(f32)
-        out_ref[q * 128 : q * 128 + 128, :] = total[0:128]
-        s[0:128, :] = total[128:256].astype(bf16)
-
-
-def last_sum_kernel(core_ref, low_ref, r0, r1, r2, o0, o1, o2, loss_ref, keep_ref, send_ref):
+def far_sum_kernel(core_ref, base_ref, got_ref, *refs):
+    total_ref = refs[0]
+    if len(refs) == 3:
+        loss_ref, total_ref, loss_out = refs
+        loss_out[...] = loss_ref[...] + join_terms(got_ref, 512)
+    total_ref[...] = base_ref[...] + got_ref[0:512, :].astype(f32)
+
+
+def near_sum_kernel(core_ref, total_ref, got_ref, *refs):
+    first = core_ref[0] == 0
+    low_ref, send_ref = refs[-2:]
+    if len(refs) == 3:
+        send_ref[256:272, :] = split_terms(refs[0][...])
+    got = got_ref[...].astype(f32)
+    low_ref[...] = total_ref[0:256, :] + jnp.where(first, 0.0, got[0:256])
+    send_ref[0:256, :] = (total_ref[256:512, :] + jnp.where(first, got[0:256], got[256:512])).astype(bf16)
+
+
+def half_sum_kernel(core_ref, low_ref, got_ref, *refs):
+    if len(refs) == 4:
+        loss_ref, out_ref, send_ref, loss_out = refs
+        loss = loss_ref[...] + join_terms(got_ref, 256)
+        loss_out[...] = loss
+        send_ref[128:144, :] = split_terms(loss)
+    else:
+        out_ref, send_ref = refs
+    total = low_ref[...] + got_ref[0:256, :].astype(f32)
+    out_ref[...] = total[0:128]
+    send_ref[0:128, :] = total[128:256].astype(bf16)
+
+
+def last_sum_kernel(core_ref, l0, l1, l2, r0, r1, r2, o0, o1, o2, loss_ref, keep_ref, send_ref):
     first = core_ref[0] == 0
     loss = loss_ref[...] + join_terms(r0, 128)
     keep_ref[384:392, :] = jnp.concatenate([loss] * 4, 1)
     send_ref[384:392, :] = jnp.concatenate([loss] * 4, 1)
-    for q, (r, own) in enumerate(((r0, o0), (r1, o1), (r2, o2))):
+    for q, (low, r, own) in enumerate(((l0, r0, o0), (l1, r1, o1), (l2, r2, o2))):
         rows, text_rows = slice(q * 64, q * 64 + 64), slice(192 + q * 64, 192 + q * 64 + 64)
-        total = low_ref[q * 128 : q * 128 + 128, :] + r[0:128, :].astype(f32)
+        total = low[...] + r[0:128, :].astype(f32)
         keep_ref[rows, :] = jnp.where(first, total[0:64] + own[0:64, :], total[64:128])
         keep_ref[text_rows, :] = own[128:192, :]
         send_ref[rows, :] = jnp.where(first, total[64:128] + own[64:128, :], total[0:64])
@@ -497,23 +502,32 @@
         bases.append(base)
         near_got.append(core_swap(send))
         owns.append(own)
-    total, loss = call(far_sum_kernel, "far_sum", [core_id, *bases, *got, loss], [shape(1536, width), shape(8, 128)])
-    low, *messages = call(
-        near_sum_kernel,
-        "near_sum",
-        [core_id, total, *near_got, loss],
-        [shape(768, width)] + [shape(272 if q == 0 else 256, width, dtype=bf16) for q in range(3)],
-    )
-    got = [flip_permute(messages[q], q + 1) for q in range(3)]
-    low, *messages, loss = call(
-        half_sum_kernel,
-        "half_sum",
-        [core_id, low, *got, loss],
-        [shape(384, width)] + [shape(144 if q == 0 else 128, width, dtype=bf16) for q in range(3)] + [shape(8, 128)],
-    )
-    got = [flip_permute(messages[q], q) for q in range(3)]
+    lows, last = [], []
+    for q in range(3):
+        extra = [loss] if q == 0 else []
+        more = [shape(8, 128)] if q == 0 else []
+        pad = 16 if q == 0 else 0
+        total, *extra = call(
+            far_sum_kernel, "far_sum", [core_id, bases[q], got[q], *extra], [shape(512, width), *more]
+        )
+        low, send = call(
+            near_sum_kernel,
+            "near_sum",
+            [core_id, total, near_got[q], *extra],
+            [shape(256, width), shape(256 + pad, width, dtype=bf16)],
+        )
+        low, send, *extra = call(
+            half_sum_kernel,
+            "half_sum",
+            [core_id, low, flip_permute(send, q + 1), *extra],
+            [shape(128, width), shape(128 + pad, width, dtype=bf16), *more],
+        )
+        lows.append(low)
+        last.append(flip_permute(send, q))
+        if q == 0:
+            loss = extra[0]
     keep, send = call(
-        last_sum_kernel, "last_sum", [core_id, low, *got, *owns, loss], [shape(392, width), shape(392, width)]
+        last_sum_kernel, "last_sum", [core_id, *lows, *last, *owns, loss], [shape(392, width), shape(392, width)]
     )
     grad_image, grad_text, loss = call(
         functools.partial(finish_kernel, count),

time: 106 us -> 101 us (0.953)
  waiting for transfers between devices: 35.7 us -> 30.4 us
    ppermute x21, waiting for transfers between devices: 27.3 us -> 21.8 us  [flip_permute(): return lax.ppermute(x, AXES, ROLE_PAIRS[dim % 3])]
    pallas_call x23 -> x29, Pallas kernels: 25.7 us -> 25.6 us  [call(): pl.pallas_call(kernel, in_specs=in_specs, out_specs=[VMEM] * len(outs), o...]
  transfers between devices with their start and end apart: 36 -> 36, of which waited for: 22 -> 22; matrix products, arithmetic and copies ran while one was open for 0% -> 0% of each run, Pallas kernels for 8% -> 9%
where the time goes in v11:
time: 101 us
  starting transfers between devices  43.4 us (43%)
  waiting for transfers between devices  30.4 us (30%)
  Pallas kernels  26.7 us (26%)
    ppermute x21, starting transfers between devices, flip_permute(): return lax.ppermute(x, AXES, ROLE_PAIRS[dim % 3])  38 us
    pallas_call x29, Pallas kernels, call(): pl.pallas_call(kernel, in_specs=in_specs, out_specs=[VMEM] * len(outs), o...  25.6 us
    ppermute x21, waiting for transfers between devices, flip_permute(): return lax.ppermute(x, AXES, ROLE_PAIRS[dim % 3])  21.8 us
    ppermute x15, waiting for transfers between devices, core_swap(): return lax.ppermute(x, 'c', SWAP)  8.58 us
    ppermute x15, starting transfers between devices, core_swap(): return lax.ppermute(x, 'c', SWAP)  5.41 us
  transfers between devices with their start and end apart: 36, of which 22 were waited for; matrix products, arithmetic and copies ran while one was open for 0% of the time, Pallas kernels for 9%

profile of v11, /device:TPU:1, one launch (start us, length us, event | category | flops | bytes accessed | tf_op | source)
XLA Modules:
  0.0 101.4 jit_solution(12788908840665075683)
XLA Ops:
  0.6 1.5 %collective-permute-start = (bf16[192,512]{1,0:T(8,128)(2,1)}, bf16[192,512]{1,0:T(8,128)(2,1)S(1)}, u32[]{:S(2)}, u32[]{:S(2)}) collective-permute-start(bf16[192,512]{1,0:T(8,128)(2,1)} %refs_10_.1), channel_id=1, source_target_pairs={{0,1},{1,0},{2,3},{3,2},{4,5},{5,4},{6,7},{7,6},{8,9},{9,8},{10,11... | collective-permute-start | bytes 589832 | tf_op jit(solution)/shard_map/ppermute | solution.py:47
  2.2 1.2 %collective-permute-done.image_got = bf16[192,512]{1,0:T(8,128)(2,1)S(1)} collective-permute-done((bf16[192,512]{1,0:T(8,128)(2,1)}, bf16[192,512]{1,0:T(8,128)(2,1)S(1)}, u32[]{:S(2)}, u32[]{:S(2)}) %collective-permute-start) | collective-permute-done | bytes 196640 | tf_op jit(solution)/shard_map/ppermute | solution.py:47
  3.8 1.1 %pair.1 = (bf16[128,512]{1,0:T(8,128)(2,1)S(1)}, bf16[128,512]{1,0:T(8,128)(2,1)S(1)}, bf16[128,512]{1,0:T(8,128)(2,1)S(1)}) custom-call(s32[1]{0:T(128)} %bitcast.core_ref, bf16[192,512]{1,0:T(8,128)(2,1)} %refs_10_.1, bf16[192,512]{1,0:T(8,128)(2,1)} %refs_11_.1, bf16[192,512]{1,0:T(8,128)(2,1)S(1)} %collective-permute-done.image_got, ...), custom_call_target="tpu_custom_call" | custom-call | tf_op jit(solution)/shard_map/pair/pallas_call | solution.py:407
  4.9 2.6 %collective-permute-start.2 = (bf16[128,512]{1,0:T(8,128)(2,1)S(1)}, bf16[128,512]{1,0:T(8,128)(2,1)S(1)}, u32[]{:S(2)}, u32[]{:S(2)}) collective-permute-start(bf16[128,512]{1,0:T(8,128)(2,1)S(1)} %get-tuple-element.70.refs_0_), channel_id=1, source_target_pairs={{0,2},{1,7},{2,0},{3,5},{4,6},{5,3},{6,4},{7,1},{8,10},{9,15},{10,... | collective-permute-start | bytes 393224 | tf_op jit(solution)/shard_map/ppermute | solution.py:43
  7.5 2.7 %collective-permute-start.3 = (bf16[128,512]{1,0:T(8,128)(2,1)S(1)}, bf16[128,512]{1,0:T(8,128)(2,1)S(1)}, u32[]{:S(2)}, u32[]{:S(2)}) collective-permute-start(bf16[128,512]{1,0:T(8,128)(2,1)S(1)} %get-tuple-element.71.refs_1_), channel_id=1, source_target_pairs={{0,8},{1,25},{2,10},{3,27},{4,12},{5,29},{6,14},{7,31},{8,0},{9,17... | collective-permute-start | bytes 393224 | tf_op jit(solution)/shard_map/ppermute | solution.py:43
  10.2 3.8 %collective-permute-start.4 = (bf16[128,512]{1,0:T(8,128)(2,1)S(1)}, bf16[128,512]{1,0:T(8,128)(2,1)S(1)}, u32[]{:S(2)}, u32[]{:S(2)}) collective-permute-start(bf16[128,512]{1,0:T(8,128)(2,1)S(1)} %get-tuple-element.72.refs_2_), channel_id=1, source_target_pairs={{0,32},{1,97},{2,34},{3,99},{4,36},{5,101},{6,38},{7,103},{8,40},{... | collective-permute-start | bytes 393224 | tf_op jit(solution)/shard_map/ppermute | solution.py:43
  14.0 2.3 %collective-permute-done.4.refs_5_ = bf16[128,512]{1,0:T(8,128)(2,1)S(1)} collective-permute-done((bf16[128,512]{1,0:T(8,128)(2,1)S(1)}, bf16[128,512]{1,0:T(8,128)(2,1)S(1)}, u32[]{:S(2)}, u32[]{:S(2)}) %collective-permute-start.4) | collective-permute-done | bytes 131104 | tf_op jit(solution)/shard_map/ppermute | solution.py:43
  16.5 2.8 %collective-permute-start.6 = (bf16[256,512]{1,0:T(8,128)(2,1)S(1)}, bf16[256,512]{1,0:T(8,128)(2,1)S(1)}, u32[]{:S(2)}, u32[]{:S(2)}) collective-permute-start(bf16[256,512]{1,0:T(8,128)(2,1)S(1)} %get-tuple-element.74.refs_1_), channel_id=1, source_target_pairs={{0,32},{1,97},{2,34},{3,99},{4,36},{5,101},{6,38},{7,103},{8,40},{... | collective-permute-start | bytes 786440 | tf_op jit(solution)/shard_map/ppermute | solution.py:43
  19.5 3.5 %collective-permute-done.5.refs_3_ = bf16[256,512]{1,0:T(8,128)(2,1)S(1)} collective-permute-done((bf16[256,512]{1,0:T(8,128)(2,1)S(1)}, bf16[256,512]{1,0:T(8,128)(2,1)S(1)}, u32[]{:S(2)}, u32[]{:S(2)}) %collective-permute-start.5) | collective-permute-done | bytes 262176 | tf_op jit(solution)/shard_map/ppermute | solution.py:43
  23.0 2.7 %collective-permute-done.7.refs_5_ = bf16[256,512]{1,0:T(8,128)(2,1)S(1)} collective-permute-done((bf16[256,512]{1,0:T(8,128)(2,1)S(1)}, bf16[256,512]{1,0:T(8,128)(2,1)S(1)}, u32[]{:S(2)}, u32[]{:S(2)}) %collective-permute-start.7) | collective-permute-done | bytes 262176 | tf_op jit(solution)/shard_map/ppermute | solution.py:43
  26.6 2.7 %collective-permute-start.11 = (bf16[512,512]{1,0:T(8,128)(2,1)S(1)}, bf16[512,512]{1,0:T(8,128)(2,1)S(1)}, u32[]{:S(2)}, u32[]{:S(2)}) collective-permute-start(bf16[512,512]{1,0:T(8,128)(2,1)S(1)} %get-tuple-element.78.m2), channel_id=1, source_target_pairs={{0,8},{1,25},{2,10},{3,27},{4,12},{5,29},{6,14},{7,31},{8,0},{9,17... | collective-permute-start | bytes 1572872 | tf_op jit(solution)/shard_map/ppermute | solution.py:43
  29.4 2.8 %near.1 = (bf16[768,512]{1,0:T(8,128)(2,1)S(1)}, bf16[1536,512]{1,0:T(8,128)(2,1)S(1)}, f32[768,1536]{1,0:T(8,128)S(1)}, f32[6,128]{1,0:T(8,128)S(1)}, f32[12,128]{1,0:T(8,128)S(1)}) custom-call(s32[1]{0:T(128)} %bitcast.core_ref, bf16[512,512]{1,0:T(8,128)(2,1)S(1)} %get-tuple-element.76.m0, bf16[512,512]{1,0:T(8,128)(2,1)S(1)} %get-tuple-element.77.m1, ...), custom_call_target="tpu_custom_call" | custom-call | flops 1207959552 | tf_op jit(solution)/shard_map/near/pallas_call | solution.py:52
  32.2 3.1 %collective-permute-done.8.value_ref = bf16[512,512]{1,0:T(8,128)(2,1)S(1)} collective-permute-done((bf16[512,512]{1,0:T(8,128)(2,1)S(1)}, bf16[512,512]{1,0:T(8,128)(2,1)S(1)}, u32[]{:S(2)}, u32[]{:S(2)}) %collective-permute-start.8) | collective-permute-done | bytes 524320 | tf_op jit(solution)/shard_map/ppermute | solution.py:43
  36.2 1.0 %collective-permute-done.12.refs_3_ = bf16[512,512]{1,0:T(8,128)(2,1)S(1)} collective-permute-done((bf16[512,512]{1,0:T(8,128)(2,1)S(1)}, bf16[512,512]{1,0:T(8,128)(2,1)S(1)}, u32[]{:S(2)}, u32[]{:S(2)}) %collective-permute-start.12) | collective-permute-done | bytes 524320 | tf_op jit(solution)/shard_map/ppermute | solution.py:47
  37.2 0.7 collective-permute-done.13.refs_4_
  38.0 0.7 collective-permute-done.14.refs_5_
  38.7 8.2 %far.1 = (bf16[768,512]{1,0:T(8,128)(2,1)S(1)}, bf16[1536,512]{1,0:T(8,128)(2,1)S(1)}, f32[256,3072]{1,0:T(8,128)S(1)}, f32[256,3072]{1,0:T(8,128)S(1)}, f32[256...) custom-call(s32[1]{0:T(128)} %bitcast.core_ref, ...), custom_call_target="tpu_custom_call" | custom-call | flops 3623878656 | tf_op jit(solution)/shard_map/far/pallas_call | solution.py:52
  47.4 0.8 collective-permute-done.15.got_ref
  48.2 1.4 %collective-permute-start.16 = (f32[32,128]{1,0:T(8,128)S(1)}, f32[32,128]{1,0:T(8,128)S(1)}, u32[]{:S(2)}, u32[]{:S(2)}) collective-permute-start(f32[32,128]{1,0:T(8,128)S(1)} %join.4.mine_ref), channel_id=1, source_target_pairs={{0,2},{1,7},{2,0},{3,5},{4,6},{5,3},{6,4},{7,1},{8,10},{9,15},{10,... | collective-permute-start | bytes 49160 | tf_op jit(solution)/shard_map/ppermute | solution.py:43
  49.6 2.5 %collective-permute-done.16.got_ref = f32[32,128]{1,0:T(8,128)S(1)} collective-permute-done((f32[32,128]{1,0:T(8,128)S(1)}, f32[32,128]{1,0:T(8,128)S(1)}, u32[]{:S(2)}, u32[]{:S(2)}) %collective-permute-start.16) | collective-permute-done | bytes 16416 | tf_op jit(solution)/shard_map/ppermute | solution.py:43
  52.1 2.7 %collective-permute-start.17 = (f32[32,128]{1,0:T(8,128)S(1)}, f32[32,128]{1,0:T(8,128)S(1)}, u32[]{:S(2)}, u32[]{:S(2)}) collective-permute-start(f32[32,128]{1,0:T(8,128)S(1)} %join.5.mine_ref), channel_id=1, source_target_pairs={{0,8},{1,25},{2,10},{3,27},{4,12},{5,29},{6,14},{7,31},{8,0},{9,17... | collective-permute-start | bytes 49160 | tf_op jit(solution)/shard_map/ppermute | solution.py:43
  54.8 1.2 %collective-permute-done.17.got_ref = f32[32,128]{1,0:T(8,128)S(1)} collective-permute-done((f32[32,128]{1,0:T(8,128)S(1)}, f32[32,128]{1,0:T(8,128)S(1)}, u32[]{:S(2)}, u32[]{:S(2)}) %collective-permute-start.17) | collective-permute-done | bytes 16416 | tf_op jit(solution)/shard_map/ppermute | solution.py:43
  56.0 2.0 %collective-permute-start.18 = (f32[32,128]{1,0:T(8,128)S(1)}, f32[32,128]{1,0:T(8,128)S(1)}, u32[]{:S(2)}, u32[]{:S(2)}) collective-permute-start(f32[32,128]{1,0:T(8,128)S(1)} %join.6.mine_ref), channel_id=1, source_target_pairs={{0,32},{1,97},{2,34},{3,99},{4,36},{5,101},{6,38},{7,103},{8,40},{... | collective-permute-start | bytes 49160 | tf_op jit(solution)/shard_map/ppermute | solution.py:43
  58.0 1.9 %collective-permute-done.18.got_ref = f32[32,128]{1,0:T(8,128)S(1)} collective-permute-done((f32[32,128]{1,0:T(8,128)S(1)}, f32[32,128]{1,0:T(8,128)S(1)}, u32[]{:S(2)}, u32[]{:S(2)}) %collective-permute-start.18) | collective-permute-done | bytes 16416 | tf_op jit(solution)/shard_map/ppermute | solution.py:43
  59.9 0.5 collective-permute-start.19
  60.4 1.0 %collective-permute-done.19.other_ref = f32[32,128]{1,0:T(8,128)S(1)} collective-permute-done((f32[32,128]{1,0:T(8,128)S(1)}, f32[32,128]{1,0:T(8,128)S(1)}, u32[]{:S(2)}, u32[]{:S(2)}) %collective-permute-start.19) | collective-permute-done | bytes 16416 | tf_op jit(solution)/shard_map/ppermute | solution.py:47
  61.4 5.4 %coeffs.1 = (bf16[1536,3072]{1,0:T(8,128)(2,1)S(1)}, bf16[256,512]{1,0:T(8,128)(2,1)S(1)}, bf16[256,512]{1,0:T(8,128)(2,1)S(1)}, bf16[256,512]{1,0:T(8,128)(2,1)...) custom-call(s32[1]{0:T(128)} %bitcast.core_ref, ...), custom_call_target="tpu_custom_call" | custom-call | flops 4831838208 | tf_op jit(solution)/shard_map/coeffs/pallas_call | solution.py:52
  66.8 1.0 %far_text.3 = (bf16[512,512]{1,0:T(8,128)(2,1)S(1)}, bf16[512,512]{1,0:T(8,128)(2,1)S(1)}) custom-call(s32[1]{0:T(128)} %bitcast.core_ref, bf16[1536,3072]{1,0:T(8,128)(2,1)S(1)} %get-tuple-element.92.coeff_ref, bf16[768,512]{1,0:T(8,128)(2,1)S(1)} %get-tuple-element.81.refs_6_.near_rows, bf16[768,512]{1,0:T(8,128)(2,1)S(1)} %get-tuple-element.93.far_rows, ...), custom_call_target="tpu_custom_call" | custom-call | flops 805306368 | tf_op jit(solution)/shard_map/far_text/pallas_call | solution.py:52
  68.1 1.0 %far_text.5 = (bf16[512,512]{1,0:T(8,128)(2,1)S(1)}, bf16[512,512]{1,0:T(8,128)(2,1)S(1)}) custom-call(s32[1]{0:T(128)} %bitcast.core_ref, bf16[1536,3072]{1,0:T(8,128)(2,1)S(1)} %get-tuple-element.92.coeff_ref, bf16[768,512]{1,0:T(8,128)(2,1)S(1)} %get-tuple-element.81.refs_6_.near_rows, bf16[768,512]{1,0:T(8,128)(2,1)S(1)} %get-tuple-element.93.far_rows, ...), custom_call_target="tpu_custom_call" | custom-call | flops 805306368 | tf_op jit(solution)/shard_map/far_text/pallas_call | solution.py:52
  69.6 1.0 %far_text.4 = (bf16[512,512]{1,0:T(8,128)(2,1)S(1)}, bf16[512,512]{1,0:T(8,128)(2,1)S(1)}) custom-call(s32[1]{0:T(128)} %bitcast.core_ref, bf16[1536,3072]{1,0:T(8,128)(2,1)S(1)} %get-tuple-element.92.coeff_ref, bf16[768,512]{1,0:T(8,128)(2,1)S(1)} %get-tuple-element.81.refs_6_.near_rows, bf16[768,512]{1,0:T(8,128)(2,1)S(1)} %get-tuple-element.93.far_rows, ...), custom_call_target="tpu_custom_call" | custom-call | flops 805306368 | tf_op jit(solution)/shard_map/far_text/pallas_call | solution.py:52
  71.0 2.0 %collective-permute-start.23 = (bf16[528,512]{1,0:T(8,128)(2,1)S(1)}, bf16[528,512]{1,0:T(8,128)(2,1)S(1)}, u32[]{:S(2)}, u32[]{:S(2)}) collective-permute-start(bf16[528,512]{1,0:T(8,128)(2,1)S(1)} %far_message.3.a0), channel_id=1, source_target_pairs={{0,32},{1,97},{2,34},{3,99},{4,36},{5,101},{6,38},{7,103},{8,40},{... | collective-permute-start | bytes 1622024 | tf_op jit(solution)/shard_map/ppermute | solution.py:43
  73.2 2.7 %collective-permute-start.29 = (bf16[512,512]{1,0:T(8,128)(2,1)S(1)}, bf16[512,512]{1,0:T(8,128)(2,1)S(1)}, u32[]{:S(2)}, u32[]{:S(2)}) collective-permute-start(bf16[512,512]{1,0:T(8,128)(2,1)S(1)} %far_message.5.a2), channel_id=1, source_target_pairs={{0,8},{1,25},{2,10},{3,27},{4,12},{5,29},{6,14},{7,31},{8,0},{9,17... | collective-permute-start | bytes 1572872 | tf_op jit(solution)/shard_map/ppermute | solution.py:43
  76.0 2.0 %collective-permute-start.26 = (bf16[512,512]{1,0:T(8,128)(2,1)S(1)}, bf16[512,512]{1,0:T(8,128)(2,1)S(1)}, u32[]{:S(2)}, u32[]{:S(2)}) collective-permute-start(bf16[512,512]{1,0:T(8,128)(2,1)S(1)} %far_message.4.a1), channel_id=1, source_target_pairs={{0,2},{1,7},{2,0},{3,5},{4,6},{5,3},{6,4},{7,1},{8,10},{9,15},{10,... | collective-permute-start | bytes 1572872 | tf_op jit(solution)/shard_map/ppermute | solution.py:43
  78.0 1.1 %near_text.5 = (f32[512,512]{1,0:T(8,128)S(1)}, bf16[512,512]{1,0:T(8,128)(2,1)S(1)}, f32[256,512]{1,0:T(8,128)S(1)}) custom-call(s32[1]{0:T(128)} %bitcast.core_ref, bf16[1536,3072]{1,0:T(8,128)(2,1)S(1)} %get-tuple-element.92.coeff_ref, bf16[768,512]{1,0:T(8,128)(2,1)S(1)} %get-tuple-element.81.refs_6_.near_rows, ...), custom_call_target="tpu_custom_call" | custom-call | flops 805306368 | tf_op jit(solution)/shard_map/near_text/pallas_call | solution.py:52
  79.2 1.1 %near_text.3 = (f32[512,512]{1,0:T(8,128)S(1)}, bf16[512,512]{1,0:T(8,128)(2,1)S(1)}, f32[256,512]{1,0:T(8,128)S(1)}) custom-call(s32[1]{0:T(128)} %bitcast.core_ref, bf16[1536,3072]{1,0:T(8,128)(2,1)S(1)} %get-tuple-element.92.coeff_ref, bf16[768,512]{1,0:T(8,128)(2,1)S(1)} %get-tuple-element.81.refs_6_.near_rows, ...), custom_call_target="tpu_custom_call" | custom-call | flops 805306368 | tf_op jit(solution)/shard_map/near_text/pallas_call | solution.py:52
  80.3 0.8 collective-permute-start.24
  81.1 1.1 %near_text.4 = (f32[512,512]{1,0:T(8,128)S(1)}, bf16[512,512]{1,0:T(8,128)(2,1)S(1)}, f32[256,512]{1,0:T(8,128)S(1)}) custom-call(s32[1]{0:T(128)} %bitcast.core_ref, bf16[1536,3072]{1,0:T(8,128)(2,1)S(1)} %get-tuple-element.92.coeff_ref, bf16[768,512]{1,0:T(8,128)(2,1)S(1)} %get-tuple-element.81.refs_6_.near_rows, ...), custom_call_target="tpu_custom_call" | custom-call | flops 805306368 | tf_op jit(solution)/shard_map/near_text/pallas_call | solution.py:52
  82.8 1.0 collective-permute-start.25
  84.0 1.3 %collective-permute-start.31 = (bf16[256,512]{1,0:T(8,128)(2,1)S(1)}, bf16[256,512]{1,0:T(8,128)(2,1)S(1)}, u32[]{:S(2)}, u32[]{:S(2)}) collective-permute-start(bf16[256,512]{1,0:T(8,128)(2,1)S(1)} %get-tuple-element.123), channel_id=1, source_target_pairs={{0,2},{1,7},{2,0},{3,5},{4,6},{5,3},{6,4},{7,1},{8,10},{9,15},{10,... | collective-permute-start | bytes 786440 | tf_op jit(solution)/shard_map/ppermute | solution.py:43
  85.6 2.7 %collective-permute-start.28 = (bf16[256,512]{1,0:T(8,128)(2,1)S(1)}, bf16[256,512]{1,0:T(8,128)(2,1)S(1)}, u32[]{:S(2)}, u32[]{:S(2)}) collective-permute-start(bf16[256,512]{1,0:T(8,128)(2,1)S(1)} %get-tuple-element.117), channel_id=1, source_target_pairs={{0,32},{1,97},{2,34},{3,99},{4,36},{5,101},{6,38},{7,103},{8,40},{... | collective-permute-start | bytes 786440 | tf_op jit(solution)/shard_map/ppermute | solution.py:43
  88.3 1.2 %collective-permute-done.25.got_ref = bf16[272,512]{1,0:T(8,128)(2,1)S(1)} collective-permute-done((bf16[272,512]{1,0:T(8,128)(2,1)S(1)}, bf16[272,512]{1,0:T(8,128)(2,1)S(1)}, u32[]{:S(2)}, u32[]{:S(2)}) %collective-permute-start.25) | collective-permute-done | bytes 278560 | tf_op jit(solution)/shard_map/ppermute | solution.py:43
  89.5 0.8 collective-permute-start.32
  90.6 2.0 %collective-permute-start.34 = (bf16[128,512]{1,0:T(8,128)(2,1)S(1)}, bf16[128,512]{1,0:T(8,128)(2,1)S(1)}, u32[]{:S(2)}, u32[]{:S(2)}) collective-permute-start(bf16[128,512]{1,0:T(8,128)(2,1)S(1)} %get-tuple-element.127), channel_id=1, source_target_pairs={{0,32},{1,97},{2,34},{3,99},{4,36},{5,101},{6,38},{7,103},{8,40},{... | collective-permute-start | bytes 393224 | tf_op jit(solution)/shard_map/ppermute | solution.py:43
  92.6 2.0 %collective-permute-start.33 = (bf16[128,512]{1,0:T(8,128)(2,1)S(1)}, bf16[128,512]{1,0:T(8,128)(2,1)S(1)}, u32[]{:S(2)}, u32[]{:S(2)}) collective-permute-start(bf16[128,512]{1,0:T(8,128)(2,1)S(1)} %get-tuple-element.126), channel_id=1, source_target_pairs={{0,8},{1,25},{2,10},{3,27},{4,12},{5,29},{6,14},{7,31},{8,0},{9,17... | collective-permute-start | bytes 393224 | tf_op jit(solution)/shard_map/ppermute | solution.py:43
  94.7 1.0 %collective-permute-done.34.r2 = bf16[128,512]{1,0:T(8,128)(2,1)S(1)} collective-permute-done((bf16[128,512]{1,0:T(8,128)(2,1)S(1)}, bf16[128,512]{1,0:T(8,128)(2,1)S(1)}, u32[]{:S(2)}, u32[]{:S(2)}) %collective-permute-start.34) | collective-permute-done | bytes 131104 | tf_op jit(solution)/shard_map/ppermute | solution.py:43
  95.7 2.1 %collective-permute-done.33.r1 = bf16[128,512]{1,0:T(8,128)(2,1)S(1)} collective-permute-done((bf16[128,512]{1,0:T(8,128)(2,1)S(1)}, bf16[128,512]{1,0:T(8,128)(2,1)S(1)}, u32[]{:S(2)}, u32[]{:S(2)}) %collective-permute-start.33) | collective-permute-done | bytes 131104 | tf_op jit(solution)/shard_map/ppermute | solution.py:43
  98.0 2.3 %collective-permute-done.35.got_ref = f32[392,512]{1,0:T(8,128)S(1)} collective-permute-done((f32[392,512]{1,0:T(8,128)S(1)}, f32[392,512]{1,0:T(8,128)S(1)}, u32[]{:S(2)}, u32[]{:S(2)}) %collective-permute-start.35) | collective-permute-done | bytes 802848 | tf_op jit(solution)/shard_map/ppermute | solution.py:47
  100.3 1.0 finish.1
  (61 shorter events, 6.3 us)
Async XLA Ops:
  0.6 2.8 %collective-permute-start = (bf16[192,512]{1,0:T(8,128)(2,1)}, bf16[192,512]{1,0:T(8,128)(2,1)S(1)}, u32[]{:S(2)}, u32[]{:S(2)}) collective-permute-start(bf16[192,512]{1,0:T(8,128)(2,1)} %refs_10_.1), channel_id=1, source_target_pairs={{0,1},{1,0},{2,3},{3,2},{4,5},{5,4},{6,7},{7,6},{8,9},{9,8},{10,11... | collective-permute-start | bytes 589832 | tf_op jit(solution)/shard_map/ppermute | solution.py:47
  2.1 1.7 %collective-permute-start.1 = (bf16[192,512]{1,0:T(8,128)(2,1)}, bf16[192,512]{1,0:T(8,128)(2,1)S(1)}, u32[]{:S(2)}, u32[]{:S(2)}) collective-permute-start(bf16[192,512]{1,0:T(8,128)(2,1)} %refs_11_.1), channel_id=1, source_target_pairs={{0,1},{1,0},{2,3},{3,2},{4,5},{5,4},{6,7},{7,6},{8,9},{9,8},{10,11... | collective-permute-start | bytes 589832 | tf_op jit(solution)/shard_map/ppermute | solution.py:47
  4.9 9.1 %collective-permute-start.2 = (bf16[128,512]{1,0:T(8,128)(2,1)S(1)}, bf16[128,512]{1,0:T(8,128)(2,1)S(1)}, u32[]{:S(2)}, u32[]{:S(2)}) collective-permute-start(bf16[128,512]{1,0:T(8,128)(2,1)S(1)} %get-tuple-element.70.refs_0_), channel_id=1, source_target_pairs={{0,2},{1,7},{2,0},{3,5},{4,6},{5,3},{6,4},{7,1},{8,10},{9,15},{10,... | collective-permute-start | bytes 393224 | tf_op jit(solution)/shard_map/ppermute | solution.py:43
  7.5 6.5 %collective-permute-start.3 = (bf16[128,512]{1,0:T(8,128)(2,1)S(1)}, bf16[128,512]{1,0:T(8,128)(2,1)S(1)}, u32[]{:S(2)}, u32[]{:S(2)}) collective-permute-start(bf16[128,512]{1,0:T(8,128)(2,1)S(1)} %get-tuple-element.71.refs_1_), channel_id=1, source_target_pairs={{0,8},{1,25},{2,10},{3,27},{4,12},{5,29},{6,14},{7,31},{8,0},{9,17... | collective-permute-start | bytes 393224 | tf_op jit(solution)/shard_map/ppermute | solution.py:43
  10.2 6.1 %collective-permute-start.4 = (bf16[128,512]{1,0:T(8,128)(2,1)S(1)}, bf16[128,512]{1,0:T(8,128)(2,1)S(1)}, u32[]{:S(2)}, u32[]{:S(2)}) collective-permute-start(bf16[128,512]{1,0:T(8,128)(2,1)S(1)} %get-tuple-element.72.refs_2_), channel_id=1, source_target_pairs={{0,32},{1,97},{2,34},{3,99},{4,36},{5,101},{6,38},{7,103},{8,40},{... | collective-permute-start | bytes 393224 | tf_op jit(solution)/shard_map/ppermute | solution.py:43
  16.4 6.5 %collective-permute-start.5 = (bf16[256,512]{1,0:T(8,128)(2,1)S(1)}, bf16[256,512]{1,0:T(8,128)(2,1)S(1)}, u32[]{:S(2)}, u32[]{:S(2)}) collective-permute-start(bf16[256,512]{1,0:T(8,128)(2,1)S(1)} %get-tuple-element.73.refs_0_), channel_id=1, source_target_pairs={{0,8},{1,25},{2,10},{3,27},{4,12},{5,29},{6,14},{7,31},{8,0},{9,17... | collective-permute-start | bytes 786440 | tf_op jit(solution)/shard_map/ppermute | solution.py:43
  16.5 6.5 %collective-permute-start.6 = (bf16[256,512]{1,0:T(8,128)(2,1)S(1)}, bf16[256,512]{1,0:T(8,128)(2,1)S(1)}, u32[]{:S(2)}, u32[]{:S(2)}) collective-permute-start(bf16[256,512]{1,0:T(8,128)(2,1)S(1)} %get-tuple-element.74.refs_1_), channel_id=1, source_target_pairs={{0,32},{1,97},{2,34},{3,99},{4,36},{5,101},{6,38},{7,103},{8,40},{... | collective-permute-start | bytes 786440 | tf_op jit(solution)/shard_map/ppermute | solution.py:43
  19.3 6.4 %collective-permute-start.7 = (bf16[256,512]{1,0:T(8,128)(2,1)S(1)}, bf16[256,512]{1,0:T(8,128)(2,1)S(1)}, u32[]{:S(2)}, u32[]{:S(2)}) collective-permute-start(bf16[256,512]{1,0:T(8,128)(2,1)S(1)} %get-tuple-element.75.refs_2_), channel_id=1, source_target_pairs={{0,2},{1,7},{2,0},{3,5},{4,6},{5,3},{6,4},{7,1},{8,10},{9,15},{10,... | collective-permute-start | bytes 786440 | tf_op jit(solution)/shard_map/ppermute | solution.py:43
  25.9 3.5 %collective-permute-start.9 = (bf16[1536,512]{1,0:T(8,128)(2,1)S(1)}, bf16[1536,512]{1,0:T(8,128)(2,1)S(1)}, u32[]{:S(2)}, u32[]{:S(2)}) collective-permute-start(bf16[1536,512]{1,0:T(8,128)(2,1)S(1)} %get-tuple-element.79), channel_id=1, source_target_pairs={{0,1},{1,0},{2,3},{3,2},{4,5},{5,4},{6,7},{7,6},{8,9},{9,8},{10,11... | collective-permute-start | bytes 4718600 | tf_op jit(solution)/shard_map/ppermute | solution.py:47
  26.0 9.3 %collective-permute-start.8 = (bf16[512,512]{1,0:T(8,128)(2,1)S(1)}, bf16[512,512]{1,0:T(8,128)(2,1)S(1)}, u32[]{:S(2)}, u32[]{:S(2)}) collective-permute-start(bf16[512,512]{1,0:T(8,128)(2,1)S(1)} %get-tuple-element.76.m0), channel_id=1, source_target_pairs={{0,32},{1,97},{2,34},{3,99},{4,36},{5,101},{6,38},{7,103},{8,40},{... | collective-permute-start | bytes 1572872 | tf_op jit(solution)/shard_map/ppermute | solution.py:43
  26.2 9.5 %collective-permute-start.10 = (bf16[512,512]{1,0:T(8,128)(2,1)S(1)}, bf16[512,512]{1,0:T(8,128)(2,1)S(1)}, u32[]{:S(2)}, u32[]{:S(2)}) collective-permute-start(bf16[512,512]{1,0:T(8,128)(2,1)S(1)} %get-tuple-element.77.m1), channel_id=1, source_target_pairs={{0,2},{1,7},{2,0},{3,5},{4,6},{5,3},{6,4},{7,1},{8,10},{9,15},{10,... | collective-permute-start | bytes 1572872 | tf_op jit(solution)/shard_map/ppermute | solution.py:43
  26.6 12.2 %copy-start = (bf16[192,512]{1,0:T(8,128)(2,1)S(1)}, bf16[192,512]{1,0:T(8,128)(2,1)}, u32[]{:S(2)}) copy-start(bf16[192,512]{1,0:T(8,128)(2,1)} %refs_10_.1) | copy-start | bytes 589828
  26.6 12.2 %copy-start.1 = (bf16[192,512]{1,0:T(8,128)(2,1)S(1)}, bf16[192,512]{1,0:T(8,128)(2,1)}, u32[]{:S(2)}) copy-start(bf16[192,512]{1,0:T(8,128)(2,1)} %refs_11_.1) | copy-start | bytes 589828
  26.6 9.3 %collective-permute-start.11 = (bf16[512,512]{1,0:T(8,128)(2,1)S(1)}, bf16[512,512]{1,0:T(8,128)(2,1)S(1)}, u32[]{:S(2)}, u32[]{:S(2)}) collective-permute-start(bf16[512,512]{1,0:T(8,128)(2,1)S(1)} %get-tuple-element.78.m2), channel_id=1, source_target_pairs={{0,8},{1,25},{2,10},{3,27},{4,12},{5,29},{6,14},{7,31},{8,0},{9,17... | collective-permute-start | bytes 1572872 | tf_op jit(solution)/shard_map/ppermute | solution.py:43
  35.3 1.9 %collective-permute-start.12 = (bf16[512,512]{1,0:T(8,128)(2,1)S(1)}, bf16[512,512]{1,0:T(8,128)(2,1)S(1)}, u32[]{:S(2)}, u32[]{:S(2)}) collective-permute-start(bf16[512,512]{1,0:T(8,128)(2,1)S(1)} %after.3.refs_0_), channel_id=1, source_target_pairs={{0,1},{1,0},{2,3},{3,2},{4,5},{5,4},{6,7},{7,6},{8,9},{9,8},{10,11... | collective-permute-start | bytes 1572872 | tf_op jit(solution)/shard_map/ppermute | solution.py:47
  35.7 2.3 %collective-permute-start.13 = (bf16[512,512]{1,0:T(8,128)(2,1)S(1)}, bf16[512,512]{1,0:T(8,128)(2,1)S(1)}, u32[]{:S(2)}, u32[]{:S(2)}) collective-permute-start(bf16[512,512]{1,0:T(8,128)(2,1)S(1)} %after.4.refs_1_), channel_id=1, source_target_pairs={{0,1},{1,0},{2,3},{3,2},{4,5},{5,4},{6,7},{7,6},{8,9},{9,8},{10,11... | collective-permute-start | bytes 1572872 | tf_op jit(solution)/shard_map/ppermute | solution.py:47
  35.9 2.8 %collective-permute-start.14 = (bf16[512,512]{1,0:T(8,128)(2,1)S(1)}, bf16[512,512]{1,0:T(8,128)(2,1)S(1)}, u32[]{:S(2)}, u32[]{:S(2)}) collective-permute-start(bf16[512,512]{1,0:T(8,128)(2,1)S(1)} %after.5.refs_2_), channel_id=1, source_target_pairs={{0,1},{1,0},{2,3},{3,2},{4,5},{5,4},{6,7},{7,6},{8,9},{9,8},{10,11... | collective-permute-start | bytes 1572872 | tf_op jit(solution)/shard_map/ppermute | solution.py:47
  47.0 1.3 %collective-permute-start.15 = (f32[32,128]{1,0:T(8,128)S(1)}, f32[32,128]{1,0:T(8,128)S(1)}, u32[]{:S(2)}, u32[]{:S(2)}) collective-permute-start(f32[32,128]{1,0:T(8,128)S(1)} %get-tuple-element.85), channel_id=1, source_target_pairs={{0,1},{1,0},{2,3},{3,2},{4,5},{5,4},{6,7},{7,6},{8,9},{9,8},{10,11... | collective-permute-start | bytes 49160 | tf_op jit(solution)/shard_map/ppermute | solution.py:47
  48.2 3.9 %collective-permute-start.16 = (f32[32,128]{1,0:T(8,128)S(1)}, f32[32,128]{1,0:T(8,128)S(1)}, u32[]{:S(2)}, u32[]{:S(2)}) collective-permute-start(f32[32,128]{1,0:T(8,128)S(1)} %join.4.mine_ref), channel_id=1, source_target_pairs={{0,2},{1,7},{2,0},{3,5},{4,6},{5,3},{6,4},{7,1},{8,10},{9,15},{10,... | collective-permute-start | bytes 49160 | tf_op jit(solution)/shard_map/ppermute | solution.py:43
  52.1 3.9 %collective-permute-start.17 = (f32[32,128]{1,0:T(8,128)S(1)}, f32[32,128]{1,0:T(8,128)S(1)}, u32[]{:S(2)}, u32[]{:S(2)}) collective-permute-start(f32[32,128]{1,0:T(8,128)S(1)} %join.5.mine_ref), channel_id=1, source_target_pairs={{0,8},{1,25},{2,10},{3,27},{4,12},{5,29},{6,14},{7,31},{8,0},{9,17... | collective-permute-start | bytes 49160 | tf_op jit(solution)/shard_map/ppermute | solution.py:43
  56.0 3.9 %collective-permute-start.18 = (f32[32,128]{1,0:T(8,128)S(1)}, f32[32,128]{1,0:T(8,128)S(1)}, u32[]{:S(2)}, u32[]{:S(2)}) collective-permute-start(f32[32,128]{1,0:T(8,128)S(1)} %join.6.mine_ref), channel_id=1, source_target_pairs={{0,32},{1,97},{2,34},{3,99},{4,36},{5,101},{6,38},{7,103},{8,40},{... | collective-permute-start | bytes 49160 | tf_op jit(solution)/shard_map/ppermute | solution.py:43
  59.9 1.5 %collective-permute-start.19 = (f32[32,128]{1,0:T(8,128)S(1)}, f32[32,128]{1,0:T(8,128)S(1)}, u32[]{:S(2)}, u32[]{:S(2)}) collective-permute-start(f32[32,128]{1,0:T(8,128)S(1)} %join.7.mine_ref), channel_id=1, source_target_pairs={{0,1},{1,0},{2,3},{3,2},{4,5},{5,4},{6,7},{7,6},{8,9},{9,8},{10,11... | collective-permute-start | bytes 49160 | tf_op jit(solution)/shard_map/ppermute | solution.py:47
  67.9 3.0 %collective-permute-start.20 = (bf16[512,512]{1,0:T(8,128)(2,1)S(1)}, bf16[512,512]{1,0:T(8,128)(2,1)S(1)}, u32[]{:S(2)}, u32[]{:S(2)}) collective-permute-start(bf16[512,512]{1,0:T(8,128)(2,1)S(1)} %get-tuple-element.98), channel_id=1, source_target_pairs={{0,1},{1,0},{2,3},{3,2},{4,5},{5,4},{6,7},{7,6},{8,9},{9,8},{10,11... | collective-permute-start | bytes 1572872 | tf_op jit(solution)/shard_map/ppermute | solution.py:47
  69.2 3.9 %collective-permute-start.22 = (bf16[512,512]{1,0:T(8,128)(2,1)S(1)}, bf16[512,512]{1,0:T(8,128)(2,1)S(1)}, u32[]{:S(2)}, u32[]{:S(2)}) collective-permute-start(bf16[512,512]{1,0:T(8,128)(2,1)S(1)} %get-tuple-element.105), channel_id=1, source_target_pairs={{0,1},{1,0},{2,3},{3,2},{4,5},{5,4},{6,7},{7,6},{8,9},{9,8},{10,11... | collective-permute-start | bytes 1572872 | tf_op jit(solution)/shard_map/ppermute | solution.py:47
  70.6 5.2 %collective-permute-start.21 = (bf16[512,512]{1,0:T(8,128)(2,1)S(1)}, bf16[512,512]{1,0:T(8,128)(2,1)S(1)}, u32[]{:S(2)}, u32[]{:S(2)}) collective-permute-start(bf16[512,512]{1,0:T(8,128)(2,1)S(1)} %get-tuple-element.102), channel_id=1, source_target_pairs={{0,1},{1,0},{2,3},{3,2},{4,5},{5,4},{6,7},{7,6},{8,9},{9,8},{10,11... | collective-permute-start | bytes 1572872 | tf_op jit(solution)/shard_map/ppermute | solution.py:47
  71.0 11.1 %collective-permute-start.23 = (bf16[528,512]{1,0:T(8,128)(2,1)S(1)}, bf16[528,512]{1,0:T(8,128)(2,1)S(1)}, u32[]{:S(2)}, u32[]{:S(2)}) collective-permute-start(bf16[528,512]{1,0:T(8,128)(2,1)S(1)} %far_message.3.a0), channel_id=1, source_target_pairs={{0,32},{1,97},{2,34},{3,99},{4,36},{5,101},{6,38},{7,103},{8,40},{... | collective-permute-start | bytes 1622024 | tf_op jit(solution)/shard_map/ppermute | solution.py:43
  73.2 10.6 %collective-permute-start.29 = (bf16[512,512]{1,0:T(8,128)(2,1)S(1)}, bf16[512,512]{1,0:T(8,128)(2,1)S(1)}, u32[]{:S(2)}, u32[]{:S(2)}) collective-permute-start(bf16[512,512]{1,0:T(8,128)(2,1)S(1)} %far_message.5.a2), channel_id=1, source_target_pairs={{0,8},{1,25},{2,10},{3,27},{4,12},{5,29},{6,14},{7,31},{8,0},{9,17... | collective-permute-start | bytes 1572872 | tf_op jit(solution)/shard_map/ppermute | solution.py:43
  76.0 9.4 %collective-permute-start.26 = (bf16[512,512]{1,0:T(8,128)(2,1)S(1)}, bf16[512,512]{1,0:T(8,128)(2,1)S(1)}, u32[]{:S(2)}, u32[]{:S(2)}) collective-permute-start(bf16[512,512]{1,0:T(8,128)(2,1)S(1)} %far_message.4.a1), channel_id=1, source_target_pairs={{0,2},{1,7},{2,0},{3,5},{4,6},{5,3},{6,4},{7,1},{8,10},{9,15},{10,... | collective-permute-start | bytes 1572872 | tf_op jit(solution)/shard_map/ppermute | solution.py:43
  79.1 4.8 %collective-permute-start.30 = (bf16[512,512]{1,0:T(8,128)(2,1)S(1)}, bf16[512,512]{1,0:T(8,128)(2,1)S(1)}, u32[]{:S(2)}, u32[]{:S(2)}) collective-permute-start(bf16[512,512]{1,0:T(8,128)(2,1)S(1)} %get-tuple-element.121), channel_id=1, source_target_pairs={{0,1},{1,0},{2,3},{3,2},{4,5},{5,4},{6,7},{7,6},{8,9},{9,8},{10,11... | collective-permute-start | bytes 1572872 | tf_op jit(solution)/shard_map/ppermute | solution.py:47
  80.3 2.4 %collective-permute-start.24 = (bf16[512,512]{1,0:T(8,128)(2,1)S(1)}, bf16[512,512]{1,0:T(8,128)(2,1)S(1)}, u32[]{:S(2)}, u32[]{:S(2)}) collective-permute-start(bf16[512,512]{1,0:T(8,128)(2,1)S(1)} %get-tuple-element.108), channel_id=1, source_target_pairs={{0,1},{1,0},{2,3},{3,2},{4,5},{5,4},{6,7},{7,6},{8,9},{9,8},{10,11... | collective-permute-start | bytes 1572872 | tf_op jit(solution)/shard_map/ppermute | solution.py:47
  82.2 3.3 %collective-permute-start.27 = (bf16[512,512]{1,0:T(8,128)(2,1)S(1)}, bf16[512,512]{1,0:T(8,128)(2,1)S(1)}, u32[]{:S(2)}, u32[]{:S(2)}) collective-permute-start(bf16[512,512]{1,0:T(8,128)(2,1)S(1)} %get-tuple-element.115), channel_id=1, source_target_pairs={{0,1},{1,0},{2,3},{3,2},{4,5},{5,4},{6,7},{7,6},{8,9},{9,8},{10,11... | collective-permute-start | bytes 1572872 | tf_op jit(solution)/shard_map/ppermute | solution.py:47
  82.8 6.7 %collective-permute-start.25 = (bf16[272,512]{1,0:T(8,128)(2,1)S(1)}, bf16[272,512]{1,0:T(8,128)(2,1)S(1)}, u32[]{:S(2)}, u32[]{:S(2)}) collective-permute-start(bf16[272,512]{1,0:T(8,128)(2,1)S(1)} %get-tuple-element.111), channel_id=1, source_target_pairs={{0,8},{1,25},{2,10},{3,27},{4,12},{5,29},{6,14},{7,31},{8,0},{9,17... | collective-permute-start | bytes 835592 | tf_op jit(solution)/shard_map/ppermute | solution.py:43
  84.0 6.5 %collective-permute-start.31 = (bf16[256,512]{1,0:T(8,128)(2,1)S(1)}, bf16[256,512]{1,0:T(8,128)(2,1)S(1)}, u32[]{:S(2)}, u32[]{:S(2)}) collective-permute-start(bf16[256,512]{1,0:T(8,128)(2,1)S(1)} %get-tuple-element.123), channel_id=1, source_target_pairs={{0,2},{1,7},{2,0},{3,5},{4,6},{5,3},{6,4},{7,1},{8,10},{9,15},{10,... | collective-permute-start | bytes 786440 | tf_op jit(solution)/shard_map/ppermute | solution.py:43
  85.6 7.0 %collective-permute-start.28 = (bf16[256,512]{1,0:T(8,128)(2,1)S(1)}, bf16[256,512]{1,0:T(8,128)(2,1)S(1)}, u32[]{:S(2)}, u32[]{:S(2)}) collective-permute-start(bf16[256,512]{1,0:T(8,128)(2,1)S(1)} %get-tuple-element.117), channel_id=1, source_target_pairs={{0,32},{1,97},{2,34},{3,99},{4,36},{5,101},{6,38},{7,103},{8,40},{... | collective-permute-start | bytes 786440 | tf_op jit(solution)/shard_map/ppermute | solution.py:43
  89.5 8.2 %collective-permute-start.32 = (bf16[144,512]{1,0:T(8,128)(2,1)S(1)}, bf16[144,512]{1,0:T(8,128)(2,1)S(1)}, u32[]{:S(2)}, u32[]{:S(2)}) collective-permute-start(bf16[144,512]{1,0:T(8,128)(2,1)S(1)} %get-tuple-element.125), channel_id=1, source_target_pairs={{0,2},{1,7},{2,0},{3,5},{4,6},{5,3},{6,4},{7,1},{8,10},{9,15},{10,... | collective-permute-start | bytes 442376 | tf_op jit(solution)/shard_map/ppermute | solution.py:43
  90.6 5.1 %collective-permute-start.34 = (bf16[128,512]{1,0:T(8,128)(2,1)S(1)}, bf16[128,512]{1,0:T(8,128)(2,1)S(1)}, u32[]{:S(2)}, u32[]{:S(2)}) collective-permute-start(bf16[128,512]{1,0:T(8,128)(2,1)S(1)} %get-tuple-element.127), channel_id=1, source_target_pairs={{0,32},{1,97},{2,34},{3,99},{4,36},{5,101},{6,38},{7,103},{8,40},{... | collective-permute-start | bytes 393224 | tf_op jit(solution)/shard_map/ppermute | solution.py:43
  92.6 5.1 %collective-permute-start.33 = (bf16[128,512]{1,0:T(8,128)(2,1)S(1)}, bf16[128,512]{1,0:T(8,128)(2,1)S(1)}, u32[]{:S(2)}, u32[]{:S(2)}) collective-permute-start(bf16[128,512]{1,0:T(8,128)(2,1)S(1)} %get-tuple-element.126), channel_id=1, source_target_pairs={{0,8},{1,25},{2,10},{3,27},{4,12},{5,29},{6,14},{7,31},{8,0},{9,17... | collective-permute-start | bytes 393224 | tf_op jit(solution)/shard_map/ppermute | solution.py:43
  98.0 2.4 %collective-permute-start.35 = (f32[392,512]{1,0:T(8,128)S(1)}, f32[392,512]{1,0:T(8,128)S(1)}, u32[]{:S(2)}, u32[]{:S(2)}) collective-permute-start(f32[392,512]{1,0:T(8,128)S(1)} %get-tuple-element.133), channel_id=1, source_target_pairs={{0,1},{1,0},{2,3},{3,2},{4,5},{5,4},{6,7},{7,6},{8,9},{9,8},{10,11... | collective-permute-start | bytes 2408456 | tf_op jit(solution)/shard_map/ppermute | solution.py:47

commit v12 on v11

--- a/solution.py
+++ b/solution.py
@@ -120,9 +120,8 @@
             cols_ref[q * 512 : q * 512 + 512, :] = mine[q][...]
 
 
-def near_kernel(core_ref, m0, m1, m2, packed_ref, rows_ref, cols_ref, logit_ref, row_out, col_out):
-    swapped = [packed_ref.at[q * 512 : q * 512 + 512] for q in range(3)]
-    place(core_ref[0] == 0, (m0, m1, m2), swapped, rows_ref, cols_ref)
+def near_kernel(core_ref, m0, m1, m2, x0, x1, x2, rows_ref, cols_ref, logit_ref, row_out, col_out):
+    place(core_ref[0] == 0, (m0, m1, m2), (x0, x1, x2), rows_ref, cols_ref)
     rows, state = [], None
     for q in range(3):
         part = slice(q * 256, q * 256 + 256)
@@ -170,15 +169,24 @@
 
 
 def stack_kernel(core_ref, *refs):
-    packed = len(refs) == 10
     for q in range(3):
         a, b, out = refs[q], refs[q + 3], refs[q + 6]
         rows = a.shape[0]
         out[0:rows, :] = a[...]
         out[rows : 2 * rows, :] = b[...]
-        if packed:
-            refs[9][q * 512 : q * 512 + rows, :] = a[...]
-            refs[9][q * 512 + rows : q * 512 + 512, :] = b[...]
+
+
+def join_rows_kernel(core_ref, *refs):
+    at = 0
+    for ref in refs[:-1]:
+        rows = ref.shape[0]
+        refs[-1][at : at + rows, :] = ref[...]
+        at += rows
+
+
+def join_rows(core_id, parts):
+    rows, width = sum(a.shape[0] for a in parts), parts[0].shape[1]
+    return call(join_rows_kernel, "join_rows", [core_id, *parts], [shape(rows, width, dtype=bf16)], limit=2)[0]
 
 
 def gate_kernel(value_ref, token_ref, out_ref):
@@ -428,12 +436,10 @@
 
     got = [core_swap(image_emb), core_swap(text_emb)]
     near = pair(core_id, image_emb, text_emb, *got)
-    for step in range(2):
-        got = [flip_permute(near[q], q + step) for q in range(3)]
-        outs = [shape(256 << step, width, dtype=bf16)] * 3 + [shape(1536, width, dtype=bf16)] * step
-        near = call(stack_kernel, "stack", [core_id, *near, *got], outs, limit=2)
-    *near, packed = near
-    near_x = [core_swap(packed)]
+    got = [flip_permute(near[q], q) for q in range(3)]
+    near = call(stack_kernel, "stack", [core_id, *near, *got], [shape(256, width, dtype=bf16)] * 3, limit=2)
+    near = [join_rows(core_id, [near[q], flip_permute(near[q], q + 1)]) for q in range(3)]
+    near_x = [core_swap(a) for a in near]
     far = [flip_permute(near[q], q + 2) for q in range(3)]
 
     near_rows, near_cols, near_logits, row, col = call(
@@ -445,7 +451,6 @@
         limit=10,
         flops=2 * 768 * 1536 * width,
     )
-    far = [after(a, row) for a in far]
     far_x = [core_swap(a) for a in far]
     far_rows, far_cols, *logits, send, keep = call(
         far_kernel,

time: 101 us -> 99.9 us (0.989)
  waiting for transfers between devices: 30.4 us -> 29 us
    ppermute x15 -> x17, waiting for transfers between devices: 8.58 us -> 5.98 us  [core_swap(): return lax.ppermute(x, 'c', SWAP)]
    ppermute x21, waiting for transfers between devices: 21.8 us -> 23 us  [flip_permute(): return lax.ppermute(x, AXES, ROLE_PAIRS[dim % 3])]
    ppermute x15 -> x17, starting transfers between devices: 5.41 us -> 5.84 us  [core_swap(): return lax.ppermute(x, 'c', SWAP)]
    pallas_call x29 -> x31, Pallas kernels: 25.6 us -> 25.6 us  [call(): pl.pallas_call(kernel, in_specs=in_specs, out_specs=[VMEM] * len(outs), o...]
  transfers between devices with their start and end apart: 36 -> 38, of which waited for: 22 -> 19; matrix products, arithmetic and copies ran while one was open for 0% -> 0% of each run, Pallas kernels for 9% -> 10%
where the time goes in v12:
time: 99.9 us; the launch traced here: 99.7 us
  starting transfers between devices  43.1 us (43%)
  waiting for transfers between devices  29 us (29%)
  Pallas kernels  26.6 us (27%)
    ppermute x21, starting transfers between devices, flip_permute(): return lax.ppermute(x, AXES, ROLE_PAIRS[dim % 3])  37.3 us
    pallas_call x31, Pallas kernels, call(): pl.pallas_call(kernel, in_specs=in_specs, out_specs=[VMEM] * len(outs), o...  25.6 us
    ppermute x21, waiting for transfers between devices, flip_permute(): return lax.ppermute(x, AXES, ROLE_PAIRS[dim % 3])  23 us
    ppermute x17, waiting for transfers between devices, core_swap(): return lax.ppermute(x, 'c', SWAP)  5.98 us
    ppermute x17, starting transfers between devices, core_swap(): return lax.ppermute(x, 'c', SWAP)  5.84 us
  transfers between devices with their start and end apart: 38, of which 19 were waited for; matrix products, arithmetic and copies ran while one was open for 0% of the time, Pallas kernels for 10%

profile of v12, /device:TPU:1, one launch (start us, length us, event | category | flops | bytes accessed | tf_op | source)
XLA Modules:
  0.0 99.7 jit_solution(15300939625304649753)
XLA Ops:
  0.6 1.5 %collective-permute-start = (bf16[192,512]{1,0:T(8,128)(2,1)}, bf16[192,512]{1,0:T(8,128)(2,1)S(1)}, u32[]{:S(2)}, u32[]{:S(2)}) collective-permute-start(bf16[192,512]{1,0:T(8,128)(2,1)} %refs_10_.1), channel_id=1, source_target_pairs={{0,1},{1,0},{2,3},{3,2},{4,5},{5,4},{6,7},{7,6},{8,9},{9,8},{10,11... | collective-permute-start | bytes 589832 | tf_op jit(solution)/shard_map/ppermute | solution.py:47
  2.2 1.2 %collective-permute-done.image_got = bf16[192,512]{1,0:T(8,128)(2,1)S(1)} collective-permute-done((bf16[192,512]{1,0:T(8,128)(2,1)}, bf16[192,512]{1,0:T(8,128)(2,1)S(1)}, u32[]{:S(2)}, u32[]{:S(2)}) %collective-permute-start) | collective-permute-done | bytes 196640 | tf_op jit(solution)/shard_map/ppermute | solution.py:47
  3.8 1.1 %pair.1 = (bf16[128,512]{1,0:T(8,128)(2,1)S(1)}, bf16[128,512]{1,0:T(8,128)(2,1)S(1)}, bf16[128,512]{1,0:T(8,128)(2,1)S(1)}) custom-call(s32[1]{0:T(128)} %bitcast.core_ref, bf16[192,512]{1,0:T(8,128)(2,1)} %refs_10_.1, bf16[192,512]{1,0:T(8,128)(2,1)} %refs_11_.1, bf16[192,512]{1,0:T(8,128)(2,1)S(1)} %collective-permute-done.image_got, ...), custom_call_target="tpu_custom_call" | custom-call | tf_op jit(solution)/shard_map/pair/pallas_call | solution.py:415
  4.9 2.6 %collective-permute-start.2 = (bf16[128,512]{1,0:T(8,128)(2,1)S(1)}, bf16[128,512]{1,0:T(8,128)(2,1)S(1)}, u32[]{:S(2)}, u32[]{:S(2)}) collective-permute-start(bf16[128,512]{1,0:T(8,128)(2,1)S(1)} %get-tuple-element.66.refs_0_), channel_id=1, source_target_pairs={{0,2},{1,7},{2,0},{3,5},{4,6},{5,3},{6,4},{7,1},{8,10},{9,15},{10,... | collective-permute-start | bytes 393224 | tf_op jit(solution)/shard_map/ppermute | solution.py:43
  7.5 2.7 %collective-permute-start.3 = (bf16[128,512]{1,0:T(8,128)(2,1)S(1)}, bf16[128,512]{1,0:T(8,128)(2,1)S(1)}, u32[]{:S(2)}, u32[]{:S(2)}) collective-permute-start(bf16[128,512]{1,0:T(8,128)(2,1)S(1)} %get-tuple-element.67.refs_1_), channel_id=1, source_target_pairs={{0,8},{1,25},{2,10},{3,27},{4,12},{5,29},{6,14},{7,31},{8,0},{9,17... | collective-permute-start | bytes 393224 | tf_op jit(solution)/shard_map/ppermute | solution.py:43
  10.2 3.8 %collective-permute-start.4 = (bf16[128,512]{1,0:T(8,128)(2,1)S(1)}, bf16[128,512]{1,0:T(8,128)(2,1)S(1)}, u32[]{:S(2)}, u32[]{:S(2)}) collective-permute-start(bf16[128,512]{1,0:T(8,128)(2,1)S(1)} %get-tuple-element.68.refs_2_), channel_id=1, source_target_pairs={{0,32},{1,97},{2,34},{3,99},{4,36},{5,101},{6,38},{7,103},{8,40},{... | collective-permute-start | bytes 393224 | tf_op jit(solution)/shard_map/ppermute | solution.py:43
  14.0 2.3 %collective-permute-done.4.refs_5_ = bf16[128,512]{1,0:T(8,128)(2,1)S(1)} collective-permute-done((bf16[128,512]{1,0:T(8,128)(2,1)S(1)}, bf16[128,512]{1,0:T(8,128)(2,1)S(1)}, u32[]{:S(2)}, u32[]{:S(2)}) %collective-permute-start.4) | collective-permute-done | bytes 131104 | tf_op jit(solution)/shard_map/ppermute | solution.py:43
  16.7 2.7 %collective-permute-start.7 = (bf16[256,512]{1,0:T(8,128)(2,1)S(1)}, bf16[256,512]{1,0:T(8,128)(2,1)S(1)}, u32[]{:S(2)}, u32[]{:S(2)}) collective-permute-start(bf16[256,512]{1,0:T(8,128)(2,1)S(1)} %get-tuple-element.70.refs_0_), channel_id=1, source_target_pairs={{0,32},{1,97},{2,34},{3,99},{4,36},{5,101},{6,38},{7,103},{8,40},{... | collective-permute-start | bytes 786440 | tf_op jit(solution)/shard_map/ppermute | solution.py:43
  19.4 3.6 %collective-permute-done.9.refs_1_ = bf16[256,512]{1,0:T(8,128)(2,1)S(1)} collective-permute-done((bf16[256,512]{1,0:T(8,128)(2,1)S(1)}, bf16[256,512]{1,0:T(8,128)(2,1)S(1)}, u32[]{:S(2)}, u32[]{:S(2)}) %collective-permute-start.9) | collective-permute-done | bytes 262176 | tf_op jit(solution)/shard_map/ppermute | solution.py:43
  23.2 2.5 %collective-permute-start.8 = (bf16[512,512]{1,0:T(8,128)(2,1)S(1)}, bf16[512,512]{1,0:T(8,128)(2,1)S(1)}, u32[]{:S(2)}, u32[]{:S(2)}) collective-permute-start(bf16[512,512]{1,0:T(8,128)(2,1)S(1)} %join_rows.4.m1), channel_id=1, source_target_pairs={{0,2},{1,7},{2,0},{3,5},{4,6},{5,3},{6,4},{7,1},{8,10},{9,15},{10,... | collective-permute-start | bytes 1572872 | tf_op jit(solution)/shard_map/ppermute | solution.py:43
  25.8 2.7 %collective-permute-start.6 = (bf16[512,512]{1,0:T(8,128)(2,1)S(1)}, bf16[512,512]{1,0:T(8,128)(2,1)S(1)}, u32[]{:S(2)}, u32[]{:S(2)}) collective-permute-start(bf16[512,512]{1,0:T(8,128)(2,1)S(1)} %join_rows.3.m0), channel_id=1, source_target_pairs={{0,32},{1,97},{2,34},{3,99},{4,36},{5,101},{6,38},{7,103},{8,40},{... | collective-permute-start | bytes 1572872 | tf_op jit(solution)/shard_map/ppermute | solution.py:43
  28.5 0.5 collective-permute-start.14
  29.0 3.4 %collective-permute-done.10.refs_2_ = bf16[512,512]{1,0:T(8,128)(2,1)S(1)} collective-permute-done((bf16[512,512]{1,0:T(8,128)(2,1)S(1)}, bf16[512,512]{1,0:T(8,128)(2,1)S(1)}, u32[]{:S(2)}, u32[]{:S(2)}) %collective-permute-start.10) | collective-permute-done | bytes 524320 | tf_op jit(solution)/shard_map/ppermute | solution.py:43
  33.0 2.1 %collective-permute-done.6.refs_0_ = bf16[512,512]{1,0:T(8,128)(2,1)S(1)} collective-permute-done((bf16[512,512]{1,0:T(8,128)(2,1)S(1)}, bf16[512,512]{1,0:T(8,128)(2,1)S(1)}, u32[]{:S(2)}, u32[]{:S(2)}) %collective-permute-start.6) | collective-permute-done | bytes 524320 | tf_op jit(solution)/shard_map/ppermute | solution.py:43
  35.2 2.9 %near.1 = (bf16[768,512]{1,0:T(8,128)(2,1)S(1)}, bf16[1536,512]{1,0:T(8,128)(2,1)S(1)}, f32[768,1536]{1,0:T(8,128)S(1)}, f32[6,128]{1,0:T(8,128)S(1)}, f32[12,128]{1,0:T(8,128)S(1)}) custom-call(s32[1]{0:T(128)} %bitcast.core_ref, bf16[512,512]{1,0:T(8,128)(2,1)S(1)} %join_rows.3.m0, bf16[512,512]{1,0:T(8,128)(2,1)S(1)} %join_rows.4.m1, ...), custom_call_target="tpu_custom_call" | custom-call | flops 1207959552 | tf_op jit(solution)/shard_map/near/pallas_call | solution.py:52
  38.1 8.2 %far.1 = (bf16[768,512]{1,0:T(8,128)(2,1)S(1)}, bf16[1536,512]{1,0:T(8,128)(2,1)S(1)}, f32[256,3072]{1,0:T(8,128)S(1)}, f32[256,3072]{1,0:T(8,128)S(1)}, f32[256...) custom-call(s32[1]{0:T(128)} %bitcast.core_ref, ...), custom_call_target="tpu_custom_call" | custom-call | flops 3623878656 | tf_op jit(solution)/shard_map/far/pallas_call | solution.py:52
  46.3 0.6 collective-permute-start.17
  46.9 0.8 collective-permute-done.17.got_ref
  47.7 2.6 %collective-permute-start.18 = (f32[32,128]{1,0:T(8,128)S(1)}, f32[32,128]{1,0:T(8,128)S(1)}, u32[]{:S(2)}, u32[]{:S(2)}) collective-permute-start(f32[32,128]{1,0:T(8,128)S(1)} %join.4.mine_ref), channel_id=1, source_target_pairs={{0,2},{1,7},{2,0},{3,5},{4,6},{5,3},{6,4},{7,1},{8,10},{9,15},{10,... | collective-permute-start | bytes 49160 | tf_op jit(solution)/shard_map/ppermute | solution.py:43
  50.3 1.3 %collective-permute-done.18.got_ref = f32[32,128]{1,0:T(8,128)S(1)} collective-permute-done((f32[32,128]{1,0:T(8,128)S(1)}, f32[32,128]{1,0:T(8,128)S(1)}, u32[]{:S(2)}, u32[]{:S(2)}) %collective-permute-start.18) | collective-permute-done | bytes 16416 | tf_op jit(solution)/shard_map/ppermute | solution.py:43
  51.6 0.5 collective-permute-start.19
  52.1 3.4 %collective-permute-done.19.got_ref = f32[32,128]{1,0:T(8,128)S(1)} collective-permute-done((f32[32,128]{1,0:T(8,128)S(1)}, f32[32,128]{1,0:T(8,128)S(1)}, u32[]{:S(2)}, u32[]{:S(2)}) %collective-permute-start.19) | collective-permute-done | bytes 16416 | tf_op jit(solution)/shard_map/ppermute | solution.py:43
  55.5 2.7 %collective-permute-start.20 = (f32[32,128]{1,0:T(8,128)S(1)}, f32[32,128]{1,0:T(8,128)S(1)}, u32[]{:S(2)}, u32[]{:S(2)}) collective-permute-start(f32[32,128]{1,0:T(8,128)S(1)} %join.6.mine_ref), channel_id=1, source_target_pairs={{0,32},{1,97},{2,34},{3,99},{4,36},{5,101},{6,38},{7,103},{8,40},{... | collective-permute-start | bytes 49160 | tf_op jit(solution)/shard_map/ppermute | solution.py:43
  58.2 1.2 %collective-permute-done.20.got_ref = f32[32,128]{1,0:T(8,128)S(1)} collective-permute-done((f32[32,128]{1,0:T(8,128)S(1)}, f32[32,128]{1,0:T(8,128)S(1)}, u32[]{:S(2)}, u32[]{:S(2)}) %collective-permute-start.20) | collective-permute-done | bytes 16416 | tf_op jit(solution)/shard_map/ppermute | solution.py:43
  59.5 0.5 collective-permute-start.21
  59.9 1.0 %collective-permute-done.21.other_ref = f32[32,128]{1,0:T(8,128)S(1)} collective-permute-done((f32[32,128]{1,0:T(8,128)S(1)}, f32[32,128]{1,0:T(8,128)S(1)}, u32[]{:S(2)}, u32[]{:S(2)}) %collective-permute-start.21) | collective-permute-done | bytes 16416 | tf_op jit(solution)/shard_map/ppermute | solution.py:47
  60.9 5.4 %coeffs.1 = (bf16[1536,3072]{1,0:T(8,128)(2,1)S(1)}, bf16[256,512]{1,0:T(8,128)(2,1)S(1)}, bf16[256,512]{1,0:T(8,128)(2,1)S(1)}, bf16[256,512]{1,0:T(8,128)(2,1)...) custom-call(s32[1]{0:T(128)} %bitcast.core_ref, ...), custom_call_target="tpu_custom_call" | custom-call | flops 4831838208 | tf_op jit(solution)/shard_map/coeffs/pallas_call | solution.py:52
  66.3 1.1 %far_text.3 = (bf16[512,512]{1,0:T(8,128)(2,1)S(1)}, bf16[512,512]{1,0:T(8,128)(2,1)S(1)}) custom-call(s32[1]{0:T(128)} %bitcast.core_ref, bf16[1536,3072]{1,0:T(8,128)(2,1)S(1)} %get-tuple-element.84.coeff_ref, bf16[768,512]{1,0:T(8,128)(2,1)S(1)} %get-tuple-element.72.refs_6_.near_rows, bf16[768,512]{1,0:T(8,128)(2,1)S(1)} %get-tuple-element.85.far_rows, ...), custom_call_target="tpu_custom_call" | custom-call | flops 805306368 | tf_op jit(solution)/shard_map/far_text/pallas_call | solution.py:52
  67.6 1.0 %far_text.5 = (bf16[512,512]{1,0:T(8,128)(2,1)S(1)}, bf16[512,512]{1,0:T(8,128)(2,1)S(1)}) custom-call(s32[1]{0:T(128)} %bitcast.core_ref, bf16[1536,3072]{1,0:T(8,128)(2,1)S(1)} %get-tuple-element.84.coeff_ref, bf16[768,512]{1,0:T(8,128)(2,1)S(1)} %get-tuple-element.72.refs_6_.near_rows, bf16[768,512]{1,0:T(8,128)(2,1)S(1)} %get-tuple-element.85.far_rows, ...), custom_call_target="tpu_custom_call" | custom-call | flops 805306368 | tf_op jit(solution)/shard_map/far_text/pallas_call | solution.py:52
  69.1 1.0 %far_text.4 = (bf16[512,512]{1,0:T(8,128)(2,1)S(1)}, bf16[512,512]{1,0:T(8,128)(2,1)S(1)}) custom-call(s32[1]{0:T(128)} %bitcast.core_ref, bf16[1536,3072]{1,0:T(8,128)(2,1)S(1)} %get-tuple-element.84.coeff_ref, bf16[768,512]{1,0:T(8,128)(2,1)S(1)} %get-tuple-element.72.refs_6_.near_rows, bf16[768,512]{1,0:T(8,128)(2,1)S(1)} %get-tuple-element.85.far_rows, ...), custom_call_target="tpu_custom_call" | custom-call | flops 805306368 | tf_op jit(solution)/shard_map/far_text/pallas_call | solution.py:52
  70.5 2.7 %collective-permute-start.25 = (bf16[528,512]{1,0:T(8,128)(2,1)S(1)}, bf16[528,512]{1,0:T(8,128)(2,1)S(1)}, u32[]{:S(2)}, u32[]{:S(2)}) collective-permute-start(bf16[528,512]{1,0:T(8,128)(2,1)S(1)} %far_message.3.a0), channel_id=1, source_target_pairs={{0,32},{1,97},{2,34},{3,99},{4,36},{5,101},{6,38},{7,103},{8,40},{... | collective-permute-start | bytes 1622024 | tf_op jit(solution)/shard_map/ppermute | solution.py:43
  73.4 0.6 collective-permute-start.31
  74.1 2.5 %collective-permute-start.28 = (bf16[512,512]{1,0:T(8,128)(2,1)S(1)}, bf16[512,512]{1,0:T(8,128)(2,1)S(1)}, u32[]{:S(2)}, u32[]{:S(2)}) collective-permute-start(bf16[512,512]{1,0:T(8,128)(2,1)S(1)} %far_message.4.a1), channel_id=1, source_target_pairs={{0,2},{1,7},{2,0},{3,5},{4,6},{5,3},{6,4},{7,1},{8,10},{9,15},{10,... | collective-permute-start | bytes 1572872 | tf_op jit(solution)/shard_map/ppermute | solution.py:43
  76.6 1.1 %near_text.5 = (f32[512,512]{1,0:T(8,128)S(1)}, bf16[512,512]{1,0:T(8,128)(2,1)S(1)}, f32[256,512]{1,0:T(8,128)S(1)}) custom-call(s32[1]{0:T(128)} %bitcast.core_ref, bf16[1536,3072]{1,0:T(8,128)(2,1)S(1)} %get-tuple-element.84.coeff_ref, bf16[768,512]{1,0:T(8,128)(2,1)S(1)} %get-tuple-element.72.refs_6_.near_rows, ...), custom_call_target="tpu_custom_call" | custom-call | flops 805306368 | tf_op jit(solution)/shard_map/near_text/pallas_call | solution.py:52
  77.8 1.1 %near_text.3 = (f32[512,512]{1,0:T(8,128)S(1)}, bf16[512,512]{1,0:T(8,128)(2,1)S(1)}, f32[256,512]{1,0:T(8,128)S(1)}) custom-call(s32[1]{0:T(128)} %bitcast.core_ref, bf16[1536,3072]{1,0:T(8,128)(2,1)S(1)} %get-tuple-element.84.coeff_ref, bf16[768,512]{1,0:T(8,128)(2,1)S(1)} %get-tuple-element.72.refs_6_.near_rows, ...), custom_call_target="tpu_custom_call" | custom-call | flops 805306368 | tf_op jit(solution)/shard_map/near_text/pallas_call | solution.py:52
  78.8 0.8 collective-permute-start.26
  79.7 1.1 %near_text.4 = (f32[512,512]{1,0:T(8,128)S(1)}, bf16[512,512]{1,0:T(8,128)(2,1)S(1)}, f32[256,512]{1,0:T(8,128)S(1)}) custom-call(s32[1]{0:T(128)} %bitcast.core_ref, bf16[1536,3072]{1,0:T(8,128)(2,1)S(1)} %get-tuple-element.84.coeff_ref, bf16[768,512]{1,0:T(8,128)(2,1)S(1)} %get-tuple-element.72.refs_6_.near_rows, ...), custom_call_target="tpu_custom_call" | custom-call | flops 805306368 | tf_op jit(solution)/shard_map/near_text/pallas_call | solution.py:52
  81.5 1.2 %collective-permute-done.31.got_ref = bf16[512,512]{1,0:T(8,128)(2,1)S(1)} collective-permute-done((bf16[512,512]{1,0:T(8,128)(2,1)S(1)}, bf16[512,512]{1,0:T(8,128)(2,1)S(1)}, u32[]{:S(2)}, u32[]{:S(2)}) %collective-permute-start.31) | collective-permute-done | bytes 524320 | tf_op jit(solution)/shard_map/ppermute | solution.py:43
  82.9 1.3 %collective-permute-start.33 = (bf16[256,512]{1,0:T(8,128)(2,1)S(1)}, bf16[256,512]{1,0:T(8,128)(2,1)S(1)}, u32[]{:S(2)}, u32[]{:S(2)}) collective-permute-start(bf16[256,512]{1,0:T(8,128)(2,1)S(1)} %get-tuple-element.115), channel_id=1, source_target_pairs={{0,2},{1,7},{2,0},{3,5},{4,6},{5,3},{6,4},{7,1},{8,10},{9,15},{10,... | collective-permute-start | bytes 786440 | tf_op jit(solution)/shard_map/ppermute | solution.py:43
  84.4 2.4 %collective-permute-start.30 = (bf16[256,512]{1,0:T(8,128)(2,1)S(1)}, bf16[256,512]{1,0:T(8,128)(2,1)S(1)}, u32[]{:S(2)}, u32[]{:S(2)}) collective-permute-start(bf16[256,512]{1,0:T(8,128)(2,1)S(1)} %get-tuple-element.109), channel_id=1, source_target_pairs={{0,32},{1,97},{2,34},{3,99},{4,36},{5,101},{6,38},{7,103},{8,40},{... | collective-permute-start | bytes 786440 | tf_op jit(solution)/shard_map/ppermute | solution.py:43
  86.9 1.2 %collective-permute-done.27.got_ref = bf16[272,512]{1,0:T(8,128)(2,1)S(1)} collective-permute-done((bf16[272,512]{1,0:T(8,128)(2,1)S(1)}, bf16[272,512]{1,0:T(8,128)(2,1)S(1)}, u32[]{:S(2)}, u32[]{:S(2)}) %collective-permute-start.27) | collective-permute-done | bytes 278560 | tf_op jit(solution)/shard_map/ppermute | solution.py:43
  88.1 1.8 %collective-permute-start.34 = (bf16[144,512]{1,0:T(8,128)(2,1)S(1)}, bf16[144,512]{1,0:T(8,128)(2,1)S(1)}, u32[]{:S(2)}, u32[]{:S(2)}) collective-permute-start(bf16[144,512]{1,0:T(8,128)(2,1)S(1)} %get-tuple-element.117), channel_id=1, source_target_pairs={{0,2},{1,7},{2,0},{3,5},{4,6},{5,3},{6,4},{7,1},{8,10},{9,15},{10,... | collective-permute-start | bytes 442376 | tf_op jit(solution)/shard_map/ppermute | solution.py:43
  90.0 0.7 collective-permute-start.36
  91.0 2.2 %collective-permute-start.35 = (bf16[128,512]{1,0:T(8,128)(2,1)S(1)}, bf16[128,512]{1,0:T(8,128)(2,1)S(1)}, u32[]{:S(2)}, u32[]{:S(2)}) collective-permute-start(bf16[128,512]{1,0:T(8,128)(2,1)S(1)} %get-tuple-element.118), channel_id=1, source_target_pairs={{0,8},{1,25},{2,10},{3,27},{4,12},{5,29},{6,14},{7,31},{8,0},{9,17... | collective-permute-start | bytes 393224 | tf_op jit(solution)/shard_map/ppermute | solution.py:43
  93.2 1.8 %collective-permute-done.36.r2 = bf16[128,512]{1,0:T(8,128)(2,1)S(1)} collective-permute-done((bf16[128,512]{1,0:T(8,128)(2,1)S(1)}, bf16[128,512]{1,0:T(8,128)(2,1)S(1)}, u32[]{:S(2)}, u32[]{:S(2)}) %collective-permute-start.36) | collective-permute-done | bytes 131104 | tf_op jit(solution)/shard_map/ppermute | solution.py:43
  95.1 1.0 %collective-permute-done.35.r1 = bf16[128,512]{1,0:T(8,128)(2,1)S(1)} collective-permute-done((bf16[128,512]{1,0:T(8,128)(2,1)S(1)}, bf16[128,512]{1,0:T(8,128)(2,1)S(1)}, u32[]{:S(2)}, u32[]{:S(2)}) %collective-permute-start.35) | collective-permute-done | bytes 131104 | tf_op jit(solution)/shard_map/ppermute | solution.py:43
  96.4 2.3 %collective-permute-done.37.got_ref = f32[392,512]{1,0:T(8,128)S(1)} collective-permute-done((f32[392,512]{1,0:T(8,128)S(1)}, f32[392,512]{1,0:T(8,128)S(1)}, u32[]{:S(2)}, u32[]{:S(2)}) %collective-permute-start.37) | collective-permute-done | bytes 802848 | tf_op jit(solution)/shard_map/ppermute | solution.py:47
  98.7 1.0 %finish.1 = (f32[192,512]{1,0:T(8,128)}, f32[192,512]{1,0:T(8,128)}, f32[1,1]{1,0:T(1,128)}) custom-call(s32[1]{0:T(128)} %bitcast.core_ref, f32[392,512]{1,0:T(8,128)S(1)} %get-tuple-element.124.keep_ref, f32[392,512]{1,0:T(8,128)S(1)} %collective-permute-done.37.got_ref), custom_call_target="tpu_custom_call" | custom-call | tf_op jit(solution)/shard_map/finish/pallas_call | solution.py:52
  (64 shorter events, 5.2 us)
Async XLA Ops:
  0.6 2.8 %collective-permute-start = (bf16[192,512]{1,0:T(8,128)(2,1)}, bf16[192,512]{1,0:T(8,128)(2,1)S(1)}, u32[]{:S(2)}, u32[]{:S(2)}) collective-permute-start(bf16[192,512]{1,0:T(8,128)(2,1)} %refs_10_.1), channel_id=1, source_target_pairs={{0,1},{1,0},{2,3},{3,2},{4,5},{5,4},{6,7},{7,6},{8,9},{9,8},{10,11... | collective-permute-start | bytes 589832 | tf_op jit(solution)/shard_map/ppermute | solution.py:47
  2.1 1.7 %collective-permute-start.1 = (bf16[192,512]{1,0:T(8,128)(2,1)}, bf16[192,512]{1,0:T(8,128)(2,1)S(1)}, u32[]{:S(2)}, u32[]{:S(2)}) collective-permute-start(bf16[192,512]{1,0:T(8,128)(2,1)} %refs_11_.1), channel_id=1, source_target_pairs={{0,1},{1,0},{2,3},{3,2},{4,5},{5,4},{6,7},{7,6},{8,9},{9,8},{10,11... | collective-permute-start | bytes 589832 | tf_op jit(solution)/shard_map/ppermute | solution.py:47
  4.9 9.1 %collective-permute-start.2 = (bf16[128,512]{1,0:T(8,128)(2,1)S(1)}, bf16[128,512]{1,0:T(8,128)(2,1)S(1)}, u32[]{:S(2)}, u32[]{:S(2)}) collective-permute-start(bf16[128,512]{1,0:T(8,128)(2,1)S(1)} %get-tuple-element.66.refs_0_), channel_id=1, source_target_pairs={{0,2},{1,7},{2,0},{3,5},{4,6},{5,3},{6,4},{7,1},{8,10},{9,15},{10,... | collective-permute-start | bytes 393224 | tf_op jit(solution)/shard_map/ppermute | solution.py:43
  7.5 6.5 %collective-permute-start.3 = (bf16[128,512]{1,0:T(8,128)(2,1)S(1)}, bf16[128,512]{1,0:T(8,128)(2,1)S(1)}, u32[]{:S(2)}, u32[]{:S(2)}) collective-permute-start(bf16[128,512]{1,0:T(8,128)(2,1)S(1)} %get-tuple-element.67.refs_1_), channel_id=1, source_target_pairs={{0,8},{1,25},{2,10},{3,27},{4,12},{5,29},{6,14},{7,31},{8,0},{9,17... | collective-permute-start | bytes 393224 | tf_op jit(solution)/shard_map/ppermute | solution.py:43
  10.2 6.1 %collective-permute-start.4 = (bf16[128,512]{1,0:T(8,128)(2,1)S(1)}, bf16[128,512]{1,0:T(8,128)(2,1)S(1)}, u32[]{:S(2)}, u32[]{:S(2)}) collective-permute-start(bf16[128,512]{1,0:T(8,128)(2,1)S(1)} %get-tuple-element.68.refs_2_), channel_id=1, source_target_pairs={{0,32},{1,97},{2,34},{3,99},{4,36},{5,101},{6,38},{7,103},{8,40},{... | collective-permute-start | bytes 393224 | tf_op jit(solution)/shard_map/ppermute | solution.py:43
  16.4 6.5 %collective-permute-start.9 = (bf16[256,512]{1,0:T(8,128)(2,1)S(1)}, bf16[256,512]{1,0:T(8,128)(2,1)S(1)}, u32[]{:S(2)}, u32[]{:S(2)}) collective-permute-start(bf16[256,512]{1,0:T(8,128)(2,1)S(1)} %get-tuple-element.71.refs_0_), channel_id=1, source_target_pairs={{0,2},{1,7},{2,0},{3,5},{4,6},{5,3},{6,4},{7,1},{8,10},{9,15},{10,... | collective-permute-start | bytes 786440 | tf_op jit(solution)/shard_map/ppermute | solution.py:43
  16.7 6.5 %collective-permute-start.7 = (bf16[256,512]{1,0:T(8,128)(2,1)S(1)}, bf16[256,512]{1,0:T(8,128)(2,1)S(1)}, u32[]{:S(2)}, u32[]{:S(2)}) collective-permute-start(bf16[256,512]{1,0:T(8,128)(2,1)S(1)} %get-tuple-element.70.refs_0_), channel_id=1, source_target_pairs={{0,32},{1,97},{2,34},{3,99},{4,36},{5,101},{6,38},{7,103},{8,40},{... | collective-permute-start | bytes 786440 | tf_op jit(solution)/shard_map/ppermute | solution.py:43
  19.4 6.4 %collective-permute-start.5 = (bf16[256,512]{1,0:T(8,128)(2,1)S(1)}, bf16[256,512]{1,0:T(8,128)(2,1)S(1)}, u32[]{:S(2)}, u32[]{:S(2)}) collective-permute-start(bf16[256,512]{1,0:T(8,128)(2,1)S(1)} %get-tuple-element.69.refs_0_), channel_id=1, source_target_pairs={{0,8},{1,25},{2,10},{3,27},{4,12},{5,29},{6,14},{7,31},{8,0},{9,17... | collective-permute-start | bytes 786440 | tf_op jit(solution)/shard_map/ppermute | solution.py:43
  23.0 15.1 %copy-start = (bf16[192,512]{1,0:T(8,128)(2,1)S(1)}, bf16[192,512]{1,0:T(8,128)(2,1)}, u32[]{:S(2)}) copy-start(bf16[192,512]{1,0:T(8,128)(2,1)} %refs_10_.1) | copy-start | bytes 589828
  23.0 15.1 %copy-start.1 = (bf16[192,512]{1,0:T(8,128)(2,1)S(1)}, bf16[192,512]{1,0:T(8,128)(2,1)}, u32[]{:S(2)}) copy-start(bf16[192,512]{1,0:T(8,128)(2,1)} %refs_11_.1) | copy-start | bytes 589828
  23.0 5.5 %collective-permute-start.16 = (bf16[512,512]{1,0:T(8,128)(2,1)S(1)}, bf16[512,512]{1,0:T(8,128)(2,1)S(1)}, u32[]{:S(2)}, u32[]{:S(2)}) collective-permute-start(bf16[512,512]{1,0:T(8,128)(2,1)S(1)} %join_rows.5.m2), channel_id=1, source_target_pairs={{0,1},{1,0},{2,3},{3,2},{4,5},{5,4},{6,7},{7,6},{8,9},{9,8},{10,11... | collective-permute-start | bytes 1572872 | tf_op jit(solution)/shard_map/ppermute | solution.py:47
  23.1 9.3 %collective-permute-start.10 = (bf16[512,512]{1,0:T(8,128)(2,1)S(1)}, bf16[512,512]{1,0:T(8,128)(2,1)S(1)}, u32[]{:S(2)}, u32[]{:S(2)}) collective-permute-start(bf16[512,512]{1,0:T(8,128)(2,1)S(1)} %join_rows.5.m2), channel_id=1, source_target_pairs={{0,8},{1,25},{2,10},{3,27},{4,12},{5,29},{6,14},{7,31},{8,0},{9,17... | collective-permute-start | bytes 1572872 | tf_op jit(solution)/shard_map/ppermute | solution.py:43
  23.2 9.5 %collective-permute-start.8 = (bf16[512,512]{1,0:T(8,128)(2,1)S(1)}, bf16[512,512]{1,0:T(8,128)(2,1)S(1)}, u32[]{:S(2)}, u32[]{:S(2)}) collective-permute-start(bf16[512,512]{1,0:T(8,128)(2,1)S(1)} %join_rows.4.m1), channel_id=1, source_target_pairs={{0,2},{1,7},{2,0},{3,5},{4,6},{5,3},{6,4},{7,1},{8,10},{9,15},{10,... | collective-permute-start | bytes 1572872 | tf_op jit(solution)/shard_map/ppermute | solution.py:43
  25.8 9.3 %collective-permute-start.6 = (bf16[512,512]{1,0:T(8,128)(2,1)S(1)}, bf16[512,512]{1,0:T(8,128)(2,1)S(1)}, u32[]{:S(2)}, u32[]{:S(2)}) collective-permute-start(bf16[512,512]{1,0:T(8,128)(2,1)S(1)} %join_rows.3.m0), channel_id=1, source_target_pairs={{0,32},{1,97},{2,34},{3,99},{4,36},{5,101},{6,38},{7,103},{8,40},{... | collective-permute-start | bytes 1572872 | tf_op jit(solution)/shard_map/ppermute | solution.py:43
  28.5 6.6 %collective-permute-start.15 = (bf16[512,512]{1,0:T(8,128)(2,1)S(1)}, bf16[512,512]{1,0:T(8,128)(2,1)S(1)}, u32[]{:S(2)}, u32[]{:S(2)}) collective-permute-start(bf16[512,512]{1,0:T(8,128)(2,1)S(1)} %join_rows.4.m1), channel_id=1, source_target_pairs={{0,1},{1,0},{2,3},{3,2},{4,5},{5,4},{6,7},{7,6},{8,9},{9,8},{10,11... | collective-permute-start | bytes 1572872 | tf_op jit(solution)/shard_map/ppermute | solution.py:47
  28.5 6.6 %collective-permute-start.14 = (bf16[512,512]{1,0:T(8,128)(2,1)S(1)}, bf16[512,512]{1,0:T(8,128)(2,1)S(1)}, u32[]{:S(2)}, u32[]{:S(2)}) collective-permute-start(bf16[512,512]{1,0:T(8,128)(2,1)S(1)} %join_rows.3.m0), channel_id=1, source_target_pairs={{0,1},{1,0},{2,3},{3,2},{4,5},{5,4},{6,7},{7,6},{8,9},{9,8},{10,11... | collective-permute-start | bytes 1572872 | tf_op jit(solution)/shard_map/ppermute | solution.py:47
  32.4 5.6 %collective-permute-start.13 = (bf16[512,512]{1,0:T(8,128)(2,1)S(1)}, bf16[512,512]{1,0:T(8,128)(2,1)S(1)}, u32[]{:S(2)}, u32[]{:S(2)}) collective-permute-start(bf16[512,512]{1,0:T(8,128)(2,1)S(1)} %collective-permute-done.10.refs_2_), channel_id=1, source_target_pairs={{0,1},{1,0},{2,3},{3,2},{4,5},{5,4},{6,7},{7,6},{8,9},{9,8},{10,11... | collective-permute-start | bytes 1572872 | tf_op jit(solution)/shard_map/ppermute | solution.py:47
  32.8 5.3 %collective-permute-start.12 = (bf16[512,512]{1,0:T(8,128)(2,1)S(1)}, bf16[512,512]{1,0:T(8,128)(2,1)S(1)}, u32[]{:S(2)}, u32[]{:S(2)}) collective-permute-start(bf16[512,512]{1,0:T(8,128)(2,1)S(1)} %collective-permute-done.8.refs_1_), channel_id=1, source_target_pairs={{0,1},{1,0},{2,3},{3,2},{4,5},{5,4},{6,7},{7,6},{8,9},{9,8},{10,11... | collective-permute-start | bytes 1572872 | tf_op jit(solution)/shard_map/ppermute | solution.py:47
  35.2 2.9 %collective-permute-start.11 = (bf16[512,512]{1,0:T(8,128)(2,1)S(1)}, bf16[512,512]{1,0:T(8,128)(2,1)S(1)}, u32[]{:S(2)}, u32[]{:S(2)}) collective-permute-start(bf16[512,512]{1,0:T(8,128)(2,1)S(1)} %collective-permute-done.6.refs_0_), channel_id=1, source_target_pairs={{0,1},{1,0},{2,3},{3,2},{4,5},{5,4},{6,7},{7,6},{8,9},{9,8},{10,11... | collective-permute-start | bytes 1572872 | tf_op jit(solution)/shard_map/ppermute | solution.py:47
  46.3 1.4 %collective-permute-start.17 = (f32[32,128]{1,0:T(8,128)S(1)}, f32[32,128]{1,0:T(8,128)S(1)}, u32[]{:S(2)}, u32[]{:S(2)}) collective-permute-start(f32[32,128]{1,0:T(8,128)S(1)} %get-tuple-element.77), channel_id=1, source_target_pairs={{0,1},{1,0},{2,3},{3,2},{4,5},{5,4},{6,7},{7,6},{8,9},{9,8},{10,11... | collective-permute-start | bytes 49160 | tf_op jit(solution)/shard_map/ppermute | solution.py:47
  47.7 3.9 %collective-permute-start.18 = (f32[32,128]{1,0:T(8,128)S(1)}, f32[32,128]{1,0:T(8,128)S(1)}, u32[]{:S(2)}, u32[]{:S(2)}) collective-permute-start(f32[32,128]{1,0:T(8,128)S(1)} %join.4.mine_ref), channel_id=1, source_target_pairs={{0,2},{1,7},{2,0},{3,5},{4,6},{5,3},{6,4},{7,1},{8,10},{9,15},{10,... | collective-permute-start | bytes 49160 | tf_op jit(solution)/shard_map/ppermute | solution.py:43
  51.6 3.9 %collective-permute-start.19 = (f32[32,128]{1,0:T(8,128)S(1)}, f32[32,128]{1,0:T(8,128)S(1)}, u32[]{:S(2)}, u32[]{:S(2)}) collective-permute-start(f32[32,128]{1,0:T(8,128)S(1)} %join.5.mine_ref), channel_id=1, source_target_pairs={{0,8},{1,25},{2,10},{3,27},{4,12},{5,29},{6,14},{7,31},{8,0},{9,17... | collective-permute-start | bytes 49160 | tf_op jit(solution)/shard_map/ppermute | solution.py:43
  55.5 3.9 %collective-permute-start.20 = (f32[32,128]{1,0:T(8,128)S(1)}, f32[32,128]{1,0:T(8,128)S(1)}, u32[]{:S(2)}, u32[]{:S(2)}) collective-permute-start(f32[32,128]{1,0:T(8,128)S(1)} %join.6.mine_ref), channel_id=1, source_target_pairs={{0,32},{1,97},{2,34},{3,99},{4,36},{5,101},{6,38},{7,103},{8,40},{... | collective-permute-start | bytes 49160 | tf_op jit(solution)/shard_map/ppermute | solution.py:43
  59.5 1.5 %collective-permute-start.21 = (f32[32,128]{1,0:T(8,128)S(1)}, f32[32,128]{1,0:T(8,128)S(1)}, u32[]{:S(2)}, u32[]{:S(2)}) collective-permute-start(f32[32,128]{1,0:T(8,128)S(1)} %join.7.mine_ref), channel_id=1, source_target_pairs={{0,1},{1,0},{2,3},{3,2},{4,5},{5,4},{6,7},{7,6},{8,9},{9,8},{10,11... | collective-permute-start | bytes 49160 | tf_op jit(solution)/shard_map/ppermute | solution.py:47
  67.4 3.0 %collective-permute-start.22 = (bf16[512,512]{1,0:T(8,128)(2,1)S(1)}, bf16[512,512]{1,0:T(8,128)(2,1)S(1)}, u32[]{:S(2)}, u32[]{:S(2)}) collective-permute-start(bf16[512,512]{1,0:T(8,128)(2,1)S(1)} %get-tuple-element.90), channel_id=1, source_target_pairs={{0,1},{1,0},{2,3},{3,2},{4,5},{5,4},{6,7},{7,6},{8,9},{9,8},{10,11... | collective-permute-start | bytes 1572872 | tf_op jit(solution)/shard_map/ppermute | solution.py:47
  68.7 4.6 %collective-permute-start.24 = (bf16[512,512]{1,0:T(8,128)(2,1)S(1)}, bf16[512,512]{1,0:T(8,128)(2,1)S(1)}, u32[]{:S(2)}, u32[]{:S(2)}) collective-permute-start(bf16[512,512]{1,0:T(8,128)(2,1)S(1)} %get-tuple-element.97), channel_id=1, source_target_pairs={{0,1},{1,0},{2,3},{3,2},{4,5},{5,4},{6,7},{7,6},{8,9},{9,8},{10,11... | collective-permute-start | bytes 1572872 | tf_op jit(solution)/shard_map/ppermute | solution.py:47
  70.2 3.8 %collective-permute-start.23 = (bf16[512,512]{1,0:T(8,128)(2,1)S(1)}, bf16[512,512]{1,0:T(8,128)(2,1)S(1)}, u32[]{:S(2)}, u32[]{:S(2)}) collective-permute-start(bf16[512,512]{1,0:T(8,128)(2,1)S(1)} %get-tuple-element.94), channel_id=1, source_target_pairs={{0,1},{1,0},{2,3},{3,2},{4,5},{5,4},{6,7},{7,6},{8,9},{9,8},{10,11... | collective-permute-start | bytes 1572872 | tf_op jit(solution)/shard_map/ppermute | solution.py:47
  70.5 10.2 %collective-permute-start.25 = (bf16[528,512]{1,0:T(8,128)(2,1)S(1)}, bf16[528,512]{1,0:T(8,128)(2,1)S(1)}, u32[]{:S(2)}, u32[]{:S(2)}) collective-permute-start(bf16[528,512]{1,0:T(8,128)(2,1)S(1)} %far_message.3.a0), channel_id=1, source_target_pairs={{0,32},{1,97},{2,34},{3,99},{4,36},{5,101},{6,38},{7,103},{8,40},{... | collective-permute-start | bytes 1622024 | tf_op jit(solution)/shard_map/ppermute | solution.py:43
  73.4 9.3 %collective-permute-start.31 = (bf16[512,512]{1,0:T(8,128)(2,1)S(1)}, bf16[512,512]{1,0:T(8,128)(2,1)S(1)}, u32[]{:S(2)}, u32[]{:S(2)}) collective-permute-start(bf16[512,512]{1,0:T(8,128)(2,1)S(1)} %far_message.5.a2), channel_id=1, source_target_pairs={{0,8},{1,25},{2,10},{3,27},{4,12},{5,29},{6,14},{7,31},{8,0},{9,17... | collective-permute-start | bytes 1572872 | tf_op jit(solution)/shard_map/ppermute | solution.py:43
  74.1 10.1 %collective-permute-start.28 = (bf16[512,512]{1,0:T(8,128)(2,1)S(1)}, bf16[512,512]{1,0:T(8,128)(2,1)S(1)}, u32[]{:S(2)}, u32[]{:S(2)}) collective-permute-start(bf16[512,512]{1,0:T(8,128)(2,1)S(1)} %far_message.4.a1), channel_id=1, source_target_pairs={{0,2},{1,7},{2,0},{3,5},{4,6},{5,3},{6,4},{7,1},{8,10},{9,15},{10,... | collective-permute-start | bytes 1572872 | tf_op jit(solution)/shard_map/ppermute | solution.py:43
  77.7 5.1 %collective-permute-start.32 = (bf16[512,512]{1,0:T(8,128)(2,1)S(1)}, bf16[512,512]{1,0:T(8,128)(2,1)S(1)}, u32[]{:S(2)}, u32[]{:S(2)}) collective-permute-start(bf16[512,512]{1,0:T(8,128)(2,1)S(1)} %get-tuple-element.113), channel_id=1, source_target_pairs={{0,1},{1,0},{2,3},{3,2},{4,5},{5,4},{6,7},{7,6},{8,9},{9,8},{10,11... | collective-permute-start | bytes 1572872 | tf_op jit(solution)/shard_map/ppermute | solution.py:47
  78.8 2.4 %collective-permute-start.26 = (bf16[512,512]{1,0:T(8,128)(2,1)S(1)}, bf16[512,512]{1,0:T(8,128)(2,1)S(1)}, u32[]{:S(2)}, u32[]{:S(2)}) collective-permute-start(bf16[512,512]{1,0:T(8,128)(2,1)S(1)} %get-tuple-element.100), channel_id=1, source_target_pairs={{0,1},{1,0},{2,3},{3,2},{4,5},{5,4},{6,7},{7,6},{8,9},{9,8},{10,11... | collective-permute-start | bytes 1572872 | tf_op jit(solution)/shard_map/ppermute | solution.py:47
  80.8 3.5 %collective-permute-start.29 = (bf16[512,512]{1,0:T(8,128)(2,1)S(1)}, bf16[512,512]{1,0:T(8,128)(2,1)S(1)}, u32[]{:S(2)}, u32[]{:S(2)}) collective-permute-start(bf16[512,512]{1,0:T(8,128)(2,1)S(1)} %get-tuple-element.107), channel_id=1, source_target_pairs={{0,1},{1,0},{2,3},{3,2},{4,5},{5,4},{6,7},{7,6},{8,9},{9,8},{10,11... | collective-permute-start | bytes 1572872 | tf_op jit(solution)/shard_map/ppermute | solution.py:47
  81.4 6.7 %collective-permute-start.27 = (bf16[272,512]{1,0:T(8,128)(2,1)S(1)}, bf16[272,512]{1,0:T(8,128)(2,1)S(1)}, u32[]{:S(2)}, u32[]{:S(2)}) collective-permute-start(bf16[272,512]{1,0:T(8,128)(2,1)S(1)} %get-tuple-element.103), channel_id=1, source_target_pairs={{0,8},{1,25},{2,10},{3,27},{4,12},{5,29},{6,14},{7,31},{8,0},{9,17... | collective-permute-start | bytes 835592 | tf_op jit(solution)/shard_map/ppermute | solution.py:43
  82.9 7.0 %collective-permute-start.33 = (bf16[256,512]{1,0:T(8,128)(2,1)S(1)}, bf16[256,512]{1,0:T(8,128)(2,1)S(1)}, u32[]{:S(2)}, u32[]{:S(2)}) collective-permute-start(bf16[256,512]{1,0:T(8,128)(2,1)S(1)} %get-tuple-element.115), channel_id=1, source_target_pairs={{0,2},{1,7},{2,0},{3,5},{4,6},{5,3},{6,4},{7,1},{8,10},{9,15},{10,... | collective-permute-start | bytes 786440 | tf_op jit(solution)/shard_map/ppermute | solution.py:43
  84.4 6.5 %collective-permute-start.30 = (bf16[256,512]{1,0:T(8,128)(2,1)S(1)}, bf16[256,512]{1,0:T(8,128)(2,1)S(1)}, u32[]{:S(2)}, u32[]{:S(2)}) collective-permute-start(bf16[256,512]{1,0:T(8,128)(2,1)S(1)} %get-tuple-element.109), channel_id=1, source_target_pairs={{0,32},{1,97},{2,34},{3,99},{4,36},{5,101},{6,38},{7,103},{8,40},{... | collective-permute-start | bytes 786440 | tf_op jit(solution)/shard_map/ppermute | solution.py:43
  88.1 8.0 %collective-permute-start.34 = (bf16[144,512]{1,0:T(8,128)(2,1)S(1)}, bf16[144,512]{1,0:T(8,128)(2,1)S(1)}, u32[]{:S(2)}, u32[]{:S(2)}) collective-permute-start(bf16[144,512]{1,0:T(8,128)(2,1)S(1)} %get-tuple-element.117), channel_id=1, source_target_pairs={{0,2},{1,7},{2,0},{3,5},{4,6},{5,3},{6,4},{7,1},{8,10},{9,15},{10,... | collective-permute-start | bytes 442376 | tf_op jit(solution)/shard_map/ppermute | solution.py:43
  90.0 5.1 %collective-permute-start.36 = (bf16[128,512]{1,0:T(8,128)(2,1)S(1)}, bf16[128,512]{1,0:T(8,128)(2,1)S(1)}, u32[]{:S(2)}, u32[]{:S(2)}) collective-permute-start(bf16[128,512]{1,0:T(8,128)(2,1)S(1)} %get-tuple-element.119), channel_id=1, source_target_pairs={{0,32},{1,97},{2,34},{3,99},{4,36},{5,101},{6,38},{7,103},{8,40},{... | collective-permute-start | bytes 393224 | tf_op jit(solution)/shard_map/ppermute | solution.py:43
  91.0 5.1 %collective-permute-start.35 = (bf16[128,512]{1,0:T(8,128)(2,1)S(1)}, bf16[128,512]{1,0:T(8,128)(2,1)S(1)}, u32[]{:S(2)}, u32[]{:S(2)}) collective-permute-start(bf16[128,512]{1,0:T(8,128)(2,1)S(1)} %get-tuple-element.118), channel_id=1, source_target_pairs={{0,8},{1,25},{2,10},{3,27},{4,12},{5,29},{6,14},{7,31},{8,0},{9,17... | collective-permute-start | bytes 393224 | tf_op jit(solution)/shard_map/ppermute | solution.py:43
  96.3 2.4 %collective-permute-start.37 = (f32[392,512]{1,0:T(8,128)S(1)}, f32[392,512]{1,0:T(8,128)S(1)}, u32[]{:S(2)}, u32[]{:S(2)}) collective-permute-start(f32[392,512]{1,0:T(8,128)S(1)} %get-tuple-element.125), channel_id=1, source_target_pairs={{0,1},{1,0},{2,3},{3,2},{4,5},{5,4},{6,7},{7,6},{8,9},{9,8},{10,11... | collective-permute-start | bytes 2408456 | tf_op jit(solution)/shard_map/ppermute | solution.py:47

commit v13 on v12

--- a/solution.py
+++ b/solution.py
@@ -393,20 +393,25 @@
     loss_out[...] = (keep_ref[384:385, 0:1] + got_ref[384:385, 0:1]) * (0.5 / count)
 
 
-def pair_kernel(core_ref, image_hbm, text_hbm, image_got, text_got, o0, o1, o2, image_ref, text_ref, sems):
-    copies = [
-        pltpu.make_async_copy(image_hbm, image_ref, sems.at[0]),
-        pltpu.make_async_copy(text_hbm, text_ref, sems.at[1]),
-    ]
-    for copy in copies:
+def pair_kernel(core_ref, image_hbm, text_hbm, image_got, text_got, o0, o1, o2, own_ref, sem):
+    first = core_ref[0] == 0
+
+    @pl.when(first)
+    def _():
+        copy = pltpu.make_async_copy(image_hbm, own_ref, sem)
         copy.start()
-    for copy in copies:
         copy.wait()
-    first = core_ref[0] == 0
+
+    @pl.when(jnp.logical_not(first))
+    def _():
+        copy = pltpu.make_async_copy(text_hbm, own_ref, sem)
+        copy.start()
+        copy.wait()
+
     for q, out in enumerate((o0, o1, o2)):
         rows = slice(q * 64, q * 64 + 64)
-        out[0:64, :] = jnp.where(first, image_ref[rows, :], text_got[rows, :])
-        out[64:128, :] = jnp.where(first, image_got[rows, :], text_ref[rows, :])
+        out[0:64, :] = jnp.where(first, own_ref[rows, :], text_got[rows, :])
+        out[64:128, :] = jnp.where(first, image_got[rows, :], own_ref[rows, :])
 
 
 def pair(core_id, image_emb, text_emb, image_got, text_got):
@@ -417,7 +422,7 @@
         in_specs=[SMEM, anywhere, anywhere, VMEM, VMEM],
         out_specs=[VMEM] * 3,
         out_shape=[shape(128, width, dtype=bf16)] * 3,
-        scratch_shapes=[pltpu.VMEM((rows, width), bf16)] * 2 + [pltpu.SemaphoreType.DMA((2,))],
+        scratch_shapes=[pltpu.VMEM((rows, width), bf16), pltpu.SemaphoreType.DMA],
         compiler_params=pltpu.CompilerParams(vmem_limit_bytes=4 << 20),
         name="pair",
     )(

time: 99.9 us -> 99.8 us (level)
  no operation moved by 1% of the time
where the time goes in v13:
time: 99.8 us; the launch traced here: 99.6 us
  starting transfers between devices  43.1 us (43%)
  waiting for transfers between devices  29.1 us (29%)
  Pallas kernels  26.5 us (27%)
    ppermute x21, starting transfers between devices, flip_permute(): return lax.ppermute(x, AXES, ROLE_PAIRS[dim % 3])  37.3 us
    pallas_call x31, Pallas kernels, call(): pl.pallas_call(kernel, in_specs=in_specs, out_specs=[VMEM] * len(outs), o...  25.6 us
    ppermute x21, waiting for transfers between devices, flip_permute(): return lax.ppermute(x, AXES, ROLE_PAIRS[dim % 3])  23.1 us
    ppermute x17, waiting for transfers between devices, core_swap(): return lax.ppermute(x, 'c', SWAP)  5.98 us
    ppermute x17, starting transfers between devices, core_swap(): return lax.ppermute(x, 'c', SWAP)  5.84 us
  transfers between devices with their start and end apart: 38, of which 19 were waited for; matrix products, arithmetic and copies ran while one was open for 0% of the time, Pallas kernels for 10%

profile of v13, /device:TPU:1, one launch (start us, length us, event | category | flops | bytes accessed | tf_op | source)
XLA Modules:
  0.0 99.6 jit_solution(10211443096150776777)
XLA Ops:
  0.6 1.5 %collective-permute-start = (bf16[192,512]{1,0:T(8,128)(2,1)}, bf16[192,512]{1,0:T(8,128)(2,1)S(1)}, u32[]{:S(2)}, u32[]{:S(2)}) collective-permute-start(bf16[192,512]{1,0:T(8,128)(2,1)} %refs_10_.1), channel_id=1, source_target_pairs={{0,1},{1,0},{2,3},{3,2},{4,5},{5,4},{6,7},{7,6},{8,9},{9,8},{10,11... | collective-permute-start | bytes 589832 | tf_op jit(solution)/shard_map/ppermute | solution.py:47
  2.2 1.2 %collective-permute-done.image_got = bf16[192,512]{1,0:T(8,128)(2,1)S(1)} collective-permute-done((bf16[192,512]{1,0:T(8,128)(2,1)}, bf16[192,512]{1,0:T(8,128)(2,1)S(1)}, u32[]{:S(2)}, u32[]{:S(2)}) %collective-permute-start) | collective-permute-done | bytes 196640 | tf_op jit(solution)/shard_map/ppermute | solution.py:47
  3.8 1.0 pair.1
  4.8 2.6 %collective-permute-start.2 = (bf16[128,512]{1,0:T(8,128)(2,1)S(1)}, bf16[128,512]{1,0:T(8,128)(2,1)S(1)}, u32[]{:S(2)}, u32[]{:S(2)}) collective-permute-start(bf16[128,512]{1,0:T(8,128)(2,1)S(1)} %get-tuple-element.66.refs_0_), channel_id=1, source_target_pairs={{0,2},{1,7},{2,0},{3,5},{4,6},{5,3},{6,4},{7,1},{8,10},{9,15},{10,... | collective-permute-start | bytes 393224 | tf_op jit(solution)/shard_map/ppermute | solution.py:43
  7.4 2.7 %collective-permute-start.3 = (bf16[128,512]{1,0:T(8,128)(2,1)S(1)}, bf16[128,512]{1,0:T(8,128)(2,1)S(1)}, u32[]{:S(2)}, u32[]{:S(2)}) collective-permute-start(bf16[128,512]{1,0:T(8,128)(2,1)S(1)} %get-tuple-element.67.refs_1_), channel_id=1, source_target_pairs={{0,8},{1,25},{2,10},{3,27},{4,12},{5,29},{6,14},{7,31},{8,0},{9,17... | collective-permute-start | bytes 393224 | tf_op jit(solution)/shard_map/ppermute | solution.py:43
  10.1 3.8 %collective-permute-start.4 = (bf16[128,512]{1,0:T(8,128)(2,1)S(1)}, bf16[128,512]{1,0:T(8,128)(2,1)S(1)}, u32[]{:S(2)}, u32[]{:S(2)}) collective-permute-start(bf16[128,512]{1,0:T(8,128)(2,1)S(1)} %get-tuple-element.68.refs_2_), channel_id=1, source_target_pairs={{0,32},{1,97},{2,34},{3,99},{4,36},{5,101},{6,38},{7,103},{8,40},{... | collective-permute-start | bytes 393224 | tf_op jit(solution)/shard_map/ppermute | solution.py:43
  13.9 2.3 %collective-permute-done.4.refs_5_ = bf16[128,512]{1,0:T(8,128)(2,1)S(1)} collective-permute-done((bf16[128,512]{1,0:T(8,128)(2,1)S(1)}, bf16[128,512]{1,0:T(8,128)(2,1)S(1)}, u32[]{:S(2)}, u32[]{:S(2)}) %collective-permute-start.4) | collective-permute-done | bytes 131104 | tf_op jit(solution)/shard_map/ppermute | solution.py:43
  16.6 2.7 %collective-permute-start.7 = (bf16[256,512]{1,0:T(8,128)(2,1)S(1)}, bf16[256,512]{1,0:T(8,128)(2,1)S(1)}, u32[]{:S(2)}, u32[]{:S(2)}) collective-permute-start(bf16[256,512]{1,0:T(8,128)(2,1)S(1)} %get-tuple-element.70.refs_0_), channel_id=1, source_target_pairs={{0,32},{1,97},{2,34},{3,99},{4,36},{5,101},{6,38},{7,103},{8,40},{... | collective-permute-start | bytes 786440 | tf_op jit(solution)/shard_map/ppermute | solution.py:43
  19.3 3.6 %collective-permute-done.9.refs_1_ = bf16[256,512]{1,0:T(8,128)(2,1)S(1)} collective-permute-done((bf16[256,512]{1,0:T(8,128)(2,1)S(1)}, bf16[256,512]{1,0:T(8,128)(2,1)S(1)}, u32[]{:S(2)}, u32[]{:S(2)}) %collective-permute-start.9) | collective-permute-done | bytes 262176 | tf_op jit(solution)/shard_map/ppermute | solution.py:43
  23.1 2.5 %collective-permute-start.8 = (bf16[512,512]{1,0:T(8,128)(2,1)S(1)}, bf16[512,512]{1,0:T(8,128)(2,1)S(1)}, u32[]{:S(2)}, u32[]{:S(2)}) collective-permute-start(bf16[512,512]{1,0:T(8,128)(2,1)S(1)} %join_rows.4.m1), channel_id=1, source_target_pairs={{0,2},{1,7},{2,0},{3,5},{4,6},{5,3},{6,4},{7,1},{8,10},{9,15},{10,... | collective-permute-start | bytes 1572872 | tf_op jit(solution)/shard_map/ppermute | solution.py:43
  25.7 2.7 %collective-permute-start.6 = (bf16[512,512]{1,0:T(8,128)(2,1)S(1)}, bf16[512,512]{1,0:T(8,128)(2,1)S(1)}, u32[]{:S(2)}, u32[]{:S(2)}) collective-permute-start(bf16[512,512]{1,0:T(8,128)(2,1)S(1)} %join_rows.3.m0), channel_id=1, source_target_pairs={{0,32},{1,97},{2,34},{3,99},{4,36},{5,101},{6,38},{7,103},{8,40},{... | collective-permute-start | bytes 1572872 | tf_op jit(solution)/shard_map/ppermute | solution.py:43
  28.4 0.5 collective-permute-start.14
  28.9 3.4 %collective-permute-done.10.refs_2_ = bf16[512,512]{1,0:T(8,128)(2,1)S(1)} collective-permute-done((bf16[512,512]{1,0:T(8,128)(2,1)S(1)}, bf16[512,512]{1,0:T(8,128)(2,1)S(1)}, u32[]{:S(2)}, u32[]{:S(2)}) %collective-permute-start.10) | collective-permute-done | bytes 524320 | tf_op jit(solution)/shard_map/ppermute | solution.py:43
  32.9 2.1 %collective-permute-done.6.refs_0_ = bf16[512,512]{1,0:T(8,128)(2,1)S(1)} collective-permute-done((bf16[512,512]{1,0:T(8,128)(2,1)S(1)}, bf16[512,512]{1,0:T(8,128)(2,1)S(1)}, u32[]{:S(2)}, u32[]{:S(2)}) %collective-permute-start.6) | collective-permute-done | bytes 524320 | tf_op jit(solution)/shard_map/ppermute | solution.py:43
  35.1 2.9 %near.1 = (bf16[768,512]{1,0:T(8,128)(2,1)S(1)}, bf16[1536,512]{1,0:T(8,128)(2,1)S(1)}, f32[768,1536]{1,0:T(8,128)S(1)}, f32[6,128]{1,0:T(8,128)S(1)}, f32[12,128]{1,0:T(8,128)S(1)}) custom-call(s32[1]{0:T(128)} %bitcast.core_ref, bf16[512,512]{1,0:T(8,128)(2,1)S(1)} %join_rows.3.m0, bf16[512,512]{1,0:T(8,128)(2,1)S(1)} %join_rows.4.m1, ...), custom_call_target="tpu_custom_call" | custom-call | flops 1207959552 | tf_op jit(solution)/shard_map/near/pallas_call | solution.py:52
  38.0 8.2 %far.1 = (bf16[768,512]{1,0:T(8,128)(2,1)S(1)}, bf16[1536,512]{1,0:T(8,128)(2,1)S(1)}, f32[256,3072]{1,0:T(8,128)S(1)}, f32[256,3072]{1,0:T(8,128)S(1)}, f32[256...) custom-call(s32[1]{0:T(128)} %bitcast.core_ref, ...), custom_call_target="tpu_custom_call" | custom-call | flops 3623878656 | tf_op jit(solution)/shard_map/far/pallas_call | solution.py:52
  46.2 0.6 collective-permute-start.17
  46.8 0.8 collective-permute-done.17.got_ref
  47.6 2.6 %collective-permute-start.18 = (f32[32,128]{1,0:T(8,128)S(1)}, f32[32,128]{1,0:T(8,128)S(1)}, u32[]{:S(2)}, u32[]{:S(2)}) collective-permute-start(f32[32,128]{1,0:T(8,128)S(1)} %join.4.mine_ref), channel_id=1, source_target_pairs={{0,2},{1,7},{2,0},{3,5},{4,6},{5,3},{6,4},{7,1},{8,10},{9,15},{10,... | collective-permute-start | bytes 49160 | tf_op jit(solution)/shard_map/ppermute | solution.py:43
  50.2 1.3 %collective-permute-done.18.got_ref = f32[32,128]{1,0:T(8,128)S(1)} collective-permute-done((f32[32,128]{1,0:T(8,128)S(1)}, f32[32,128]{1,0:T(8,128)S(1)}, u32[]{:S(2)}, u32[]{:S(2)}) %collective-permute-start.18) | collective-permute-done | bytes 16416 | tf_op jit(solution)/shard_map/ppermute | solution.py:43
  51.5 0.5 collective-permute-start.19
  52.0 3.4 %collective-permute-done.19.got_ref = f32[32,128]{1,0:T(8,128)S(1)} collective-permute-done((f32[32,128]{1,0:T(8,128)S(1)}, f32[32,128]{1,0:T(8,128)S(1)}, u32[]{:S(2)}, u32[]{:S(2)}) %collective-permute-start.19) | collective-permute-done | bytes 16416 | tf_op jit(solution)/shard_map/ppermute | solution.py:43
  55.4 2.7 %collective-permute-start.20 = (f32[32,128]{1,0:T(8,128)S(1)}, f32[32,128]{1,0:T(8,128)S(1)}, u32[]{:S(2)}, u32[]{:S(2)}) collective-permute-start(f32[32,128]{1,0:T(8,128)S(1)} %join.6.mine_ref), channel_id=1, source_target_pairs={{0,32},{1,97},{2,34},{3,99},{4,36},{5,101},{6,38},{7,103},{8,40},{... | collective-permute-start | bytes 49160 | tf_op jit(solution)/shard_map/ppermute | solution.py:43
  58.1 1.2 %collective-permute-done.20.got_ref = f32[32,128]{1,0:T(8,128)S(1)} collective-permute-done((f32[32,128]{1,0:T(8,128)S(1)}, f32[32,128]{1,0:T(8,128)S(1)}, u32[]{:S(2)}, u32[]{:S(2)}) %collective-permute-start.20) | collective-permute-done | bytes 16416 | tf_op jit(solution)/shard_map/ppermute | solution.py:43
  59.3 0.5 collective-permute-start.21
  59.8 1.0 %collective-permute-done.21.other_ref = f32[32,128]{1,0:T(8,128)S(1)} collective-permute-done((f32[32,128]{1,0:T(8,128)S(1)}, f32[32,128]{1,0:T(8,128)S(1)}, u32[]{:S(2)}, u32[]{:S(2)}) %collective-permute-start.21) | collective-permute-done | bytes 16416 | tf_op jit(solution)/shard_map/ppermute | solution.py:47
  60.8 5.4 %coeffs.1 = (bf16[1536,3072]{1,0:T(8,128)(2,1)S(1)}, bf16[256,512]{1,0:T(8,128)(2,1)S(1)}, bf16[256,512]{1,0:T(8,128)(2,1)S(1)}, bf16[256,512]{1,0:T(8,128)(2,1)...) custom-call(s32[1]{0:T(128)} %bitcast.core_ref, ...), custom_call_target="tpu_custom_call" | custom-call | flops 4831838208 | tf_op jit(solution)/shard_map/coeffs/pallas_call | solution.py:52
  66.2 1.1 %far_text.3 = (bf16[512,512]{1,0:T(8,128)(2,1)S(1)}, bf16[512,512]{1,0:T(8,128)(2,1)S(1)}) custom-call(s32[1]{0:T(128)} %bitcast.core_ref, bf16[1536,3072]{1,0:T(8,128)(2,1)S(1)} %get-tuple-element.84.coeff_ref, bf16[768,512]{1,0:T(8,128)(2,1)S(1)} %get-tuple-element.72.refs_6_.near_rows, bf16[768,512]{1,0:T(8,128)(2,1)S(1)} %get-tuple-element.85.far_rows, ...), custom_call_target="tpu_custom_call" | custom-call | flops 805306368 | tf_op jit(solution)/shard_map/far_text/pallas_call | solution.py:52
  67.5 1.0 %far_text.5 = (bf16[512,512]{1,0:T(8,128)(2,1)S(1)}, bf16[512,512]{1,0:T(8,128)(2,1)S(1)}) custom-call(s32[1]{0:T(128)} %bitcast.core_ref, bf16[1536,3072]{1,0:T(8,128)(2,1)S(1)} %get-tuple-element.84.coeff_ref, bf16[768,512]{1,0:T(8,128)(2,1)S(1)} %get-tuple-element.72.refs_6_.near_rows, bf16[768,512]{1,0:T(8,128)(2,1)S(1)} %get-tuple-element.85.far_rows, ...), custom_call_target="tpu_custom_call" | custom-call | flops 805306368 | tf_op jit(solution)/shard_map/far_text/pallas_call | solution.py:52
  69.0 1.0 %far_text.4 = (bf16[512,512]{1,0:T(8,128)(2,1)S(1)}, bf16[512,512]{1,0:T(8,128)(2,1)S(1)}) custom-call(s32[1]{0:T(128)} %bitcast.core_ref, bf16[1536,3072]{1,0:T(8,128)(2,1)S(1)} %get-tuple-element.84.coeff_ref, bf16[768,512]{1,0:T(8,128)(2,1)S(1)} %get-tuple-element.72.refs_6_.near_rows, bf16[768,512]{1,0:T(8,128)(2,1)S(1)} %get-tuple-element.85.far_rows, ...), custom_call_target="tpu_custom_call" | custom-call | flops 805306368 | tf_op jit(solution)/shard_map/far_text/pallas_call | solution.py:52
  70.4 2.7 %collective-permute-start.25 = (bf16[528,512]{1,0:T(8,128)(2,1)S(1)}, bf16[528,512]{1,0:T(8,128)(2,1)S(1)}, u32[]{:S(2)}, u32[]{:S(2)}) collective-permute-start(bf16[528,512]{1,0:T(8,128)(2,1)S(1)} %far_message.3.a0), channel_id=1, source_target_pairs={{0,32},{1,97},{2,34},{3,99},{4,36},{5,101},{6,38},{7,103},{8,40},{... | collective-permute-start | bytes 1622024 | tf_op jit(solution)/shard_map/ppermute | solution.py:43
  73.3 0.6 collective-permute-start.31
  74.0 2.5 %collective-permute-start.28 = (bf16[512,512]{1,0:T(8,128)(2,1)S(1)}, bf16[512,512]{1,0:T(8,128)(2,1)S(1)}, u32[]{:S(2)}, u32[]{:S(2)}) collective-permute-start(bf16[512,512]{1,0:T(8,128)(2,1)S(1)} %far_message.4.a1), channel_id=1, source_target_pairs={{0,2},{1,7},{2,0},{3,5},{4,6},{5,3},{6,4},{7,1},{8,10},{9,15},{10,... | collective-permute-start | bytes 1572872 | tf_op jit(solution)/shard_map/ppermute | solution.py:43
  76.5 1.1 %near_text.5 = (f32[512,512]{1,0:T(8,128)S(1)}, bf16[512,512]{1,0:T(8,128)(2,1)S(1)}, f32[256,512]{1,0:T(8,128)S(1)}) custom-call(s32[1]{0:T(128)} %bitcast.core_ref, bf16[1536,3072]{1,0:T(8,128)(2,1)S(1)} %get-tuple-element.84.coeff_ref, bf16[768,512]{1,0:T(8,128)(2,1)S(1)} %get-tuple-element.72.refs_6_.near_rows, ...), custom_call_target="tpu_custom_call" | custom-call | flops 805306368 | tf_op jit(solution)/shard_map/near_text/pallas_call | solution.py:52
  77.6 1.1 %near_text.3 = (f32[512,512]{1,0:T(8,128)S(1)}, bf16[512,512]{1,0:T(8,128)(2,1)S(1)}, f32[256,512]{1,0:T(8,128)S(1)}) custom-call(s32[1]{0:T(128)} %bitcast.core_ref, bf16[1536,3072]{1,0:T(8,128)(2,1)S(1)} %get-tuple-element.84.coeff_ref, bf16[768,512]{1,0:T(8,128)(2,1)S(1)} %get-tuple-element.72.refs_6_.near_rows, ...), custom_call_target="tpu_custom_call" | custom-call | flops 805306368 | tf_op jit(solution)/shard_map/near_text/pallas_call | solution.py:52
  78.7 0.8 collective-permute-start.26
  79.6 1.1 %near_text.4 = (f32[512,512]{1,0:T(8,128)S(1)}, bf16[512,512]{1,0:T(8,128)(2,1)S(1)}, f32[256,512]{1,0:T(8,128)S(1)}) custom-call(s32[1]{0:T(128)} %bitcast.core_ref, bf16[1536,3072]{1,0:T(8,128)(2,1)S(1)} %get-tuple-element.84.coeff_ref, bf16[768,512]{1,0:T(8,128)(2,1)S(1)} %get-tuple-element.72.refs_6_.near_rows, ...), custom_call_target="tpu_custom_call" | custom-call | flops 805306368 | tf_op jit(solution)/shard_map/near_text/pallas_call | solution.py:52
  81.4 1.2 %collective-permute-done.31.got_ref = bf16[512,512]{1,0:T(8,128)(2,1)S(1)} collective-permute-done((bf16[512,512]{1,0:T(8,128)(2,1)S(1)}, bf16[512,512]{1,0:T(8,128)(2,1)S(1)}, u32[]{:S(2)}, u32[]{:S(2)}) %collective-permute-start.31) | collective-permute-done | bytes 524320 | tf_op jit(solution)/shard_map/ppermute | solution.py:43
  82.8 1.3 %collective-permute-start.33 = (bf16[256,512]{1,0:T(8,128)(2,1)S(1)}, bf16[256,512]{1,0:T(8,128)(2,1)S(1)}, u32[]{:S(2)}, u32[]{:S(2)}) collective-permute-start(bf16[256,512]{1,0:T(8,128)(2,1)S(1)} %get-tuple-element.115), channel_id=1, source_target_pairs={{0,2},{1,7},{2,0},{3,5},{4,6},{5,3},{6,4},{7,1},{8,10},{9,15},{10,... | collective-permute-start | bytes 786440 | tf_op jit(solution)/shard_map/ppermute | solution.py:43
  84.3 2.4 %collective-permute-start.30 = (bf16[256,512]{1,0:T(8,128)(2,1)S(1)}, bf16[256,512]{1,0:T(8,128)(2,1)S(1)}, u32[]{:S(2)}, u32[]{:S(2)}) collective-permute-start(bf16[256,512]{1,0:T(8,128)(2,1)S(1)} %get-tuple-element.109), channel_id=1, source_target_pairs={{0,32},{1,97},{2,34},{3,99},{4,36},{5,101},{6,38},{7,103},{8,40},{... | collective-permute-start | bytes 786440 | tf_op jit(solution)/shard_map/ppermute | solution.py:43
  86.7 1.2 %collective-permute-done.27.got_ref = bf16[272,512]{1,0:T(8,128)(2,1)S(1)} collective-permute-done((bf16[272,512]{1,0:T(8,128)(2,1)S(1)}, bf16[272,512]{1,0:T(8,128)(2,1)S(1)}, u32[]{:S(2)}, u32[]{:S(2)}) %collective-permute-start.27) | collective-permute-done | bytes 278560 | tf_op jit(solution)/shard_map/ppermute | solution.py:43
  88.0 1.8 %collective-permute-start.34 = (bf16[144,512]{1,0:T(8,128)(2,1)S(1)}, bf16[144,512]{1,0:T(8,128)(2,1)S(1)}, u32[]{:S(2)}, u32[]{:S(2)}) collective-permute-start(bf16[144,512]{1,0:T(8,128)(2,1)S(1)} %get-tuple-element.117), channel_id=1, source_target_pairs={{0,2},{1,7},{2,0},{3,5},{4,6},{5,3},{6,4},{7,1},{8,10},{9,15},{10,... | collective-permute-start | bytes 442376 | tf_op jit(solution)/shard_map/ppermute | solution.py:43
  89.9 0.7 collective-permute-start.36
  90.9 2.2 %collective-permute-start.35 = (bf16[128,512]{1,0:T(8,128)(2,1)S(1)}, bf16[128,512]{1,0:T(8,128)(2,1)S(1)}, u32[]{:S(2)}, u32[]{:S(2)}) collective-permute-start(bf16[128,512]{1,0:T(8,128)(2,1)S(1)} %get-tuple-element.118), channel_id=1, source_target_pairs={{0,8},{1,25},{2,10},{3,27},{4,12},{5,29},{6,14},{7,31},{8,0},{9,17... | collective-permute-start | bytes 393224 | tf_op jit(solution)/shard_map/ppermute | solution.py:43
  93.1 1.9 %collective-permute-done.36.r2 = bf16[128,512]{1,0:T(8,128)(2,1)S(1)} collective-permute-done((bf16[128,512]{1,0:T(8,128)(2,1)S(1)}, bf16[128,512]{1,0:T(8,128)(2,1)S(1)}, u32[]{:S(2)}, u32[]{:S(2)}) %collective-permute-start.36) | collective-permute-done | bytes 131104 | tf_op jit(solution)/shard_map/ppermute | solution.py:43
  95.0 1.1 %collective-permute-done.35.r1 = bf16[128,512]{1,0:T(8,128)(2,1)S(1)} collective-permute-done((bf16[128,512]{1,0:T(8,128)(2,1)S(1)}, bf16[128,512]{1,0:T(8,128)(2,1)S(1)}, u32[]{:S(2)}, u32[]{:S(2)}) %collective-permute-start.35) | collective-permute-done | bytes 131104 | tf_op jit(solution)/shard_map/ppermute | solution.py:43
  96.3 2.3 %collective-permute-done.37.got_ref = f32[392,512]{1,0:T(8,128)S(1)} collective-permute-done((f32[392,512]{1,0:T(8,128)S(1)}, f32[392,512]{1,0:T(8,128)S(1)}, u32[]{:S(2)}, u32[]{:S(2)}) %collective-permute-start.37) | collective-permute-done | bytes 802848 | tf_op jit(solution)/shard_map/ppermute | solution.py:47
  98.6 1.0 %finish.1 = (f32[192,512]{1,0:T(8,128)}, f32[192,512]{1,0:T(8,128)}, f32[1,1]{1,0:T(1,128)}) custom-call(s32[1]{0:T(128)} %bitcast.core_ref, f32[392,512]{1,0:T(8,128)S(1)} %get-tuple-element.124.keep_ref, f32[392,512]{1,0:T(8,128)S(1)} %collective-permute-done.37.got_ref), custom_call_target="tpu_custom_call" | custom-call | tf_op jit(solution)/shard_map/finish/pallas_call | solution.py:52
  (64 shorter events, 5.3 us)
Async XLA Ops:
  0.6 2.8 %collective-permute-start = (bf16[192,512]{1,0:T(8,128)(2,1)}, bf16[192,512]{1,0:T(8,128)(2,1)S(1)}, u32[]{:S(2)}, u32[]{:S(2)}) collective-permute-start(bf16[192,512]{1,0:T(8,128)(2,1)} %refs_10_.1), channel_id=1, source_target_pairs={{0,1},{1,0},{2,3},{3,2},{4,5},{5,4},{6,7},{7,6},{8,9},{9,8},{10,11... | collective-permute-start | bytes 589832 | tf_op jit(solution)/shard_map/ppermute | solution.py:47
  2.1 1.7 %collective-permute-start.1 = (bf16[192,512]{1,0:T(8,128)(2,1)}, bf16[192,512]{1,0:T(8,128)(2,1)S(1)}, u32[]{:S(2)}, u32[]{:S(2)}) collective-permute-start(bf16[192,512]{1,0:T(8,128)(2,1)} %refs_11_.1), channel_id=1, source_target_pairs={{0,1},{1,0},{2,3},{3,2},{4,5},{5,4},{6,7},{7,6},{8,9},{9,8},{10,11... | collective-permute-start | bytes 589832 | tf_op jit(solution)/shard_map/ppermute | solution.py:47
  4.8 9.1 %collective-permute-start.2 = (bf16[128,512]{1,0:T(8,128)(2,1)S(1)}, bf16[128,512]{1,0:T(8,128)(2,1)S(1)}, u32[]{:S(2)}, u32[]{:S(2)}) collective-permute-start(bf16[128,512]{1,0:T(8,128)(2,1)S(1)} %get-tuple-element.66.refs_0_), channel_id=1, source_target_pairs={{0,2},{1,7},{2,0},{3,5},{4,6},{5,3},{6,4},{7,1},{8,10},{9,15},{10,... | collective-permute-start | bytes 393224 | tf_op jit(solution)/shard_map/ppermute | solution.py:43
  7.4 6.5 %collective-permute-start.3 = (bf16[128,512]{1,0:T(8,128)(2,1)S(1)}, bf16[128,512]{1,0:T(8,128)(2,1)S(1)}, u32[]{:S(2)}, u32[]{:S(2)}) collective-permute-start(bf16[128,512]{1,0:T(8,128)(2,1)S(1)} %get-tuple-element.67.refs_1_), channel_id=1, source_target_pairs={{0,8},{1,25},{2,10},{3,27},{4,12},{5,29},{6,14},{7,31},{8,0},{9,17... | collective-permute-start | bytes 393224 | tf_op jit(solution)/shard_map/ppermute | solution.py:43
  10.1 6.1 %collective-permute-start.4 = (bf16[128,512]{1,0:T(8,128)(2,1)S(1)}, bf16[128,512]{1,0:T(8,128)(2,1)S(1)}, u32[]{:S(2)}, u32[]{:S(2)}) collective-permute-start(bf16[128,512]{1,0:T(8,128)(2,1)S(1)} %get-tuple-element.68.refs_2_), channel_id=1, source_target_pairs={{0,32},{1,97},{2,34},{3,99},{4,36},{5,101},{6,38},{7,103},{8,40},{... | collective-permute-start | bytes 393224 | tf_op jit(solution)/shard_map/ppermute | solution.py:43
  16.3 6.5 %collective-permute-start.9 = (bf16[256,512]{1,0:T(8,128)(2,1)S(1)}, bf16[256,512]{1,0:T(8,128)(2,1)S(1)}, u32[]{:S(2)}, u32[]{:S(2)}) collective-permute-start(bf16[256,512]{1,0:T(8,128)(2,1)S(1)} %get-tuple-element.71.refs_0_), channel_id=1, source_target_pairs={{0,2},{1,7},{2,0},{3,5},{4,6},{5,3},{6,4},{7,1},{8,10},{9,15},{10,... | collective-permute-start | bytes 786440 | tf_op jit(solution)/shard_map/ppermute | solution.py:43
  16.6 6.5 %collective-permute-start.7 = (bf16[256,512]{1,0:T(8,128)(2,1)S(1)}, bf16[256,512]{1,0:T(8,128)(2,1)S(1)}, u32[]{:S(2)}, u32[]{:S(2)}) collective-permute-start(bf16[256,512]{1,0:T(8,128)(2,1)S(1)} %get-tuple-element.70.refs_0_), channel_id=1, source_target_pairs={{0,32},{1,97},{2,34},{3,99},{4,36},{5,101},{6,38},{7,103},{8,40},{... | collective-permute-start | bytes 786440 | tf_op jit(solution)/shard_map/ppermute | solution.py:43
  19.3 6.4 %collective-permute-start.5 = (bf16[256,512]{1,0:T(8,128)(2,1)S(1)}, bf16[256,512]{1,0:T(8,128)(2,1)S(1)}, u32[]{:S(2)}, u32[]{:S(2)}) collective-permute-start(bf16[256,512]{1,0:T(8,128)(2,1)S(1)} %get-tuple-element.69.refs_0_), channel_id=1, source_target_pairs={{0,8},{1,25},{2,10},{3,27},{4,12},{5,29},{6,14},{7,31},{8,0},{9,17... | collective-permute-start | bytes 786440 | tf_op jit(solution)/shard_map/ppermute | solution.py:43
  22.9 15.1 %copy-start = (bf16[192,512]{1,0:T(8,128)(2,1)S(1)}, bf16[192,512]{1,0:T(8,128)(2,1)}, u32[]{:S(2)}) copy-start(bf16[192,512]{1,0:T(8,128)(2,1)} %refs_10_.1) | copy-start | bytes 589828
  22.9 15.1 %copy-start.1 = (bf16[192,512]{1,0:T(8,128)(2,1)S(1)}, bf16[192,512]{1,0:T(8,128)(2,1)}, u32[]{:S(2)}) copy-start(bf16[192,512]{1,0:T(8,128)(2,1)} %refs_11_.1) | copy-start | bytes 589828
  22.9 5.5 %collective-permute-start.16 = (bf16[512,512]{1,0:T(8,128)(2,1)S(1)}, bf16[512,512]{1,0:T(8,128)(2,1)S(1)}, u32[]{:S(2)}, u32[]{:S(2)}) collective-permute-start(bf16[512,512]{1,0:T(8,128)(2,1)S(1)} %join_rows.5.m2), channel_id=1, source_target_pairs={{0,1},{1,0},{2,3},{3,2},{4,5},{5,4},{6,7},{7,6},{8,9},{9,8},{10,11... | collective-permute-start | bytes 1572872 | tf_op jit(solution)/shard_map/ppermute | solution.py:47
  23.0 9.3 %collective-permute-start.10 = (bf16[512,512]{1,0:T(8,128)(2,1)S(1)}, bf16[512,512]{1,0:T(8,128)(2,1)S(1)}, u32[]{:S(2)}, u32[]{:S(2)}) collective-permute-start(bf16[512,512]{1,0:T(8,128)(2,1)S(1)} %join_rows.5.m2), channel_id=1, source_target_pairs={{0,8},{1,25},{2,10},{3,27},{4,12},{5,29},{6,14},{7,31},{8,0},{9,17... | collective-permute-start | bytes 1572872 | tf_op jit(solution)/shard_map/ppermute | solution.py:43
  23.1 9.5 %collective-permute-start.8 = (bf16[512,512]{1,0:T(8,128)(2,1)S(1)}, bf16[512,512]{1,0:T(8,128)(2,1)S(1)}, u32[]{:S(2)}, u32[]{:S(2)}) collective-permute-start(bf16[512,512]{1,0:T(8,128)(2,1)S(1)} %join_rows.4.m1), channel_id=1, source_target_pairs={{0,2},{1,7},{2,0},{3,5},{4,6},{5,3},{6,4},{7,1},{8,10},{9,15},{10,... | collective-permute-start | bytes 1572872 | tf_op jit(solution)/shard_map/ppermute | solution.py:43
  25.7 9.3 %collective-permute-start.6 = (bf16[512,512]{1,0:T(8,128)(2,1)S(1)}, bf16[512,512]{1,0:T(8,128)(2,1)S(1)}, u32[]{:S(2)}, u32[]{:S(2)}) collective-permute-start(bf16[512,512]{1,0:T(8,128)(2,1)S(1)} %join_rows.3.m0), channel_id=1, source_target_pairs={{0,32},{1,97},{2,34},{3,99},{4,36},{5,101},{6,38},{7,103},{8,40},{... | collective-permute-start | bytes 1572872 | tf_op jit(solution)/shard_map/ppermute | solution.py:43
  28.4 6.6 %collective-permute-start.15 = (bf16[512,512]{1,0:T(8,128)(2,1)S(1)}, bf16[512,512]{1,0:T(8,128)(2,1)S(1)}, u32[]{:S(2)}, u32[]{:S(2)}) collective-permute-start(bf16[512,512]{1,0:T(8,128)(2,1)S(1)} %join_rows.4.m1), channel_id=1, source_target_pairs={{0,1},{1,0},{2,3},{3,2},{4,5},{5,4},{6,7},{7,6},{8,9},{9,8},{10,11... | collective-permute-start | bytes 1572872 | tf_op jit(solution)/shard_map/ppermute | solution.py:47
  28.4 6.6 %collective-permute-start.14 = (bf16[512,512]{1,0:T(8,128)(2,1)S(1)}, bf16[512,512]{1,0:T(8,128)(2,1)S(1)}, u32[]{:S(2)}, u32[]{:S(2)}) collective-permute-start(bf16[512,512]{1,0:T(8,128)(2,1)S(1)} %join_rows.3.m0), channel_id=1, source_target_pairs={{0,1},{1,0},{2,3},{3,2},{4,5},{5,4},{6,7},{7,6},{8,9},{9,8},{10,11... | collective-permute-start | bytes 1572872 | tf_op jit(solution)/shard_map/ppermute | solution.py:47
  32.3 5.6 %collective-permute-start.13 = (bf16[512,512]{1,0:T(8,128)(2,1)S(1)}, bf16[512,512]{1,0:T(8,128)(2,1)S(1)}, u32[]{:S(2)}, u32[]{:S(2)}) collective-permute-start(bf16[512,512]{1,0:T(8,128)(2,1)S(1)} %collective-permute-done.10.refs_2_), channel_id=1, source_target_pairs={{0,1},{1,0},{2,3},{3,2},{4,5},{5,4},{6,7},{7,6},{8,9},{9,8},{10,11... | collective-permute-start | bytes 1572872 | tf_op jit(solution)/shard_map/ppermute | solution.py:47
  32.7 5.3 %collective-permute-start.12 = (bf16[512,512]{1,0:T(8,128)(2,1)S(1)}, bf16[512,512]{1,0:T(8,128)(2,1)S(1)}, u32[]{:S(2)}, u32[]{:S(2)}) collective-permute-start(bf16[512,512]{1,0:T(8,128)(2,1)S(1)} %collective-permute-done.8.refs_1_), channel_id=1, source_target_pairs={{0,1},{1,0},{2,3},{3,2},{4,5},{5,4},{6,7},{7,6},{8,9},{9,8},{10,11... | collective-permute-start | bytes 1572872 | tf_op jit(solution)/shard_map/ppermute | solution.py:47
  35.1 2.9 %collective-permute-start.11 = (bf16[512,512]{1,0:T(8,128)(2,1)S(1)}, bf16[512,512]{1,0:T(8,128)(2,1)S(1)}, u32[]{:S(2)}, u32[]{:S(2)}) collective-permute-start(bf16[512,512]{1,0:T(8,128)(2,1)S(1)} %collective-permute-done.6.refs_0_), channel_id=1, source_target_pairs={{0,1},{1,0},{2,3},{3,2},{4,5},{5,4},{6,7},{7,6},{8,9},{9,8},{10,11... | collective-permute-start | bytes 1572872 | tf_op jit(solution)/shard_map/ppermute | solution.py:47
  46.2 1.4 %collective-permute-start.17 = (f32[32,128]{1,0:T(8,128)S(1)}, f32[32,128]{1,0:T(8,128)S(1)}, u32[]{:S(2)}, u32[]{:S(2)}) collective-permute-start(f32[32,128]{1,0:T(8,128)S(1)} %get-tuple-element.77), channel_id=1, source_target_pairs={{0,1},{1,0},{2,3},{3,2},{4,5},{5,4},{6,7},{7,6},{8,9},{9,8},{10,11... | collective-permute-start | bytes 49160 | tf_op jit(solution)/shard_map/ppermute | solution.py:47
  47.6 3.9 %collective-permute-start.18 = (f32[32,128]{1,0:T(8,128)S(1)}, f32[32,128]{1,0:T(8,128)S(1)}, u32[]{:S(2)}, u32[]{:S(2)}) collective-permute-start(f32[32,128]{1,0:T(8,128)S(1)} %join.4.mine_ref), channel_id=1, source_target_pairs={{0,2},{1,7},{2,0},{3,5},{4,6},{5,3},{6,4},{7,1},{8,10},{9,15},{10,... | collective-permute-start | bytes 49160 | tf_op jit(solution)/shard_map/ppermute | solution.py:43
  51.5 3.9 %collective-permute-start.19 = (f32[32,128]{1,0:T(8,128)S(1)}, f32[32,128]{1,0:T(8,128)S(1)}, u32[]{:S(2)}, u32[]{:S(2)}) collective-permute-start(f32[32,128]{1,0:T(8,128)S(1)} %join.5.mine_ref), channel_id=1, source_target_pairs={{0,8},{1,25},{2,10},{3,27},{4,12},{5,29},{6,14},{7,31},{8,0},{9,17... | collective-permute-start | bytes 49160 | tf_op jit(solution)/shard_map/ppermute | solution.py:43
  55.4 3.9 %collective-permute-start.20 = (f32[32,128]{1,0:T(8,128)S(1)}, f32[32,128]{1,0:T(8,128)S(1)}, u32[]{:S(2)}, u32[]{:S(2)}) collective-permute-start(f32[32,128]{1,0:T(8,128)S(1)} %join.6.mine_ref), channel_id=1, source_target_pairs={{0,32},{1,97},{2,34},{3,99},{4,36},{5,101},{6,38},{7,103},{8,40},{... | collective-permute-start | bytes 49160 | tf_op jit(solution)/shard_map/ppermute | solution.py:43
  59.3 1.5 %collective-permute-start.21 = (f32[32,128]{1,0:T(8,128)S(1)}, f32[32,128]{1,0:T(8,128)S(1)}, u32[]{:S(2)}, u32[]{:S(2)}) collective-permute-start(f32[32,128]{1,0:T(8,128)S(1)} %join.7.mine_ref), channel_id=1, source_target_pairs={{0,1},{1,0},{2,3},{3,2},{4,5},{5,4},{6,7},{7,6},{8,9},{9,8},{10,11... | collective-permute-start | bytes 49160 | tf_op jit(solution)/shard_map/ppermute | solution.py:47
  67.3 3.0 %collective-permute-start.22 = (bf16[512,512]{1,0:T(8,128)(2,1)S(1)}, bf16[512,512]{1,0:T(8,128)(2,1)S(1)}, u32[]{:S(2)}, u32[]{:S(2)}) collective-permute-start(bf16[512,512]{1,0:T(8,128)(2,1)S(1)} %get-tuple-element.90), channel_id=1, source_target_pairs={{0,1},{1,0},{2,3},{3,2},{4,5},{5,4},{6,7},{7,6},{8,9},{9,8},{10,11... | collective-permute-start | bytes 1572872 | tf_op jit(solution)/shard_map/ppermute | solution.py:47
  68.6 4.6 %collective-permute-start.24 = (bf16[512,512]{1,0:T(8,128)(2,1)S(1)}, bf16[512,512]{1,0:T(8,128)(2,1)S(1)}, u32[]{:S(2)}, u32[]{:S(2)}) collective-permute-start(bf16[512,512]{1,0:T(8,128)(2,1)S(1)} %get-tuple-element.97), channel_id=1, source_target_pairs={{0,1},{1,0},{2,3},{3,2},{4,5},{5,4},{6,7},{7,6},{8,9},{9,8},{10,11... | collective-permute-start | bytes 1572872 | tf_op jit(solution)/shard_map/ppermute | solution.py:47
  70.0 3.8 %collective-permute-start.23 = (bf16[512,512]{1,0:T(8,128)(2,1)S(1)}, bf16[512,512]{1,0:T(8,128)(2,1)S(1)}, u32[]{:S(2)}, u32[]{:S(2)}) collective-permute-start(bf16[512,512]{1,0:T(8,128)(2,1)S(1)} %get-tuple-element.94), channel_id=1, source_target_pairs={{0,1},{1,0},{2,3},{3,2},{4,5},{5,4},{6,7},{7,6},{8,9},{9,8},{10,11... | collective-permute-start | bytes 1572872 | tf_op jit(solution)/shard_map/ppermute | solution.py:47
  70.4 10.2 %collective-permute-start.25 = (bf16[528,512]{1,0:T(8,128)(2,1)S(1)}, bf16[528,512]{1,0:T(8,128)(2,1)S(1)}, u32[]{:S(2)}, u32[]{:S(2)}) collective-permute-start(bf16[528,512]{1,0:T(8,128)(2,1)S(1)} %far_message.3.a0), channel_id=1, source_target_pairs={{0,32},{1,97},{2,34},{3,99},{4,36},{5,101},{6,38},{7,103},{8,40},{... | collective-permute-start | bytes 1622024 | tf_op jit(solution)/shard_map/ppermute | solution.py:43
  73.3 9.3 %collective-permute-start.31 = (bf16[512,512]{1,0:T(8,128)(2,1)S(1)}, bf16[512,512]{1,0:T(8,128)(2,1)S(1)}, u32[]{:S(2)}, u32[]{:S(2)}) collective-permute-start(bf16[512,512]{1,0:T(8,128)(2,1)S(1)} %far_message.5.a2), channel_id=1, source_target_pairs={{0,8},{1,25},{2,10},{3,27},{4,12},{5,29},{6,14},{7,31},{8,0},{9,17... | collective-permute-start | bytes 1572872 | tf_op jit(solution)/shard_map/ppermute | solution.py:43
  74.0 10.1 %collective-permute-start.28 = (bf16[512,512]{1,0:T(8,128)(2,1)S(1)}, bf16[512,512]{1,0:T(8,128)(2,1)S(1)}, u32[]{:S(2)}, u32[]{:S(2)}) collective-permute-start(bf16[512,512]{1,0:T(8,128)(2,1)S(1)} %far_message.4.a1), channel_id=1, source_target_pairs={{0,2},{1,7},{2,0},{3,5},{4,6},{5,3},{6,4},{7,1},{8,10},{9,15},{10,... | collective-permute-start | bytes 1572872 | tf_op jit(solution)/shard_map/ppermute | solution.py:43
  77.5 5.1 %collective-permute-start.32 = (bf16[512,512]{1,0:T(8,128)(2,1)S(1)}, bf16[512,512]{1,0:T(8,128)(2,1)S(1)}, u32[]{:S(2)}, u32[]{:S(2)}) collective-permute-start(bf16[512,512]{1,0:T(8,128)(2,1)S(1)} %get-tuple-element.113), channel_id=1, source_target_pairs={{0,1},{1,0},{2,3},{3,2},{4,5},{5,4},{6,7},{7,6},{8,9},{9,8},{10,11... | collective-permute-start | bytes 1572872 | tf_op jit(solution)/shard_map/ppermute | solution.py:47
  78.7 2.4 %collective-permute-start.26 = (bf16[512,512]{1,0:T(8,128)(2,1)S(1)}, bf16[512,512]{1,0:T(8,128)(2,1)S(1)}, u32[]{:S(2)}, u32[]{:S(2)}) collective-permute-start(bf16[512,512]{1,0:T(8,128)(2,1)S(1)} %get-tuple-element.100), channel_id=1, source_target_pairs={{0,1},{1,0},{2,3},{3,2},{4,5},{5,4},{6,7},{7,6},{8,9},{9,8},{10,11... | collective-permute-start | bytes 1572872 | tf_op jit(solution)/shard_map/ppermute | solution.py:47
  80.6 3.5 %collective-permute-start.29 = (bf16[512,512]{1,0:T(8,128)(2,1)S(1)}, bf16[512,512]{1,0:T(8,128)(2,1)S(1)}, u32[]{:S(2)}, u32[]{:S(2)}) collective-permute-start(bf16[512,512]{1,0:T(8,128)(2,1)S(1)} %get-tuple-element.107), channel_id=1, source_target_pairs={{0,1},{1,0},{2,3},{3,2},{4,5},{5,4},{6,7},{7,6},{8,9},{9,8},{10,11... | collective-permute-start | bytes 1572872 | tf_op jit(solution)/shard_map/ppermute | solution.py:47
  81.2 6.7 %collective-permute-start.27 = (bf16[272,512]{1,0:T(8,128)(2,1)S(1)}, bf16[272,512]{1,0:T(8,128)(2,1)S(1)}, u32[]{:S(2)}, u32[]{:S(2)}) collective-permute-start(bf16[272,512]{1,0:T(8,128)(2,1)S(1)} %get-tuple-element.103), channel_id=1, source_target_pairs={{0,8},{1,25},{2,10},{3,27},{4,12},{5,29},{6,14},{7,31},{8,0},{9,17... | collective-permute-start | bytes 835592 | tf_op jit(solution)/shard_map/ppermute | solution.py:43
  82.8 7.0 %collective-permute-start.33 = (bf16[256,512]{1,0:T(8,128)(2,1)S(1)}, bf16[256,512]{1,0:T(8,128)(2,1)S(1)}, u32[]{:S(2)}, u32[]{:S(2)}) collective-permute-start(bf16[256,512]{1,0:T(8,128)(2,1)S(1)} %get-tuple-element.115), channel_id=1, source_target_pairs={{0,2},{1,7},{2,0},{3,5},{4,6},{5,3},{6,4},{7,1},{8,10},{9,15},{10,... | collective-permute-start | bytes 786440 | tf_op jit(solution)/shard_map/ppermute | solution.py:43
  84.3 6.5 %collective-permute-start.30 = (bf16[256,512]{1,0:T(8,128)(2,1)S(1)}, bf16[256,512]{1,0:T(8,128)(2,1)S(1)}, u32[]{:S(2)}, u32[]{:S(2)}) collective-permute-start(bf16[256,512]{1,0:T(8,128)(2,1)S(1)} %get-tuple-element.109), channel_id=1, source_target_pairs={{0,32},{1,97},{2,34},{3,99},{4,36},{5,101},{6,38},{7,103},{8,40},{... | collective-permute-start | bytes 786440 | tf_op jit(solution)/shard_map/ppermute | solution.py:43
  88.0 8.0 %collective-permute-start.34 = (bf16[144,512]{1,0:T(8,128)(2,1)S(1)}, bf16[144,512]{1,0:T(8,128)(2,1)S(1)}, u32[]{:S(2)}, u32[]{:S(2)}) collective-permute-start(bf16[144,512]{1,0:T(8,128)(2,1)S(1)} %get-tuple-element.117), channel_id=1, source_target_pairs={{0,2},{1,7},{2,0},{3,5},{4,6},{5,3},{6,4},{7,1},{8,10},{9,15},{10,... | collective-permute-start | bytes 442376 | tf_op jit(solution)/shard_map/ppermute | solution.py:43
  89.9 5.1 %collective-permute-start.36 = (bf16[128,512]{1,0:T(8,128)(2,1)S(1)}, bf16[128,512]{1,0:T(8,128)(2,1)S(1)}, u32[]{:S(2)}, u32[]{:S(2)}) collective-permute-start(bf16[128,512]{1,0:T(8,128)(2,1)S(1)} %get-tuple-element.119), channel_id=1, source_target_pairs={{0,32},{1,97},{2,34},{3,99},{4,36},{5,101},{6,38},{7,103},{8,40},{... | collective-permute-start | bytes 393224 | tf_op jit(solution)/shard_map/ppermute | solution.py:43
  90.9 5.1 %collective-permute-start.35 = (bf16[128,512]{1,0:T(8,128)(2,1)S(1)}, bf16[128,512]{1,0:T(8,128)(2,1)S(1)}, u32[]{:S(2)}, u32[]{:S(2)}) collective-permute-start(bf16[128,512]{1,0:T(8,128)(2,1)S(1)} %get-tuple-element.118), channel_id=1, source_target_pairs={{0,8},{1,25},{2,10},{3,27},{4,12},{5,29},{6,14},{7,31},{8,0},{9,17... | collective-permute-start | bytes 393224 | tf_op jit(solution)/shard_map/ppermute | solution.py:43
  96.2 2.4 %collective-permute-start.37 = (f32[392,512]{1,0:T(8,128)S(1)}, f32[392,512]{1,0:T(8,128)S(1)}, u32[]{:S(2)}, u32[]{:S(2)}) collective-permute-start(f32[392,512]{1,0:T(8,128)S(1)} %get-tuple-element.125), channel_id=1, source_target_pairs={{0,1},{1,0},{2,3},{3,2},{4,5},{5,4},{6,7},{7,6},{8,9},{9,8},{10,11... | collective-permute-start | bytes 2408456 | tf_op jit(solution)/shard_map/ppermute | solution.py:47
